TPU v7x, 32 devices: a whole 2x2x4 slice. The times are simulated.
32 devices in a mesh: tiles: 4 (over y, core), coef: 8 (over z, x).
Axes of the slice: x: 2, y: 2, z: 4, core: 2. Of those that a mesh axis runs over, the one named last changes fastest.
Arguments:
- fields: bfloat16 [256, 2048], P('coef', 'tiles'), may hold values from -6 to 6
- adjoints: bfloat16 [256, 2048], P('coef', 'tiles'), may hold values from -6 to 6
- couple: bfloat16 [30, 256, 256], replicated, may hold values from -0.0625 to 0.0625
- tmatrices: bfloat16 [16, 256, 256], P('tiles', 'coef'), may hold values from -0.375 to 0.375
- neighbours: int32 [2048, 30], P('tiles'), may hold values from -1 to 2047, as said below
- classes: int32 [2048], P('tiles'), may hold values from 0 to 15
Outputs:
- forward_out: bfloat16 [256, 2048], P('coef', 'tiles')
- adjoint_out: bfloat16 [256, 2048], P('coef', 'tiles')
Inputs may be any that keep to these rules, and one draw needn't show every extreme that they name: neighbours[i, m] is -1 or i + m - 15 for m < 15, or i + m - 14 for m >= 15; links are mutual: neighbours[i, m] = j >= 0 exactly when neighbours[j, 29 - m] = i; slots 15 - 1 and 15 are filled wherever the neighbouring pillar exists.
All inputs are finite; a program needn't handle non-finite values.
Results may differ from a plain program's by a relative error of at most 0.0037.
Values may be sent and summed in bfloat16 or wider, within the bound.
No kernel may reach another device: no remote copies, remote signals or barrier semaphores. Data moves between devices by JAX's collectives and lax.ppermute only.
A program may use at most 64 MiB of HBM per device.

v0:
```python
import jax
import jax.numpy as jnp
from jax import lax
from jax.sharding import PartitionSpec as P

SLOTS = 30
HW = 15


def padded_2(cells, sides, width):
    for axis, dim in sides:
        count = lax.axis_size(axis)
        ends = count - 1
        head = lax.slice_in_dim(cells, 0, width, axis=dim)
        tail = lax.slice_in_dim(cells, cells.shape[dim] - width, cells.shape[dim], axis=dim)
        cells = jnp.concatenate(
            [
                lax.ppermute(tail, axis, [(i, (i + 1) % count) for i in range(ends)]),
                cells,
                lax.ppermute(head, axis, [((i + 1) % count, i) for i in range(ends)]),
            ],
            axis=dim,
        )
    return cells


def slot_columns(padded, weight_table, starts, width):
    pieces = [
        padded[:, start : start + width] * weight_table[slot][None, :]
        for slot, start in enumerate(starts)
    ]
    return jnp.stack(pieces, axis=1)


def local(fields, adjoints, couple, tmatrices, neighbours, classes):
    row_count = fields.shape[0]
    tile_len = fields.shape[1]
    coef_index = lax.axis_index("coef")
    is_valid = neighbours >= 0
    slot_weight = is_valid.astype(jnp.bfloat16).T
    forward_starts = [slot + (1 if slot >= HW else 0) for slot in range(SLOTS)]
    adjoint_starts = forward_starts[::-1]
    own_first = coef_index * row_count

    def translate(source, weight_table, starts, adjoint_mode):
        padded = padded_2(source, (("tiles", 1),), HW)
        own_mats = lax.dynamic_slice_in_dim(couple, own_first, row_count, 2 if adjoint_mode else 1)

        def add_piece(arrived):
            selected = slot_columns(arrived, weight_table, starts, tile_len)
            if adjoint_mode:
                block_mat = own_mats
                return jnp.einsum(
                    "nkr,kni->ri", block_mat, selected, preferred_element_type=jnp.float32
                )
            block_mat = own_mats
            return jnp.einsum(
                "nrk,kni->ri", block_mat, selected, preferred_element_type=jnp.float32
            )

        return add_piece(lax.all_gather(padded, "coef", axis=0, tiled=True))

    coupled = translate(fields, slot_weight, forward_starts, False).astype(jnp.bfloat16)
    class_rows = lax.all_gather(tmatrices, "tiles", axis=0, tiled=True)
    sub_table = class_rows
    picked = jnp.take(sub_table, classes, axis=0)
    applied = jnp.einsum(
        "irk,ki->ri",
        picked,
        lax.all_gather(coupled, "coef", axis=0, tiled=True),
        preferred_element_type=jnp.float32,
    )
    forward_out = (fields.astype(jnp.float32) - applied).astype(jnp.bfloat16)
    class_cols = lax.all_to_all(class_rows, "coef", split_axis=2, concat_axis=1, tiled=True)
    sub_table = class_cols
    picked = jnp.take(sub_table, classes, axis=0)
    scattered_sum = jnp.einsum(
        "irk,ri->ki",
        picked,
        lax.all_gather(adjoints, "coef", axis=0, tiled=True),
        preferred_element_type=jnp.float32,
    )
    scattered = scattered_sum.astype(jnp.bfloat16)
    returned = translate(scattered, slot_weight[::-1], adjoint_starts, True)
    adjoint_out = (adjoints.astype(jnp.float32) - returned).astype(jnp.bfloat16)
    return (forward_out, adjoint_out)


def solution(mesh):
    placed = (
        P("coef", "tiles"),
        P("coef", "tiles"),
        P(),
        P("tiles", "coef", None),
        P("tiles", None),
        P("tiles"),
    )
    return jax.shard_map(
        local,
        mesh=mesh,
        in_specs=placed,
        out_specs=(P("coef", "tiles"), P("coef", "tiles")),
        check_vma=False,
    )
```

profile of v0, /device:TPU:0, one launch (start us, length us, event | category | flops | bytes accessed | tf_op | source)
XLA Modules:
  0.0 210.4 jit_solution(16854447265328975594)
XLA Ops:
  0.6 0.8 fusion.138
  1.4 2.3 %collective-permute-start = (bf16[32,15]{1,0:T(8,128)(2,1)S(1)}, bf16[32,15]{1,0:T(8,128)(2,1)S(1)}, u32[]{:S(2)}, u32[]{:S(2)}) collective-permute-start(bf16[32,15]{1,0:T(8,128)(2,1)S(1)} %get-tuple-element.36), channel_id=1, source_target_pairs={{0,8},{8,16},{16,24},{1,9},{9,17},{17,25},{2,10},{10,18},{18,26},{... | collective-permute-start | bytes 2888 | tf_op jit(solution)/shard_map/ppermute | solution.py:18
  3.8 1.3 collective-permute-start.1
  5.1 9.3 %all_gather.17 = bf16[16,32,256]{2,1,0:T(8,128)(2,1)S(1)} all-gather(bf16[4,32,256]{2,1,0:T(8,128)(2,1)} %param.9), channel_id=1, replica_groups=mesh['tiles'=4,'coef'=8] {'tiles'}, dimensions={0}, use_global_device_ids=true | all-gather | bytes 327680 | tf_op jit(solution)/shard_map/all_gather | solution.py:64
  14.4 0.9 copy.12
  15.4 1.7 reshape.63
  17.0 5.8 %all-to-all-start = ((bf16[8,2,8192]{2,1,0:T(2,128)(2,1)}), bf16[8,2,8192]{2,1,0:T(2,128)(2,1)S(1)}, u32[]{:S(2)}, u32[]{:S(2)}) async-start(bf16[8,2,8192]{2,1,0:T(2,128)(2,1)} %reshape.63), calls=%async_computation | async-start | bytes 524288 | tf_op jit(solution)/shard_map/all_to_all | solution.py:74
  22.8 0.7 compare_and_fusion
  23.5 0.7 compare_select_fusion
  24.2 0.8 fusion.134
  25.3 31.5 %all_gather.18 = bf16[256,512]{1,0:T(8,128)(2,1)S(1)} all-gather(bf16[32,512]{1,0:T(8,128)(2,1)} %param.7), channel_id=1, replica_groups=mesh['tiles'=4,'coef'=8] {'coef'}, dimensions={0}, use_global_device_ids=true | all-gather | bytes 294912 | tf_op jit(solution)/shard_map/all_gather | solution.py:80
  57.1 13.5 %gather_fusion = bf16[512,32,256]{2,1,0:T(8,128)(2,1)} fusion(bf16[16,32,256]{2,1,0:T(8,128)(2,1)S(1)} %all_gather.17, s32[1024]{0:T(1024)S(1)} %pad_clamp_fusion), kind=kCustom, calls=%fused_computation | custom fusion | bytes 16779264 | tf_op jit(solution)/shard_map/jit(_take)/gather | solution.py:66
  70.6 31.0 %all_gather.15 = bf16[256,542]{1,0:T(8,128)(2,1)S(1)} all-gather(bf16[32,542]{1,0:T(8,128)(2,1)S(1)} %pad_maximum_fusion), channel_id=1, replica_groups=mesh['tiles'=4,'coef'=8] {'coef'}, dimensions={0}, use_global_device_ids=true | all-gather | bytes 312192 | tf_op jit(solution)/shard_map/all_gather | solution.py:61
  106.0 2.5 %fusion.8 = bf16[32,512]{1,0:T(8,128)(2,1)S(1)} fusion(bf16[256,30,512]{2,0,1:T(8,128)(2,1)S(1)} %fusion.74, bf16[30,256,256]{2,1,0:T(8,128)(2,1)} %param.8, s32[]{:T(128)S(6)} %select_n.19), kind=kOutput, calls=%fused_computation.9 | convolution fusion | flops 251674624 | bytes 8388612 | tf_op jit(solution)/shard_map/nrk,kni->ri/dot_general | solution.py:57
  108.5 31.0 %all_gather.16 = bf16[256,512]{1,0:T(8,128)(2,1)S(1)} all-gather(bf16[32,512]{1,0:T(8,128)(2,1)S(1)} %fusion.8), channel_id=1, replica_groups=mesh['tiles'=4,'coef'=8] {'coef'}, dimensions={0}, use_global_device_ids=true | all-gather | bytes 294912 | tf_op jit(solution)/shard_map/all_gather | solution.py:70
  140.2 0.7 copy.29
  140.9 0.7 all_to_all.16
  141.6 13.4 %gather_fusion.1 = bf16[512,256,32]{1,2,0:T(8,128)(2,1)} fusion(bf16[16,256,32]{1,2,0:T(8,128)(2,1)S(1)} %all_to_all.16, s32[1024]{0:T(1024)S(1)} %pad_clamp_fusion), kind=kCustom, calls=%fused_computation.1 | custom fusion | bytes 16779264 | tf_op jit(solution)/shard_map/jit(_take)/gather | solution.py:76
  155.1 11.0 %multiply_reduce_fusion = (bf16[512,32]{1,0:T(8,128)(2,1)S(1)}, f32[512,32]{1,0:T(8,128)S(1)}) fusion(f32[512,256]{1,0:T(8,128)S(1)} %copy.27, bf16[512,256,32]{1,2,0:T(8,128)(2,1)} %gather_fusion.1, pred[512]{0:T(512)(128)(4,1)S(1)} %compare_and_fusion, bf16[512,32,256]{2,1,0:T(8,128)(2,1)} %gather_fusion, f32[512,256]{1,0:T(8,128)S(1)} %copy.26), kind=kLoop, calls=%fused_computation.2 | loop fusion | flops 33521664 | bytes 17924608
  166.3 1.3 collective-permute-start.2
  167.6 1.3 collective-permute-start.3
  169.6 2.8 %collective-permute-done.3 = bf16[32,15]{1,0:T(8,128)(2,1)S(1)} collective-permute-done((bf16[32,15]{1,0:T(8,128)(2,1)S(1)}, bf16[32,15]{1,0:T(8,128)(2,1)S(1)}, u32[]{:S(2)}, u32[]{:S(2)}) %collective-permute-start.3) | collective-permute-done | bytes 992 | tf_op jit(solution)/shard_map/ppermute | solution.py:20
  172.5 31.1 %all_gather.19 = bf16[256,542]{1,0:T(8,128)(2,1)S(1)} all-gather(bf16[32,542]{1,0:T(8,128)(2,1)S(1)} %pad_maximum_fusion.1), channel_id=1, replica_groups=mesh['tiles'=4,'coef'=8] {'coef'}, dimensions={0}, use_global_device_ids=true | all-gather | bytes 312192 | tf_op jit(solution)/shard_map/all_gather | solution.py:61
  207.9 2.5 %fusion.9 = bf16[32,512]{1,0:T(8,128)(2,1)} fusion(bf16[256,30,512]{2,0,1:T(8,128)(2,1)S(1)} %fusion.14, bf16[30,256,256]{2,1,0:T(8,128)(2,1)S(1)} %copy-done, s32[]{:T(128)S(6)} %select_n.19, bf16[32,512]{1,0:T(8,128)(2,1)S(1)} %copy-done.2), kind=kOutput, calls=%fused_computation.10 | convolution fusion | flops 251707392 | bytes 9895940 | tf_op jit(solution)/shard_map/nkr,kni->ri/dot_general | solution.py:53
  (84 shorter events, 10.5 us)
Async XLA Ops:
  1.4 69.1 %collective-permute-start = (bf16[32,15]{1,0:T(8,128)(2,1)S(1)}, bf16[32,15]{1,0:T(8,128)(2,1)S(1)}, u32[]{:S(2)}, u32[]{:S(2)}) collective-permute-start(bf16[32,15]{1,0:T(8,128)(2,1)S(1)} %get-tuple-element.36), channel_id=1, source_target_pairs={{0,8},{8,16},{16,24},{1,9},{9,17},{17,25},{2,10},{10,18},{18,26},{... | collective-permute-start | bytes 2888 | tf_op jit(solution)/shard_map/ppermute | solution.py:18
  3.8 66.8 %collective-permute-start.1 = (bf16[32,15]{1,0:T(8,128)(2,1)S(1)}, bf16[32,15]{1,0:T(8,128)(2,1)S(1)}, u32[]{:S(2)}, u32[]{:S(2)}) collective-permute-start(bf16[32,15]{1,0:T(8,128)(2,1)S(1)} %get-tuple-element.37), channel_id=1, source_target_pairs={{8,0},{16,8},{24,16},{9,1},{17,9},{25,17},{10,2},{18,10},{26,18},{... | collective-permute-start | bytes 2888 | tf_op jit(solution)/shard_map/ppermute | solution.py:20
  17.0 122.7 %all-to-all-start = ((bf16[8,2,8192]{2,1,0:T(2,128)(2,1)}), bf16[8,2,8192]{2,1,0:T(2,128)(2,1)S(1)}, u32[]{:S(2)}, u32[]{:S(2)}) async-start(bf16[8,2,8192]{2,1,0:T(2,128)(2,1)} %reshape.63), calls=%async_computation | async-start | bytes 524288 | tf_op jit(solution)/shard_map/all_to_all | solution.py:74
  57.1 13.5 %copy-start.1 = (bf16[32,512]{1,0:T(8,128)(2,1)S(1)}, bf16[32,512]{1,0:T(8,128)(2,1)}, u32[]{:S(2)}) copy-start(bf16[32,512]{1,0:T(8,128)(2,1)} %param.6) | copy-start | bytes 98308
  166.3 3.3 %collective-permute-start.2 = (bf16[32,15]{1,0:T(8,128)(2,1)S(1)}, bf16[32,15]{1,0:T(8,128)(2,1)S(1)}, u32[]{:S(2)}, u32[]{:S(2)}) collective-permute-start(bf16[32,15]{1,0:T(8,128)(2,1)S(1)} %get-tuple-element.34), channel_id=1, source_target_pairs={{0,8},{8,16},{16,24},{1,9},{9,17},{17,25},{2,10},{10,18},{18,26},{... | collective-permute-start | bytes 2888 | tf_op jit(solution)/shard_map/ppermute | solution.py:18
  167.6 4.8 %collective-permute-start.3 = (bf16[32,15]{1,0:T(8,128)(2,1)S(1)}, bf16[32,15]{1,0:T(8,128)(2,1)S(1)}, u32[]{:S(2)}, u32[]{:S(2)}) collective-permute-start(bf16[32,15]{1,0:T(8,128)(2,1)S(1)} %get-tuple-element.35), channel_id=1, source_target_pairs={{8,0},{16,8},{24,16},{9,1},{17,9},{25,17},{10,2},{18,10},{26,18},{... | collective-permute-start | bytes 2888 | tf_op jit(solution)/shard_map/ppermute | solution.py:20
  203.6 4.3 %copy-start = (bf16[30,256,256]{2,1,0:T(8,128)(2,1)S(1)}, bf16[30,256,256]{2,1,0:T(8,128)(2,1)}, u32[]{:S(2)}) copy-start(bf16[30,256,256]{2,1,0:T(8,128)(2,1)} %param.8) | copy-start | bytes 11796484
  203.6 4.3 %copy-start.2 = (bf16[32,512]{1,0:T(8,128)(2,1)S(1)}, bf16[32,512]{1,0:T(8,128)(2,1)}, u32[]{:S(2)}) copy-start(bf16[32,512]{1,0:T(8,128)(2,1)} %param.7) | copy-start | bytes 98308
where the time goes:
time: 211 us; the launch traced here: 210 us
  blocking collectives  134 us (64%)
  local copies, waits for them, and re-layouts  33 us (16%)
  other arithmetic  22.4 us (11%)
  starting transfers between devices  12 us (6%)
  matrix products  4.95 us (2%)
  waiting for transfers between devices  2.79 us (1%)
    all_gather x2, blocking collectives, translate(): return add_piece(lax.all_gather(padded, 'coef', axis=0, tiled=True))  62.1 us
    all_gather x1, blocking collectives, local(): lax.all_gather(adjoints, 'coef', axis=0, tiled=True)  31.5 us
    all_gather x1, blocking collectives, local(): lax.all_gather(coupled, 'coef', axis=0, tiled=True)  31 us
    gather x2, local copies, waits for them, and re-layouts, local(): picked = jnp.take(sub_table, classes, axis=0)  26.9 us
    unnamed x61, other arithmetic  19.1 us
    all_gather x1, blocking collectives, local(): class_rows = lax.all_gather(tmatrices, 'tiles', axis=0, tiled=True)  9.35 us
    all_to_all x1, starting transfers between devices, local(): lax.all_to_all(class_rows, 'coef', split_axis=2, concat_axis=1, tiled=True)  5.81 us
  transfers between devices with their start and end apart: 5, of which 1 were waited for; matrix products, arithmetic and copies ran while one was open for 13% of the time, Pallas kernels for 0%

commit v1 on v0

v1 whole, which is shorter than its diff:
```python
import functools

import jax
import jax.numpy as jnp
from jax import lax
from jax.experimental import pallas as pl
from jax.experimental.pallas import tpu as pltpu
from jax.sharding import PartitionSpec as P

SLOTS = 30
HW = 15
EDGE = 128
CHUNK = 3
OFFSETS = [slot - HW + (1 if slot >= HW else 0) for slot in range(SLOTS)]
BF16 = jnp.bfloat16
F32 = jnp.float32
VMEM = pl.BlockSpec(memory_space=pltpu.VMEM)
SMEM = pl.BlockSpec(memory_space=pltpu.SMEM)
ANY = pl.BlockSpec(memory_space=pl.ANY)
PARAMS = pltpu.CompilerParams(vmem_limit_bytes=32 * 1024 * 1024)


def edges_of(cells):
    width = cells.shape[1]
    head, tail = cells[:, :EDGE], cells[:, width - EDGE :]
    lane = lax.broadcasted_iota(jnp.int32, head.shape, 1)
    return jnp.where(lane < EDGE // 2, head, tail)


def pack_kernel(t_ref, f_ref, a_ref, class_ref, near_ref, far_ref):
    count, rows, depth = t_ref.shape
    mats = count * rows
    width = f_ref.shape[1]
    fields, adjoints = f_ref[...], a_ref[...]
    class_edge = edges_of(class_ref[...]).astype(F32).astype(BF16)
    class_rows = jnp.broadcast_to(class_edge, (16, EDGE))
    for out_ref in (near_ref, far_ref):
        out_ref[:mats, :] = t_ref[...].reshape(mats, depth)
        out_ref[mats : mats + rows, :EDGE] = edges_of(fields)
        out_ref[mats : mats + rows, EDGE : 2 * EDGE] = edges_of(adjoints)
        out_ref[mats + rows : mats + rows + 16, :EDGE] = class_rows
        out_ref[mats + rows : mats + rows + 16, EDGE : 2 * EDGE] = class_rows
    base = mats + rows + 16
    for part in range(width // depth):
        lanes = slice(part * depth, (part + 1) * depth)
        far_ref[base + 2 * part * rows : base + (2 * part + 1) * rows, :] = fields[:, lanes]
        far_ref[base + (2 * part + 1) * rows : base + (2 * part + 2) * rows, :] = adjoints[:, lanes]


def pick_halo(place, piece_refs, masks, row_slice, lane_slice):
    tile = place[0]
    shape = (row_slice.stop - row_slice.start, EDGE)
    lane = lax.broadcasted_iota(jnp.int32, shape, 1)
    above = jnp.zeros(shape, F32)
    below = jnp.zeros(shape, F32)
    for piece_ref, mask in zip(piece_refs, masks):
        cells = piece_ref[row_slice, lane_slice].astype(F32)
        owner = tile ^ mask
        above = jnp.where(owner == tile + 1, cells, above)
        below = jnp.where(owner == tile - 1, cells, below)
    return jnp.where(lane < EDGE // 2, above, below)


def own_and_far(place, own, far):
    odd = place[1] == 1
    own32, far32 = own.astype(F32), far.astype(F32)
    return jnp.where(odd, far32, own32).astype(BF16), jnp.where(odd, own32, far32).astype(BF16)


def fields_kernel(masks, count, place, f_ref, far_ref, *refs):
    half = len(masks)
    near, across, out_ref = refs[:half], refs[half : 2 * half], refs[-1]
    rows, width = f_ref.shape
    depth = far_ref.shape[1]
    mats = count * rows
    base = mats + rows + 16
    edge_rows = slice(mats, mats + rows)
    lanes = slice(0, EDGE)
    first = pl.multiple_of(place[1] * rows, rows)
    second = pl.multiple_of((1 - place[1]) * rows, rows)
    out_ref[pl.ds(first, rows), :width] = f_ref[...]
    out_ref[pl.ds(first, rows), width:] = pick_halo(place, near, masks, edge_rows, lanes).astype(BF16)
    for part in range(width // depth):
        out_ref[pl.ds(second, rows), part * depth : (part + 1) * depth] = far_ref[
            base + 2 * part * rows : base + (2 * part + 1) * rows, :
        ]
    out_ref[pl.ds(second, rows), width:] = pick_halo(place, across, masks, edge_rows, lanes).astype(BF16)


def start_chunks(couple_ref, held, sems):
    for chunk in range(SLOTS // CHUNK):
        span = pl.ds(chunk * CHUNK, CHUNK)
        pltpu.make_async_copy(couple_ref.at[span], held.at[span], sems.at[chunk]).start()


def wait_chunk(couple_ref, held, sems, chunk):
    span = pl.ds(chunk * CHUNK, CHUNK)
    pltpu.make_async_copy(couple_ref.at[span], held.at[span], sems.at[chunk]).wait()


def couple_all(source, weight_ref, couple_ref, held, sems, adjoint_mode):
    span = source.shape[1]
    width = weight_ref.shape[1]
    total = None
    for chunk in range(SLOTS // CHUNK):
        wait_chunk(couple_ref, held, sems, chunk)
        for mat in range(chunk * CHUNK, (chunk + 1) * CHUNK):
            slot = SLOTS - 1 - mat if adjoint_mode else mat
            moved = pltpu.roll(source, (-OFFSETS[slot]) % span, 1)[:, :width]
            selected = moved * weight_ref[slot : slot + 1, :]
            dims = (((0 if adjoint_mode else 1,), (0,)), ((), ()))
            product = lax.dot_general(held[mat], selected, dims, preferred_element_type=F32)
            total = product if total is None else total + product
    return total


def adjoint_kernel(
    masks, place, ids_ref, a_ref, far_ref, class_ref, weight_ref, couple_ref, *refs
):
    half = len(masks)
    near, across = refs[:half], refs[half : 2 * half]
    send_ref, keep_ref, total_ref, expanded, stacked, held, sems = refs[2 * half :]
    start_chunks(couple_ref, held, sems)
    rows, width = a_ref.shape
    depth = far_ref.shape[1]
    count = ids_ref.shape[0] // half
    mats = count * rows
    base = mats + rows + 16
    edge_rows = slice(mats, mats + rows)
    lanes = slice(EDGE, 2 * EDGE)
    far_own = jnp.concatenate(
        [
            far_ref[base + (2 * part + 1) * rows : base + (2 * part + 2) * rows, :]
            for part in range(width // depth)
        ],
        axis=1,
    )
    padded = [
        jnp.concatenate([own, pick_halo(place, pieces, masks, edge_rows, lanes).astype(BF16)], axis=1)
        for own, pieces in ((a_ref[...], near), (far_own, across))
    ]
    class_halo = pick_halo(place, near, masks, slice(mats + rows, mats + rows + 16), slice(0, EDGE))
    labels = jnp.concatenate(
        [class_ref[...], class_halo[0:1, :].astype(jnp.int32)], axis=1
    )
    zero = jnp.zeros((), BF16)
    at = 0
    for piece in range(half):
        for which, pieces in ((0, near), (1, across)):
            stacked[at : at + mats, :] = pieces[piece][:mats, :]
            for local_class in range(count):
                hit = labels == ids_ref[piece * count + local_class]
                factor = jnp.where(hit, 1.0, 0.0).astype(BF16)
                expanded[at : at + rows, :] = padded[which] * factor
                at += rows
    scattered = lax.dot_general(
        stacked[...], expanded[...], (((0,), (0,)), ((), ())), preferred_element_type=F32
    ).astype(BF16)
    total_ref[...] = couple_all(scattered, weight_ref, couple_ref, held, sems, True)
    steps = keep_ref.shape[0]
    for rel in range(steps):
        start = pl.multiple_of(((place[2] ^ rel) * 2 + place[1]) * rows, rows)
        keep_ref[rel] = total_ref[pl.ds(start, rows), :]
        start = pl.multiple_of(((place[2] ^ (rel + steps)) * 2 + place[1]) * rows, rows)
        send_ref[rel] = total_ref[pl.ds(start, rows), :].astype(BF16)


def forward_kernel(
    masks, rels, place, ids_ref, f_ref, class_ref, weight_ref, couple_ref, *refs
):
    half, parts = len(masks), len(rels)
    near, pieces = refs[:half], refs[half : half + parts]
    out_ref, padded, held, sems = refs[half + parts :]
    start_chunks(couple_ref, held, sems)
    rows, width = f_ref.shape
    count = ids_ref.shape[0] // half
    mats = count * rows
    block = 2 * rows
    for rel, piece_ref in zip(rels, pieces):
        start = pl.multiple_of((place[2] ^ rel) * block, block)
        padded[pl.ds(start, block), :] = piece_ref[...]
    coupled = couple_all(padded[...], weight_ref, couple_ref, held, sems, False).astype(BF16)
    applied = jnp.zeros((rows, width), F32)
    labels = class_ref[...]
    for piece in range(half):
        product = jnp.dot(near[piece][:mats, :], coupled, preferred_element_type=F32)
        for local_class in range(count):
            hit = labels == ids_ref[piece * count + local_class]
            applied = jnp.where(hit, product[local_class * rows : (local_class + 1) * rows, :], applied)
    out_ref[...] = (f_ref[...].astype(F32) - applied).astype(BF16)


def local(fields, adjoints, couple, tmatrices, neighbours, classes):
    tiles, coefs = lax.axis_size("tiles"), lax.axis_size("coef")
    tile, coef = lax.axis_index("tiles"), lax.axis_index("coef")
    rows, width = fields.shape
    count, unused, depth = tmatrices.shape
    place = jnp.stack([tile, coef % 2, coef // 2]).astype(jnp.int32)

    def swap(cells, tile_mask, coef_mask):
        pairs = [
            (i * coefs + j, (i ^ tile_mask) * coefs + (j ^ coef_mask))
            for i in range(tiles)
            for j in range(coefs)
        ]
        return lax.ppermute(cells, ("tiles", "coef"), pairs)

    weights = (neighbours >= 0).astype(BF16).T
    labels = classes.reshape(1, width)
    mats = count * rows
    near_rows = mats + rows + 16
    far_rows = near_rows + 2 * rows * (width // depth)
    near_own, far_own = pl.pallas_call(
        pack_kernel,
        out_shape=(
            jax.ShapeDtypeStruct((near_rows, depth), BF16),
            jax.ShapeDtypeStruct((far_rows, depth), BF16),
        ),
        in_specs=[VMEM] * 4,
        out_specs=(VMEM, VMEM),
        compiler_params=PARAMS,
    )(tmatrices, fields, adjoints, labels)

    top = tiles // 2
    far = swap(far_own, 0, 1)
    near = {0: near_own, top: swap(near_own, top, 0)}
    across = {0: far, top: swap(near_own, top, 1)}
    bit = top // 2
    while bit >= 1:
        for group in (near, across):
            for mask, piece in list(group.items()):
                source = piece[:near_rows] if group is across else piece
                group[mask ^ bit] = swap(source, bit, 0)
        bit //= 2
    masks = sorted(near)
    near_list = [near[mask] for mask in masks]
    across_list = [across[mask] for mask in masks]
    ids = (
        (tile ^ jnp.array(masks, jnp.int32))[:, None] * count + jnp.arange(count, dtype=jnp.int32)
    ).reshape(-1).astype(jnp.int32)

    padded_fields = pl.pallas_call(
        functools.partial(fields_kernel, masks, count),
        out_shape=jax.ShapeDtypeStruct((2 * rows, width + EDGE), BF16),
        in_specs=[SMEM] + [VMEM] * (2 + 2 * len(masks)),
        out_specs=VMEM,
        compiler_params=PARAMS,
    )(place, fields, far, *near_list, *across_list)

    groups = coefs // 2
    gathered = {0: padded_fields}
    bit = groups // 2
    while bit >= 1:
        for rel, piece in list(gathered.items()):
            gathered[rel ^ bit] = swap(piece, 0, 2 * bit)
        bit //= 2
    rels = sorted(gathered)

    held = pltpu.VMEM((SLOTS,) + couple.shape[1:], BF16)
    sems = pltpu.SemaphoreType.DMA((SLOTS // CHUNK,))
    steps = groups // 2
    total_rows = couple.shape[1]
    send, keep = pl.pallas_call(
        functools.partial(adjoint_kernel, masks),
        out_shape=(
            jax.ShapeDtypeStruct((steps, rows, width), BF16),
            jax.ShapeDtypeStruct((steps, rows, width), F32),
        ),
        in_specs=[SMEM, SMEM] + [VMEM] * 4 + [ANY] + [VMEM] * (2 * len(masks)),
        out_specs=(VMEM, VMEM),
        scratch_shapes=[
            pltpu.VMEM((total_rows, width), F32),
            pltpu.VMEM((2 * len(masks) * mats, width + EDGE), BF16),
            pltpu.VMEM((2 * len(masks) * mats, depth), BF16),
            held,
            sems,
        ],
        compiler_params=PARAMS,
    )(place, ids, adjoints, far, labels, weights, couple, *near_list, *across_list)

    bit = groups // 2
    while bit >= 1:
        arrived = swap(send, 0, 2 * bit)
        merged = keep + arrived.astype(F32)
        bit //= 2
        if bit >= 1:
            keep, send = merged[:bit], merged[bit:].astype(BF16)
    adjoint_out = (adjoints.astype(F32) - merged[0]).astype(BF16)

    forward_out = pl.pallas_call(
        functools.partial(forward_kernel, masks, rels),
        out_shape=jax.ShapeDtypeStruct((rows, width), BF16),
        in_specs=[SMEM, SMEM] + [VMEM] * 3 + [ANY] + [VMEM] * (len(masks) + len(rels)),
        out_specs=VMEM,
        scratch_shapes=[pltpu.VMEM((total_rows, width + EDGE), BF16), held, sems],
        compiler_params=PARAMS,
    )(place, ids, fields, labels, weights, couple, *near_list, *[gathered[rel] for rel in rels])
    return (forward_out, adjoint_out)


def solution(mesh):
    placed = (
        P("coef", "tiles"),
        P("coef", "tiles"),
        P(),
        P("tiles", "coef", None),
        P("tiles", None),
        P("tiles"),
    )
    return jax.shard_map(
        local,
        mesh=mesh,
        in_specs=placed,
        out_specs=(P("coef", "tiles"), P("coef", "tiles")),
        check_vma=False,
    )
```

time: 211 us -> 51.3 us (0.24)
  blocking collectives: 134 us -> 0 us
  local copies, waits for them, and re-layouts: 33 us -> 6.69 us
  other arithmetic: 22.4 us -> 1.65 us
  Pallas kernels: 0 us -> 16.9 us
  waiting for transfers between devices: 2.79 us -> 13.8 us
  matrix products: 4.95 us -> 0 us
    all_gather x5 -> x0, blocking collectives: 134 us -> none  [the longest x2 62.1 us: translate(): return add_piece(lax.all_gather(padded, 'coef', axis=0, tiled=True))]
    gather x2 -> x0, local copies, waits for them, and re-layouts: 26.9 us -> none  [local(): picked = jnp.take(sub_table, classes, axis=0)]
    unnamed x61 -> x0, other arithmetic: 19.1 us -> none
    pallas_call x0 -> x4, Pallas kernels: none -> 16.9 us  [the longest x1 8.32 us: local(): pl.pallas_call(functools.partial(adjoint_kernel, masks), out_shape=(jax.S...]
    ppermute x4 -> x12, waiting for transfers between devices: 2.79 us -> 13.8 us  [swap(): return lax.ppermute(cells, ('tiles', 'coef'), pairs)]
    all_to_all x1 -> x0, starting transfers between devices: 5.81 us -> none  [local(): lax.all_to_all(class_rows, 'coef', split_axis=2, concat_axis=1, tiled=True)]
    dot_general x2 -> x0, matrix products: 4.95 us -> none  [the longest x1 2.47 us: add_piece(): jnp.einsum('nrk,kni->ri', block_mat, selected, preferred_element_type=jnp...]
    ppermute x4 -> x12, starting transfers between devices: 6.22 us -> 11.1 us  [swap(): return lax.ppermute(cells, ('tiles', 'coef'), pairs)]
  transfers between devices with their start and end apart: 5 -> 12, of which waited for: 1 -> 8; matrix products, arithmetic and copies ran while one was open for 13% -> 3% of each run, Pallas kernels for 0% -> 1%
where the time goes in v1:
time: 51.3 us; the launch traced here: 50.8 us
  Pallas kernels  16.9 us (33%)
  waiting for transfers between devices  13.8 us (27%)
  starting transfers between devices  11.1 us (22%)
  local copies, waits for them, and re-layouts  6.69 us (13%)
  other arithmetic  1.65 us (3%)
  between operations  0.7 us (1%)
    ppermute x12, waiting for transfers between devices, swap(): return lax.ppermute(cells, ('tiles', 'coef'), pairs)  13.8 us
    ppermute x12, starting transfers between devices, swap(): return lax.ppermute(cells, ('tiles', 'coef'), pairs)  11.1 us
    pallas_call x1, Pallas kernels, local(): pl.pallas_call(functools.partial(adjoint_kernel, masks), out_shape=(jax.S...  8.32 us
    pallas_call x1, Pallas kernels, local(): pl.pallas_call(functools.partial(forward_kernel, masks, rels), out_shape=...  8.03 us
    unnamed x20, local copies, waits for them, and re-layouts  6.59 us
  transfers between devices with their start and end apart: 12, of which 8 were waited for; matrix products, arithmetic and copies ran while one was open for 3% of the time, Pallas kernels for 1%

profile of v1, /device:TPU:0, one launch (start us, length us, event | category | flops | bytes accessed | tf_op | source)
XLA Modules:
  0.0 50.8 jit_solution(267575625003777884)
XLA Ops:
  0.6 0.7 %copy-done.2 = bf16[32,512]{1,0:T(8,128)(2,1)S(1)} copy-done((bf16[32,512]{1,0:T(8,128)(2,1)S(1)}, bf16[32,512]{1,0:T(8,128)(2,1)}, u32[]{:S(2)}) %copy-start.2) | copy-done | bytes 32792
  1.4 0.8 %copy-done.5 = bf16[32,512]{1,0:T(8,128)(2,1)S(1)} copy-done((bf16[32,512]{1,0:T(8,128)(2,1)S(1)}, bf16[32,512]{1,0:T(8,128)(2,1)}, u32[]{:S(2)}) %copy-start.5) | copy-done | bytes 32792
  2.2 0.8 %copy-done.7 = bf16[4,32,256]{2,1,0:T(8,128)(2,1)S(1)} copy-done((bf16[4,32,256]{2,1,0:T(8,128)(2,1)S(1)}, bf16[4,32,256]{2,1,0:T(8,128)(2,1)}, u32[]{:S(2)}) %copy-start.7) | copy-done | bytes 65560
  3.0 0.7 %copy-done.8 = s32[512]{0:T(512)S(1)} copy-done((s32[512]{0:T(512)S(1)}, s32[512]{0:T(512)}, u32[]{:S(2)}) %copy-start.8) | copy-done | bytes 2072
  3.7 4.0 %collective-permute-start.5 = (bf16[176,256]{1,0:T(8,128)(2,1)S(1)}, bf16[176,256]{1,0:T(8,128)(2,1)S(1)}, u32[]{:S(2)}, u32[]{:S(2)}) collective-permute-start(bf16[176,256]{1,0:T(8,128)(2,1)S(1)} %get-tuple-element.6.refs_0_), channel_id=1, source_target_pairs={{0,17},{1,16},{2,19},{3,18},{4,21},{5,20},{6,23},{7,22},{8,25},{9,... | collective-permute-start | bytes 270344 | tf_op jit(solution)/shard_map/ppermute | solution.py:206
  8.3 0.8 %fusion.3.weight_ref = bf16[30,512]{1,0:T(8,128)(2,1)S(1)} fusion(s32[512,30]{0,1:T(8,128)} %param.11), kind=kLoop, calls=%fused_computation.7 | loop fusion | flops 30720 | bytes 92160 | tf_op jit(solution)/shard_map/transpose | solution.py:208
  9.3 1.0 %collective-permute-done.5.refs_6_ = bf16[176,256]{1,0:T(8,128)(2,1)S(1)} collective-permute-done((bf16[176,256]{1,0:T(8,128)(2,1)S(1)}, bf16[176,256]{1,0:T(8,128)(2,1)S(1)}, u32[]{:S(2)}, u32[]{:S(2)}) %collective-permute-start.5) | collective-permute-done | bytes 90144 | tf_op jit(solution)/shard_map/ppermute | solution.py:206
  10.3 1.9 %collective-permute-done.1.refs_2_ = bf16[176,256]{1,0:T(8,128)(2,1)S(1)} collective-permute-done((bf16[176,256]{1,0:T(8,128)(2,1)S(1)}, bf16[176,256]{1,0:T(8,128)(2,1)S(1)}, u32[]{:S(2)}, u32[]{:S(2)}) %collective-permute-start.1) | collective-permute-done | bytes 90144 | tf_op jit(solution)/shard_map/ppermute | solution.py:206
  12.2 2.4 %collective-permute-done.3.far_ref.refs_4_ = bf16[304,256]{1,0:T(8,128)(2,1)S(1)} collective-permute-done((bf16[304,256]{1,0:T(8,128)(2,1)S(1)}, bf16[304,256]{1,0:T(8,128)(2,1)S(1)}, u32[]{:S(2)}, u32[]{:S(2)}) %collective-permute-start.3) | collective-permute-done | bytes 155680 | tf_op jit(solution)/shard_map/ppermute | solution.py:206
  14.8 1.2 %collective-permute-done.4.refs_5_ = bf16[176,256]{1,0:T(8,128)(2,1)S(1)} collective-permute-done((bf16[176,256]{1,0:T(8,128)(2,1)S(1)}, bf16[176,256]{1,0:T(8,128)(2,1)S(1)}, u32[]{:S(2)}, u32[]{:S(2)}) %collective-permute-start.4) | collective-permute-done | bytes 90144 | tf_op jit(solution)/shard_map/ppermute | solution.py:206
  16.0 2.1 %copy-done = bf16[30,256,256]{2,1,0:T(8,128)(2,1)S(1)} copy-done((bf16[30,256,256]{2,1,0:T(8,128)(2,1)S(1)}, bf16[30,256,256]{2,1,0:T(8,128)(2,1)}, u32[]{:S(2)}) %copy-start) | copy-done | bytes 3932184
  18.1 0.8 %copy-done.3 = bf16[32,512]{1,0:T(8,128)(2,1)S(1)} copy-done((bf16[32,512]{1,0:T(8,128)(2,1)S(1)}, bf16[32,512]{1,0:T(8,128)(2,1)}, u32[]{:S(2)}) %copy-start.3) | copy-done | bytes 32792
  18.8 0.7 %copy-done.9 = s32[512]{0:T(512)S(1)} copy-done((s32[512]{0:T(512)S(1)}, s32[512]{0:T(512)}, u32[]{:S(2)}) %copy-start.9) | copy-done | bytes 2072
  19.5 8.3 %shard_map.89 = (bf16[2,32,512]{2,1,0:T(8,128)(2,1)S(1)}, f32[2,32,512]{2,1,0:T(8,128)S(1)}) custom-call(s32[3]{0:T(128)S(1)} %pad_add_fusion.place, s32[16]{0:T(128)S(1)} %add.32.ids_ref, bf16[32,512]{1,0:T(8,128)(2,1)S(1)} %copy-done.3, bf16[304,256]{1,0:T(8,128)(2,1)S(1)} %collective-permute-done.3.far_ref.refs_4_, s32[1,512]{1,0:T(1,128)S(1)} %bitcast.13, ...), custom_call_target="tpu_custom_call" | custom-call | tf_op jit(solution)/shard_map/pallas_call | solution.py:263
  27.8 2.7 %collective-permute-start.10 = (bf16[2,32,512]{2,1,0:T(8,128)(2,1)S(1)}, bf16[2,32,512]{2,1,0:T(8,128)(2,1)S(1)}, u32[]{:S(2)}, u32[]{:S(2)}) collective-permute-start(bf16[2,32,512]{2,1,0:T(8,128)(2,1)S(1)} %get-tuple-element.9), channel_id=1, source_target_pairs={{0,4},{1,5},{2,6},{3,7},{4,0},{5,1},{6,2},{7,3},{8,12},{9,13},{10,... | collective-permute-start | bytes 196616 | tf_op jit(solution)/shard_map/ppermute | solution.py:206
  30.5 0.6 %shard_map.87.refs_4_ = bf16[64,640]{1,0:T(8,128)(2,1)S(1)} custom-call(s32[3]{0:T(128)S(1)} %pad_add_fusion.place, bf16[32,512]{1,0:T(8,128)(2,1)S(1)} %copy-done.6, bf16[304,256]{1,0:T(8,128)(2,1)S(1)} %collective-permute-done.3.far_ref.refs_4_, bf16[176,256]{1,0:T(8,128)(2,1)S(1)} %get-tuple-element.6.refs_0_, ...), custom_call_target="tpu_custom_call" | custom-call | tf_op jit(solution)/shard_map/pallas_call | solution.py:242
  31.5 3.0 %collective-permute-done.10 = bf16[2,32,512]{2,1,0:T(8,128)(2,1)S(1)} collective-permute-done((bf16[2,32,512]{2,1,0:T(8,128)(2,1)S(1)}, bf16[2,32,512]{2,1,0:T(8,128)(2,1)S(1)}, u32[]{:S(2)}, u32[]{:S(2)}) %collective-permute-start.10) | collective-permute-done | bytes 65568 | tf_op jit(solution)/shard_map/ppermute | solution.py:206
  34.5 2.4 %collective-permute-start.11 = (bf16[1,32,512]{2,1,0:T(8,128)(2,1)S(1)}, bf16[1,32,512]{2,1,0:T(8,128)(2,1)S(1)}, u32[]{:S(2)}, u32[]{:S(2)}) collective-permute-start(bf16[1,32,512]{2,1,0:T(8,128)(2,1)S(1)} %slice.24), channel_id=1, source_target_pairs={{0,2},{1,3},{2,0},{3,1},{4,6},{5,7},{6,4},{7,5},{8,10},{9,11},{10,... | collective-permute-start | bytes 98312 | tf_op jit(solution)/shard_map/ppermute | solution.py:206
  37.0 1.1 %collective-permute-done.8.refs_6_ = bf16[64,640]{1,0:T(8,128)(2,1)S(1)} collective-permute-done((bf16[64,640]{1,0:T(8,128)(2,1)S(1)}, bf16[64,640]{1,0:T(8,128)(2,1)S(1)}, u32[]{:S(2)}, u32[]{:S(2)}) %collective-permute-start.8) | collective-permute-done | bytes 81952 | tf_op jit(solution)/shard_map/ppermute | solution.py:206
  38.2 0.8 %collective-permute-start.9 = (bf16[64,640]{1,0:T(8,128)(2,1)S(1)}, bf16[64,640]{1,0:T(8,128)(2,1)S(1)}, u32[]{:S(2)}, u32[]{:S(2)}) collective-permute-start(bf16[64,640]{1,0:T(8,128)(2,1)S(1)} %collective-permute-done.8.refs_6_), channel_id=1, source_target_pairs={{0,2},{1,3},{2,0},{3,1},{4,6},{5,7},{6,4},{7,5},{8,10},{9,11},{10,... | collective-permute-start | bytes 245768 | tf_op jit(solution)/shard_map/ppermute | solution.py:206
  39.0 0.6 %fusion.2 = bf16[32,512]{1,0:T(8,128)(2,1)} fusion(f32[2,32,512]{2,1,0:T(8,128)S(1)} %convert_add_fusion, bf16[1,32,512]{2,1,0:T(8,128)(2,1)S(1)} %collective-permute-done.11, bf16[32,512]{1,0:T(8,128)(2,1)S(1)} %copy-done.4), kind=kLoop, calls=%fused_computation.5 | loop fusion | flops 81920 | bytes 163840 | tf_op jit(solution)/shard_map/convert_element_type | solution.py:288
  39.6 2.2 %collective-permute-done.7.refs_5_ = bf16[64,640]{1,0:T(8,128)(2,1)S(1)} collective-permute-done((bf16[64,640]{1,0:T(8,128)(2,1)S(1)}, bf16[64,640]{1,0:T(8,128)(2,1)S(1)}, u32[]{:S(2)}, u32[]{:S(2)}) %collective-permute-start.7) | collective-permute-done | bytes 81952 | tf_op jit(solution)/shard_map/ppermute | solution.py:206
  41.9 0.9 %collective-permute-done.9.refs_7_ = bf16[64,640]{1,0:T(8,128)(2,1)S(1)} collective-permute-done((bf16[64,640]{1,0:T(8,128)(2,1)S(1)}, bf16[64,640]{1,0:T(8,128)(2,1)S(1)}, u32[]{:S(2)}, u32[]{:S(2)}) %collective-permute-start.9) | collective-permute-done | bytes 81952 | tf_op jit(solution)/shard_map/ppermute | solution.py:206
  42.8 8.0 %shard_map.88 = bf16[32,512]{1,0:T(8,128)(2,1)} custom-call(s32[3]{0:T(128)S(1)} %pad_add_fusion.place, s32[16]{0:T(128)S(1)} %add.32.ids_ref, bf16[32,512]{1,0:T(8,128)(2,1)S(1)} %copy-done.6, s32[1,512]{1,0:T(1,128)S(1)} %bitcast.14, bf16[30,512]{1,0:T(8,128)(2,1)S(1)} %fusion.3.weight_ref, bf16[30,256,256]{2,1,0:T(8,128)(2,1)S(1)} %copy-done.1, ...), custom_call_target="tpu_custom_call" | custom-call | tf_op jit(solution)/shard_map/pallas_call | solution.py:290
  (33 shorter events, 1.5 us)
Async XLA Ops:
  0.6 0.8 %copy-start.2 = (bf16[32,512]{1,0:T(8,128)(2,1)S(1)}, bf16[32,512]{1,0:T(8,128)(2,1)}, u32[]{:S(2)}) copy-start(bf16[32,512]{1,0:T(8,128)(2,1)} %a_ref.3) | copy-start | bytes 98308
  1.4 0.8 %copy-start.5 = (bf16[32,512]{1,0:T(8,128)(2,1)S(1)}, bf16[32,512]{1,0:T(8,128)(2,1)}, u32[]{:S(2)}) copy-start(bf16[32,512]{1,0:T(8,128)(2,1)} %f_ref.5) | copy-start | bytes 98308
  2.1 0.8 %copy-start.7 = (bf16[4,32,256]{2,1,0:T(8,128)(2,1)S(1)}, bf16[4,32,256]{2,1,0:T(8,128)(2,1)}, u32[]{:S(2)}) copy-start(bf16[4,32,256]{2,1,0:T(8,128)(2,1)} %t_ref.1) | copy-start | bytes 196612
  3.0 0.7 %copy-start.8 = (s32[512]{0:T(512)S(1)}, s32[512]{0:T(512)}, u32[]{:S(2)}) copy-start(s32[512]{0:T(512)} %param.12) | copy-start | bytes 6148
  3.7 26.8 %copy-start.6 = (bf16[32,512]{1,0:T(8,128)(2,1)S(1)}, bf16[32,512]{1,0:T(8,128)(2,1)}, u32[]{:S(2)}) copy-start(bf16[32,512]{1,0:T(8,128)(2,1)} %f_ref.5) | copy-start | bytes 98308
  3.7 35.3 %copy-start.4 = (bf16[32,512]{1,0:T(8,128)(2,1)S(1)}, bf16[32,512]{1,0:T(8,128)(2,1)}, u32[]{:S(2)}) copy-start(bf16[32,512]{1,0:T(8,128)(2,1)} %a_ref.3) | copy-start | bytes 98308
  3.7 6.6 %collective-permute-start.5 = (bf16[176,256]{1,0:T(8,128)(2,1)S(1)}, bf16[176,256]{1,0:T(8,128)(2,1)S(1)}, u32[]{:S(2)}, u32[]{:S(2)}) collective-permute-start(bf16[176,256]{1,0:T(8,128)(2,1)S(1)} %get-tuple-element.6.refs_0_), channel_id=1, source_target_pairs={{0,17},{1,16},{2,19},{3,18},{4,21},{5,20},{6,23},{7,22},{8,25},{9,... | collective-permute-start | bytes 270344 | tf_op jit(solution)/shard_map/ppermute | solution.py:206
  7.7 4.5 %collective-permute-start.1 = (bf16[176,256]{1,0:T(8,128)(2,1)S(1)}, bf16[176,256]{1,0:T(8,128)(2,1)S(1)}, u32[]{:S(2)}, u32[]{:S(2)}) collective-permute-start(bf16[176,256]{1,0:T(8,128)(2,1)S(1)} %get-tuple-element.6.refs_0_), channel_id=1, source_target_pairs={{0,16},{1,17},{2,18},{3,19},{4,20},{5,21},{6,22},{7,23},{8,24},{9,... | collective-permute-start | bytes 270344 | tf_op jit(solution)/shard_map/ppermute | solution.py:206
  8.2 6.6 %collective-permute-start = (bf16[176,256]{1,0:T(8,128)(2,1)S(1)}, bf16[176,256]{1,0:T(8,128)(2,1)S(1)}, u32[]{:S(2)}, u32[]{:S(2)}) collective-permute-start(bf16[176,256]{1,0:T(8,128)(2,1)S(1)} %get-tuple-element.6.refs_0_), channel_id=1, source_target_pairs={{0,8},{1,9},{2,10},{3,11},{4,12},{5,13},{6,14},{7,15},{8,0},{9,1},... | collective-permute-start | bytes 270344 | tf_op jit(solution)/shard_map/ppermute | solution.py:206
  8.2 6.4 %collective-permute-start.3 = (bf16[304,256]{1,0:T(8,128)(2,1)S(1)}, bf16[304,256]{1,0:T(8,128)(2,1)S(1)}, u32[]{:S(2)}, u32[]{:S(2)}) collective-permute-start(bf16[304,256]{1,0:T(8,128)(2,1)S(1)} %get-tuple-element.7), channel_id=1, source_target_pairs={{0,1},{1,0},{2,3},{3,2},{4,5},{5,4},{6,7},{7,6},{8,9},{9,8},{10,11... | collective-permute-start | bytes 466952 | tf_op jit(solution)/shard_map/ppermute | solution.py:206
  10.3 4.4 %collective-permute-start.6 = (bf16[176,256]{1,0:T(8,128)(2,1)S(1)}, bf16[176,256]{1,0:T(8,128)(2,1)S(1)}, u32[]{:S(2)}, u32[]{:S(2)}) collective-permute-start(bf16[176,256]{1,0:T(8,128)(2,1)S(1)} %collective-permute-done.5.refs_6_), channel_id=1, source_target_pairs={{0,8},{1,9},{2,10},{3,11},{4,12},{5,13},{6,14},{7,15},{8,0},{9,1},... | collective-permute-start | bytes 270344 | tf_op jit(solution)/shard_map/ppermute | solution.py:206
  12.2 2.6 %collective-permute-start.2 = (bf16[176,256]{1,0:T(8,128)(2,1)S(1)}, bf16[176,256]{1,0:T(8,128)(2,1)S(1)}, u32[]{:S(2)}, u32[]{:S(2)}) collective-permute-start(bf16[176,256]{1,0:T(8,128)(2,1)S(1)} %collective-permute-done.1.refs_2_), channel_id=1, source_target_pairs={{0,8},{1,9},{2,10},{3,11},{4,12},{5,13},{6,14},{7,15},{8,0},{9,1},... | collective-permute-start | bytes 270344 | tf_op jit(solution)/shard_map/ppermute | solution.py:206
  14.6 1.4 %collective-permute-start.4 = (bf16[176,256]{1,0:T(8,128)(2,1)S(1)}, bf16[176,256]{1,0:T(8,128)(2,1)S(1)}, u32[]{:S(2)}, u32[]{:S(2)}) collective-permute-start(bf16[176,256]{1,0:T(8,128)(2,1)S(1)} %slice.13), channel_id=1, source_target_pairs={{0,8},{1,9},{2,10},{3,11},{4,12},{5,13},{6,14},{7,15},{8,0},{9,1},... | collective-permute-start | bytes 270344 | tf_op jit(solution)/shard_map/ppermute | solution.py:206
  16.0 2.1 %copy-start = (bf16[30,256,256]{2,1,0:T(8,128)(2,1)S(1)}, bf16[30,256,256]{2,1,0:T(8,128)(2,1)}, u32[]{:S(2)}) copy-start(bf16[30,256,256]{2,1,0:T(8,128)(2,1)} %couple_ref.3) | copy-start | bytes 11796484
  18.1 0.8 %copy-start.3 = (bf16[32,512]{1,0:T(8,128)(2,1)S(1)}, bf16[32,512]{1,0:T(8,128)(2,1)}, u32[]{:S(2)}) copy-start(bf16[32,512]{1,0:T(8,128)(2,1)} %a_ref.3) | copy-start | bytes 98308
  18.8 0.7 %copy-start.9 = (s32[512]{0:T(512)S(1)}, s32[512]{0:T(512)}, u32[]{:S(2)}) copy-start(s32[512]{0:T(512)} %param.12) | copy-start | bytes 6148
  19.5 23.2 %copy-start.1 = (bf16[30,256,256]{2,1,0:T(8,128)(2,1)S(1)}, bf16[30,256,256]{2,1,0:T(8,128)(2,1)}, u32[]{:S(2)}) copy-start(bf16[30,256,256]{2,1,0:T(8,128)(2,1)} %couple_ref.3) | copy-start | bytes 11796484
  27.8 6.6 %collective-permute-start.10 = (bf16[2,32,512]{2,1,0:T(8,128)(2,1)S(1)}, bf16[2,32,512]{2,1,0:T(8,128)(2,1)S(1)}, u32[]{:S(2)}, u32[]{:S(2)}) collective-permute-start(bf16[2,32,512]{2,1,0:T(8,128)(2,1)S(1)} %get-tuple-element.9), channel_id=1, source_target_pairs={{0,4},{1,5},{2,6},{3,7},{4,0},{5,1},{6,2},{7,3},{8,12},{9,13},{10,... | collective-permute-start | bytes 196616 | tf_op jit(solution)/shard_map/ppermute | solution.py:206
  31.1 7.1 %collective-permute-start.8 = (bf16[64,640]{1,0:T(8,128)(2,1)S(1)}, bf16[64,640]{1,0:T(8,128)(2,1)S(1)}, u32[]{:S(2)}, u32[]{:S(2)}) collective-permute-start(bf16[64,640]{1,0:T(8,128)(2,1)S(1)} %shard_map.87.refs_4_), channel_id=1, source_target_pairs={{0,4},{1,5},{2,6},{3,7},{4,0},{5,1},{6,2},{7,3},{8,12},{9,13},{10,... | collective-permute-start | bytes 245768 | tf_op jit(solution)/shard_map/ppermute | solution.py:206
  34.5 4.5 %collective-permute-start.11 = (bf16[1,32,512]{2,1,0:T(8,128)(2,1)S(1)}, bf16[1,32,512]{2,1,0:T(8,128)(2,1)S(1)}, u32[]{:S(2)}, u32[]{:S(2)}) collective-permute-start(bf16[1,32,512]{2,1,0:T(8,128)(2,1)S(1)} %slice.24), channel_id=1, source_target_pairs={{0,2},{1,3},{2,0},{3,1},{4,6},{5,7},{6,4},{7,5},{8,10},{9,11},{10,... | collective-permute-start | bytes 98312 | tf_op jit(solution)/shard_map/ppermute | solution.py:206
  37.0 4.9 %collective-permute-start.7 = (bf16[64,640]{1,0:T(8,128)(2,1)S(1)}, bf16[64,640]{1,0:T(8,128)(2,1)S(1)}, u32[]{:S(2)}, u32[]{:S(2)}) collective-permute-start(bf16[64,640]{1,0:T(8,128)(2,1)S(1)} %shard_map.87.refs_4_), channel_id=1, source_target_pairs={{0,2},{1,3},{2,0},{3,1},{4,6},{5,7},{6,4},{7,5},{8,10},{9,11},{10,... | collective-permute-start | bytes 245768 | tf_op jit(solution)/shard_map/ppermute | solution.py:206
  38.2 4.6 %collective-permute-start.9 = (bf16[64,640]{1,0:T(8,128)(2,1)S(1)}, bf16[64,640]{1,0:T(8,128)(2,1)S(1)}, u32[]{:S(2)}, u32[]{:S(2)}) collective-permute-start(bf16[64,640]{1,0:T(8,128)(2,1)S(1)} %collective-permute-done.8.refs_6_), channel_id=1, source_target_pairs={{0,2},{1,3},{2,0},{3,1},{4,6},{5,7},{6,4},{7,5},{8,10},{9,11},{10,... | collective-permute-start | bytes 245768 | tf_op jit(solution)/shard_map/ppermute | solution.py:206

commit v2 on v1

--- a/solution.py
+++ b/solution.py
@@ -10,14 +10,16 @@
 SLOTS = 30
 HW = 15
 EDGE = 128
-CHUNK = 3
+CHUNK = 5
 OFFSETS = [slot - HW + (1 if slot >= HW else 0) for slot in range(SLOTS)]
 BF16 = jnp.bfloat16
 F32 = jnp.float32
 VMEM = pl.BlockSpec(memory_space=pltpu.VMEM)
 SMEM = pl.BlockSpec(memory_space=pltpu.SMEM)
 ANY = pl.BlockSpec(memory_space=pl.ANY)
-PARAMS = pltpu.CompilerParams(vmem_limit_bytes=32 * 1024 * 1024)
+HBM = pl.BlockSpec(memory_space=pltpu.HBM)
+PARAMS = pltpu.CompilerParams(vmem_limit_bytes=24 * 1024 * 1024)
+FULL = pltpu.CompilerParams(vmem_limit_bytes=58 * 1024 * 1024)
 
 
 def edges_of(cells):
@@ -27,7 +29,17 @@
     return jnp.where(lane < EDGE // 2, head, tail)
 
 
-def pack_kernel(t_ref, f_ref, a_ref, class_ref, near_ref, far_ref):
+def pack_kernel(t_any, f_any, a_any, class_any, near_ref, far_ref, f_ref, a_ref, class_ref, t_ref, sems):
+    copies = [
+        pltpu.make_async_copy(source, target, sems.at[at])
+        for at, (source, target) in enumerate(
+            ((t_any, t_ref), (f_any, f_ref), (a_any, a_ref), (class_any, class_ref))
+        )
+    ]
+    for copy in copies:
+        copy.start()
+    for copy in copies:
+        copy.wait()
     count, rows, depth = t_ref.shape
     mats = count * rows
     width = f_ref.shape[1]
@@ -87,40 +99,39 @@
     out_ref[pl.ds(second, rows), width:] = pick_halo(place, across, masks, edge_rows, lanes).astype(BF16)
 
 
-def start_chunks(couple_ref, held, sems):
+def prepare_kernel(couple_ref, after_ref, plain_ref, turned_ref, sems):
+    copies = []
     for chunk in range(SLOTS // CHUNK):
         span = pl.ds(chunk * CHUNK, CHUNK)
-        pltpu.make_async_copy(couple_ref.at[span], held.at[span], sems.at[chunk]).start()
-
-
-def wait_chunk(couple_ref, held, sems, chunk):
-    span = pl.ds(chunk * CHUNK, CHUNK)
-    pltpu.make_async_copy(couple_ref.at[span], held.at[span], sems.at[chunk]).wait()
-
-
-def couple_all(source, weight_ref, couple_ref, held, sems, adjoint_mode):
+        copies.append(
+            pltpu.make_async_copy(couple_ref.at[span], plain_ref.at[span], sems.at[chunk])
+        )
+    for copy in copies:
+        copy.start()
+    for chunk, copy in enumerate(copies):
+        copy.wait()
+        for mat in range(chunk * CHUNK, (chunk + 1) * CHUNK):
+            turned_ref[SLOTS - 1 - mat] = plain_ref[mat].T
+
+
+def couple_all(source, weight_ref, mats_ref):
     span = source.shape[1]
     width = weight_ref.shape[1]
     total = None
-    for chunk in range(SLOTS // CHUNK):
-        wait_chunk(couple_ref, held, sems, chunk)
-        for mat in range(chunk * CHUNK, (chunk + 1) * CHUNK):
-            slot = SLOTS - 1 - mat if adjoint_mode else mat
-            moved = pltpu.roll(source, (-OFFSETS[slot]) % span, 1)[:, :width]
-            selected = moved * weight_ref[slot : slot + 1, :]
-            dims = (((0 if adjoint_mode else 1,), (0,)), ((), ()))
-            product = lax.dot_general(held[mat], selected, dims, preferred_element_type=F32)
-            total = product if total is None else total + product
+    for slot in range(SLOTS):
+        moved = pltpu.roll(source, (-OFFSETS[slot]) % span, 1)[:, :width]
+        selected = moved * weight_ref[slot : slot + 1, :]
+        product = jnp.dot(mats_ref[slot], selected, preferred_element_type=F32)
+        total = product if total is None else total + product
     return total
 
 
 def adjoint_kernel(
-    masks, place, ids_ref, a_ref, far_ref, class_ref, weight_ref, couple_ref, *refs
+    masks, place, ids_ref, a_ref, far_ref, class_ref, weight_ref, mats_ref, after_ref, *refs
 ):
     half = len(masks)
     near, across = refs[:half], refs[half : 2 * half]
-    send_ref, keep_ref, total_ref, expanded, stacked, held, sems = refs[2 * half :]
-    start_chunks(couple_ref, held, sems)
+    send_ref, keep_ref, total_ref, expanded, stacked = refs[2 * half :]
     rows, width = a_ref.shape
     depth = far_ref.shape[1]
     count = ids_ref.shape[0] // half
@@ -143,7 +154,6 @@
     labels = jnp.concatenate(
         [class_ref[...], class_halo[0:1, :].astype(jnp.int32)], axis=1
     )
-    zero = jnp.zeros((), BF16)
     at = 0
     for piece in range(half):
         for which, pieces in ((0, near), (1, across)):
@@ -156,7 +166,7 @@
     scattered = lax.dot_general(
         stacked[...], expanded[...], (((0,), (0,)), ((), ())), preferred_element_type=F32
     ).astype(BF16)
-    total_ref[...] = couple_all(scattered, weight_ref, couple_ref, held, sems, True)
+    total_ref[...] = couple_all(scattered, weight_ref, mats_ref)
     steps = keep_ref.shape[0]
     for rel in range(steps):
         start = pl.multiple_of(((place[2] ^ rel) * 2 + place[1]) * rows, rows)
@@ -165,29 +175,31 @@
         send_ref[rel] = total_ref[pl.ds(start, rows), :].astype(BF16)
 
 
-def forward_kernel(
-    masks, rels, place, ids_ref, f_ref, class_ref, weight_ref, couple_ref, *refs
-):
-    half, parts = len(masks), len(rels)
-    near, pieces = refs[:half], refs[half : half + parts]
-    out_ref, padded, held, sems = refs[half + parts :]
-    start_chunks(couple_ref, held, sems)
-    rows, width = f_ref.shape
-    count = ids_ref.shape[0] // half
-    mats = count * rows
-    block = 2 * rows
+def forward_kernel(rels, place, weight_ref, mats_ref, *refs):
+    pieces, out_ref, padded = refs[:-2], refs[-2], refs[-1]
+    block = pieces[0].shape[0]
     for rel, piece_ref in zip(rels, pieces):
         start = pl.multiple_of((place[2] ^ rel) * block, block)
         padded[pl.ds(start, block), :] = piece_ref[...]
-    coupled = couple_all(padded[...], weight_ref, couple_ref, held, sems, False).astype(BF16)
+    out_ref[...] = couple_all(padded[...], weight_ref, mats_ref).astype(BF16)
+
+
+def finish_kernel(masks, ids_ref, coupled_ref, f_ref, a_ref, class_ref, kept_ref, last_ref, *refs):
+    near, forward_ref, adjoint_ref = refs[:-2], refs[-2], refs[-1]
+    rows, width = f_ref.shape
+    count = ids_ref.shape[0] // len(masks)
+    mats = count * rows
+    coupled = coupled_ref[...]
     applied = jnp.zeros((rows, width), F32)
     labels = class_ref[...]
-    for piece in range(half):
+    for piece in range(len(masks)):
         product = jnp.dot(near[piece][:mats, :], coupled, preferred_element_type=F32)
         for local_class in range(count):
             hit = labels == ids_ref[piece * count + local_class]
             applied = jnp.where(hit, product[local_class * rows : (local_class + 1) * rows, :], applied)
-    out_ref[...] = (f_ref[...].astype(F32) - applied).astype(BF16)
+    forward_ref[...] = (f_ref[...].astype(F32) - applied).astype(BF16)
+    returned = kept_ref[0] + last_ref[0].astype(F32)
+    adjoint_ref[...] = (a_ref[...].astype(F32) - returned).astype(BF16)
 
 
 def local(fields, adjoints, couple, tmatrices, neighbours, classes):
@@ -210,16 +222,29 @@
     mats = count * rows
     near_rows = mats + rows + 16
     far_rows = near_rows + 2 * rows * (width // depth)
-    near_own, far_own = pl.pallas_call(
+    near_own, far_own, fields, adjoints, labels = pl.pallas_call(
         pack_kernel,
         out_shape=(
             jax.ShapeDtypeStruct((near_rows, depth), BF16),
             jax.ShapeDtypeStruct((far_rows, depth), BF16),
+            jax.ShapeDtypeStruct(fields.shape, BF16),
+            jax.ShapeDtypeStruct(adjoints.shape, BF16),
+            jax.ShapeDtypeStruct(labels.shape, jnp.int32),
         ),
-        in_specs=[VMEM] * 4,
+        in_specs=[HBM] * 4,
+        out_specs=(VMEM,) * 5,
+        scratch_shapes=[pltpu.VMEM(tmatrices.shape, BF16), pltpu.SemaphoreType.DMA((4,))],
+        compiler_params=FULL,
+    )(tmatrices, fields, adjoints, labels)
+    mats_plain, mats_turned = pl.pallas_call(
+        prepare_kernel,
+        out_shape=(jax.ShapeDtypeStruct(couple.shape, BF16),) * 2,
+        in_specs=[HBM, ANY],
         out_specs=(VMEM, VMEM),
-        compiler_params=PARAMS,
-    )(tmatrices, fields, adjoints, labels)
+        scratch_shapes=[pltpu.SemaphoreType.DMA((SLOTS // CHUNK,))],
+        cost_estimate=pl.CostEstimate(flops=0, bytes_accessed=4 * couple.size, transcendentals=0),
+        compiler_params=PARAMS,
+    )(couple, near_own)
 
     top = tiles // 2
     far = swap(far_own, 0, 1)
@@ -256,46 +281,50 @@
         bit //= 2
     rels = sorted(gathered)
 
-    held = pltpu.VMEM((SLOTS,) + couple.shape[1:], BF16)
-    sems = pltpu.SemaphoreType.DMA((SLOTS // CHUNK,))
     steps = groups // 2
     total_rows = couple.shape[1]
+    work = pl.CostEstimate(flops=2 * couple.size * width, bytes_accessed=2 * couple.size, transcendentals=0)
     send, keep = pl.pallas_call(
         functools.partial(adjoint_kernel, masks),
         out_shape=(
             jax.ShapeDtypeStruct((steps, rows, width), BF16),
             jax.ShapeDtypeStruct((steps, rows, width), F32),
         ),
-        in_specs=[SMEM, SMEM] + [VMEM] * 4 + [ANY] + [VMEM] * (2 * len(masks)),
+        in_specs=[SMEM, SMEM] + [VMEM] * 5 + [ANY] + [VMEM] * (2 * len(masks)),
         out_specs=(VMEM, VMEM),
         scratch_shapes=[
             pltpu.VMEM((total_rows, width), F32),
             pltpu.VMEM((2 * len(masks) * mats, width + EDGE), BF16),
             pltpu.VMEM((2 * len(masks) * mats, depth), BF16),
-            held,
-            sems,
         ],
-        compiler_params=PARAMS,
-    )(place, ids, adjoints, far, labels, weights, couple, *near_list, *across_list)
+        cost_estimate=work,
+        compiler_params=PARAMS,
+    )(place, ids, adjoints, far, labels, weights, mats_turned, padded_fields, *near_list, *across_list)
 
     bit = groups // 2
-    while bit >= 1:
-        arrived = swap(send, 0, 2 * bit)
+    arrived = swap(send, 0, 2 * bit)
+    while bit > 1:
         merged = keep + arrived.astype(F32)
         bit //= 2
-        if bit >= 1:
-            keep, send = merged[:bit], merged[bit:].astype(BF16)
-    adjoint_out = (adjoints.astype(F32) - merged[0]).astype(BF16)
-
-    forward_out = pl.pallas_call(
-        functools.partial(forward_kernel, masks, rels),
-        out_shape=jax.ShapeDtypeStruct((rows, width), BF16),
-        in_specs=[SMEM, SMEM] + [VMEM] * 3 + [ANY] + [VMEM] * (len(masks) + len(rels)),
+        keep = merged[:bit]
+        arrived = swap(merged[bit:].astype(BF16), 0, 2 * bit)
+
+    coupled = pl.pallas_call(
+        functools.partial(forward_kernel, rels),
+        out_shape=jax.ShapeDtypeStruct((total_rows, width), BF16),
+        in_specs=[SMEM] + [VMEM] * (2 + len(rels)),
         out_specs=VMEM,
-        scratch_shapes=[pltpu.VMEM((total_rows, width + EDGE), BF16), held, sems],
-        compiler_params=PARAMS,
-    )(place, ids, fields, labels, weights, couple, *near_list, *[gathered[rel] for rel in rels])
-    return (forward_out, adjoint_out)
+        scratch_shapes=[pltpu.VMEM((total_rows, width + EDGE), BF16)],
+        cost_estimate=work,
+        compiler_params=PARAMS,
+    )(place, weights, mats_plain, *[gathered[rel] for rel in rels])
+    return pl.pallas_call(
+        functools.partial(finish_kernel, masks),
+        out_shape=(jax.ShapeDtypeStruct((rows, width), BF16),) * 2,
+        in_specs=[SMEM] + [VMEM] * (6 + len(masks)),
+        out_specs=(VMEM, VMEM),
+        compiler_params=PARAMS,
+    )(ids, coupled, fields, adjoints, labels, keep, arrived, *near_list)
 
 
 def solution(mesh):

time: 51.3 us -> 42.6 us (0.83)
  waiting for transfers between devices: 13.8 us -> 5.33 us
  Pallas kernels: 16.9 us -> 14.2 us
  local copies, waits for them, and re-layouts: 6.69 us -> 8.96 us
  starting transfers between devices: 11.1 us -> 12 us
  other arithmetic: 1.65 us -> 1.01 us
    ppermute x12, waiting for transfers between devices: 13.8 us -> 5.33 us  [swap(): return lax.ppermute(cells, ('tiles', 'coef'), pairs)]
    pallas_call x1, Pallas kernels: 8.32 us -> 4.2 us  [local(): pl.pallas_call(functools.partial(adjoint_kernel, masks), out_shape=(jax.S...]
    unnamed x20, local copies, waits for them, and re-layouts: 6.59 us -> 8.86 us
    pallas_call x1, Pallas kernels: 0.02 us -> 1.62 us  [local(): pl.pallas_call(pack_kernel, out_shape=(jax.ShapeDtypeStruct((near_rows, d...]
    ppermute x12, starting transfers between devices: 11.1 us -> 12 us  [swap(): return lax.ppermute(cells, ('tiles', 'coef'), pairs)]
    convert_element_type x1 -> x0, other arithmetic: 0.63 us -> none  [local(): adjoint_out = (adjoints.astype(F32) - merged[0]).astype(BF16)]
    pallas_call x1 -> x3, Pallas kernels: 8.03 us -> 7.85 us  [the longest x1 3.76 us: local(): pl.pallas_call(functools.partial(forward_kernel, rels), out_shape=jax.Sha...]
  transfers between devices with their start and end apart: 12 -> 12, of which waited for: 8 -> 5; matrix products, arithmetic and copies ran while one was open for 3% -> 3% of each run, Pallas kernels for 1% -> 25%
where the time goes in v2:
time: 42.6 us; the launch traced here: 42.3 us
  Pallas kernels  14.2 us (33%)
  starting transfers between devices  12 us (28%)
  local copies, waits for them, and re-layouts  8.96 us (21%)
  waiting for transfers between devices  5.33 us (13%)
  other arithmetic  1.01 us (2%)
  between operations  0.75 us (2%)
    ppermute x12, starting transfers between devices, swap(): return lax.ppermute(cells, ('tiles', 'coef'), pairs)  12 us
    unnamed x20, local copies, waits for them, and re-layouts  8.86 us
    ppermute x12, waiting for transfers between devices, swap(): return lax.ppermute(cells, ('tiles', 'coef'), pairs)  5.33 us
    pallas_call x1, Pallas kernels, local(): pl.pallas_call(functools.partial(adjoint_kernel, masks), out_shape=(jax.S...  4.2 us
    pallas_call x1, Pallas kernels, local(): pl.pallas_call(functools.partial(forward_kernel, rels), out_shape=jax.Sha...  3.76 us
    pallas_call x1, Pallas kernels, local(): pl.pallas_call(prepare_kernel, out_shape=(jax.ShapeDtypeStruct(couple.sha...  2.62 us
    pallas_call x1, Pallas kernels, local(): pl.pallas_call(pack_kernel, out_shape=(jax.ShapeDtypeStruct((near_rows, d...  1.62 us
    pallas_call x1, Pallas kernels, local(): pl.pallas_call(functools.partial(finish_kernel, masks), out_shape=(jax.Sh...  1.47 us
  transfers between devices with their start and end apart: 12, of which 5 were waited for; matrix products, arithmetic and copies ran while one was open for 3% of the time, Pallas kernels for 25%

profile of v2, /device:TPU:0, one launch (start us, length us, event | category | flops | bytes accessed | tf_op | source)
XLA Modules:
  0.0 42.3 jit_solution(3726444160660104737)
XLA Ops:
  0.6 1.6 %shard_map.86 = (bf16[176,256]{1,0:T(8,128)(2,1)}, bf16[304,256]{1,0:T(8,128)(2,1)}, bf16[32,512]{1,0:T(8,128)(2,1)}, bf16[32,512]{1,0:T(8,128)(2,1)}, s32[1,512]{1,0:T(1,128)}) custom-call(bf16[4,32,256]{2,1,0:T(8,128)(2,1)} %t_any.1, bf16[32,512]{1,0:T(8,128)(2,1)} %f_any.1, bf16[32,512]{1,0:T(8,128)(2,1)} %a_any.1, s32[1,512]{1,0:T(1,128)} %bitcast.6), custom_call_target="tpu_custom_call" | custom-call | tf_op jit(solution)/shard_map/pallas_call | solution.py:225
  2.3 3.0 %collective-permute-start.2 = (bf16[176,256]{1,0:T(8,128)(2,1)}, bf16[176,256]{1,0:T(8,128)(2,1)S(1)}, u32[]{:S(2)}, u32[]{:S(2)}) collective-permute-start(bf16[176,256]{1,0:T(8,128)(2,1)} %get-tuple-element.11.after_ref.refs_0_), channel_id=1, source_target_pairs={{0,16},{1,17},{2,18},{3,19},{4,20},{5,21},{6,22},{7,23},{8,24},{9,... | collective-permute-start | bytes 270344 | tf_op jit(solution)/shard_map/ppermute | solution.py:218
  5.3 1.4 %collective-permute-start.5 = (bf16[176,256]{1,0:T(8,128)(2,1)}, bf16[176,256]{1,0:T(8,128)(2,1)S(1)}, u32[]{:S(2)}, u32[]{:S(2)}) collective-permute-start(bf16[176,256]{1,0:T(8,128)(2,1)} %get-tuple-element.11.after_ref.refs_0_), channel_id=1, source_target_pairs={{0,17},{1,16},{2,19},{3,18},{4,21},{5,20},{6,23},{7,22},{8,25},{9,... | collective-permute-start | bytes 270344 | tf_op jit(solution)/shard_map/ppermute | solution.py:218
  6.9 0.8 %fusion.weight_ref = bf16[30,512]{1,0:T(8,128)(2,1)S(1)} fusion(s32[512,30]{0,1:T(8,128)} %param.11), kind=kLoop, calls=%fused_computation.3 | loop fusion | flops 30720 | bytes 92160 | tf_op jit(solution)/shard_map/transpose | solution.py:220
  7.8 2.1 %copy-done = bf16[30,256,256]{2,1,0:T(8,128)(2,1)S(1)} copy-done((bf16[30,256,256]{2,1,0:T(8,128)(2,1)S(1)}, bf16[30,256,256]{2,1,0:T(8,128)(2,1)}, u32[]{:S(2)}) %copy-start) | copy-done | bytes 3932184
  9.9 0.9 %copy-done.1 = bf16[176,256]{1,0:T(8,128)(2,1)S(1)} copy-done((bf16[176,256]{1,0:T(8,128)(2,1)S(1)}, bf16[176,256]{1,0:T(8,128)(2,1)}, u32[]{:S(2)}) %copy-start.1) | copy-done | bytes 90136
  10.8 2.6 %shard_map.87 = (bf16[30,256,256]{2,1,0:T(8,128)(2,1)S(1)}, bf16[30,256,256]{2,1,0:T(8,128)(2,1)S(1)}) custom-call(bf16[30,256,256]{2,1,0:T(8,128)(2,1)S(1)} %copy-done, bf16[176,256]{1,0:T(8,128)(2,1)S(1)} %copy-done.1), custom_call_target="tpu_custom_call" | custom-call | bytes 7864320 | tf_op jit(solution)/shard_map/pallas_call | solution.py:239
  13.4 1.8 %copy-done.6 = bf16[30,256,256]{2,1,0:T(8,128)(2,1)} copy-done((bf16[30,256,256]{2,1,0:T(8,128)(2,1)}, bf16[30,256,256]{2,1,0:T(8,128)(2,1)S(1)}, u32[]{:S(2)}) %copy-start.6) | copy-done | bytes 3932184
  15.3 1.9 %copy-done.8 = bf16[30,256,256]{2,1,0:T(8,128)(2,1)} copy-done((bf16[30,256,256]{2,1,0:T(8,128)(2,1)}, bf16[30,256,256]{2,1,0:T(8,128)(2,1)S(1)}, u32[]{:S(2)}) %copy-start.8) | copy-done | bytes 3932184
  17.2 0.4 collective-permute-start.3
  17.8 0.5 %collective-permute-start.4 = (bf16[176,256]{1,0:T(8,128)(2,1)S(1)}, bf16[176,256]{1,0:T(8,128)(2,1)S(1)}, u32[]{:S(2)}, u32[]{:S(2)}) collective-permute-start(bf16[176,256]{1,0:T(8,128)(2,1)S(1)} %slice.13), channel_id=1, source_target_pairs={{0,8},{1,9},{2,10},{3,11},{4,12},{5,13},{6,14},{7,15},{8,0},{9,1},... | collective-permute-start | bytes 270344 | tf_op jit(solution)/shard_map/ppermute | solution.py:218
  18.3 0.3 collective-permute-done.3.refs_3_
  18.6 0.4 collective-permute-done.6.refs_7_
  18.9 0.2 collective-permute-done.4.refs_5_
  19.2 0.6 %shard_map.88.refs_0_.after_ref = bf16[64,640]{1,0:T(8,128)(2,1)S(1)} custom-call(s32[3]{0:T(128)S(1)} %pad_add_fusion.place, bf16[32,512]{1,0:T(8,128)(2,1)S(1)} %copy-done.3, bf16[304,256]{1,0:T(8,128)(2,1)S(1)} %collective-permute-done.far_ref.refs_4_, bf16[176,256]{1,0:T(8,128)(2,1)S(1)} %copy-done.2, ...), custom_call_target="tpu_custom_call" | custom-call | tf_op jit(solution)/shard_map/pallas_call | solution.py:267
  19.8 3.0 %collective-permute-start.8 = (bf16[64,640]{1,0:T(8,128)(2,1)S(1)}, bf16[64,640]{1,0:T(8,128)(2,1)S(1)}, u32[]{:S(2)}, u32[]{:S(2)}) collective-permute-start(bf16[64,640]{1,0:T(8,128)(2,1)S(1)} %shard_map.88.refs_0_.after_ref), channel_id=1, source_target_pairs={{0,4},{1,5},{2,6},{3,7},{4,0},{5,1},{6,2},{7,3},{8,12},{9,13},{10,... | collective-permute-start | bytes 245768 | tf_op jit(solution)/shard_map/ppermute | solution.py:218
  22.8 2.1 %copy-done.9 = bf16[30,256,256]{2,1,0:T(8,128)(2,1)S(1)} copy-done((bf16[30,256,256]{2,1,0:T(8,128)(2,1)S(1)}, bf16[30,256,256]{2,1,0:T(8,128)(2,1)}, u32[]{:S(2)}) %copy-start.9) | copy-done | bytes 3932184
  24.9 4.2 %shard_map.90 = (bf16[2,32,512]{2,1,0:T(8,128)(2,1)S(1)}, f32[2,32,512]{2,1,0:T(8,128)S(1)}) custom-call(s32[3]{0:T(128)S(1)} %pad_add_fusion.place, s32[16]{0:T(128)S(1)} %add.28.ids_ref, bf16[32,512]{1,0:T(8,128)(2,1)S(1)} %copy-done.4, bf16[304,256]{1,0:T(8,128)(2,1)S(1)} %collective-permute-done.far_ref.refs_4_, s32[1,512]{1,0:T(1,128)S(1)} %copy-done.5, ...), custom_call_target="tpu_custom_call" | custom-call | flops 2013265920 | bytes 3932160 | tf_op jit(solution)/shard_map/pallas_call | solution.py:287
  29.2 1.9 %collective-permute-start.7 = (bf16[64,640]{1,0:T(8,128)(2,1)S(1)}, bf16[64,640]{1,0:T(8,128)(2,1)S(1)}, u32[]{:S(2)}, u32[]{:S(2)}) collective-permute-start(bf16[64,640]{1,0:T(8,128)(2,1)S(1)} %shard_map.88.refs_0_.after_ref), channel_id=1, source_target_pairs={{0,2},{1,3},{2,0},{3,1},{4,6},{5,7},{6,4},{7,5},{8,10},{9,11},{10,... | collective-permute-start | bytes 245768 | tf_op jit(solution)/shard_map/ppermute | solution.py:218
  31.3 4.1 %collective-permute-done.10 = bf16[2,32,512]{2,1,0:T(8,128)(2,1)S(1)} collective-permute-done((bf16[2,32,512]{2,1,0:T(8,128)(2,1)S(1)}, bf16[2,32,512]{2,1,0:T(8,128)(2,1)S(1)}, u32[]{:S(2)}, u32[]{:S(2)}) %collective-permute-start.10) | collective-permute-done | bytes 65568 | tf_op jit(solution)/shard_map/ppermute | solution.py:218
  35.5 1.3 %collective-permute-start.11 = (bf16[1,32,512]{2,1,0:T(8,128)(2,1)S(1)}, bf16[1,32,512]{2,1,0:T(8,128)(2,1)S(1)}, u32[]{:S(2)}, u32[]{:S(2)}) collective-permute-start(bf16[1,32,512]{2,1,0:T(8,128)(2,1)S(1)} %slice.17), channel_id=1, source_target_pairs={{0,2},{1,3},{2,0},{3,1},{4,6},{5,7},{6,4},{7,5},{8,10},{9,11},{10,... | collective-permute-start | bytes 98312 | tf_op jit(solution)/shard_map/ppermute | solution.py:218
  36.7 0.3 collective-permute-done.9.refs_3_
  37.1 3.8 %shard_map.89.coupled_ref = bf16[256,512]{1,0:T(8,128)(2,1)S(1)} custom-call(s32[3]{0:T(128)S(1)} %pad_add_fusion.place, bf16[30,512]{1,0:T(8,128)(2,1)S(1)} %fusion.weight_ref, bf16[30,256,256]{2,1,0:T(8,128)(2,1)S(1)} %copy-done.7, bf16[64,640]{1,0:T(8,128)(2,1)S(1)} %shard_map.88.refs_0_.after_ref, bf16[64,640]{1,0:T(8,128)(2,1)S(1)} %collective-permute-done.7.refs_1_, ...), custom_call_target="tpu_custom_call" | custom-call | flops 2013265920 | bytes 3932160 | tf_op jit(solution)/shard_map/pallas_call | solution.py:312
  40.8 1.5 %shard_map.91 = (bf16[32,512]{1,0:T(8,128)(2,1)}, bf16[32,512]{1,0:T(8,128)(2,1)}) custom-call(s32[16]{0:T(128)S(1)} %add.28.ids_ref, bf16[256,512]{1,0:T(8,128)(2,1)S(1)} %shard_map.89.coupled_ref, bf16[32,512]{1,0:T(8,128)(2,1)S(1)} %copy-done.3, bf16[32,512]{1,0:T(8,128)(2,1)S(1)} %copy-done.4, s32[1,512]{1,0:T(1,128)S(1)} %copy-done.5, ...), custom_call_target="tpu_custom_call" | custom-call | tf_op jit(solution)/shard_map/pallas_call | solution.py:321
  (35 shorter events, 0.8 us)
Async XLA Ops:
  2.3 16.9 %copy-start.2 = (bf16[176,256]{1,0:T(8,128)(2,1)S(1)}, bf16[176,256]{1,0:T(8,128)(2,1)}, u32[]{:S(2)}) copy-start(bf16[176,256]{1,0:T(8,128)(2,1)} %get-tuple-element.11.after_ref.refs_0_) | copy-start | bytes 270340
  2.3 16.9 %copy-start.3 = (bf16[32,512]{1,0:T(8,128)(2,1)S(1)}, bf16[32,512]{1,0:T(8,128)(2,1)}, u32[]{:S(2)}) copy-start(bf16[32,512]{1,0:T(8,128)(2,1)} %get-tuple-element.13.f_ref) | copy-start | bytes 98308
  2.3 20.5 %copy-start.5 = (s32[1,512]{1,0:T(1,128)S(1)}, s32[1,512]{1,0:T(1,128)}, u32[]{:S(2)}) copy-start(s32[1,512]{1,0:T(1,128)} %get-tuple-element.16.class_ref) | copy-start | bytes 6148
  2.3 14.9 %collective-permute-start.2 = (bf16[176,256]{1,0:T(8,128)(2,1)}, bf16[176,256]{1,0:T(8,128)(2,1)S(1)}, u32[]{:S(2)}, u32[]{:S(2)}) collective-permute-start(bf16[176,256]{1,0:T(8,128)(2,1)} %get-tuple-element.11.after_ref.refs_0_), channel_id=1, source_target_pairs={{0,16},{1,17},{2,18},{3,19},{4,20},{5,21},{6,22},{7,23},{8,24},{9,... | collective-permute-start | bytes 270344 | tf_op jit(solution)/shard_map/ppermute | solution.py:218
  5.3 12.3 %collective-permute-start.5 = (bf16[176,256]{1,0:T(8,128)(2,1)}, bf16[176,256]{1,0:T(8,128)(2,1)S(1)}, u32[]{:S(2)}, u32[]{:S(2)}) collective-permute-start(bf16[176,256]{1,0:T(8,128)(2,1)} %get-tuple-element.11.after_ref.refs_0_), channel_id=1, source_target_pairs={{0,17},{1,16},{2,19},{3,18},{4,21},{5,20},{6,23},{7,22},{8,25},{9,... | collective-permute-start | bytes 270344 | tf_op jit(solution)/shard_map/ppermute | solution.py:218
  6.8 11.6 %collective-permute-start.1 = (bf16[176,256]{1,0:T(8,128)(2,1)}, bf16[176,256]{1,0:T(8,128)(2,1)S(1)}, u32[]{:S(2)}, u32[]{:S(2)}) collective-permute-start(bf16[176,256]{1,0:T(8,128)(2,1)} %get-tuple-element.11.after_ref.refs_0_), channel_id=1, source_target_pairs={{0,8},{1,9},{2,10},{3,11},{4,12},{5,13},{6,14},{7,15},{8,0},{9,1},... | collective-permute-start | bytes 270344 | tf_op jit(solution)/shard_map/ppermute | solution.py:218
  6.8 11.0 %collective-permute-start = (bf16[304,256]{1,0:T(8,128)(2,1)}, bf16[304,256]{1,0:T(8,128)(2,1)S(1)}, u32[]{:S(2)}, u32[]{:S(2)}) collective-permute-start(bf16[304,256]{1,0:T(8,128)(2,1)} %get-tuple-element.14), channel_id=1, source_target_pairs={{0,1},{1,0},{2,3},{3,2},{4,5},{5,4},{6,7},{7,6},{8,9},{9,8},{10,11... | collective-permute-start | bytes 466952 | tf_op jit(solution)/shard_map/ppermute | solution.py:218
  7.8 2.1 %copy-start = (bf16[30,256,256]{2,1,0:T(8,128)(2,1)S(1)}, bf16[30,256,256]{2,1,0:T(8,128)(2,1)}, u32[]{:S(2)}) copy-start(bf16[30,256,256]{2,1,0:T(8,128)(2,1)} %couple_ref.1) | copy-start | bytes 11796484
  9.9 0.9 %copy-start.1 = (bf16[176,256]{1,0:T(8,128)(2,1)S(1)}, bf16[176,256]{1,0:T(8,128)(2,1)}, u32[]{:S(2)}) copy-start(bf16[176,256]{1,0:T(8,128)(2,1)} %get-tuple-element.11.after_ref.refs_0_) | copy-start | bytes 270340
  10.8 12.0 %copy-start.4 = (bf16[32,512]{1,0:T(8,128)(2,1)S(1)}, bf16[32,512]{1,0:T(8,128)(2,1)}, u32[]{:S(2)}) copy-start(bf16[32,512]{1,0:T(8,128)(2,1)} %get-tuple-element.15.a_ref) | copy-start | bytes 98308
  13.4 1.9 %copy-start.6 = (bf16[30,256,256]{2,1,0:T(8,128)(2,1)}, bf16[30,256,256]{2,1,0:T(8,128)(2,1)S(1)}, u32[]{:S(2)}) copy-start(bf16[30,256,256]{2,1,0:T(8,128)(2,1)S(1)} %get-tuple-element.12.mats_ref) | copy-start | bytes 11796484
  15.3 1.9 %copy-start.8 = (bf16[30,256,256]{2,1,0:T(8,128)(2,1)}, bf16[30,256,256]{2,1,0:T(8,128)(2,1)S(1)}, u32[]{:S(2)}) copy-start(bf16[30,256,256]{2,1,0:T(8,128)(2,1)S(1)} %get-tuple-element.17.mats_ref) | copy-start | bytes 11796484
  17.2 1.3 %collective-permute-start.3 = (bf16[176,256]{1,0:T(8,128)(2,1)S(1)}, bf16[176,256]{1,0:T(8,128)(2,1)S(1)}, u32[]{:S(2)}, u32[]{:S(2)}) collective-permute-start(bf16[176,256]{1,0:T(8,128)(2,1)S(1)} %collective-permute-done.2.refs_2_), channel_id=1, source_target_pairs={{0,8},{1,9},{2,10},{3,11},{4,12},{5,13},{6,14},{7,15},{8,0},{9,1},... | collective-permute-start | bytes 270344 | tf_op jit(solution)/shard_map/ppermute | solution.py:218
  17.6 1.3 %collective-permute-start.6 = (bf16[176,256]{1,0:T(8,128)(2,1)S(1)}, bf16[176,256]{1,0:T(8,128)(2,1)S(1)}, u32[]{:S(2)}, u32[]{:S(2)}) collective-permute-start(bf16[176,256]{1,0:T(8,128)(2,1)S(1)} %collective-permute-done.5.refs_6_), channel_id=1, source_target_pairs={{0,8},{1,9},{2,10},{3,11},{4,12},{5,13},{6,14},{7,15},{8,0},{9,1},... | collective-permute-start | bytes 270344 | tf_op jit(solution)/shard_map/ppermute | solution.py:218
  17.8 1.4 %collective-permute-start.4 = (bf16[176,256]{1,0:T(8,128)(2,1)S(1)}, bf16[176,256]{1,0:T(8,128)(2,1)S(1)}, u32[]{:S(2)}, u32[]{:S(2)}) collective-permute-start(bf16[176,256]{1,0:T(8,128)(2,1)S(1)} %slice.13), channel_id=1, source_target_pairs={{0,8},{1,9},{2,10},{3,11},{4,12},{5,13},{6,14},{7,15},{8,0},{9,1},... | collective-permute-start | bytes 270344 | tf_op jit(solution)/shard_map/ppermute | solution.py:218
  19.8 11.3 %collective-permute-start.8 = (bf16[64,640]{1,0:T(8,128)(2,1)S(1)}, bf16[64,640]{1,0:T(8,128)(2,1)S(1)}, u32[]{:S(2)}, u32[]{:S(2)}) collective-permute-start(bf16[64,640]{1,0:T(8,128)(2,1)S(1)} %shard_map.88.refs_0_.after_ref), channel_id=1, source_target_pairs={{0,4},{1,5},{2,6},{3,7},{4,0},{5,1},{6,2},{7,3},{8,12},{9,13},{10,... | collective-permute-start | bytes 245768 | tf_op jit(solution)/shard_map/ppermute | solution.py:218
  22.8 2.1 %copy-start.9 = (bf16[30,256,256]{2,1,0:T(8,128)(2,1)S(1)}, bf16[30,256,256]{2,1,0:T(8,128)(2,1)}, u32[]{:S(2)}) copy-start(bf16[30,256,256]{2,1,0:T(8,128)(2,1)} %copy-done.8) | copy-start | bytes 11796484
  24.9 12.2 %copy-start.7 = (bf16[30,256,256]{2,1,0:T(8,128)(2,1)S(1)}, bf16[30,256,256]{2,1,0:T(8,128)(2,1)}, u32[]{:S(2)}) copy-start(bf16[30,256,256]{2,1,0:T(8,128)(2,1)} %copy-done.6) | copy-start | bytes 11796484
  29.1 6.3 %collective-permute-start.10 = (bf16[2,32,512]{2,1,0:T(8,128)(2,1)S(1)}, bf16[2,32,512]{2,1,0:T(8,128)(2,1)S(1)}, u32[]{:S(2)}, u32[]{:S(2)}) collective-permute-start(bf16[2,32,512]{2,1,0:T(8,128)(2,1)S(1)} %get-tuple-element.19), channel_id=1, source_target_pairs={{0,4},{1,5},{2,6},{3,7},{4,0},{5,1},{6,2},{7,3},{8,12},{9,13},{10,... | collective-permute-start | bytes 196616 | tf_op jit(solution)/shard_map/ppermute | solution.py:218
  29.2 7.5 %collective-permute-start.7 = (bf16[64,640]{1,0:T(8,128)(2,1)S(1)}, bf16[64,640]{1,0:T(8,128)(2,1)S(1)}, u32[]{:S(2)}, u32[]{:S(2)}) collective-permute-start(bf16[64,640]{1,0:T(8,128)(2,1)S(1)} %shard_map.88.refs_0_.after_ref), channel_id=1, source_target_pairs={{0,2},{1,3},{2,0},{3,1},{4,6},{5,7},{6,4},{7,5},{8,10},{9,11},{10,... | collective-permute-start | bytes 245768 | tf_op jit(solution)/shard_map/ppermute | solution.py:218
  31.1 6.0 %collective-permute-start.9 = (bf16[64,640]{1,0:T(8,128)(2,1)S(1)}, bf16[64,640]{1,0:T(8,128)(2,1)S(1)}, u32[]{:S(2)}, u32[]{:S(2)}) collective-permute-start(bf16[64,640]{1,0:T(8,128)(2,1)S(1)} %collective-permute-done.8.refs_2_), channel_id=1, source_target_pairs={{0,2},{1,3},{2,0},{3,1},{4,6},{5,7},{6,4},{7,5},{8,10},{9,11},{10,... | collective-permute-start | bytes 245768 | tf_op jit(solution)/shard_map/ppermute | solution.py:218
  35.5 5.4 %collective-permute-start.11 = (bf16[1,32,512]{2,1,0:T(8,128)(2,1)S(1)}, bf16[1,32,512]{2,1,0:T(8,128)(2,1)S(1)}, u32[]{:S(2)}, u32[]{:S(2)}) collective-permute-start(bf16[1,32,512]{2,1,0:T(8,128)(2,1)S(1)} %slice.17), channel_id=1, source_target_pairs={{0,2},{1,3},{2,0},{3,1},{4,6},{5,7},{6,4},{7,5},{8,10},{9,11},{10,... | collective-permute-start | bytes 98312 | tf_op jit(solution)/shard_map/ppermute | solution.py:218

commit v3 on v2

v3 whole, which is shorter than its diff:
```python
import functools

import jax
import jax.numpy as jnp
from jax import lax
from jax.experimental import pallas as pl
from jax.experimental.pallas import tpu as pltpu
from jax.sharding import PartitionSpec as P

SLOTS = 30
HW = 15
EDGE = 128
CHUNK = 5
EARLY = 22
OFFSETS = [slot - HW + (1 if slot >= HW else 0) for slot in range(SLOTS)]
BF16 = jnp.bfloat16
F32 = jnp.float32
VMEM = pl.BlockSpec(memory_space=pltpu.VMEM)
SMEM = pl.BlockSpec(memory_space=pltpu.SMEM)
ANY = pl.BlockSpec(memory_space=pl.ANY)
HBM = pl.BlockSpec(memory_space=pltpu.HBM)
PARAMS = pltpu.CompilerParams(vmem_limit_bytes=24 * 1024 * 1024)
WIDE = pltpu.CompilerParams(vmem_limit_bytes=24 * 1024 * 1024)
FULL = pltpu.CompilerParams(vmem_limit_bytes=58 * 1024 * 1024)


def edges_of(cells):
    width = cells.shape[1]
    head, tail = cells[:, :EDGE], cells[:, width - EDGE :]
    lane = lax.broadcasted_iota(jnp.int32, head.shape, 1)
    return jnp.where(lane < EDGE // 2, head, tail)


def pack_kernel(
    spot, t_any, f_any, a_any, class_any, place, near_ref, far_ref, f_ref, a_ref, class_ref, t_ref, sems
):
    place[0] = spot[0]
    place[1] = spot[1] & 1
    place[2] = spot[1] >> 1
    copies = [
        pltpu.make_async_copy(source, target, sems.at[at])
        for at, (source, target) in enumerate(
            ((t_any, t_ref), (f_any, f_ref), (a_any, a_ref), (class_any, class_ref))
        )
    ]
    for copy in copies:
        copy.start()
    for copy in copies:
        copy.wait()
    count, rows, depth = t_ref.shape
    mats = count * rows
    width = f_ref.shape[1]
    fields, adjoints = f_ref[...], a_ref[...]
    class_edge = edges_of(class_ref[...]).astype(F32).astype(BF16)
    class_rows = jnp.broadcast_to(class_edge, (16, EDGE))
    for out_ref in (near_ref, far_ref):
        out_ref[:mats, :] = t_ref[...].reshape(mats, depth)
        out_ref[mats : mats + rows, :EDGE] = edges_of(fields)
        out_ref[mats : mats + rows, EDGE : 2 * EDGE] = edges_of(adjoints)
        out_ref[mats + rows : mats + rows + 16, :EDGE] = class_rows
        out_ref[mats + rows : mats + rows + 16, EDGE : 2 * EDGE] = class_rows
    base = mats + rows + 16
    for part in range(width // depth):
        lanes = slice(part * depth, (part + 1) * depth)
        far_ref[base + 2 * part * rows : base + (2 * part + 1) * rows, :] = fields[:, lanes]
        far_ref[base + (2 * part + 1) * rows : base + (2 * part + 2) * rows, :] = adjoints[:, lanes]


def relay_kernel(near_ref, top_ref, far_ref, cross_ref, after_ref, out_ref):
    rows = near_ref.shape[0]
    out_ref[0] = near_ref[...]
    out_ref[1] = top_ref[...]
    out_ref[2] = far_ref[:rows, :]
    out_ref[3] = cross_ref[...]


def merge_kernel(keep_ref, arrived_ref, after_ref, kept_ref, send_ref):
    half = kept_ref.shape[0]
    kept_ref[...] = keep_ref[:half] + arrived_ref[:half].astype(F32)
    send_ref[...] = (keep_ref[half:] + arrived_ref[half:].astype(F32)).astype(BF16)


def pick_halo(place, pieces, masks, row_slice, lane_slice):
    tile = place[0]
    shape = (row_slice.stop - row_slice.start, EDGE)
    lane = lax.broadcasted_iota(jnp.int32, shape, 1)
    above = jnp.zeros(shape, F32)
    below = jnp.zeros(shape, F32)
    for (piece_ref, at), mask in zip(pieces, masks):
        cells = piece_ref[at, row_slice, lane_slice].astype(F32)
        owner = tile ^ mask
        above = jnp.where(owner == tile + 1, cells, above)
        below = jnp.where(owner == tile - 1, cells, below)
    return jnp.where(lane < EDGE // 2, above, below)


def split_pieces(refs):
    near = [(ref, at) for ref in refs for at in (0, 1)]
    across = [(ref, at) for ref in refs for at in (2, 3)]
    return near, across


def fields_kernel(masks, count, place, f_ref, far_ref, *refs):
    (near, across), out_ref = split_pieces(refs[:-1]), refs[-1]
    rows, width = f_ref.shape
    depth = far_ref.shape[1]
    mats = count * rows
    base = mats + rows + 16
    edge_rows = slice(mats, mats + rows)
    lanes = slice(0, EDGE)
    first = pl.multiple_of(place[1] * rows, rows)
    second = pl.multiple_of((1 - place[1]) * rows, rows)
    out_ref[pl.ds(first, rows), :width] = f_ref[...]
    out_ref[pl.ds(first, rows), width:] = pick_halo(place, near, masks, edge_rows, lanes).astype(BF16)
    for part in range(width // depth):
        out_ref[pl.ds(second, rows), part * depth : (part + 1) * depth] = far_ref[
            base + 2 * part * rows : base + (2 * part + 1) * rows, :
        ]
    out_ref[pl.ds(second, rows), width:] = pick_halo(place, across, masks, edge_rows, lanes).astype(BF16)


def prepare_kernel(couple_ref, after_ref, plain_ref, turned_ref, sems):
    copies = []
    for chunk in range(SLOTS // CHUNK):
        span = pl.ds(chunk * CHUNK, CHUNK)
        copies.append(
            pltpu.make_async_copy(couple_ref.at[span], plain_ref.at[span], sems.at[chunk])
        )
    for copy in copies:
        copy.start()
    for chunk, copy in enumerate(copies):
        copy.wait()
        for mat in range(chunk * CHUNK, (chunk + 1) * CHUNK):
            turned_ref[SLOTS - 1 - mat] = plain_ref[mat].T


def couple_slots(source, weight_ref, mats_ref, slots, total=None):
    span = source.shape[1]
    width = weight_ref.shape[1]
    for slot in slots:
        moved = pltpu.roll(source, (-OFFSETS[slot]) % span, 1)[:, :width]
        selected = moved * weight_ref[slot : slot + 1, :]
        product = jnp.dot(mats_ref[slot], selected, preferred_element_type=F32)
        total = product if total is None else total + product
    return total


def adjoint_kernel(
    masks, count, place, a_ref, far_ref, class_ref, weight_ref, mats_ref, after_ref, *refs
):
    half = len(masks)
    near, across = split_pieces(refs[:-5])
    send_ref, keep_ref, total_ref, expanded, stacked = refs[-5:]
    rows, width = a_ref.shape
    depth = far_ref.shape[1]
    mats = count * rows
    base = mats + rows + 16
    edge_rows = slice(mats, mats + rows)
    lanes = slice(EDGE, 2 * EDGE)
    far_own = jnp.concatenate(
        [
            far_ref[base + (2 * part + 1) * rows : base + (2 * part + 2) * rows, :]
            for part in range(width // depth)
        ],
        axis=1,
    )
    padded = [
        jnp.concatenate([own, pick_halo(place, pieces, masks, edge_rows, lanes).astype(BF16)], axis=1)
        for own, pieces in ((a_ref[...], near), (far_own, across))
    ]
    class_halo = pick_halo(place, near, masks, slice(mats + rows, mats + rows + 16), slice(0, EDGE))
    labels = jnp.concatenate(
        [class_ref[...], class_halo[0:1, :].astype(jnp.int32)], axis=1
    )
    at = 0
    for piece in range(half):
        for which, pieces in ((0, near), (1, across)):
            ref, spot = pieces[piece]
            stacked[at : at + mats, :] = ref[spot, :mats, :]
            for local_class in range(count):
                hit = labels == (place[0] ^ masks[piece]) * count + local_class
                factor = jnp.where(hit, 1.0, 0.0).astype(BF16)
                expanded[at : at + rows, :] = padded[which] * factor
                at += rows
    scattered = lax.dot_general(
        stacked[...], expanded[...], (((0,), (0,)), ((), ())), preferred_element_type=F32
    ).astype(BF16)
    total_ref[...] = couple_slots(scattered, weight_ref, mats_ref, range(SLOTS))
    steps = keep_ref.shape[0]
    for rel in range(steps):
        start = pl.multiple_of(((place[2] ^ rel) * 2 + place[1]) * rows, rows)
        keep_ref[rel] = total_ref[pl.ds(start, rows), :]
        start = pl.multiple_of(((place[2] ^ (rel + steps)) * 2 + place[1]) * rows, rows)
        send_ref[rel] = total_ref[pl.ds(start, rows), :].astype(BF16)


def gather_kernel(rels, place, weight_ref, mats_ref, *refs):
    pieces, total_ref, padded = refs[:-2], refs[-2], refs[-1]
    block = pieces[0].shape[0]
    for rel, piece_ref in zip(rels, pieces):
        start = pl.multiple_of((place[2] ^ rel) * block, block)
        padded[pl.ds(start, block), :] = piece_ref[...]
    total_ref[...] = couple_slots(padded[...], weight_ref, mats_ref, range(EARLY))


def forward_kernel(masks, count, place, f_ref, class_ref, weight_ref, mats_ref, total_ref, padded, *refs):
    (near, across), out_ref = split_pieces(refs[:-1]), refs[-1]
    rows, width = f_ref.shape
    mats = count * rows
    coupled = couple_slots(
        padded[...], weight_ref, mats_ref, range(EARLY, SLOTS), total_ref[...]
    ).astype(BF16)
    applied = jnp.zeros((rows, width), F32)
    labels = class_ref[...]
    for piece in range(len(masks)):
        ref, spot = near[piece]
        product = jnp.dot(ref[spot, :mats, :], coupled, preferred_element_type=F32)
        for local_class in range(count):
            hit = labels == (place[0] ^ masks[piece]) * count + local_class
            applied = jnp.where(hit, product[local_class * rows : (local_class + 1) * rows, :], applied)
    out_ref[...] = (f_ref[...].astype(F32) - applied).astype(BF16)


def local(fields, adjoints, couple, tmatrices, neighbours, classes):
    tiles, coefs = lax.axis_size("tiles"), lax.axis_size("coef")
    tile, coef = lax.axis_index("tiles"), lax.axis_index("coef")
    rows, width = fields.shape
    count, unused, depth = tmatrices.shape
    spot = jnp.stack([tile, coef]).astype(jnp.int32)

    def swap(cells, tile_mask, coef_mask):
        pairs = [
            (i * coefs + j, (i ^ tile_mask) * coefs + (j ^ coef_mask))
            for i in range(tiles)
            for j in range(coefs)
        ]
        return lax.ppermute(cells, ("tiles", "coef"), pairs)

    weights = (neighbours >= 0).astype(BF16).T
    labels = classes.reshape(1, width)
    mats = count * rows
    near_rows = mats + rows + 16
    far_rows = near_rows + 2 * rows * (width // depth)
    place, near_own, far_own, fields, adjoints, labels = pl.pallas_call(
        pack_kernel,
        out_shape=(
            jax.ShapeDtypeStruct((3,), jnp.int32),
            jax.ShapeDtypeStruct((near_rows, depth), BF16),
            jax.ShapeDtypeStruct((far_rows, depth), BF16),
            jax.ShapeDtypeStruct(fields.shape, BF16),
            jax.ShapeDtypeStruct(adjoints.shape, BF16),
            jax.ShapeDtypeStruct(labels.shape, jnp.int32),
        ),
        in_specs=[SMEM] + [HBM] * 4,
        out_specs=(SMEM,) + (VMEM,) * 5,
        scratch_shapes=[pltpu.VMEM(tmatrices.shape, BF16), pltpu.SemaphoreType.DMA((4,))],
        compiler_params=FULL,
    )(spot, tmatrices, fields, adjoints, labels)
    mats_plain, mats_turned = pl.pallas_call(
        prepare_kernel,
        out_shape=(jax.ShapeDtypeStruct(couple.shape, BF16),) * 2,
        in_specs=[HBM, SMEM],
        out_specs=(VMEM, VMEM),
        scratch_shapes=[pltpu.SemaphoreType.DMA((SLOTS // CHUNK,))],
        cost_estimate=pl.CostEstimate(flops=0, bytes_accessed=4 * couple.size, transcendentals=0),
        compiler_params=WIDE,
    )(couple, place)

    top = tiles // 2
    far = swap(far_own, 0, 1)
    first = pl.pallas_call(
        relay_kernel,
        out_shape=jax.ShapeDtypeStruct((4, near_rows, depth), BF16),
        in_specs=[VMEM] * 5,
        out_specs=VMEM,
        compiler_params=PARAMS,
    )(near_own, swap(near_own, top, 0), far, swap(near_own, top, 1), mats_turned)
    held, lows = [first], [0]
    bit = top // 2
    while bit >= 1:
        held += [swap(block, bit, 0) for block in held]
        lows += [low ^ bit for low in lows]
        bit //= 2
    masks = [low ^ high for low in lows for high in (0, top)]

    padded_fields = pl.pallas_call(
        functools.partial(fields_kernel, masks, count),
        out_shape=jax.ShapeDtypeStruct((2 * rows, width + EDGE), BF16),
        in_specs=[SMEM] + [VMEM] * (2 + len(held)),
        out_specs=VMEM,
        compiler_params=PARAMS,
    )(place, fields, far, *held)

    groups = coefs // 2
    gathered = {0: padded_fields}
    for rel in range(1, groups):
        gathered[rel] = swap(padded_fields, 0, 2 * rel)
    rels = sorted(gathered)

    steps = groups // 2
    total_rows = couple.shape[1]

    def work(slots):
        size = slots * total_rows * total_rows
        return pl.CostEstimate(flops=2 * size * width, bytes_accessed=2 * size, transcendentals=0)

    send, keep = pl.pallas_call(
        functools.partial(adjoint_kernel, masks, count),
        out_shape=(
            jax.ShapeDtypeStruct((steps, rows, width), BF16),
            jax.ShapeDtypeStruct((steps, rows, width), F32),
        ),
        in_specs=[SMEM] + [VMEM] * 5 + [ANY] + [VMEM] * len(held),
        out_specs=(VMEM, VMEM),
        scratch_shapes=[
            pltpu.VMEM((total_rows, width), F32),
            pltpu.VMEM((2 * len(masks) * mats, width + EDGE), BF16),
            pltpu.VMEM((2 * len(masks) * mats, depth), BF16),
        ],
        cost_estimate=work(SLOTS + 8),
        compiler_params=PARAMS,
    )(place, adjoints, far, labels, weights, mats_turned, padded_fields, *held)

    partial, all_fields = pl.pallas_call(
        functools.partial(gather_kernel, rels),
        out_shape=(
            jax.ShapeDtypeStruct((total_rows, width), F32),
            jax.ShapeDtypeStruct((total_rows, width + EDGE), BF16),
        ),
        in_specs=[SMEM] + [VMEM] * (2 + len(rels)),
        out_specs=(VMEM, VMEM),
        cost_estimate=work(EARLY),
        compiler_params=PARAMS,
    )(place, weights, mats_plain, *[gathered[rel] for rel in rels])
    bit = groups // 2
    arrived = swap(send, 0, 2 * bit)
    while bit > 1:
        bit //= 2
        keep, send = pl.pallas_call(
            merge_kernel,
            out_shape=(
                jax.ShapeDtypeStruct((bit, rows, width), F32),
                jax.ShapeDtypeStruct((bit, rows, width), BF16),
            ),
            in_specs=[VMEM] * 3,
            out_specs=(VMEM, VMEM),
            compiler_params=PARAMS,
        )(keep, arrived, partial)
        arrived = swap(send, 0, 2 * bit)
    returned = keep[0] + arrived[0].astype(F32)
    adjoint_out = (adjoints.astype(F32) - returned).astype(BF16)

    forward_out = pl.pallas_call(
        functools.partial(forward_kernel, masks, count),
        out_shape=jax.ShapeDtypeStruct((rows, width), BF16),
        in_specs=[SMEM] + [VMEM] * (6 + len(held)),
        out_specs=VMEM,
        cost_estimate=work(SLOTS - EARLY + 8),
        compiler_params=PARAMS,
    )(place, fields, labels, weights, mats_plain, partial, all_fields, *held)
    return (forward_out, adjoint_out)


def solution(mesh):
    placed = (
        P("coef", "tiles"),
        P("coef", "tiles"),
        P(),
        P("tiles", "coef", None),
        P("tiles", None),
        P("tiles"),
    )
    return jax.shard_map(
        local,
        mesh=mesh,
        in_specs=placed,
        out_specs=(P("coef", "tiles"), P("coef", "tiles")),
        check_vma=False,
    )
```

time: 42.6 us -> 36.1 us (0.85)
  local copies, waits for them, and re-layouts: 8.96 us -> 2.73 us
  waiting for transfers between devices: 5.33 us -> 2.04 us
  starting transfers between devices: 12 us -> 13.5 us
  Pallas kernels: 14.2 us -> 15.6 us
    unnamed x20 -> x14, local copies, waits for them, and re-layouts: 8.86 us -> 2.73 us
    ppermute x12 -> x9, waiting for transfers between devices: 5.33 us -> 2.04 us  [swap(): return lax.ppermute(cells, ('tiles', 'coef'), pairs)]
    ppermute x12 -> x9, starting transfers between devices: 12 us -> 13.5 us  [swap(): return lax.ppermute(cells, ('tiles', 'coef'), pairs)]
    pallas_call x4 -> x6, Pallas kernels: 11 us -> 11.9 us  [the longest x1 3.98 us: local(): pl.pallas_call(functools.partial(adjoint_kernel, masks, count), out_shape...]
    transpose x1, other arithmetic: 0.85 us -> 0.01 us  [local(): weights = (neighbours >= 0).astype(BF16).T]
    convert_element_type x0 -> x1, other arithmetic: none -> 0.63 us  [local(): adjoint_out = (adjoints.astype(F32) - returned).astype(BF16)]
    another operation x1, other arithmetic: 0.08 us -> 0.65 us  [local(): spot = jnp.stack([tile, coef]).astype(jnp.int32)]
    pallas_call x1, Pallas kernels: 2.62 us -> 3.17 us  [local(): pl.pallas_call(prepare_kernel, out_shape=(jax.ShapeDtypeStruct(couple.sha...]
  transfers between devices with their start and end apart: 12 -> 9, of which waited for: 5 -> 3; matrix products, arithmetic and copies ran while one was open for 3% -> 0% of each run, Pallas kernels for 25% -> 36%
where the time goes in v3:
time: 36.1 us; the launch traced here: 35.9 us
  Pallas kernels  15.6 us (43%)
  starting transfers between devices  13.5 us (37%)
  local copies, waits for them, and re-layouts  2.73 us (8%)
  waiting for transfers between devices  2.04 us (6%)
  other arithmetic  1.29 us (4%)
  between operations  0.74 us (2%)
    ppermute x9, starting transfers between devices, swap(): return lax.ppermute(cells, ('tiles', 'coef'), pairs)  13.5 us
    pallas_call x1, Pallas kernels, local(): pl.pallas_call(functools.partial(adjoint_kernel, masks, count), out_shape...  3.98 us
    pallas_call x1, Pallas kernels, local(): pl.pallas_call(prepare_kernel, out_shape=(jax.ShapeDtypeStruct(couple.sha...  3.17 us
    pallas_call x1, Pallas kernels, local(): pl.pallas_call(functools.partial(gather_kernel, rels), out_shape=(jax.Sha...  3.05 us
    unnamed x14, local copies, waits for them, and re-layouts  2.73 us
    pallas_call x1, Pallas kernels, local(): pl.pallas_call(functools.partial(forward_kernel, masks, count), out_shape...  2.56 us
    pallas_call x1, Pallas kernels, local(): pl.pallas_call(pack_kernel, out_shape=(jax.ShapeDtypeStruct((3,), jnp.int...  2.27 us
    ppermute x9, waiting for transfers between devices, swap(): return lax.ppermute(cells, ('tiles', 'coef'), pairs)  2.04 us
  transfers between devices with their start and end apart: 9, of which 3 were waited for; matrix products, arithmetic and copies ran while one was open for 0% of the time, Pallas kernels for 36%

profile of v3, /device:TPU:0, one launch (start us, length us, event | category | flops | bytes accessed | tf_op | source)
XLA Modules:
  0.0 35.9 jit_solution(13193593246517680494)
XLA Ops:
  0.6 0.7 %pad_add_fusion.spot = s32[2]{0:T(128)} fusion(s32[1]{0:T(128)} %bitcast.1, s32[1]{0:T(128)} %bitcast), kind=kLoop, calls=%fused_computation.4 | loop fusion | flops 2 | bytes 16 | tf_op jit(solution)/shard_map/stack | solution.py:229
  1.3 2.3 %shard_map.77 = (s32[3]{0:T(128)}, bf16[176,256]{1,0:T(8,128)(2,1)}, bf16[304,256]{1,0:T(8,128)(2,1)}, bf16[32,512]{1,0:T(8,128)(2,1)}, bf16[32,512]{1,0:T(8,128)(2,1)}, /*index=5*/s32[1,512]{1,0:T(1,128)}) custom-call(s32[2]{0:T(128)} %pad_add_fusion.spot, bf16[4,32,256]{2,1,0:T(8,128)(2,1)} %t_any.1, bf16[32,512]{1,0:T(8,128)(2,1)} %f_any.1, ...), custom_call_target="tpu_custom_call" | custom-call | tf_op jit(solution)/shard_map/pallas_call | solution.py:244
  3.6 3.0 %collective-permute-start = (bf16[304,256]{1,0:T(8,128)(2,1)}, bf16[304,256]{1,0:T(8,128)(2,1)S(1)}, u32[]{:S(2)}, u32[]{:S(2)}) collective-permute-start(bf16[304,256]{1,0:T(8,128)(2,1)} %get-tuple-element.20), channel_id=1, source_target_pairs={{0,1},{1,0},{2,3},{3,2},{4,5},{5,4},{6,7},{7,6},{8,9},{9,8},{10,11... | collective-permute-start | bytes 466952 | tf_op jit(solution)/shard_map/ppermute | solution.py:237
  6.6 1.5 %collective-permute-start.2 = (bf16[176,256]{1,0:T(8,128)(2,1)}, bf16[176,256]{1,0:T(8,128)(2,1)S(1)}, u32[]{:S(2)}, u32[]{:S(2)}) collective-permute-start(bf16[176,256]{1,0:T(8,128)(2,1)} %get-tuple-element.21.near_ref), channel_id=1, source_target_pairs={{0,17},{1,16},{2,19},{3,18},{4,21},{5,20},{6,23},{7,22},{8,25},{9,... | collective-permute-start | bytes 270344 | tf_op jit(solution)/shard_map/ppermute | solution.py:237
  8.1 0.0 collective-permute-start.1
  8.1 2.1 %copy-done = bf16[30,256,256]{2,1,0:T(8,128)(2,1)S(1)} copy-done((bf16[30,256,256]{2,1,0:T(8,128)(2,1)S(1)}, bf16[30,256,256]{2,1,0:T(8,128)(2,1)}, u32[]{:S(2)}) %copy-start) | copy-done | bytes 3932184
  10.2 0.6 %copy-done.4 = s32[3]{0:T(128)S(1)} copy-done((s32[3]{0:T(128)S(1)}, s32[3]{0:T(128)}, u32[]{:S(2)}) %copy-start.4) | copy-done | bytes 36
  10.8 3.2 %shard_map.78 = (bf16[30,256,256]{2,1,0:T(8,128)(2,1)S(1)}, bf16[30,256,256]{2,1,0:T(8,128)(2,1)S(1)}) custom-call(bf16[30,256,256]{2,1,0:T(8,128)(2,1)S(1)} %copy-done, s32[3]{0:T(128)S(1)} %copy-done.4), custom_call_target="tpu_custom_call" | custom-call | bytes 7864320 | tf_op jit(solution)/shard_map/pallas_call | solution.py:259
  14.0 0.0 collective-permute-done.2.cross_ref
  14.0 0.2 collective-permute-done.1.top_ref
  14.2 0.0 collective-permute-done.far_ref
  14.3 0.1 collective-permute-start.3
  14.4 1.6 %collective-permute-done.3.refs_1_ = bf16[4,176,256]{2,1,0:T(8,128)(2,1)S(1)} collective-permute-done((bf16[4,176,256]{2,1,0:T(8,128)(2,1)S(1)}, bf16[4,176,256]{2,1,0:T(8,128)(2,1)S(1)}, u32[]{:S(2)}, u32[]{:S(2)}) %collective-permute-start.3) | collective-permute-done | bytes 360480 | tf_op jit(solution)/shard_map/ppermute | solution.py:237
  16.0 0.6 %shard_map.80.refs_0_.after_ref = bf16[64,640]{1,0:T(8,128)(2,1)S(1)} custom-call(s32[3]{0:T(128)S(1)} %copy-done.4, bf16[32,512]{1,0:T(8,128)(2,1)S(1)} %copy-done.1, bf16[304,256]{1,0:T(8,128)(2,1)S(1)} %collective-permute-done.far_ref, bf16[4,176,256]{2,1,0:T(8,128)(2,1)S(1)} %shard_map.79.refs_0_, bf16[4,176,256]{2,1,0:T(8,128)(2,1)S(1)} %collective-permute-done.3.refs_1_), custom_call_target="tpu_custom_call" | custom-call | tf_op jit(solution)/shard_map/pallas_call | solution.py:286
  16.6 3.9 %collective-permute-start.6 = (bf16[64,640]{1,0:T(8,128)(2,1)S(1)}, bf16[64,640]{1,0:T(8,128)(2,1)S(1)}, u32[]{:S(2)}, u32[]{:S(2)}) collective-permute-start(bf16[64,640]{1,0:T(8,128)(2,1)S(1)} %shard_map.80.refs_0_.after_ref), channel_id=1, source_target_pairs={{0,6},{1,7},{2,4},{3,5},{4,2},{5,3},{6,0},{7,1},{8,14},{9,15},{10,... | collective-permute-start | bytes 245768 | tf_op jit(solution)/shard_map/ppermute | solution.py:237
  20.5 0.6 %collective-permute-start.4 = (bf16[64,640]{1,0:T(8,128)(2,1)S(1)}, bf16[64,640]{1,0:T(8,128)(2,1)S(1)}, u32[]{:S(2)}, u32[]{:S(2)}) collective-permute-start(bf16[64,640]{1,0:T(8,128)(2,1)S(1)} %shard_map.80.refs_0_.after_ref), channel_id=1, source_target_pairs={{0,2},{1,3},{2,0},{3,1},{4,6},{5,7},{6,4},{7,5},{8,10},{9,11},{10,... | collective-permute-start | bytes 245768 | tf_op jit(solution)/shard_map/ppermute | solution.py:237
  21.2 4.0 %shard_map.83 = (bf16[2,32,512]{2,1,0:T(8,128)(2,1)S(1)}, f32[2,32,512]{2,1,0:T(8,128)S(1)}) custom-call(s32[3]{0:T(128)S(1)} %copy-done.4, bf16[32,512]{1,0:T(8,128)(2,1)S(1)} %copy-done.3, bf16[304,256]{1,0:T(8,128)(2,1)S(1)} %collective-permute-done.far_ref, s32[1,512]{1,0:T(1,128)S(1)} %copy-done.5, bf16[30,512]{1,0:T(8,128)(2,1)S(1)} %fusion.1.weight_ref, ...), custom_call_target="tpu_custom_call" | custom-call | flops 2550136832 | bytes 4980736 | tf_op jit(solution)/shard_map/pallas_call | solution.py:307
  25.2 2.4 %collective-permute-start.7 = (bf16[2,32,512]{2,1,0:T(8,128)(2,1)S(1)}, bf16[2,32,512]{2,1,0:T(8,128)(2,1)S(1)}, u32[]{:S(2)}, u32[]{:S(2)}) collective-permute-start(bf16[2,32,512]{2,1,0:T(8,128)(2,1)S(1)} %get-tuple-element.27), channel_id=1, source_target_pairs={{0,4},{1,5},{2,6},{3,7},{4,0},{5,1},{6,2},{7,3},{8,12},{9,13},{10,... | collective-permute-start | bytes 196616 | tf_op jit(solution)/shard_map/ppermute | solution.py:237
  27.5 0.0 collective-permute-done.6.refs_3_
  27.5 0.2 collective-permute-done.5.refs_2_
  27.7 3.0 %shard_map.81 = (f32[256,512]{1,0:T(8,128)S(1)}, bf16[256,640]{1,0:T(8,128)(2,1)S(1)}) custom-call(s32[3]{0:T(128)S(1)} %copy-done.4, bf16[30,512]{1,0:T(8,128)(2,1)S(1)} %fusion.1.weight_ref, bf16[30,256,256]{2,1,0:T(8,128)(2,1)S(1)} %get-tuple-element.19.mats_ref, bf16[64,640]{1,0:T(8,128)(2,1)S(1)} %shard_map.80.refs_0_.after_ref, ...), custom_call_target="tpu_custom_call" | custom-call | flops 1476395008 | bytes 2883584 | tf_op jit(solution)/shard_map/pallas_call | solution.py:324
  30.8 1.9 %collective-permute-start.8 = (bf16[1,32,512]{2,1,0:T(8,128)(2,1)S(1)}, bf16[1,32,512]{2,1,0:T(8,128)(2,1)S(1)}, u32[]{:S(2)}, u32[]{:S(2)}) collective-permute-start(bf16[1,32,512]{2,1,0:T(8,128)(2,1)S(1)} %get-tuple-element.29), channel_id=1, source_target_pairs={{0,2},{1,3},{2,0},{3,1},{4,6},{5,7},{6,4},{7,5},{8,10},{9,11},{10,... | collective-permute-start | bytes 98312 | tf_op jit(solution)/shard_map/ppermute | solution.py:237
  32.7 2.6 %shard_map.82 = bf16[32,512]{1,0:T(8,128)(2,1)} custom-call(s32[3]{0:T(128)S(1)} %copy-done.4, bf16[32,512]{1,0:T(8,128)(2,1)S(1)} %copy-done.1, s32[1,512]{1,0:T(1,128)S(1)} %copy-done.5, bf16[30,512]{1,0:T(8,128)(2,1)S(1)} %fusion.1.weight_ref, bf16[30,256,256]{2,1,0:T(8,128)(2,1)S(1)} %get-tuple-element.19.mats_ref, ...), custom_call_target="tpu_custom_call" | custom-call | flops 1073741824 | bytes 2097152 | tf_op jit(solution)/shard_map/pallas_call | solution.py:353
  35.3 0.6 %fusion = bf16[32,512]{1,0:T(8,128)(2,1)} fusion(f32[1,32,512]{2,1,0:T(8,128)S(1)} %get-tuple-element.28, bf16[1,32,512]{2,1,0:T(8,128)(2,1)S(1)} %collective-permute-done.8, bf16[32,512]{1,0:T(8,128)(2,1)S(1)} %copy-done.3), kind=kLoop, calls=%fused_computation.1 | loop fusion | flops 81920 | bytes 163840 | tf_op jit(solution)/shard_map/convert_element_type | solution.py:351
  (19 shorter events, 0.1 us)
Async XLA Ops:
  3.6 10.7 %collective-permute-start = (bf16[304,256]{1,0:T(8,128)(2,1)}, bf16[304,256]{1,0:T(8,128)(2,1)S(1)}, u32[]{:S(2)}, u32[]{:S(2)}) collective-permute-start(bf16[304,256]{1,0:T(8,128)(2,1)} %get-tuple-element.20), channel_id=1, source_target_pairs={{0,1},{1,0},{2,3},{3,2},{4,5},{5,4},{6,7},{7,6},{8,9},{9,8},{10,11... | collective-permute-start | bytes 466952 | tf_op jit(solution)/shard_map/ppermute | solution.py:237
  6.6 7.5 %collective-permute-start.2 = (bf16[176,256]{1,0:T(8,128)(2,1)}, bf16[176,256]{1,0:T(8,128)(2,1)S(1)}, u32[]{:S(2)}, u32[]{:S(2)}) collective-permute-start(bf16[176,256]{1,0:T(8,128)(2,1)} %get-tuple-element.21.near_ref), channel_id=1, source_target_pairs={{0,17},{1,16},{2,19},{3,18},{4,21},{5,20},{6,23},{7,22},{8,25},{9,... | collective-permute-start | bytes 270344 | tf_op jit(solution)/shard_map/ppermute | solution.py:237
  8.1 6.2 %collective-permute-start.1 = (bf16[176,256]{1,0:T(8,128)(2,1)}, bf16[176,256]{1,0:T(8,128)(2,1)S(1)}, u32[]{:S(2)}, u32[]{:S(2)}) collective-permute-start(bf16[176,256]{1,0:T(8,128)(2,1)} %get-tuple-element.21.near_ref), channel_id=1, source_target_pairs={{0,16},{1,17},{2,18},{3,19},{4,20},{5,21},{6,22},{7,23},{8,24},{9,... | collective-permute-start | bytes 270344 | tf_op jit(solution)/shard_map/ppermute | solution.py:237
  8.1 2.1 %copy-start = (bf16[30,256,256]{2,1,0:T(8,128)(2,1)S(1)}, bf16[30,256,256]{2,1,0:T(8,128)(2,1)}, u32[]{:S(2)}) copy-start(bf16[30,256,256]{2,1,0:T(8,128)(2,1)} %couple_ref.1) | copy-start | bytes 11796484
  10.2 0.6 %copy-start.4 = (s32[3]{0:T(128)S(1)}, s32[3]{0:T(128)}, u32[]{:S(2)}) copy-start(s32[3]{0:T(128)} %get-tuple-element.16.after_ref.place) | copy-start | bytes 40
  10.8 3.4 %copy-start.2 = (bf16[176,256]{1,0:T(8,128)(2,1)S(1)}, bf16[176,256]{1,0:T(8,128)(2,1)}, u32[]{:S(2)}) copy-start(bf16[176,256]{1,0:T(8,128)(2,1)} %get-tuple-element.21.near_ref) | copy-start | bytes 270340
  10.8 3.5 %copy-start.6 = (s32[512,30]{0,1:T(8,128)S(1)}, s32[512,30]{0,1:T(8,128)}, u32[]{:S(2)}) copy-start(s32[512,30]{0,1:T(8,128)} %param.10) | copy-start | bytes 184324
  10.8 5.2 %copy-start.1 = (bf16[32,512]{1,0:T(8,128)(2,1)S(1)}, bf16[32,512]{1,0:T(8,128)(2,1)}, u32[]{:S(2)}) copy-start(bf16[32,512]{1,0:T(8,128)(2,1)} %get-tuple-element.17.f_ref) | copy-start | bytes 98308
  10.8 10.4 %copy-start.3 = (bf16[32,512]{1,0:T(8,128)(2,1)S(1)}, bf16[32,512]{1,0:T(8,128)(2,1)}, u32[]{:S(2)}) copy-start(bf16[32,512]{1,0:T(8,128)(2,1)} %get-tuple-element.25.a_ref) | copy-start | bytes 98308
  10.8 10.3 %copy-start.5 = (s32[1,512]{1,0:T(1,128)S(1)}, s32[1,512]{1,0:T(1,128)}, u32[]{:S(2)}) copy-start(s32[1,512]{1,0:T(1,128)} %get-tuple-element.18.class_ref) | copy-start | bytes 6148
  14.3 1.7 %collective-permute-start.3 = (bf16[4,176,256]{2,1,0:T(8,128)(2,1)S(1)}, bf16[4,176,256]{2,1,0:T(8,128)(2,1)S(1)}, u32[]{:S(2)}, u32[]{:S(2)}) collective-permute-start(bf16[4,176,256]{2,1,0:T(8,128)(2,1)S(1)} %shard_map.79.refs_0_), channel_id=1, source_target_pairs={{0,8},{1,9},{2,10},{3,11},{4,12},{5,13},{6,14},{7,15},{8,0},{9,1},... | collective-permute-start | bytes 1081352 | tf_op jit(solution)/shard_map/ppermute | solution.py:237
  16.6 10.9 %collective-permute-start.6 = (bf16[64,640]{1,0:T(8,128)(2,1)S(1)}, bf16[64,640]{1,0:T(8,128)(2,1)S(1)}, u32[]{:S(2)}, u32[]{:S(2)}) collective-permute-start(bf16[64,640]{1,0:T(8,128)(2,1)S(1)} %shard_map.80.refs_0_.after_ref), channel_id=1, source_target_pairs={{0,6},{1,7},{2,4},{3,5},{4,2},{5,3},{6,0},{7,1},{8,14},{9,15},{10,... | collective-permute-start | bytes 245768 | tf_op jit(solution)/shard_map/ppermute | solution.py:237
  20.5 7.2 %collective-permute-start.5 = (bf16[64,640]{1,0:T(8,128)(2,1)S(1)}, bf16[64,640]{1,0:T(8,128)(2,1)S(1)}, u32[]{:S(2)}, u32[]{:S(2)}) collective-permute-start(bf16[64,640]{1,0:T(8,128)(2,1)S(1)} %shard_map.80.refs_0_.after_ref), channel_id=1, source_target_pairs={{0,4},{1,5},{2,6},{3,7},{4,0},{5,1},{6,2},{7,3},{8,12},{9,13},{10,... | collective-permute-start | bytes 245768 | tf_op jit(solution)/shard_map/ppermute | solution.py:237
  20.5 7.2 %collective-permute-start.4 = (bf16[64,640]{1,0:T(8,128)(2,1)S(1)}, bf16[64,640]{1,0:T(8,128)(2,1)S(1)}, u32[]{:S(2)}, u32[]{:S(2)}) collective-permute-start(bf16[64,640]{1,0:T(8,128)(2,1)S(1)} %shard_map.80.refs_0_.after_ref), channel_id=1, source_target_pairs={{0,2},{1,3},{2,0},{3,1},{4,6},{5,7},{6,4},{7,5},{8,10},{9,11},{10,... | collective-permute-start | bytes 245768 | tf_op jit(solution)/shard_map/ppermute | solution.py:237
  25.2 5.6 %collective-permute-start.7 = (bf16[2,32,512]{2,1,0:T(8,128)(2,1)S(1)}, bf16[2,32,512]{2,1,0:T(8,128)(2,1)S(1)}, u32[]{:S(2)}, u32[]{:S(2)}) collective-permute-start(bf16[2,32,512]{2,1,0:T(8,128)(2,1)S(1)} %get-tuple-element.27), channel_id=1, source_target_pairs={{0,4},{1,5},{2,6},{3,7},{4,0},{5,1},{6,2},{7,3},{8,12},{9,13},{10,... | collective-permute-start | bytes 196616 | tf_op jit(solution)/shard_map/ppermute | solution.py:237
  30.8 4.5 %collective-permute-start.8 = (bf16[1,32,512]{2,1,0:T(8,128)(2,1)S(1)}, bf16[1,32,512]{2,1,0:T(8,128)(2,1)S(1)}, u32[]{:S(2)}, u32[]{:S(2)}) collective-permute-start(bf16[1,32,512]{2,1,0:T(8,128)(2,1)S(1)} %get-tuple-element.29), channel_id=1, source_target_pairs={{0,2},{1,3},{2,0},{3,1},{4,6},{5,7},{6,4},{7,5},{8,10},{9,11},{10,... | collective-permute-start | bytes 98312 | tf_op jit(solution)/shard_map/ppermute | solution.py:237

commit v4 on v3

--- a/solution.py
+++ b/solution.py
@@ -20,8 +20,10 @@
 ANY = pl.BlockSpec(memory_space=pl.ANY)
 HBM = pl.BlockSpec(memory_space=pltpu.HBM)
 PARAMS = pltpu.CompilerParams(vmem_limit_bytes=24 * 1024 * 1024)
-WIDE = pltpu.CompilerParams(vmem_limit_bytes=24 * 1024 * 1024)
-FULL = pltpu.CompilerParams(vmem_limit_bytes=58 * 1024 * 1024)
+
+
+def in_hbm(cells):
+    return pltpu.with_memory_space_constraint(cells, pltpu.HBM)
 
 
 def edges_of(cells):
@@ -32,11 +34,12 @@
 
 
 def pack_kernel(
-    spot, t_any, f_any, a_any, class_any, place, near_ref, far_ref, f_ref, a_ref, class_ref, t_ref, sems
+    t_any, f_any, a_any, class_any, place, near_ref, far_ref, f_ref, a_ref, class_ref, t_ref, sems
 ):
-    place[0] = spot[0]
-    place[1] = spot[1] & 1
-    place[2] = spot[1] >> 1
+    coef = lax.axis_index("coef")
+    place[0] = lax.axis_index("tiles")
+    place[1] = coef & 1
+    place[2] = coef >> 1
     copies = [
         pltpu.make_async_copy(source, target, sems.at[at])
         for at, (source, target) in enumerate(
@@ -223,10 +226,8 @@
 
 def local(fields, adjoints, couple, tmatrices, neighbours, classes):
     tiles, coefs = lax.axis_size("tiles"), lax.axis_size("coef")
-    tile, coef = lax.axis_index("tiles"), lax.axis_index("coef")
     rows, width = fields.shape
     count, unused, depth = tmatrices.shape
-    spot = jnp.stack([tile, coef]).astype(jnp.int32)
 
     def swap(cells, tile_mask, coef_mask):
         pairs = [
@@ -251,11 +252,11 @@
             jax.ShapeDtypeStruct(adjoints.shape, BF16),
             jax.ShapeDtypeStruct(labels.shape, jnp.int32),
         ),
-        in_specs=[SMEM] + [HBM] * 4,
+        in_specs=[HBM] * 4,
         out_specs=(SMEM,) + (VMEM,) * 5,
         scratch_shapes=[pltpu.VMEM(tmatrices.shape, BF16), pltpu.SemaphoreType.DMA((4,))],
-        compiler_params=FULL,
-    )(spot, tmatrices, fields, adjoints, labels)
+        compiler_params=PARAMS,
+    )(*[in_hbm(cells) for cells in (tmatrices, fields, adjoints, labels)])
     mats_plain, mats_turned = pl.pallas_call(
         prepare_kernel,
         out_shape=(jax.ShapeDtypeStruct(couple.shape, BF16),) * 2,
@@ -263,8 +264,8 @@
         out_specs=(VMEM, VMEM),
         scratch_shapes=[pltpu.SemaphoreType.DMA((SLOTS // CHUNK,))],
         cost_estimate=pl.CostEstimate(flops=0, bytes_accessed=4 * couple.size, transcendentals=0),
-        compiler_params=WIDE,
-    )(couple, place)
+        compiler_params=PARAMS,
+    )(in_hbm(couple), place)
 
     top = tiles // 2
     far = swap(far_own, 0, 1)

time: 36.1 us -> 34.2 us (0.947)
  local copies, waits for them, and re-layouts: 2.73 us -> 0.01 us
  waiting for transfers between devices: 2.04 us -> 4.6 us
  Pallas kernels: 15.6 us -> 14.8 us
  other arithmetic: 1.29 us -> 0.64 us
    unnamed x14 -> x2, local copies, waits for them, and re-layouts: 2.73 us -> 0.01 us
    ppermute x9, waiting for transfers between devices: 2.04 us -> 4.6 us  [swap(): return lax.ppermute(cells, ('tiles', 'coef'), pairs)]
    pallas_call x1, Pallas kernels: 2.27 us -> 1.47 us  [local(): pl.pallas_call(pack_kernel, out_shape=(jax.ShapeDtypeStruct((3,), jnp.int...]
    another operation x1 -> x0, other arithmetic: 0.65 us -> none  [local(): spot = jnp.stack([tile, coef]).astype(jnp.int32)]
  transfers between devices with their start and end apart: 9 -> 9, of which waited for: 3 -> 4; matrix products, arithmetic and copies ran while one was open for 0% -> 0% of each run, Pallas kernels for 36% -> 37%
where the time goes in v4:
time: 34.2 us; the launch traced here: 34.1 us
  Pallas kernels  14.8 us (43%)
  starting transfers between devices  13.3 us (39%)
  waiting for transfers between devices  4.6 us (13%)
  between operations  0.72 us (2%)
  other arithmetic  0.64 us (2%)
    ppermute x9, starting transfers between devices, swap(): return lax.ppermute(cells, ('tiles', 'coef'), pairs)  13.3 us
    ppermute x9, waiting for transfers between devices, swap(): return lax.ppermute(cells, ('tiles', 'coef'), pairs)  4.6 us
    pallas_call x1, Pallas kernels, local(): pl.pallas_call(functools.partial(adjoint_kernel, masks, count), out_shape...  4.09 us
    pallas_call x1, Pallas kernels, local(): pl.pallas_call(functools.partial(gather_kernel, rels), out_shape=(jax.Sha...  3.05 us
    pallas_call x1, Pallas kernels, local(): pl.pallas_call(prepare_kernel, out_shape=(jax.ShapeDtypeStruct(couple.sha...  3.02 us
    pallas_call x1, Pallas kernels, local(): pl.pallas_call(functools.partial(forward_kernel, masks, count), out_shape...  2.55 us
    pallas_call x1, Pallas kernels, local(): pl.pallas_call(pack_kernel, out_shape=(jax.ShapeDtypeStruct((3,), jnp.int...  1.47 us
  transfers between devices with their start and end apart: 9, of which 4 were waited for; matrix products, arithmetic and copies ran while one was open for 0% of the time, Pallas kernels for 37%

profile of v4, /device:TPU:0, one launch (start us, length us, event | category | flops | bytes accessed | tf_op | source)
XLA Modules:
  0.0 34.1 jit_solution(13713562342719914752)
XLA Ops:
  0.6 1.5 %shard_map.77 = (s32[3]{0:T(128)S(1)}, bf16[176,256]{1,0:T(8,128)(2,1)S(1)}, bf16[304,256]{1,0:T(8,128)(2,1)S(1)}, bf16[32,512]{1,0:T(8,128)(2,1)S(1)}, bf16[32,...) custom-call(bf16[4,32,256]{2,1,0:T(8,128)(2,1)} %t_any.1, bf16[32,512]{1,0:T(8,128)(2,1)} %f_any.1, bf16[32,512]{1,0:T(8,128)(2,1)} %a_any.1, ...), custom_call_target="tpu_custom_call" | custom-call | tf_op jit(solution)/shard_map/pallas_call | solution.py:245
  2.1 3.0 %collective-permute-start = (bf16[304,256]{1,0:T(8,128)(2,1)S(1)}, bf16[304,256]{1,0:T(8,128)(2,1)S(1)}, u32[]{:S(2)}, u32[]{:S(2)}) collective-permute-start(bf16[304,256]{1,0:T(8,128)(2,1)S(1)} %get-tuple-element.20), channel_id=1, source_target_pairs={{0,1},{1,0},{2,3},{3,2},{4,5},{5,4},{6,7},{7,6},{8,9},{9,8},{10,11... | collective-permute-start | bytes 466952 | tf_op jit(solution)/shard_map/ppermute | solution.py:238
  5.1 1.5 %collective-permute-start.2 = (bf16[176,256]{1,0:T(8,128)(2,1)S(1)}, bf16[176,256]{1,0:T(8,128)(2,1)S(1)}, u32[]{:S(2)}, u32[]{:S(2)}) collective-permute-start(bf16[176,256]{1,0:T(8,128)(2,1)S(1)} %get-tuple-element.21.near_ref), channel_id=1, source_target_pairs={{0,17},{1,16},{2,19},{3,18},{4,21},{5,20},{6,23},{7,22},{8,25},{9,... | collective-permute-start | bytes 270344 | tf_op jit(solution)/shard_map/ppermute | solution.py:238
  6.6 0.1 collective-permute-start.1
  6.7 3.0 %shard_map.78 = (bf16[30,256,256]{2,1,0:T(8,128)(2,1)S(1)}, bf16[30,256,256]{2,1,0:T(8,128)(2,1)S(1)}) custom-call(bf16[30,256,256]{2,1,0:T(8,128)(2,1)} %couple_ref.1, s32[3]{0:T(128)S(1)} %get-tuple-element.16.after_ref.place), custom_call_target="tpu_custom_call" | custom-call | bytes 7864320 | tf_op jit(solution)/shard_map/pallas_call | solution.py:260
  9.7 2.7 %collective-permute-done.2.cross_ref = bf16[176,256]{1,0:T(8,128)(2,1)S(1)} collective-permute-done((bf16[176,256]{1,0:T(8,128)(2,1)S(1)}, bf16[176,256]{1,0:T(8,128)(2,1)S(1)}, u32[]{:S(2)}, u32[]{:S(2)}) %collective-permute-start.2) | collective-permute-done | bytes 90144 | tf_op jit(solution)/shard_map/ppermute | solution.py:238
  12.4 0.2 collective-permute-done.1.top_ref
  12.6 0.0 collective-permute-done.far_ref
  12.6 0.1 collective-permute-start.3
  12.7 1.6 %collective-permute-done.3.refs_1_ = bf16[4,176,256]{2,1,0:T(8,128)(2,1)S(1)} collective-permute-done((bf16[4,176,256]{2,1,0:T(8,128)(2,1)S(1)}, bf16[4,176,256]{2,1,0:T(8,128)(2,1)S(1)}, u32[]{:S(2)}, u32[]{:S(2)}) %collective-permute-start.3) | collective-permute-done | bytes 360480 | tf_op jit(solution)/shard_map/ppermute | solution.py:238
  14.4 0.6 %shard_map.80.refs_0_.after_ref = bf16[64,640]{1,0:T(8,128)(2,1)S(1)} custom-call(s32[3]{0:T(128)S(1)} %get-tuple-element.16.after_ref.place, bf16[32,512]{1,0:T(8,128)(2,1)S(1)} %get-tuple-element.17.f_ref, bf16[304,256]{1,0:T(8,128)(2,1)S(1)} %collective-permute-done.far_ref, bf16[4,176,256]{2,1,0:T(8,128)(2,1)S(1)} %shard_map.79.refs_0_, ...), custom_call_target="tpu_custom_call" | custom-call | tf_op jit(solution)/shard_map/pallas_call | solution.py:287
  14.9 3.7 %collective-permute-start.6 = (bf16[64,640]{1,0:T(8,128)(2,1)S(1)}, bf16[64,640]{1,0:T(8,128)(2,1)S(1)}, u32[]{:S(2)}, u32[]{:S(2)}) collective-permute-start(bf16[64,640]{1,0:T(8,128)(2,1)S(1)} %shard_map.80.refs_0_.after_ref), channel_id=1, source_target_pairs={{0,6},{1,7},{2,4},{3,5},{4,2},{5,3},{6,0},{7,1},{8,14},{9,15},{10,... | collective-permute-start | bytes 245768 | tf_op jit(solution)/shard_map/ppermute | solution.py:238
  18.6 0.0 collective-permute-start.5
  18.6 0.8 %collective-permute-start.4 = (bf16[64,640]{1,0:T(8,128)(2,1)S(1)}, bf16[64,640]{1,0:T(8,128)(2,1)S(1)}, u32[]{:S(2)}, u32[]{:S(2)}) collective-permute-start(bf16[64,640]{1,0:T(8,128)(2,1)S(1)} %shard_map.80.refs_0_.after_ref), channel_id=1, source_target_pairs={{0,2},{1,3},{2,0},{3,1},{4,6},{5,7},{6,4},{7,5},{8,10},{9,11},{10,... | collective-permute-start | bytes 245768 | tf_op jit(solution)/shard_map/ppermute | solution.py:238
  19.4 4.1 %shard_map.83 = (bf16[2,32,512]{2,1,0:T(8,128)(2,1)S(1)}, f32[2,32,512]{2,1,0:T(8,128)S(1)}) custom-call(s32[3]{0:T(128)S(1)} %get-tuple-element.16.after_ref.place, bf16[32,512]{1,0:T(8,128)(2,1)S(1)} %get-tuple-element.25.a_ref, bf16[304,256]{1,0:T(8,128)(2,1)S(1)} %collective-permute-done.far_ref, s32[1,512]{1,0:T(1,128)S(1)} %get-tuple-element.18.class_ref, ...), custom_call_target="tpu_custom_call" | custom-call | flops 2550136832 | bytes 4980736 | tf_op jit(solution)/shard_map/pallas_call | solution.py:308
  23.5 2.2 %collective-permute-start.7 = (bf16[2,32,512]{2,1,0:T(8,128)(2,1)S(1)}, bf16[2,32,512]{2,1,0:T(8,128)(2,1)S(1)}, u32[]{:S(2)}, u32[]{:S(2)}) collective-permute-start(bf16[2,32,512]{2,1,0:T(8,128)(2,1)S(1)} %get-tuple-element.27), channel_id=1, source_target_pairs={{0,4},{1,5},{2,6},{3,7},{4,0},{5,1},{6,2},{7,3},{8,12},{9,13},{10,... | collective-permute-start | bytes 196616 | tf_op jit(solution)/shard_map/ppermute | solution.py:238
  25.7 0.0 collective-permute-done.6.refs_3_
  25.7 0.1 collective-permute-done.5.refs_2_
  25.8 3.1 %shard_map.81 = (f32[256,512]{1,0:T(8,128)S(1)}, bf16[256,640]{1,0:T(8,128)(2,1)S(1)}) custom-call(s32[3]{0:T(128)S(1)} %get-tuple-element.16.after_ref.place, bf16[30,512]{1,0:T(8,128)(2,1)S(1)} %fusion.1.weight_ref, bf16[30,256,256]{2,1,0:T(8,128)(2,1)S(1)} %get-tuple-element.19.mats_ref, bf16[64,640]{1,0:T(8,128)(2,1)S(1)} %shard_map.80.refs_0_.after_ref, ...), custom_call_target="tpu_custom_call" | custom-call | flops 1476395008 | bytes 2883584 | tf_op jit(solution)/shard_map/pallas_call | solution.py:325
  28.8 0.0 collective-permute-done.7.arrived_ref
  28.9 2.0 %collective-permute-start.8 = (bf16[1,32,512]{2,1,0:T(8,128)(2,1)S(1)}, bf16[1,32,512]{2,1,0:T(8,128)(2,1)S(1)}, u32[]{:S(2)}, u32[]{:S(2)}) collective-permute-start(bf16[1,32,512]{2,1,0:T(8,128)(2,1)S(1)} %get-tuple-element.29), channel_id=1, source_target_pairs={{0,2},{1,3},{2,0},{3,1},{4,6},{5,7},{6,4},{7,5},{8,10},{9,11},{10,... | collective-permute-start | bytes 98312 | tf_op jit(solution)/shard_map/ppermute | solution.py:238
  30.9 2.6 %shard_map.82 = bf16[32,512]{1,0:T(8,128)(2,1)} custom-call(s32[3]{0:T(128)S(1)} %get-tuple-element.16.after_ref.place, bf16[32,512]{1,0:T(8,128)(2,1)S(1)} %get-tuple-element.17.f_ref, s32[1,512]{1,0:T(1,128)S(1)} %get-tuple-element.18.class_ref, bf16[30,512]{1,0:T(8,128)(2,1)S(1)} %fusion.1.weight_ref, ...), custom_call_target="tpu_custom_call" | custom-call | flops 1073741824 | bytes 2097152 | tf_op jit(solution)/shard_map/pallas_call | solution.py:354
  33.4 0.0 collective-permute-done.8
  33.4 0.6 %fusion = bf16[32,512]{1,0:T(8,128)(2,1)} fusion(f32[1,32,512]{2,1,0:T(8,128)S(1)} %get-tuple-element.28, bf16[1,32,512]{2,1,0:T(8,128)(2,1)S(1)} %collective-permute-done.8, bf16[32,512]{1,0:T(8,128)(2,1)S(1)} %get-tuple-element.25.a_ref), kind=kLoop, calls=%fused_computation.1 | loop fusion | flops 81920 | bytes 163840 | tf_op jit(solution)/shard_map/convert_element_type | solution.py:352
  (6 shorter events, 0.1 us)
Async XLA Ops:
  2.1 10.5 %collective-permute-start = (bf16[304,256]{1,0:T(8,128)(2,1)S(1)}, bf16[304,256]{1,0:T(8,128)(2,1)S(1)}, u32[]{:S(2)}, u32[]{:S(2)}) collective-permute-start(bf16[304,256]{1,0:T(8,128)(2,1)S(1)} %get-tuple-element.20), channel_id=1, source_target_pairs={{0,1},{1,0},{2,3},{3,2},{4,5},{5,4},{6,7},{7,6},{8,9},{9,8},{10,11... | collective-permute-start | bytes 466952 | tf_op jit(solution)/shard_map/ppermute | solution.py:238
  5.1 7.3 %collective-permute-start.2 = (bf16[176,256]{1,0:T(8,128)(2,1)S(1)}, bf16[176,256]{1,0:T(8,128)(2,1)S(1)}, u32[]{:S(2)}, u32[]{:S(2)}) collective-permute-start(bf16[176,256]{1,0:T(8,128)(2,1)S(1)} %get-tuple-element.21.near_ref), channel_id=1, source_target_pairs={{0,17},{1,16},{2,19},{3,18},{4,21},{5,20},{6,23},{7,22},{8,25},{9,... | collective-permute-start | bytes 270344 | tf_op jit(solution)/shard_map/ppermute | solution.py:238
  6.6 6.0 %collective-permute-start.1 = (bf16[176,256]{1,0:T(8,128)(2,1)S(1)}, bf16[176,256]{1,0:T(8,128)(2,1)S(1)}, u32[]{:S(2)}, u32[]{:S(2)}) collective-permute-start(bf16[176,256]{1,0:T(8,128)(2,1)S(1)} %get-tuple-element.21.near_ref), channel_id=1, source_target_pairs={{0,16},{1,17},{2,18},{3,19},{4,20},{5,21},{6,22},{7,23},{8,24},{9,... | collective-permute-start | bytes 270344 | tf_op jit(solution)/shard_map/ppermute | solution.py:238
  6.7 6.0 %copy-start = (s32[512,30]{0,1:T(8,128)S(1)}, s32[512,30]{0,1:T(8,128)}, u32[]{:S(2)}) copy-start(s32[512,30]{0,1:T(8,128)} %param.10) | copy-start | bytes 184324
  12.6 1.7 %collective-permute-start.3 = (bf16[4,176,256]{2,1,0:T(8,128)(2,1)S(1)}, bf16[4,176,256]{2,1,0:T(8,128)(2,1)S(1)}, u32[]{:S(2)}, u32[]{:S(2)}) collective-permute-start(bf16[4,176,256]{2,1,0:T(8,128)(2,1)S(1)} %shard_map.79.refs_0_), channel_id=1, source_target_pairs={{0,8},{1,9},{2,10},{3,11},{4,12},{5,13},{6,14},{7,15},{8,0},{9,1},... | collective-permute-start | bytes 1081352 | tf_op jit(solution)/shard_map/ppermute | solution.py:238
  14.9 10.8 %collective-permute-start.6 = (bf16[64,640]{1,0:T(8,128)(2,1)S(1)}, bf16[64,640]{1,0:T(8,128)(2,1)S(1)}, u32[]{:S(2)}, u32[]{:S(2)}) collective-permute-start(bf16[64,640]{1,0:T(8,128)(2,1)S(1)} %shard_map.80.refs_0_.after_ref), channel_id=1, source_target_pairs={{0,6},{1,7},{2,4},{3,5},{4,2},{5,3},{6,0},{7,1},{8,14},{9,15},{10,... | collective-permute-start | bytes 245768 | tf_op jit(solution)/shard_map/ppermute | solution.py:238
  18.6 7.2 %collective-permute-start.5 = (bf16[64,640]{1,0:T(8,128)(2,1)S(1)}, bf16[64,640]{1,0:T(8,128)(2,1)S(1)}, u32[]{:S(2)}, u32[]{:S(2)}) collective-permute-start(bf16[64,640]{1,0:T(8,128)(2,1)S(1)} %shard_map.80.refs_0_.after_ref), channel_id=1, source_target_pairs={{0,4},{1,5},{2,6},{3,7},{4,0},{5,1},{6,2},{7,3},{8,12},{9,13},{10,... | collective-permute-start | bytes 245768 | tf_op jit(solution)/shard_map/ppermute | solution.py:238
  18.6 7.2 %collective-permute-start.4 = (bf16[64,640]{1,0:T(8,128)(2,1)S(1)}, bf16[64,640]{1,0:T(8,128)(2,1)S(1)}, u32[]{:S(2)}, u32[]{:S(2)}) collective-permute-start(bf16[64,640]{1,0:T(8,128)(2,1)S(1)} %shard_map.80.refs_0_.after_ref), channel_id=1, source_target_pairs={{0,2},{1,3},{2,0},{3,1},{4,6},{5,7},{6,4},{7,5},{8,10},{9,11},{10,... | collective-permute-start | bytes 245768 | tf_op jit(solution)/shard_map/ppermute | solution.py:238
  23.5 5.3 %collective-permute-start.7 = (bf16[2,32,512]{2,1,0:T(8,128)(2,1)S(1)}, bf16[2,32,512]{2,1,0:T(8,128)(2,1)S(1)}, u32[]{:S(2)}, u32[]{:S(2)}) collective-permute-start(bf16[2,32,512]{2,1,0:T(8,128)(2,1)S(1)} %get-tuple-element.27), channel_id=1, source_target_pairs={{0,4},{1,5},{2,6},{3,7},{4,0},{5,1},{6,2},{7,3},{8,12},{9,13},{10,... | collective-permute-start | bytes 196616 | tf_op jit(solution)/shard_map/ppermute | solution.py:238
  28.9 4.6 %collective-permute-start.8 = (bf16[1,32,512]{2,1,0:T(8,128)(2,1)S(1)}, bf16[1,32,512]{2,1,0:T(8,128)(2,1)S(1)}, u32[]{:S(2)}, u32[]{:S(2)}) collective-permute-start(bf16[1,32,512]{2,1,0:T(8,128)(2,1)S(1)} %get-tuple-element.29), channel_id=1, source_target_pairs={{0,2},{1,3},{2,0},{3,1},{4,6},{5,7},{6,4},{7,5},{8,10},{9,11},{10,... | collective-permute-start | bytes 98312 | tf_op jit(solution)/shard_map/ppermute | solution.py:238

commit v5 on v4

--- a/solution.py
+++ b/solution.py
@@ -12,6 +12,9 @@
 EDGE = 128
 CHUNK = 5
 EARLY = 22
+LEAD = 16
+A_SHIFT = 32
+C_SHIFT = 64
 OFFSETS = [slot - HW + (1 if slot >= HW else 0) for slot in range(SLOTS)]
 BF16 = jnp.bfloat16
 F32 = jnp.float32
@@ -31,6 +34,10 @@
     head, tail = cells[:, :EDGE], cells[:, width - EDGE :]
     lane = lax.broadcasted_iota(jnp.int32, head.shape, 1)
     return jnp.where(lane < EDGE // 2, head, tail)
+
+
+def edge_parts(rows):
+    return 2 if rows % 32 == 0 else 1
 
 
 def pack_kernel(
@@ -54,15 +61,26 @@
     mats = count * rows
     width = f_ref.shape[1]
     fields, adjoints = f_ref[...], a_ref[...]
-    class_edge = edges_of(class_ref[...]).astype(F32).astype(BF16)
-    class_rows = jnp.broadcast_to(class_edge, (16, EDGE))
+    own = edges_of(fields).astype(F32)
+    turned = pltpu.roll(edges_of(adjoints).astype(F32), A_SHIFT, 1)
+    class_edge = pltpu.roll(
+        jnp.broadcast_to(edges_of(class_ref[...]).astype(F32), (rows, EDGE)), C_SHIFT, 1
+    )
+    lane = lax.broadcasted_iota(jnp.int32, own.shape, 1)
+    edge = jnp.where(
+        (lane < HW) | (lane >= EDGE - HW),
+        own,
+        jnp.where((lane >= A_SHIFT - HW) & (lane < A_SHIFT + HW), turned, class_edge),
+    ).astype(BF16)
+    parts = edge_parts(rows)
+    base = mats + rows // parts
     for out_ref in (near_ref, far_ref):
         out_ref[:mats, :] = t_ref[...].reshape(mats, depth)
-        out_ref[mats : mats + rows, :EDGE] = edges_of(fields)
-        out_ref[mats : mats + rows, EDGE : 2 * EDGE] = edges_of(adjoints)
-        out_ref[mats + rows : mats + rows + 16, :EDGE] = class_rows
-        out_ref[mats + rows : mats + rows + 16, EDGE : 2 * EDGE] = class_rows
-    base = mats + rows + 16
+        for part in range(parts):
+            band = edge[part * (rows // parts) : (part + 1) * (rows // parts), :]
+            out_ref[mats:base, part * EDGE : (part + 1) * EDGE] = band
+        for part in range(parts, depth // EDGE):
+            out_ref[mats:base, part * EDGE : (part + 1) * EDGE] = edge[: base - mats, :]
     for part in range(width // depth):
         lanes = slice(part * depth, (part + 1) * depth)
         far_ref[base + 2 * part * rows : base + (2 * part + 1) * rows, :] = fields[:, lanes]
@@ -83,17 +101,30 @@
     send_ref[...] = (keep_ref[half:] + arrived_ref[half:].astype(F32)).astype(BF16)
 
 
-def pick_halo(place, pieces, masks, row_slice, lane_slice):
+def pick_halo(place, pieces, masks, mats, rows):
     tile = place[0]
-    shape = (row_slice.stop - row_slice.start, EDGE)
-    lane = lax.broadcasted_iota(jnp.int32, shape, 1)
-    above = jnp.zeros(shape, F32)
-    below = jnp.zeros(shape, F32)
+    parts = edge_parts(rows)
+    lane = lax.broadcasted_iota(jnp.int32, (rows, EDGE), 1)
+    above = jnp.zeros((rows, EDGE), F32)
+    below = jnp.zeros((rows, EDGE), F32)
     for (piece_ref, at), mask in zip(pieces, masks):
-        cells = piece_ref[at, row_slice, lane_slice].astype(F32)
+        bands = [
+            piece_ref[at, mats : mats + rows // parts, part * EDGE : (part + 1) * EDGE]
+            for part in range(parts)
+        ]
+        cells = jnp.concatenate(bands, axis=0).astype(F32)
         owner = tile ^ mask
         above = jnp.where(owner == tile + 1, cells, above)
         below = jnp.where(owner == tile - 1, cells, below)
+    return above, below
+
+
+def join_halo(halo, shift):
+    above, below = halo
+    lane = lax.broadcasted_iota(jnp.int32, above.shape, 1)
+    back = (EDGE - shift) % EDGE
+    if back:
+        above, below = pltpu.roll(above, back, 1), pltpu.roll(below, back, 1)
     return jnp.where(lane < EDGE // 2, above, below)
 
 
@@ -108,58 +139,81 @@
     rows, width = f_ref.shape
     depth = far_ref.shape[1]
     mats = count * rows
-    base = mats + rows + 16
-    edge_rows = slice(mats, mats + rows)
-    lanes = slice(0, EDGE)
+    base = mats + rows // edge_parts(rows)
     first = pl.multiple_of(place[1] * rows, rows)
     second = pl.multiple_of((1 - place[1]) * rows, rows)
     out_ref[pl.ds(first, rows), :width] = f_ref[...]
-    out_ref[pl.ds(first, rows), width:] = pick_halo(place, near, masks, edge_rows, lanes).astype(BF16)
+    halo = join_halo(pick_halo(place, near, masks, mats, rows), 0)
+    out_ref[pl.ds(first, rows), width:] = halo.astype(BF16)
     for part in range(width // depth):
         out_ref[pl.ds(second, rows), part * depth : (part + 1) * depth] = far_ref[
             base + 2 * part * rows : base + (2 * part + 1) * rows, :
         ]
-    out_ref[pl.ds(second, rows), width:] = pick_halo(place, across, masks, edge_rows, lanes).astype(BF16)
-
-
-def prepare_kernel(couple_ref, after_ref, plain_ref, turned_ref, sems):
+    halo = join_halo(pick_halo(place, across, masks, mats, rows), 0)
+    out_ref[pl.ds(second, rows), width:] = halo.astype(BF16)
+
+
+def prepare_kernel(couple_ref, weight_ref, after_ref, mats_ref, spread_ref, sems):
     copies = []
     for chunk in range(SLOTS // CHUNK):
         span = pl.ds(chunk * CHUNK, CHUNK)
-        copies.append(
-            pltpu.make_async_copy(couple_ref.at[span], plain_ref.at[span], sems.at[chunk])
-        )
+        copies.append(pltpu.make_async_copy(couple_ref.at[span], mats_ref.at[span], sems.at[chunk]))
     for copy in copies:
         copy.start()
-    for chunk, copy in enumerate(copies):
+    weights = weight_ref[...].astype(F32).astype(BF16)
+    row = lax.broadcasted_iota(jnp.int32, (weights.shape[0], 2 * EDGE), 0)
+    lane = lax.broadcasted_iota(jnp.int32, (weights.shape[0], 2 * EDGE), 1)
+    for pair in range(SLOTS // 2):
+        chosen = row == 2 * pair + (lane >= EDGE).astype(jnp.int32)
+        unit = jnp.where(chosen, 1.0, 0.0).astype(BF16)
+        spread = lax.dot_general(
+            weights, unit, (((0,), (0,)), ((), ())), preferred_element_type=F32
+        ).astype(BF16)
+        spread_ref[2 * pair] = spread[:, :EDGE]
+        spread_ref[2 * pair + 1] = spread[:, EDGE:]
+    for copy in copies:
         copy.wait()
-        for mat in range(chunk * CHUNK, (chunk + 1) * CHUNK):
-            turned_ref[SLOTS - 1 - mat] = plain_ref[mat].T
-
-
-def couple_slots(source, weight_ref, mats_ref, slots, total=None):
-    span = source.shape[1]
-    width = weight_ref.shape[1]
+
+
+def stand_up(cells, upright):
+    width = cells.shape[1] - EDGE
+    turned = cells.astype(F32).T
+    for half in range(upright.shape[0]):
+        lanes = slice(half * EDGE, (half + 1) * EDGE)
+        upright[half, LEAD : LEAD + width, :] = turned[:width, lanes]
+        upright[half, LEAD + width :, :] = turned[width : width + LEAD, lanes]
+        upright[half, :LEAD, :] = turned[width + EDGE - LEAD :, lanes]
+
+
+def couple_slots(upright, spread_ref, mats_ref, slots, adjoint_mode, total=None):
+    width = spread_ref.shape[1]
     for slot in slots:
-        moved = pltpu.roll(source, (-OFFSETS[slot]) % span, 1)[:, :width]
-        selected = moved * weight_ref[slot : slot + 1, :]
-        product = jnp.dot(mats_ref[slot], selected, preferred_element_type=F32)
+        start = LEAD + OFFSETS[slot]
+        weight = spread_ref[slot]
+        selected = jnp.concatenate(
+            [
+                upright[half, start : start + width, :].astype(BF16) * weight
+                for half in range(upright.shape[0])
+            ],
+            axis=1,
+        )
+        mat = mats_ref[SLOTS - 1 - slot if adjoint_mode else slot]
+        dims = (((1,), (0 if adjoint_mode else 1,)), ((), ()))
+        product = lax.dot_general(selected, mat, dims, preferred_element_type=F32)
         total = product if total is None else total + product
     return total
 
 
 def adjoint_kernel(
-    masks, count, place, a_ref, far_ref, class_ref, weight_ref, mats_ref, after_ref, *refs
+    masks, count, place, a_ref, far_ref, class_ref, spread_ref, mats_ref, after_ref, *refs
 ):
     half = len(masks)
-    near, across = split_pieces(refs[:-5])
-    send_ref, keep_ref, total_ref, expanded, stacked = refs[-5:]
+    near, across = split_pieces(refs[:-6])
+    send_ref, keep_ref, total_ref, expanded, stacked, upright = refs[-6:]
     rows, width = a_ref.shape
     depth = far_ref.shape[1]
     mats = count * rows
-    base = mats + rows + 16
-    edge_rows = slice(mats, mats + rows)
-    lanes = slice(EDGE, 2 * EDGE)
+    base = mats + rows // edge_parts(rows)
     far_own = jnp.concatenate(
         [
             far_ref[base + (2 * part + 1) * rows : base + (2 * part + 2) * rows, :]
@@ -167,14 +221,13 @@
         ],
         axis=1,
     )
+    halos = [pick_halo(place, pieces, masks, mats, rows) for pieces in (near, across)]
     padded = [
-        jnp.concatenate([own, pick_halo(place, pieces, masks, edge_rows, lanes).astype(BF16)], axis=1)
-        for own, pieces in ((a_ref[...], near), (far_own, across))
+        jnp.concatenate([own, join_halo(halo, A_SHIFT).astype(BF16)], axis=1)
+        for own, halo in ((a_ref[...], halos[0]), (far_own, halos[1]))
     ]
-    class_halo = pick_halo(place, near, masks, slice(mats + rows, mats + rows + 16), slice(0, EDGE))
-    labels = jnp.concatenate(
-        [class_ref[...], class_halo[0:1, :].astype(jnp.int32)], axis=1
-    )
+    class_halo = join_halo(tuple(cells[0:8, :] for cells in halos[0]), C_SHIFT)
+    labels = jnp.concatenate([class_ref[...], class_halo[0:1, :].astype(jnp.int32)], axis=1)
     at = 0
     for piece in range(half):
         for which, pieces in ((0, near), (1, across)):
@@ -187,8 +240,9 @@
                 at += rows
     scattered = lax.dot_general(
         stacked[...], expanded[...], (((0,), (0,)), ((), ())), preferred_element_type=F32
-    ).astype(BF16)
-    total_ref[...] = couple_slots(scattered, weight_ref, mats_ref, range(SLOTS))
+    )
+    stand_up(scattered.astype(BF16), upright)
+    total_ref[...] = couple_slots(upright, spread_ref, mats_ref, range(SLOTS), True).T
     steps = keep_ref.shape[0]
     for rel in range(steps):
         start = pl.multiple_of(((place[2] ^ rel) * 2 + place[1]) * rows, rows)
@@ -197,27 +251,30 @@
         send_ref[rel] = total_ref[pl.ds(start, rows), :].astype(BF16)
 
 
-def gather_kernel(rels, place, weight_ref, mats_ref, *refs):
-    pieces, total_ref, padded = refs[:-2], refs[-2], refs[-1]
+def gather_kernel(rels, place, spread_ref, mats_ref, *refs):
+    pieces, total_ref, upright, padded = refs[:-3], refs[-3], refs[-2], refs[-1]
     block = pieces[0].shape[0]
     for rel, piece_ref in zip(rels, pieces):
         start = pl.multiple_of((place[2] ^ rel) * block, block)
         padded[pl.ds(start, block), :] = piece_ref[...]
-    total_ref[...] = couple_slots(padded[...], weight_ref, mats_ref, range(EARLY))
-
-
-def forward_kernel(masks, count, place, f_ref, class_ref, weight_ref, mats_ref, total_ref, padded, *refs):
+    stand_up(padded[...], upright)
+    total_ref[...] = couple_slots(upright, spread_ref, mats_ref, range(EARLY), False)
+
+
+def forward_kernel(masks, count, place, f_ref, class_ref, spread_ref, mats_ref, total_ref, upright, *refs):
     (near, across), out_ref = split_pieces(refs[:-1]), refs[-1]
     rows, width = f_ref.shape
     mats = count * rows
     coupled = couple_slots(
-        padded[...], weight_ref, mats_ref, range(EARLY, SLOTS), total_ref[...]
+        upright, spread_ref, mats_ref, range(EARLY, SLOTS), False, total_ref[...]
     ).astype(BF16)
     applied = jnp.zeros((rows, width), F32)
     labels = class_ref[...]
     for piece in range(len(masks)):
         ref, spot = near[piece]
-        product = jnp.dot(ref[spot, :mats, :], coupled, preferred_element_type=F32)
+        product = lax.dot_general(
+            ref[spot, :mats, :], coupled, (((1,), (1,)), ((), ())), preferred_element_type=F32
+        )
         for local_class in range(count):
             hit = labels == (place[0] ^ masks[piece]) * count + local_class
             applied = jnp.where(hit, product[local_class * rows : (local_class + 1) * rows, :], applied)
@@ -238,9 +295,10 @@
         return lax.ppermute(cells, ("tiles", "coef"), pairs)
 
     weights = (neighbours >= 0).astype(BF16).T
+    weights = jnp.pad(weights, ((0, -SLOTS % 16), (0, 0)))
     labels = classes.reshape(1, width)
     mats = count * rows
-    near_rows = mats + rows + 16
+    near_rows = mats + rows // edge_parts(rows)
     far_rows = near_rows + 2 * rows * (width // depth)
     place, near_own, far_own, fields, adjoints, labels = pl.pallas_call(
         pack_kernel,
@@ -257,15 +315,18 @@
         scratch_shapes=[pltpu.VMEM(tmatrices.shape, BF16), pltpu.SemaphoreType.DMA((4,))],
         compiler_params=PARAMS,
     )(*[in_hbm(cells) for cells in (tmatrices, fields, adjoints, labels)])
-    mats_plain, mats_turned = pl.pallas_call(
+    mats_held, spread = pl.pallas_call(
         prepare_kernel,
-        out_shape=(jax.ShapeDtypeStruct(couple.shape, BF16),) * 2,
-        in_specs=[HBM, SMEM],
+        out_shape=(
+            jax.ShapeDtypeStruct(couple.shape, BF16),
+            jax.ShapeDtypeStruct((SLOTS, width, EDGE), BF16),
+        ),
+        in_specs=[HBM, VMEM, SMEM],
         out_specs=(VMEM, VMEM),
         scratch_shapes=[pltpu.SemaphoreType.DMA((SLOTS // CHUNK,))],
         cost_estimate=pl.CostEstimate(flops=0, bytes_accessed=4 * couple.size, transcendentals=0),
         compiler_params=PARAMS,
-    )(in_hbm(couple), place)
+    )(in_hbm(couple), weights, place)
 
     top = tiles // 2
     far = swap(far_own, 0, 1)
@@ -275,7 +336,7 @@
         in_specs=[VMEM] * 5,
         out_specs=VMEM,
         compiler_params=PARAMS,
-    )(near_own, swap(near_own, top, 0), far, swap(near_own, top, 1), mats_turned)
+    )(near_own, swap(near_own, top, 0), far, swap(near_own, top, 1), mats_held)
     held, lows = [first], [0]
     bit = top // 2
     while bit >= 1:
@@ -317,22 +378,24 @@
             pltpu.VMEM((total_rows, width), F32),
             pltpu.VMEM((2 * len(masks) * mats, width + EDGE), BF16),
             pltpu.VMEM((2 * len(masks) * mats, depth), BF16),
+            pltpu.VMEM((total_rows // EDGE, width + 2 * LEAD, EDGE), F32),
         ],
         cost_estimate=work(SLOTS + 8),
         compiler_params=PARAMS,
-    )(place, adjoints, far, labels, weights, mats_turned, padded_fields, *held)
+    )(place, adjoints, far, labels, spread, mats_held, padded_fields, *held)
 
     partial, all_fields = pl.pallas_call(
         functools.partial(gather_kernel, rels),
         out_shape=(
-            jax.ShapeDtypeStruct((total_rows, width), F32),
-            jax.ShapeDtypeStruct((total_rows, width + EDGE), BF16),
+            jax.ShapeDtypeStruct((width, total_rows), F32),
+            jax.ShapeDtypeStruct((total_rows // EDGE, width + 2 * LEAD, EDGE), F32),
         ),
         in_specs=[SMEM] + [VMEM] * (2 + len(rels)),
         out_specs=(VMEM, VMEM),
+        scratch_shapes=[pltpu.VMEM((total_rows, width + EDGE), BF16)],
         cost_estimate=work(EARLY),
         compiler_params=PARAMS,
-    )(place, weights, mats_plain, *[gathered[rel] for rel in rels])
+    )(place, spread, mats_held, *[gathered[rel] for rel in rels])
     bit = groups // 2
     arrived = swap(send, 0, 2 * bit)
     while bit > 1:
@@ -358,7 +421,7 @@
         out_specs=VMEM,
         cost_estimate=work(SLOTS - EARLY + 8),
         compiler_params=PARAMS,
-    )(place, fields, labels, weights, mats_plain, partial, all_fields, *held)
+    )(place, fields, labels, spread, mats_held, partial, all_fields, *held)
     return (forward_out, adjoint_out)
 
 

time: 34.2 us -> 35.4 us (1.035)
  waiting for transfers between devices: 4.6 us -> 5.92 us
  Pallas kernels: 14.8 us -> 13.6 us
  other arithmetic: 0.64 us -> 1.49 us
    ppermute x9, waiting for transfers between devices: 4.6 us -> 5.92 us  [swap(): return lax.ppermute(cells, ('tiles', 'coef'), pairs)]
    transpose x1, other arithmetic: 0.01 us -> 0.85 us  [local(): weights = (neighbours >= 0).astype(BF16).T]
    pallas_call x1, Pallas kernels: 3.05 us -> 2.45 us  [local(): pl.pallas_call(functools.partial(gather_kernel, rels), out_shape=(jax.Sha...]
    pallas_call x1, Pallas kernels: 4.09 us -> 3.62 us  [local(): pl.pallas_call(functools.partial(adjoint_kernel, masks, count), out_shape...]
    pallas_call x1, Pallas kernels: 3.02 us -> 2.67 us  [local(): pl.pallas_call(prepare_kernel, out_shape=(jax.ShapeDtypeStruct(couple.sha...]
  transfers between devices with their start and end apart: 9 -> 9, of which waited for: 4 -> 5; matrix products, arithmetic and copies ran while one was open for 0% -> 2% of each run, Pallas kernels for 37% -> 33%
where the time goes in v5:
time: 35.4 us; the launch traced here: 35.2 us
  Pallas kernels  13.6 us (38%)
  starting transfers between devices  13.5 us (38%)
  waiting for transfers between devices  5.92 us (17%)
  other arithmetic  1.49 us (4%)
  between operations  0.71 us (2%)
    ppermute x9, starting transfers between devices, swap(): return lax.ppermute(cells, ('tiles', 'coef'), pairs)  13.5 us
    ppermute x9, waiting for transfers between devices, swap(): return lax.ppermute(cells, ('tiles', 'coef'), pairs)  5.92 us
    pallas_call x1, Pallas kernels, local(): pl.pallas_call(functools.partial(adjoint_kernel, masks, count), out_shape...  3.62 us
    pallas_call x1, Pallas kernels, local(): pl.pallas_call(functools.partial(forward_kernel, masks, count), out_shape...  2.75 us
    pallas_call x1, Pallas kernels, local(): pl.pallas_call(prepare_kernel, out_shape=(jax.ShapeDtypeStruct(couple.sha...  2.67 us
    pallas_call x1, Pallas kernels, local(): pl.pallas_call(functools.partial(gather_kernel, rels), out_shape=(jax.Sha...  2.45 us
    pallas_call x1, Pallas kernels, local(): pl.pallas_call(pack_kernel, out_shape=(jax.ShapeDtypeStruct((3,), jnp.int...  1.48 us
    transpose x1, other arithmetic, local(): weights = (neighbours >= 0).astype(BF16).T  0.85 us
  transfers between devices with their start and end apart: 9, of which 5 were waited for; matrix products, arithmetic and copies ran while one was open for 2% of the time, Pallas kernels for 33%

profile of v5, /device:TPU:0, one launch (start us, length us, event | category | flops | bytes accessed | tf_op | source)
XLA Modules:
  0.0 35.2 jit_solution(8541458349712600757)
XLA Ops:
  0.6 1.5 %shard_map.77 = (s32[3]{0:T(128)S(1)}, bf16[144,256]{1,0:T(8,128)(2,1)S(1)}, bf16[272,256]{1,0:T(8,128)(2,1)S(1)}, bf16[32,512]{1,0:T(8,128)(2,1)S(1)}, bf16[32,...) custom-call(bf16[4,32,256]{2,1,0:T(8,128)(2,1)} %t_any.1, bf16[32,512]{1,0:T(8,128)(2,1)} %f_any.1, bf16[32,512]{1,0:T(8,128)(2,1)} %a_any.1, ...), custom_call_target="tpu_custom_call" | custom-call | tf_op jit(solution)/shard_map/pallas_call | solution.py:303
  2.1 3.0 %collective-permute-start.1 = (bf16[144,256]{1,0:T(8,128)(2,1)S(1)}, bf16[144,256]{1,0:T(8,128)(2,1)S(1)}, u32[]{:S(2)}, u32[]{:S(2)}) collective-permute-start(bf16[144,256]{1,0:T(8,128)(2,1)S(1)} %get-tuple-element.22.near_ref), channel_id=1, source_target_pairs={{0,16},{1,17},{2,18},{3,19},{4,20},{5,21},{6,22},{7,23},{8,24},{9,... | collective-permute-start | bytes 221192 | tf_op jit(solution)/shard_map/ppermute | solution.py:295
  5.2 1.4 %collective-permute-start.2 = (bf16[144,256]{1,0:T(8,128)(2,1)S(1)}, bf16[144,256]{1,0:T(8,128)(2,1)S(1)}, u32[]{:S(2)}, u32[]{:S(2)}) collective-permute-start(bf16[144,256]{1,0:T(8,128)(2,1)S(1)} %get-tuple-element.22.near_ref), channel_id=1, source_target_pairs={{0,17},{1,16},{2,19},{3,18},{4,21},{5,20},{6,23},{7,22},{8,25},{9,... | collective-permute-start | bytes 221192 | tf_op jit(solution)/shard_map/ppermute | solution.py:295
  6.6 0.1 collective-permute-start
  6.7 0.9 %compare_bitcast_fusion = pred[30,512]{1,0:T(8,128)(4,1)S(1)} fusion(s32[512,30]{0,1:T(8,128)} %param.10), kind=kLoop, calls=%fused_computation.3 | loop fusion | flops 15360 | bytes 76800 | tf_op jit(solution)/shard_map/transpose | solution.py:297
  7.6 2.7 %shard_map.78 = (bf16[30,256,256]{2,1,0:T(8,128)(2,1)S(1)}, bf16[30,512,128]{2,1,0:T(8,128)(2,1)S(1)}) custom-call(bf16[30,256,256]{2,1,0:T(8,128)(2,1)} %couple_ref.1, bf16[32,512]{1,0:T(8,128)(2,1)S(1)} %pad_convert_fusion.weight_ref, s32[3]{0:T(128)S(1)} %get-tuple-element.16.after_ref.place), custom_call_target="tpu_custom_call" | custom-call | bytes 7864320 | tf_op jit(solution)/shard_map/pallas_call | solution.py:318
  10.2 0.0 collective-permute-done.1.top_ref
  10.3 0.9 %collective-permute-done.2.cross_ref = bf16[144,256]{1,0:T(8,128)(2,1)S(1)} collective-permute-done((bf16[144,256]{1,0:T(8,128)(2,1)S(1)}, bf16[144,256]{1,0:T(8,128)(2,1)S(1)}, u32[]{:S(2)}, u32[]{:S(2)}) %collective-permute-start.2) | collective-permute-done | bytes 73760 | tf_op jit(solution)/shard_map/ppermute | solution.py:295
  11.2 0.8 %collective-permute-done.far_ref = bf16[272,256]{1,0:T(8,128)(2,1)S(1)} collective-permute-done((bf16[272,256]{1,0:T(8,128)(2,1)S(1)}, bf16[272,256]{1,0:T(8,128)(2,1)S(1)}, u32[]{:S(2)}, u32[]{:S(2)}) %collective-permute-start) | collective-permute-done | bytes 139296 | tf_op jit(solution)/shard_map/ppermute | solution.py:295
  12.0 0.1 collective-permute-start.3
  12.1 1.6 %collective-permute-done.3.refs_1_ = bf16[4,144,256]{2,1,0:T(8,128)(2,1)S(1)} collective-permute-done((bf16[4,144,256]{2,1,0:T(8,128)(2,1)S(1)}, bf16[4,144,256]{2,1,0:T(8,128)(2,1)S(1)}, u32[]{:S(2)}, u32[]{:S(2)}) %collective-permute-start.3) | collective-permute-done | bytes 294944 | tf_op jit(solution)/shard_map/ppermute | solution.py:295
  13.7 0.6 %shard_map.80.refs_0_.after_ref = bf16[64,640]{1,0:T(8,128)(2,1)S(1)} custom-call(s32[3]{0:T(128)S(1)} %get-tuple-element.16.after_ref.place, bf16[32,512]{1,0:T(8,128)(2,1)S(1)} %get-tuple-element.17.f_ref, bf16[272,256]{1,0:T(8,128)(2,1)S(1)} %collective-permute-done.far_ref, bf16[4,144,256]{2,1,0:T(8,128)(2,1)S(1)} %shard_map.79.refs_0_, ...), custom_call_target="tpu_custom_call" | custom-call | tf_op jit(solution)/shard_map/pallas_call | solution.py:348
  14.3 1.9 %collective-permute-start.4 = (bf16[64,640]{1,0:T(8,128)(2,1)S(1)}, bf16[64,640]{1,0:T(8,128)(2,1)S(1)}, u32[]{:S(2)}, u32[]{:S(2)}) collective-permute-start(bf16[64,640]{1,0:T(8,128)(2,1)S(1)} %shard_map.80.refs_0_.after_ref), channel_id=1, source_target_pairs={{0,2},{1,3},{2,0},{3,1},{4,6},{5,7},{6,4},{7,5},{8,10},{9,11},{10,... | collective-permute-start | bytes 245768 | tf_op jit(solution)/shard_map/ppermute | solution.py:295
  16.1 2.6 %collective-permute-start.5 = (bf16[64,640]{1,0:T(8,128)(2,1)S(1)}, bf16[64,640]{1,0:T(8,128)(2,1)S(1)}, u32[]{:S(2)}, u32[]{:S(2)}) collective-permute-start(bf16[64,640]{1,0:T(8,128)(2,1)S(1)} %shard_map.80.refs_0_.after_ref), channel_id=1, source_target_pairs={{0,4},{1,5},{2,6},{3,7},{4,0},{5,1},{6,2},{7,3},{8,12},{9,13},{10,... | collective-permute-start | bytes 245768 | tf_op jit(solution)/shard_map/ppermute | solution.py:295
  18.7 3.6 %shard_map.83 = (bf16[2,32,512]{2,1,0:T(8,128)(2,1)S(1)}, f32[2,32,512]{2,1,0:T(8,128)S(1)}) custom-call(s32[3]{0:T(128)S(1)} %get-tuple-element.16.after_ref.place, bf16[32,512]{1,0:T(8,128)(2,1)S(1)} %get-tuple-element.25.a_ref, bf16[272,256]{1,0:T(8,128)(2,1)S(1)} %collective-permute-done.far_ref, s32[1,512]{1,0:T(1,128)S(1)} %get-tuple-element.18.class_ref, ...), custom_call_target="tpu_custom_call" | custom-call | flops 2550136832 | bytes 4980736 | tf_op jit(solution)/shard_map/pallas_call | solution.py:369
  22.3 2.0 %collective-permute-start.7 = (bf16[2,32,512]{2,1,0:T(8,128)(2,1)S(1)}, bf16[2,32,512]{2,1,0:T(8,128)(2,1)S(1)}, u32[]{:S(2)}, u32[]{:S(2)}) collective-permute-start(bf16[2,32,512]{2,1,0:T(8,128)(2,1)S(1)} %get-tuple-element.27), channel_id=1, source_target_pairs={{0,4},{1,5},{2,6},{3,7},{4,0},{5,1},{6,2},{7,3},{8,12},{9,13},{10,... | collective-permute-start | bytes 196616 | tf_op jit(solution)/shard_map/ppermute | solution.py:295
  24.3 0.0 collective-permute-done.4.refs_1_
  24.3 1.3 %collective-permute-done.5.refs_2_ = bf16[64,640]{1,0:T(8,128)(2,1)S(1)} collective-permute-done((bf16[64,640]{1,0:T(8,128)(2,1)S(1)}, bf16[64,640]{1,0:T(8,128)(2,1)S(1)}, u32[]{:S(2)}, u32[]{:S(2)}) %collective-permute-start.5) | collective-permute-done | bytes 81952 | tf_op jit(solution)/shard_map/ppermute | solution.py:295
  25.6 0.0 collective-permute-done.6.refs_3_
  25.6 2.5 %shard_map.81 = (f32[512,256]{1,0:T(8,128)S(1)}, f32[2,544,128]{2,1,0:T(8,128)S(1)}) custom-call(s32[3]{0:T(128)S(1)} %get-tuple-element.16.after_ref.place, bf16[30,512,128]{2,1,0:T(8,128)(2,1)S(1)} %get-tuple-element.19.spread_ref, bf16[30,256,256]{2,1,0:T(8,128)(2,1)S(1)} %get-tuple-element.20.after_ref.mats_ref, ...), custom_call_target="tpu_custom_call" | custom-call | flops 1476395008 | bytes 2883584 | tf_op jit(solution)/shard_map/pallas_call | solution.py:387
  28.1 1.3 %collective-permute-done.7.arrived_ref = bf16[2,32,512]{2,1,0:T(8,128)(2,1)S(1)} collective-permute-done((bf16[2,32,512]{2,1,0:T(8,128)(2,1)S(1)}, bf16[2,32,512]{2,1,0:T(8,128)(2,1)S(1)}, u32[]{:S(2)}, u32[]{:S(2)}) %collective-permute-start.7) | collective-permute-done | bytes 65568 | tf_op jit(solution)/shard_map/ppermute | solution.py:295
  29.4 2.4 %collective-permute-start.8 = (bf16[1,32,512]{2,1,0:T(8,128)(2,1)S(1)}, bf16[1,32,512]{2,1,0:T(8,128)(2,1)S(1)}, u32[]{:S(2)}, u32[]{:S(2)}) collective-permute-start(bf16[1,32,512]{2,1,0:T(8,128)(2,1)S(1)} %get-tuple-element.29), channel_id=1, source_target_pairs={{0,2},{1,3},{2,0},{3,1},{4,6},{5,7},{6,4},{7,5},{8,10},{9,11},{10,... | collective-permute-start | bytes 98312 | tf_op jit(solution)/shard_map/ppermute | solution.py:295
  31.8 2.7 %shard_map.82 = bf16[32,512]{1,0:T(8,128)(2,1)} custom-call(s32[3]{0:T(128)S(1)} %get-tuple-element.16.after_ref.place, bf16[32,512]{1,0:T(8,128)(2,1)S(1)} %get-tuple-element.17.f_ref, s32[1,512]{1,0:T(1,128)S(1)} %get-tuple-element.18.class_ref, bf16[30,512,128]{2,1,0:T(8,128)(2,1)S(1)} %get-tuple-element.19.spread_ref, ...), custom_call_target="tpu_custom_call" | custom-call | flops 1073741824 | bytes 2097152 | tf_op jit(solution)/shard_map/pallas_call | solution.py:417
  34.5 0.6 %fusion = bf16[32,512]{1,0:T(8,128)(2,1)} fusion(f32[1,32,512]{2,1,0:T(8,128)S(1)} %get-tuple-element.28, bf16[1,32,512]{2,1,0:T(8,128)(2,1)S(1)} %collective-permute-done.8, bf16[32,512]{1,0:T(8,128)(2,1)S(1)} %get-tuple-element.25.a_ref), kind=kLoop, calls=%fused_computation.1 | loop fusion | flops 81920 | bytes 163840 | tf_op jit(solution)/shard_map/convert_element_type | solution.py:415
  (5 shorter events, 0.1 us)
Async XLA Ops:
  2.1 8.1 %collective-permute-start.1 = (bf16[144,256]{1,0:T(8,128)(2,1)S(1)}, bf16[144,256]{1,0:T(8,128)(2,1)S(1)}, u32[]{:S(2)}, u32[]{:S(2)}) collective-permute-start(bf16[144,256]{1,0:T(8,128)(2,1)S(1)} %get-tuple-element.22.near_ref), channel_id=1, source_target_pairs={{0,16},{1,17},{2,18},{3,19},{4,20},{5,21},{6,22},{7,23},{8,24},{9,... | collective-permute-start | bytes 221192 | tf_op jit(solution)/shard_map/ppermute | solution.py:295
  5.2 6.0 %collective-permute-start.2 = (bf16[144,256]{1,0:T(8,128)(2,1)S(1)}, bf16[144,256]{1,0:T(8,128)(2,1)S(1)}, u32[]{:S(2)}, u32[]{:S(2)}) collective-permute-start(bf16[144,256]{1,0:T(8,128)(2,1)S(1)} %get-tuple-element.22.near_ref), channel_id=1, source_target_pairs={{0,17},{1,16},{2,19},{3,18},{4,21},{5,20},{6,23},{7,22},{8,25},{9,... | collective-permute-start | bytes 221192 | tf_op jit(solution)/shard_map/ppermute | solution.py:295
  6.6 5.4 %collective-permute-start = (bf16[272,256]{1,0:T(8,128)(2,1)S(1)}, bf16[272,256]{1,0:T(8,128)(2,1)S(1)}, u32[]{:S(2)}, u32[]{:S(2)}) collective-permute-start(bf16[272,256]{1,0:T(8,128)(2,1)S(1)} %get-tuple-element.21), channel_id=1, source_target_pairs={{0,1},{1,0},{2,3},{3,2},{4,5},{5,4},{6,7},{7,6},{8,9},{9,8},{10,11... | collective-permute-start | bytes 417800 | tf_op jit(solution)/shard_map/ppermute | solution.py:295
  12.0 1.6 %collective-permute-start.3 = (bf16[4,144,256]{2,1,0:T(8,128)(2,1)S(1)}, bf16[4,144,256]{2,1,0:T(8,128)(2,1)S(1)}, u32[]{:S(2)}, u32[]{:S(2)}) collective-permute-start(bf16[4,144,256]{2,1,0:T(8,128)(2,1)S(1)} %shard_map.79.refs_0_), channel_id=1, source_target_pairs={{0,8},{1,9},{2,10},{3,11},{4,12},{5,13},{6,14},{7,15},{8,0},{9,1},... | collective-permute-start | bytes 884744 | tf_op jit(solution)/shard_map/ppermute | solution.py:295
  14.3 10.1 %collective-permute-start.4 = (bf16[64,640]{1,0:T(8,128)(2,1)S(1)}, bf16[64,640]{1,0:T(8,128)(2,1)S(1)}, u32[]{:S(2)}, u32[]{:S(2)}) collective-permute-start(bf16[64,640]{1,0:T(8,128)(2,1)S(1)} %shard_map.80.refs_0_.after_ref), channel_id=1, source_target_pairs={{0,2},{1,3},{2,0},{3,1},{4,6},{5,7},{6,4},{7,5},{8,10},{9,11},{10,... | collective-permute-start | bytes 245768 | tf_op jit(solution)/shard_map/ppermute | solution.py:295
  16.1 9.5 %collective-permute-start.5 = (bf16[64,640]{1,0:T(8,128)(2,1)S(1)}, bf16[64,640]{1,0:T(8,128)(2,1)S(1)}, u32[]{:S(2)}, u32[]{:S(2)}) collective-permute-start(bf16[64,640]{1,0:T(8,128)(2,1)S(1)} %shard_map.80.refs_0_.after_ref), channel_id=1, source_target_pairs={{0,4},{1,5},{2,6},{3,7},{4,0},{5,1},{6,2},{7,3},{8,12},{9,13},{10,... | collective-permute-start | bytes 245768 | tf_op jit(solution)/shard_map/ppermute | solution.py:295
  18.7 6.9 %collective-permute-start.6 = (bf16[64,640]{1,0:T(8,128)(2,1)S(1)}, bf16[64,640]{1,0:T(8,128)(2,1)S(1)}, u32[]{:S(2)}, u32[]{:S(2)}) collective-permute-start(bf16[64,640]{1,0:T(8,128)(2,1)S(1)} %shard_map.80.refs_0_.after_ref), channel_id=1, source_target_pairs={{0,6},{1,7},{2,4},{3,5},{4,2},{5,3},{6,0},{7,1},{8,14},{9,15},{10,... | collective-permute-start | bytes 245768 | tf_op jit(solution)/shard_map/ppermute | solution.py:295
  22.3 7.0 %collective-permute-start.7 = (bf16[2,32,512]{2,1,0:T(8,128)(2,1)S(1)}, bf16[2,32,512]{2,1,0:T(8,128)(2,1)S(1)}, u32[]{:S(2)}, u32[]{:S(2)}) collective-permute-start(bf16[2,32,512]{2,1,0:T(8,128)(2,1)S(1)} %get-tuple-element.27), channel_id=1, source_target_pairs={{0,4},{1,5},{2,6},{3,7},{4,0},{5,1},{6,2},{7,3},{8,12},{9,13},{10,... | collective-permute-start | bytes 196616 | tf_op jit(solution)/shard_map/ppermute | solution.py:295
  29.4 5.2 %collective-permute-start.8 = (bf16[1,32,512]{2,1,0:T(8,128)(2,1)S(1)}, bf16[1,32,512]{2,1,0:T(8,128)(2,1)S(1)}, u32[]{:S(2)}, u32[]{:S(2)}) collective-permute-start(bf16[1,32,512]{2,1,0:T(8,128)(2,1)S(1)} %get-tuple-element.29), channel_id=1, source_target_pairs={{0,2},{1,3},{2,0},{3,1},{4,6},{5,7},{6,4},{7,5},{8,10},{9,11},{10,... | collective-permute-start | bytes 98312 | tf_op jit(solution)/shard_map/ppermute | solution.py:295

commit v6 on v5

--- a/solution.py
+++ b/solution.py
@@ -87,7 +87,7 @@
         far_ref[base + (2 * part + 1) * rows : base + (2 * part + 2) * rows, :] = adjoints[:, lanes]
 
 
-def relay_kernel(near_ref, top_ref, far_ref, cross_ref, after_ref, out_ref):
+def relay_kernel(far_ref, cross_ref, top_ref, near_ref, after_ref, out_ref):
     rows = near_ref.shape[0]
     out_ref[0] = near_ref[...]
     out_ref[1] = top_ref[...]
@@ -134,8 +134,8 @@
     return near, across
 
 
-def fields_kernel(masks, count, place, f_ref, far_ref, *refs):
-    (near, across), out_ref = split_pieces(refs[:-1]), refs[-1]
+def fields_kernel(masks, count, place, f_ref, *refs):
+    (near, across), far_ref, out_ref = split_pieces(refs[:-2]), refs[-2], refs[-1]
     rows, width = f_ref.shape
     depth = far_ref.shape[1]
     mats = count * rows
@@ -336,7 +336,7 @@
         in_specs=[VMEM] * 5,
         out_specs=VMEM,
         compiler_params=PARAMS,
-    )(near_own, swap(near_own, top, 0), far, swap(near_own, top, 1), mats_held)
+    )(far, swap(near_own, top, 1), swap(near_own, top, 0), near_own, mats_held)
     held, lows = [first], [0]
     bit = top // 2
     while bit >= 1:
@@ -351,13 +351,13 @@
         in_specs=[SMEM] + [VMEM] * (2 + len(held)),
         out_specs=VMEM,
         compiler_params=PARAMS,
-    )(place, fields, far, *held)
+    )(place, fields, *held, far)
 
     groups = coefs // 2
     gathered = {0: padded_fields}
     for rel in range(1, groups):
         gathered[rel] = swap(padded_fields, 0, 2 * rel)
-    rels = sorted(gathered)
+    rels = sorted(gathered, reverse=True)
 
     steps = groups // 2
     total_rows = couple.shape[1]

time: 35.4 us -> 32.7 us (0.924)
  waiting for transfers between devices: 5.92 us -> 3.79 us
  starting transfers between devices: 13.5 us -> 12.9 us
    ppermute x9, waiting for transfers between devices: 5.92 us -> 3.79 us  [swap(): return lax.ppermute(cells, ('tiles', 'coef'), pairs)]
    ppermute x9, starting transfers between devices: 13.5 us -> 12.9 us  [swap(): return lax.ppermute(cells, ('tiles', 'coef'), pairs)]
  transfers between devices with their start and end apart: 9 -> 9, of which waited for: 5 -> 4; matrix products, arithmetic and copies ran while one was open for 2% -> 3% of each run, Pallas kernels for 33% -> 35%
where the time goes in v6:
time: 32.7 us; the launch traced here: 32.4 us
  Pallas kernels  13.6 us (42%)
  starting transfers between devices  12.9 us (39%)
  waiting for transfers between devices  3.79 us (12%)
  other arithmetic  1.49 us (5%)
  between operations  0.71 us (2%)
    ppermute x9, starting transfers between devices, swap(): return lax.ppermute(cells, ('tiles', 'coef'), pairs)  12.9 us
    ppermute x9, waiting for transfers between devices, swap(): return lax.ppermute(cells, ('tiles', 'coef'), pairs)  3.79 us
    pallas_call x1, Pallas kernels, local(): pl.pallas_call(functools.partial(adjoint_kernel, masks, count), out_shape...  3.62 us
    pallas_call x1, Pallas kernels, local(): pl.pallas_call(functools.partial(forward_kernel, masks, count), out_shape...  2.75 us
    pallas_call x1, Pallas kernels, local(): pl.pallas_call(prepare_kernel, out_shape=(jax.ShapeDtypeStruct(couple.sha...  2.67 us
    pallas_call x1, Pallas kernels, local(): pl.pallas_call(functools.partial(gather_kernel, rels), out_shape=(jax.Sha...  2.45 us
    pallas_call x1, Pallas kernels, local(): pl.pallas_call(pack_kernel, out_shape=(jax.ShapeDtypeStruct((3,), jnp.int...  1.48 us
    transpose x1, other arithmetic, local(): weights = (neighbours >= 0).astype(BF16).T  0.85 us
  transfers between devices with their start and end apart: 9, of which 4 were waited for; matrix products, arithmetic and copies ran while one was open for 3% of the time, Pallas kernels for 35%

profile of v6, /device:TPU:0, one launch (start us, length us, event | category | flops | bytes accessed | tf_op | source)
XLA Modules:
  0.0 32.4 jit_solution(925768243658221935)
XLA Ops:
  0.6 1.5 %shard_map.77 = (s32[3]{0:T(128)S(1)}, bf16[144,256]{1,0:T(8,128)(2,1)S(1)}, bf16[272,256]{1,0:T(8,128)(2,1)S(1)}, bf16[32,512]{1,0:T(8,128)(2,1)S(1)}, bf16[32,...) custom-call(bf16[4,32,256]{2,1,0:T(8,128)(2,1)} %t_any.1, bf16[32,512]{1,0:T(8,128)(2,1)} %f_any.1, bf16[32,512]{1,0:T(8,128)(2,1)} %a_any.1, ...), custom_call_target="tpu_custom_call" | custom-call | tf_op jit(solution)/shard_map/pallas_call | solution.py:303
  2.1 4.0 %collective-permute-start.1 = (bf16[144,256]{1,0:T(8,128)(2,1)S(1)}, bf16[144,256]{1,0:T(8,128)(2,1)S(1)}, u32[]{:S(2)}, u32[]{:S(2)}) collective-permute-start(bf16[144,256]{1,0:T(8,128)(2,1)S(1)} %get-tuple-element.22.near_ref), channel_id=1, source_target_pairs={{0,17},{1,16},{2,19},{3,18},{4,21},{5,20},{6,23},{7,22},{8,25},{9,... | collective-permute-start | bytes 221192 | tf_op jit(solution)/shard_map/ppermute | solution.py:295
  6.1 0.5 %collective-permute-start.2 = (bf16[144,256]{1,0:T(8,128)(2,1)S(1)}, bf16[144,256]{1,0:T(8,128)(2,1)S(1)}, u32[]{:S(2)}, u32[]{:S(2)}) collective-permute-start(bf16[144,256]{1,0:T(8,128)(2,1)S(1)} %get-tuple-element.22.near_ref), channel_id=1, source_target_pairs={{0,16},{1,17},{2,18},{3,19},{4,20},{5,21},{6,22},{7,23},{8,24},{9,... | collective-permute-start | bytes 221192 | tf_op jit(solution)/shard_map/ppermute | solution.py:295
  6.6 0.1 collective-permute-start
  6.7 0.9 %compare_bitcast_fusion = pred[30,512]{1,0:T(8,128)(4,1)S(1)} fusion(s32[512,30]{0,1:T(8,128)} %param.10), kind=kLoop, calls=%fused_computation.3 | loop fusion | flops 15360 | bytes 76800 | tf_op jit(solution)/shard_map/transpose | solution.py:297
  7.6 2.7 %shard_map.78 = (bf16[30,256,256]{2,1,0:T(8,128)(2,1)S(1)}, bf16[30,512,128]{2,1,0:T(8,128)(2,1)S(1)}) custom-call(bf16[30,256,256]{2,1,0:T(8,128)(2,1)} %couple_ref.1, bf16[32,512]{1,0:T(8,128)(2,1)S(1)} %pad_convert_fusion.weight_ref, s32[3]{0:T(128)S(1)} %get-tuple-element.16.after_ref.place), custom_call_target="tpu_custom_call" | custom-call | bytes 7864320 | tf_op jit(solution)/shard_map/pallas_call | solution.py:318
  10.3 0.2 collective-permute-done.2.top_ref
  10.4 1.5 %collective-permute-done.far_ref.refs_2_ = bf16[272,256]{1,0:T(8,128)(2,1)S(1)} collective-permute-done((bf16[272,256]{1,0:T(8,128)(2,1)S(1)}, bf16[272,256]{1,0:T(8,128)(2,1)S(1)}, u32[]{:S(2)}, u32[]{:S(2)}) %collective-permute-start) | collective-permute-done | bytes 139296 | tf_op jit(solution)/shard_map/ppermute | solution.py:295
  12.0 0.1 collective-permute-start.3
  12.0 1.6 %collective-permute-done.3.refs_1_ = bf16[4,144,256]{2,1,0:T(8,128)(2,1)S(1)} collective-permute-done((bf16[4,144,256]{2,1,0:T(8,128)(2,1)S(1)}, bf16[4,144,256]{2,1,0:T(8,128)(2,1)S(1)}, u32[]{:S(2)}, u32[]{:S(2)}) %collective-permute-start.3) | collective-permute-done | bytes 294944 | tf_op jit(solution)/shard_map/ppermute | solution.py:295
  13.6 0.6 %shard_map.80.refs_3_.after_ref = bf16[64,640]{1,0:T(8,128)(2,1)S(1)} custom-call(s32[3]{0:T(128)S(1)} %get-tuple-element.16.after_ref.place, bf16[32,512]{1,0:T(8,128)(2,1)S(1)} %get-tuple-element.17.f_ref, bf16[4,144,256]{2,1,0:T(8,128)(2,1)S(1)} %shard_map.79.refs_0_, bf16[4,144,256]{2,1,0:T(8,128)(2,1)S(1)} %collective-permute-done.3.refs_1_, ...), custom_call_target="tpu_custom_call" | custom-call | tf_op jit(solution)/shard_map/pallas_call | solution.py:348
  14.2 3.7 %collective-permute-start.4 = (bf16[64,640]{1,0:T(8,128)(2,1)S(1)}, bf16[64,640]{1,0:T(8,128)(2,1)S(1)}, u32[]{:S(2)}, u32[]{:S(2)}) collective-permute-start(bf16[64,640]{1,0:T(8,128)(2,1)S(1)} %shard_map.80.refs_3_.after_ref), channel_id=1, source_target_pairs={{0,6},{1,7},{2,4},{3,5},{4,2},{5,3},{6,0},{7,1},{8,14},{9,15},{10,... | collective-permute-start | bytes 245768 | tf_op jit(solution)/shard_map/ppermute | solution.py:295
  17.8 0.0 collective-permute-start.5
  17.8 0.8 %collective-permute-start.6 = (bf16[64,640]{1,0:T(8,128)(2,1)S(1)}, bf16[64,640]{1,0:T(8,128)(2,1)S(1)}, u32[]{:S(2)}, u32[]{:S(2)}) collective-permute-start(bf16[64,640]{1,0:T(8,128)(2,1)S(1)} %shard_map.80.refs_3_.after_ref), channel_id=1, source_target_pairs={{0,2},{1,3},{2,0},{3,1},{4,6},{5,7},{6,4},{7,5},{8,10},{9,11},{10,... | collective-permute-start | bytes 245768 | tf_op jit(solution)/shard_map/ppermute | solution.py:295
  18.6 3.6 %shard_map.83 = (bf16[2,32,512]{2,1,0:T(8,128)(2,1)S(1)}, f32[2,32,512]{2,1,0:T(8,128)S(1)}) custom-call(s32[3]{0:T(128)S(1)} %get-tuple-element.16.after_ref.place, bf16[32,512]{1,0:T(8,128)(2,1)S(1)} %get-tuple-element.25.a_ref, bf16[272,256]{1,0:T(8,128)(2,1)S(1)} %collective-permute-done.far_ref.refs_2_, s32[1,512]{1,0:T(1,128)S(1)} %get-tuple-element.18.class_ref, ...), custom_call_target="tpu_custom_call" | custom-call | flops 2550136832 | bytes 4980736 | tf_op jit(solution)/shard_map/pallas_call | solution.py:369
  22.3 2.2 %collective-permute-start.7 = (bf16[2,32,512]{2,1,0:T(8,128)(2,1)S(1)}, bf16[2,32,512]{2,1,0:T(8,128)(2,1)S(1)}, u32[]{:S(2)}, u32[]{:S(2)}) collective-permute-start(bf16[2,32,512]{2,1,0:T(8,128)(2,1)S(1)} %get-tuple-element.27), channel_id=1, source_target_pairs={{0,4},{1,5},{2,6},{3,7},{4,0},{5,1},{6,2},{7,3},{8,12},{9,13},{10,... | collective-permute-start | bytes 196616 | tf_op jit(solution)/shard_map/ppermute | solution.py:295
  24.5 0.5 %collective-permute-done.5.refs_1_ = bf16[64,640]{1,0:T(8,128)(2,1)S(1)} collective-permute-done((bf16[64,640]{1,0:T(8,128)(2,1)S(1)}, bf16[64,640]{1,0:T(8,128)(2,1)S(1)}, u32[]{:S(2)}, u32[]{:S(2)}) %collective-permute-start.5) | collective-permute-done | bytes 81952 | tf_op jit(solution)/shard_map/ppermute | solution.py:295
  25.0 0.0 collective-permute-done.6.refs_2_
  25.0 2.5 %shard_map.81 = (f32[512,256]{1,0:T(8,128)S(1)}, f32[2,544,128]{2,1,0:T(8,128)S(1)}) custom-call(s32[3]{0:T(128)S(1)} %get-tuple-element.16.after_ref.place, bf16[30,512,128]{2,1,0:T(8,128)(2,1)S(1)} %get-tuple-element.19.spread_ref, bf16[30,256,256]{2,1,0:T(8,128)(2,1)S(1)} %get-tuple-element.20.after_ref.mats_ref, ...), custom_call_target="tpu_custom_call" | custom-call | flops 1476395008 | bytes 2883584 | tf_op jit(solution)/shard_map/pallas_call | solution.py:387
  27.5 0.0 collective-permute-done.7.arrived_ref
  27.5 1.5 %collective-permute-start.8 = (bf16[1,32,512]{2,1,0:T(8,128)(2,1)S(1)}, bf16[1,32,512]{2,1,0:T(8,128)(2,1)S(1)}, u32[]{:S(2)}, u32[]{:S(2)}) collective-permute-start(bf16[1,32,512]{2,1,0:T(8,128)(2,1)S(1)} %get-tuple-element.29), channel_id=1, source_target_pairs={{0,2},{1,3},{2,0},{3,1},{4,6},{5,7},{6,4},{7,5},{8,10},{9,11},{10,... | collective-permute-start | bytes 98312 | tf_op jit(solution)/shard_map/ppermute | solution.py:295
  29.1 2.7 %shard_map.82 = bf16[32,512]{1,0:T(8,128)(2,1)} custom-call(s32[3]{0:T(128)S(1)} %get-tuple-element.16.after_ref.place, bf16[32,512]{1,0:T(8,128)(2,1)S(1)} %get-tuple-element.17.f_ref, s32[1,512]{1,0:T(1,128)S(1)} %get-tuple-element.18.class_ref, bf16[30,512,128]{2,1,0:T(8,128)(2,1)S(1)} %get-tuple-element.19.spread_ref, ...), custom_call_target="tpu_custom_call" | custom-call | flops 1073741824 | bytes 2097152 | tf_op jit(solution)/shard_map/pallas_call | solution.py:417
  31.8 0.0 collective-permute-done.8
  31.8 0.6 %fusion = bf16[32,512]{1,0:T(8,128)(2,1)} fusion(f32[1,32,512]{2,1,0:T(8,128)S(1)} %get-tuple-element.28, bf16[1,32,512]{2,1,0:T(8,128)(2,1)S(1)} %collective-permute-done.8, bf16[32,512]{1,0:T(8,128)(2,1)S(1)} %get-tuple-element.25.a_ref), kind=kLoop, calls=%fused_computation.1 | loop fusion | flops 81920 | bytes 163840 | tf_op jit(solution)/shard_map/convert_element_type | solution.py:415
  (5 shorter events, 0.1 us)
Async XLA Ops:
  2.1 8.2 %collective-permute-start.1 = (bf16[144,256]{1,0:T(8,128)(2,1)S(1)}, bf16[144,256]{1,0:T(8,128)(2,1)S(1)}, u32[]{:S(2)}, u32[]{:S(2)}) collective-permute-start(bf16[144,256]{1,0:T(8,128)(2,1)S(1)} %get-tuple-element.22.near_ref), channel_id=1, source_target_pairs={{0,17},{1,16},{2,19},{3,18},{4,21},{5,20},{6,23},{7,22},{8,25},{9,... | collective-permute-start | bytes 221192 | tf_op jit(solution)/shard_map/ppermute | solution.py:295
  6.1 4.4 %collective-permute-start.2 = (bf16[144,256]{1,0:T(8,128)(2,1)S(1)}, bf16[144,256]{1,0:T(8,128)(2,1)S(1)}, u32[]{:S(2)}, u32[]{:S(2)}) collective-permute-start(bf16[144,256]{1,0:T(8,128)(2,1)S(1)} %get-tuple-element.22.near_ref), channel_id=1, source_target_pairs={{0,16},{1,17},{2,18},{3,19},{4,20},{5,21},{6,22},{7,23},{8,24},{9,... | collective-permute-start | bytes 221192 | tf_op jit(solution)/shard_map/ppermute | solution.py:295
  6.6 5.3 %collective-permute-start = (bf16[272,256]{1,0:T(8,128)(2,1)S(1)}, bf16[272,256]{1,0:T(8,128)(2,1)S(1)}, u32[]{:S(2)}, u32[]{:S(2)}) collective-permute-start(bf16[272,256]{1,0:T(8,128)(2,1)S(1)} %get-tuple-element.21), channel_id=1, source_target_pairs={{0,1},{1,0},{2,3},{3,2},{4,5},{5,4},{6,7},{7,6},{8,9},{9,8},{10,11... | collective-permute-start | bytes 417800 | tf_op jit(solution)/shard_map/ppermute | solution.py:295
  12.0 1.6 %collective-permute-start.3 = (bf16[4,144,256]{2,1,0:T(8,128)(2,1)S(1)}, bf16[4,144,256]{2,1,0:T(8,128)(2,1)S(1)}, u32[]{:S(2)}, u32[]{:S(2)}) collective-permute-start(bf16[4,144,256]{2,1,0:T(8,128)(2,1)S(1)} %shard_map.79.refs_0_), channel_id=1, source_target_pairs={{0,8},{1,9},{2,10},{3,11},{4,12},{5,13},{6,14},{7,15},{8,0},{9,1},... | collective-permute-start | bytes 884744 | tf_op jit(solution)/shard_map/ppermute | solution.py:295
  14.2 10.3 %collective-permute-start.4 = (bf16[64,640]{1,0:T(8,128)(2,1)S(1)}, bf16[64,640]{1,0:T(8,128)(2,1)S(1)}, u32[]{:S(2)}, u32[]{:S(2)}) collective-permute-start(bf16[64,640]{1,0:T(8,128)(2,1)S(1)} %shard_map.80.refs_3_.after_ref), channel_id=1, source_target_pairs={{0,6},{1,7},{2,4},{3,5},{4,2},{5,3},{6,0},{7,1},{8,14},{9,15},{10,... | collective-permute-start | bytes 245768 | tf_op jit(solution)/shard_map/ppermute | solution.py:295
  17.8 7.2 %collective-permute-start.5 = (bf16[64,640]{1,0:T(8,128)(2,1)S(1)}, bf16[64,640]{1,0:T(8,128)(2,1)S(1)}, u32[]{:S(2)}, u32[]{:S(2)}) collective-permute-start(bf16[64,640]{1,0:T(8,128)(2,1)S(1)} %shard_map.80.refs_3_.after_ref), channel_id=1, source_target_pairs={{0,4},{1,5},{2,6},{3,7},{4,0},{5,1},{6,2},{7,3},{8,12},{9,13},{10,... | collective-permute-start | bytes 245768 | tf_op jit(solution)/shard_map/ppermute | solution.py:295
  17.8 7.2 %collective-permute-start.6 = (bf16[64,640]{1,0:T(8,128)(2,1)S(1)}, bf16[64,640]{1,0:T(8,128)(2,1)S(1)}, u32[]{:S(2)}, u32[]{:S(2)}) collective-permute-start(bf16[64,640]{1,0:T(8,128)(2,1)S(1)} %shard_map.80.refs_3_.after_ref), channel_id=1, source_target_pairs={{0,2},{1,3},{2,0},{3,1},{4,6},{5,7},{6,4},{7,5},{8,10},{9,11},{10,... | collective-permute-start | bytes 245768 | tf_op jit(solution)/shard_map/ppermute | solution.py:295
  22.3 5.2 %collective-permute-start.7 = (bf16[2,32,512]{2,1,0:T(8,128)(2,1)S(1)}, bf16[2,32,512]{2,1,0:T(8,128)(2,1)S(1)}, u32[]{:S(2)}, u32[]{:S(2)}) collective-permute-start(bf16[2,32,512]{2,1,0:T(8,128)(2,1)S(1)} %get-tuple-element.27), channel_id=1, source_target_pairs={{0,4},{1,5},{2,6},{3,7},{4,0},{5,1},{6,2},{7,3},{8,12},{9,13},{10,... | collective-permute-start | bytes 196616 | tf_op jit(solution)/shard_map/ppermute | solution.py:295
  27.5 4.3 %collective-permute-start.8 = (bf16[1,32,512]{2,1,0:T(8,128)(2,1)S(1)}, bf16[1,32,512]{2,1,0:T(8,128)(2,1)S(1)}, u32[]{:S(2)}, u32[]{:S(2)}) collective-permute-start(bf16[1,32,512]{2,1,0:T(8,128)(2,1)S(1)} %get-tuple-element.29), channel_id=1, source_target_pairs={{0,2},{1,3},{2,0},{3,1},{4,6},{5,7},{6,4},{7,5},{8,10},{9,11},{10,... | collective-permute-start | bytes 98312 | tf_op jit(solution)/shard_map/ppermute | solution.py:295

commit v7 on v6

v7 whole, which is shorter than its diff:
```python
import functools

import jax
import jax.numpy as jnp
from jax import lax
from jax.experimental import pallas as pl
from jax.experimental.pallas import tpu as pltpu
from jax.sharding import PartitionSpec as P

SLOTS = 30
HW = 15
EDGE = 128
CHUNK = 5
LEAD = 16
BAND = 128
A_SHIFT = 32
C_SHIFT = 64
OFFSETS = [slot - HW + (1 if slot >= HW else 0) for slot in range(SLOTS)]
BF16 = jnp.bfloat16
F32 = jnp.float32
VMEM = pl.BlockSpec(memory_space=pltpu.VMEM)
SMEM = pl.BlockSpec(memory_space=pltpu.SMEM)
ANY = pl.BlockSpec(memory_space=pl.ANY)
HBM = pl.BlockSpec(memory_space=pltpu.HBM)
PARAMS = pltpu.CompilerParams(vmem_limit_bytes=24 * 1024 * 1024)


def in_hbm(cells):
    return pltpu.with_memory_space_constraint(cells, pltpu.HBM)


def edges_of(cells):
    width = cells.shape[1]
    head, tail = cells[:, :EDGE], cells[:, width - EDGE :]
    lane = lax.broadcasted_iota(jnp.int32, head.shape, 1)
    return jnp.where(lane < EDGE // 2, head, tail)


def edge_parts(rows):
    return 2 if rows % 32 == 0 else 1


def far_spans(base, rows, width, depth, which):
    starts = [base + (2 * part + which) * rows for part in range(width // depth)]
    return [slice(start, start + rows) for start in starts]


def far_cells(far_ref, base, rows, width, which):
    spans = far_spans(base, rows, width, far_ref.shape[1], which)
    return jnp.concatenate([far_ref[span, :] for span in spans], axis=1)


def pack_kernel(
    t_any, f_any, a_any, class_any, place, near_ref, far_ref, both_ref, class_ref, t_ref, sems
):
    coef = lax.axis_index("coef")
    place[0] = lax.axis_index("tiles")
    place[1] = coef & 1
    place[2] = coef >> 1
    copies = [
        pltpu.make_async_copy(source, target, sems.at[at])
        for at, (source, target) in enumerate(
            (
                (t_any, t_ref),
                (f_any, both_ref.at[0]),
                (a_any, both_ref.at[1]),
                (class_any, class_ref),
            )
        )
    ]
    for copy in copies:
        copy.start()
    for copy in copies:
        copy.wait()
    count, rows, depth = t_ref.shape
    mats = count * rows
    fields, adjoints = both_ref[0], both_ref[1]
    own = edges_of(fields).astype(F32)
    turned = pltpu.roll(edges_of(adjoints).astype(F32), A_SHIFT, 1)
    class_edge = pltpu.roll(
        jnp.broadcast_to(edges_of(class_ref[...]).astype(F32), (rows, EDGE)), C_SHIFT, 1
    )
    lane = lax.broadcasted_iota(jnp.int32, own.shape, 1)
    edge = jnp.where(
        (lane < HW) | (lane >= EDGE - HW),
        own,
        jnp.where((lane >= A_SHIFT - HW) & (lane < A_SHIFT + HW), turned, class_edge),
    ).astype(BF16)
    parts = edge_parts(rows)
    base = mats + rows // parts
    near_ref[:mats, :] = t_ref[...].reshape(mats, depth)
    for part in range(depth // EDGE):
        start = part * (rows // parts) if part < parts else 0
        near_ref[mats:base, part * EDGE : (part + 1) * EDGE] = edge[start : start + base - mats, :]
    far_ref[:base, :] = near_ref[...]
    for which, cells in enumerate((fields, adjoints)):
        for part, span in enumerate(far_spans(base, rows, cells.shape[1], depth, which)):
            far_ref[span, :] = cells[:, part * depth : (part + 1) * depth]


def relay_kernel(far_ref, cross_ref, top_ref, near_ref, after_ref, out_ref):
    out_ref[0] = near_ref[...]
    out_ref[1] = top_ref[...]
    out_ref[2] = far_ref[: near_ref.shape[0], :]
    out_ref[3] = cross_ref[...]


def pick_halo(place, pieces, masks, mats, rows):
    tile = place[0]
    parts = edge_parts(rows)
    lane = lax.broadcasted_iota(jnp.int32, (rows, EDGE), 1)
    above = jnp.zeros((rows, EDGE), F32)
    below = jnp.zeros((rows, EDGE), F32)
    for (piece_ref, at), mask in zip(pieces, masks):
        bands = [
            piece_ref[at, mats : mats + rows // parts, part * EDGE : (part + 1) * EDGE]
            for part in range(parts)
        ]
        cells = jnp.concatenate(bands, axis=0).astype(F32)
        owner = tile ^ mask
        above = jnp.where(owner == tile + 1, cells, above)
        below = jnp.where(owner == tile - 1, cells, below)
    return above, below


def join_halo(halo, shift):
    above, below = halo
    lane = lax.broadcasted_iota(jnp.int32, above.shape, 1)
    back = (EDGE - shift) % EDGE
    if back:
        above, below = pltpu.roll(above, back, 1), pltpu.roll(below, back, 1)
    return jnp.where(lane < EDGE // 2, above, below)


def split_pieces(refs):
    near = [(ref, at) for ref in refs for at in (0, 1)]
    across = [(ref, at) for ref in refs for at in (2, 3)]
    return near, across


def fields_kernel(masks, count, place, both_ref, *refs):
    (near, across), far_ref, out_ref = split_pieces(refs[:-2]), refs[-2], refs[-1]
    unused, rows, width = both_ref.shape
    mats = count * rows
    far_own = far_cells(far_ref, mats + rows // edge_parts(rows), rows, width, 0)
    for start, source, pieces in ((place[1], both_ref[0], near), (1 - place[1], far_own, across)):
        start = pl.multiple_of(start * rows, rows)
        out_ref[pl.ds(start, rows), :width] = source
        halo = join_halo(pick_halo(place, pieces, masks, mats, rows), 0)
        out_ref[pl.ds(start, rows), width:] = halo.astype(BF16)


def prepare_kernel(rows, couple_ref, links_ref, place, mats_ref, own_ref, spread_ref, links, weights, sems):
    copies = []
    for chunk in range(SLOTS // CHUNK):
        span = pl.ds(chunk * CHUNK, CHUNK)
        copies.append(pltpu.make_async_copy(couple_ref.at[span], mats_ref.at[span], sems.at[chunk]))
    linked = pltpu.make_async_copy(links_ref, links, sems.at[len(copies)])
    linked.start()
    for copy in copies:
        copy.start()
    linked.wait()
    weights[...] = jnp.zeros_like(weights)
    weights[:SLOTS, :] = jnp.where(links[...] >= 0, 1.0, 0.0)
    filled = weights[...].astype(BF16)
    row = lax.broadcasted_iota(jnp.int32, (filled.shape[0], 2 * EDGE), 0)
    lane = lax.broadcasted_iota(jnp.int32, (filled.shape[0], 2 * EDGE), 1)
    for pair in range(SLOTS // 2):
        chosen = row == 2 * pair + (lane >= EDGE).astype(jnp.int32)
        unit = jnp.where(chosen, 1.0, 0.0).astype(BF16)
        spread = lax.dot_general(
            filled, unit, (((0,), (0,)), ((), ())), preferred_element_type=F32
        ).astype(BF16)
        spread_ref[2 * pair] = spread[:, :EDGE]
        spread_ref[2 * pair + 1] = spread[:, EDGE:]
    depth = mats_ref.shape[1]
    odd = place[1]
    lane = lax.broadcasted_iota(jnp.int32, (depth, EDGE), 1)
    first = jnp.where((lane // rows) % 2 == odd, 1.0, 0.0).astype(BF16)
    second = (1.0 - first).astype(BF16)
    shift = jnp.where(odd == 1, EDGE - rows, rows)
    for chunk, copy in enumerate(copies):
        copy.wait()
        for mat in range(chunk * CHUNK, (chunk + 1) * CHUNK):
            moved = pltpu.roll(mats_ref[mat, :, EDGE : 2 * EDGE], shift, 1)
            chosen = mats_ref[mat, :, :EDGE] * first + moved * second
            slot = SLOTS - 1 - mat
            side = (slot % 2) * EDGE
            own_ref[slot // 2, :, side : side + EDGE] = chosen


def stand_up(cells, upright):
    width = cells.shape[1] - EDGE
    turned = cells.astype(F32).T
    for half in range(upright.shape[0]):
        lanes = slice(half * EDGE, (half + 1) * EDGE)
        upright[half, LEAD : LEAD + width, :] = turned[:width, lanes]
        upright[half, LEAD + width :, :] = turned[width : width + LEAD, lanes]
        upright[half, :LEAD, :] = turned[width + EDGE - LEAD :, lanes]


def couple_slots(upright, spread_ref, mats_ref, slots, total=None):
    width = spread_ref.shape[1]
    for slot in slots:
        start = LEAD + OFFSETS[slot]
        weight = spread_ref[slot]
        selected = jnp.concatenate(
            [
                upright[half, start : start + width, :].astype(BF16) * weight
                for half in range(upright.shape[0])
            ],
            axis=1,
        )
        product = lax.dot_general(
            selected, mats_ref[slot], (((1,), (1,)), ((), ())), preferred_element_type=F32
        )
        total = product if total is None else total + product
    return total


def couple_own(upright, spread_ref, own_ref, products):
    width = spread_ref.shape[1]
    for pair in range(SLOTS // 2):
        both = jnp.dot(upright, own_ref[pair], preferred_element_type=F32)
        products[2 * pair] = both[:, :EDGE]
        products[2 * pair + 1] = both[:, EDGE:]
    bands = []
    for band in range(0, width, BAND):
        total = None
        for slot in range(SLOTS):
            start = LEAD + OFFSETS[slot] + band
            term = products[slot, start : start + BAND, :] * spread_ref[slot, band : band + BAND, :].astype(F32)
            total = term if total is None else total + term
        bands.append(total)
    return jnp.concatenate(bands, axis=0)


def adjoint_kernel(
    masks, count, sends, place, both_ref, far_ref, class_ref, spread_ref, own_ref, after_ref, *refs
):
    half = len(masks)
    near, across = split_pieces(refs[: -sends - 4])
    keep_ref, *send_refs = refs[-sends - 4 : -4]
    total_ref, expanded, stacked, products = refs[-4:]
    unused, rows, width = both_ref.shape
    mats = count * rows
    far_own = far_cells(far_ref, mats + rows // edge_parts(rows), rows, width, 1)
    halos = [pick_halo(place, pieces, masks, mats, rows) for pieces in (near, across)]
    padded = [
        jnp.concatenate([own, join_halo(halo, A_SHIFT).astype(BF16)], axis=1)
        for own, halo in ((both_ref[1], halos[0]), (far_own, halos[1]))
    ]
    class_halo = join_halo(tuple(cells[0:8, :] for cells in halos[0]), C_SHIFT)
    labels = jnp.concatenate([class_ref[...], class_halo[0:1, :].astype(jnp.int32)], axis=1)
    at = 0
    for piece in range(half):
        for which, pieces in ((0, near), (1, across)):
            ref, spot = pieces[piece]
            stacked[at : at + mats, :] = ref[spot, :mats, :]
            for local_class in range(count):
                hit = labels == (place[0] ^ masks[piece]) * count + local_class
                factor = jnp.where(hit, 1.0, 0.0).astype(BF16)
                expanded[at : at + rows, :] = padded[which] * factor
                at += rows
    scattered = lax.dot_general(
        stacked[...], expanded[...], (((0,), (0,)), ((), ())), preferred_element_type=F32
    )
    turned = scattered.astype(BF16).T
    upright = jnp.concatenate(
        [turned[width + EDGE - LEAD :], turned[:width], turned[width : width + LEAD]], axis=0
    )
    total_ref[...] = couple_own(upright, spread_ref, own_ref, products).T

    def block(rel):
        start = ((place[2] ^ rel) * 2 + place[1]) * rows
        moved = start - EDGE + jnp.where(place[1] == 1, -rows, rows)
        return pl.ds(pl.multiple_of(jnp.where(start < EDGE, start, moved), rows), rows)

    keep_ref[...] = total_ref[block(0), :]
    for rel, send_ref in enumerate(send_refs, 1):
        send_ref[...] = total_ref[block(rel), :].astype(BF16)


def forward_kernel(
    masks, count, rels, place, both_ref, class_ref, spread_ref, mats_ref, *refs
):
    pieces, refs = refs[: len(rels)], refs[len(rels) :]
    (near, across), (out_ref, padded, upright, stacked) = split_pieces(refs[:-4]), refs[-4:]
    unused, rows, width = both_ref.shape
    mats = count * rows
    block = 2 * rows
    for rel, piece_ref in zip(rels, pieces):
        start = pl.multiple_of((place[2] ^ rel) * block, block)
        padded[pl.ds(start, block), :] = piece_ref[...]
    stand_up(padded[...], upright)
    coupled = couple_slots(upright, spread_ref, mats_ref, range(SLOTS)).astype(BF16)
    for piece, (ref, spot) in enumerate(near):
        stacked[piece * mats : (piece + 1) * mats, :] = ref[spot, :mats, :]
    product = lax.dot_general(
        stacked[...], coupled, (((1,), (1,)), ((), ())), preferred_element_type=F32
    )
    applied = jnp.zeros((rows, width), F32)
    labels = class_ref[...]
    for piece in range(len(masks)):
        for local_class in range(count):
            hit = labels == (place[0] ^ masks[piece]) * count + local_class
            at = piece * mats + local_class * rows
            applied = jnp.where(hit, product[at : at + rows, :], applied)
    out_ref[...] = (both_ref[0].astype(F32) - applied).astype(BF16)


def finish_kernel(both_ref, keep_ref, after_ref, *refs):
    arrived, out_ref = refs[:-1], refs[-1]
    returned = keep_ref[...]
    for ref in arrived:
        returned = returned + ref[...].astype(F32)
    out_ref[...] = (both_ref[1].astype(F32) - returned).astype(BF16)


def local(fields, adjoints, couple, tmatrices, neighbours, classes):
    tiles, coefs = lax.axis_size("tiles"), lax.axis_size("coef")
    rows, width = fields.shape
    count, unused, depth = tmatrices.shape

    def swap(cells, tile_mask, coef_mask):
        pairs = [
            (i * coefs + j, (i ^ tile_mask) * coefs + (j ^ coef_mask))
            for i in range(tiles)
            for j in range(coefs)
        ]
        return lax.ppermute(cells, ("tiles", "coef"), pairs)

    labels = classes.reshape(1, width)
    mats = count * rows
    near_rows = mats + rows // edge_parts(rows)
    total_rows = couple.shape[1]
    place, near_own, far_own, both, labels = pl.pallas_call(
        pack_kernel,
        out_shape=(
            jax.ShapeDtypeStruct((3,), jnp.int32),
            jax.ShapeDtypeStruct((near_rows, depth), BF16),
            jax.ShapeDtypeStruct((near_rows + 2 * rows * (width // depth), depth), BF16),
            jax.ShapeDtypeStruct((2, rows, width), BF16),
            jax.ShapeDtypeStruct(labels.shape, jnp.int32),
        ),
        in_specs=[HBM] * 4,
        out_specs=(SMEM,) + (VMEM,) * 4,
        scratch_shapes=[pltpu.VMEM(tmatrices.shape, BF16), pltpu.SemaphoreType.DMA((4,))],
        compiler_params=PARAMS,
    )(*[in_hbm(cells) for cells in (tmatrices, fields, adjoints, labels)])
    mats_held, mats_own, spread = pl.pallas_call(
        functools.partial(prepare_kernel, rows),
        out_shape=(
            jax.ShapeDtypeStruct(couple.shape, BF16),
            jax.ShapeDtypeStruct((SLOTS // 2, total_rows, 2 * EDGE), BF16),
            jax.ShapeDtypeStruct((SLOTS, width, EDGE), BF16),
        ),
        in_specs=[HBM, HBM, SMEM],
        out_specs=(VMEM,) * 3,
        scratch_shapes=[
            pltpu.VMEM((SLOTS, width), jnp.int32),
            pltpu.VMEM((SLOTS + -SLOTS % 16, width), F32),
            pltpu.SemaphoreType.DMA((SLOTS // CHUNK + 1,)),
        ],
        cost_estimate=pl.CostEstimate(flops=0, bytes_accessed=4 * couple.size, transcendentals=0),
        compiler_params=PARAMS,
    )(in_hbm(couple), in_hbm(neighbours.T), place)

    top = tiles // 2
    far = swap(far_own, 0, 1)
    first = pl.pallas_call(
        relay_kernel,
        out_shape=jax.ShapeDtypeStruct((4, near_rows, depth), BF16),
        in_specs=[VMEM] * 5,
        out_specs=VMEM,
        compiler_params=PARAMS,
    )(far, swap(near_own, top, 1), swap(near_own, top, 0), near_own, mats_held)
    held, lows = [first], [0]
    bit = top // 2
    while bit >= 1:
        held += [swap(block, bit, 0) for block in held]
        lows += [low ^ bit for low in lows]
        bit //= 2
    masks = [low ^ high for low in lows for high in (0, top)]

    padded_fields = pl.pallas_call(
        functools.partial(fields_kernel, masks, count),
        out_shape=jax.ShapeDtypeStruct((2 * rows, width + EDGE), BF16),
        in_specs=[SMEM] + [VMEM] * (2 + len(held)),
        out_specs=VMEM,
        compiler_params=PARAMS,
    )(place, both, *held, far)

    groups = coefs // 2
    gathered = {0: padded_fields}
    for rel in range(1, groups):
        gathered[rel] = swap(padded_fields, 0, 2 * rel)
    rels = sorted(gathered, reverse=False)


    def work(slots):
        size = slots * total_rows * total_rows
        return pl.CostEstimate(flops=2 * size * width, bytes_accessed=2 * size, transcendentals=0)

    keep, *sent = pl.pallas_call(
        functools.partial(adjoint_kernel, masks, count, groups),
        out_shape=(jax.ShapeDtypeStruct((rows, width), F32),)
        + (jax.ShapeDtypeStruct((rows, width), BF16),) * (groups - 1),
        in_specs=[SMEM] + [VMEM] * 5 + [ANY] + [VMEM] * len(held),
        out_specs=(VMEM,) * groups,
        scratch_shapes=[
            pltpu.VMEM((EDGE, width), F32),
            pltpu.VMEM((2 * len(masks) * mats, width + EDGE), BF16),
            pltpu.VMEM((2 * len(masks) * mats, depth), BF16),
            pltpu.VMEM((SLOTS, width + 2 * LEAD, EDGE), F32),
        ],
        cost_estimate=work(SLOTS + 8),
        compiler_params=PARAMS,
    )(place, both, far, labels, spread, mats_own, padded_fields, *held)
    arrived = [swap(block, 0, 2 * rel) for rel, block in enumerate(sent, 1)]

    forward_out = pl.pallas_call(
        functools.partial(forward_kernel, masks, count, rels),
        out_shape=jax.ShapeDtypeStruct((rows, width), BF16),
        in_specs=[SMEM] + [VMEM] * (4 + len(rels) + len(held)),
        out_specs=VMEM,
        scratch_shapes=[
            pltpu.VMEM((total_rows, width + EDGE), BF16),
            pltpu.VMEM((total_rows // EDGE, width + 2 * LEAD, EDGE), F32),
            pltpu.VMEM((len(masks) * mats, depth), BF16),
        ],
        cost_estimate=work(SLOTS + 8),
        compiler_params=PARAMS,
    )(place, both, labels, spread, mats_held, *[gathered[rel] for rel in rels], *held)
    adjoint_out = pl.pallas_call(
        finish_kernel,
        out_shape=jax.ShapeDtypeStruct((rows, width), BF16),
        in_specs=[VMEM] * 2 + [HBM] + [VMEM] * len(arrived),
        out_specs=VMEM,
        compiler_params=PARAMS,
    )(both, keep, in_hbm(forward_out), *arrived[::-1])
    return (forward_out, adjoint_out)


def solution(mesh):
    placed = (
        P("coef", "tiles"),
        P("coef", "tiles"),
        P(),
        P("tiles", "coef", None),
        P("tiles", None),
        P("tiles"),
    )
    return jax.shard_map(
        local,
        mesh=mesh,
        in_specs=placed,
        out_specs=(P("coef", "tiles"), P("coef", "tiles")),
        check_vma=False,
    )
```

time: 32.7 us -> 30.7 us (0.939)
  other arithmetic: 1.49 us -> 0 us
  starting transfers between devices: 12.9 us -> 13.5 us
  waiting for transfers between devices: 3.79 us -> 3.21 us
  Pallas kernels: 13.6 us -> 13.2 us
    transpose x1 -> x0, other arithmetic: 0.85 us -> none  [local(): weights = (neighbours >= 0).astype(BF16).T]
    ppermute x9 -> x10, starting transfers between devices: 12.9 us -> 13.5 us  [swap(): return lax.ppermute(cells, ('tiles', 'coef'), pairs)]
    convert_element_type x1 -> x0, other arithmetic: 0.63 us -> none  [local(): adjoint_out = (adjoints.astype(F32) - returned).astype(BF16)]
    ppermute x9 -> x10, waiting for transfers between devices: 3.79 us -> 3.21 us  [swap(): return lax.ppermute(cells, ('tiles', 'coef'), pairs)]
    pallas_call x5 -> x4, Pallas kernels: 11.5 us -> 11.1 us  [the longest x1 4.04 us: local(): pl.pallas_call(functools.partial(forward_kernel, masks, count, rels), out...]
  transfers between devices with their start and end apart: 9 -> 10, of which waited for: 4 -> 2; matrix products, arithmetic and copies ran while one was open for 3% -> 0% of each run, Pallas kernels for 35% -> 34%
where the time goes in v7:
time: 30.7 us; the launch traced here: 30.6 us
  starting transfers between devices  13.5 us (44%)
  Pallas kernels  13.2 us (43%)
  waiting for transfers between devices  3.21 us (10%)
  between operations  0.69 us (2%)
    ppermute x10, starting transfers between devices, swap(): return lax.ppermute(cells, ('tiles', 'coef'), pairs)  13.5 us
    pallas_call x1, Pallas kernels, local(): pl.pallas_call(functools.partial(forward_kernel, masks, count, rels), out...  4.04 us
    pallas_call x1, Pallas kernels, local(): pl.pallas_call(functools.partial(prepare_kernel, rows), out_shape=(jax.Sh...  3.59 us
    ppermute x10, waiting for transfers between devices, swap(): return lax.ppermute(cells, ('tiles', 'coef'), pairs)  3.21 us
    pallas_call x1, Pallas kernels, local(): pl.pallas_call(functools.partial(adjoint_kernel, masks, count, groups), o...  2.8 us
    pallas_call x1, Pallas kernels, local(): pl.pallas_call(pack_kernel, out_shape=(jax.ShapeDtypeStruct((3,), jnp.int...  1.48 us
    pallas_call x1, Pallas kernels, local(): pl.pallas_call(finish_kernel, out_shape=jax.ShapeDtypeStruct((rows, width...  0.64 us
  transfers between devices with their start and end apart: 10, of which 2 were waited for; matrix products, arithmetic and copies ran while one was open for 0% of the time, Pallas kernels for 34%

profile of v7, /device:TPU:0, one launch (start us, length us, event | category | flops | bytes accessed | tf_op | source)
XLA Modules:
  0.0 30.6 jit_solution(17570636916674221544)
XLA Ops:
  0.6 1.5 %shard_map.77 = (s32[3]{0:T(128)S(1)}, bf16[144,256]{1,0:T(8,128)(2,1)S(1)}, bf16[272,256]{1,0:T(8,128)(2,1)S(1)}, bf16[2,32,512]{2,1,0:T(8,128)(2,1)S(1)}, s32[1,512]{1,0:T(1,128)S(1)}) custom-call(bf16[4,32,256]{2,1,0:T(8,128)(2,1)} %t_any.1, bf16[32,512]{1,0:T(8,128)(2,1)} %f_any.1, bf16[32,512]{1,0:T(8,128)(2,1)} %a_any.1, s32[1,512]{1,0:T(1,128)} %bitcast.3), custom_call_target="tpu_custom_call" | custom-call | tf_op jit(solution)/shard_map/pallas_call | solution.py:337
  2.1 3.0 %collective-permute-start = (bf16[272,256]{1,0:T(8,128)(2,1)S(1)}, bf16[272,256]{1,0:T(8,128)(2,1)S(1)}, u32[]{:S(2)}, u32[]{:S(2)}) collective-permute-start(bf16[272,256]{1,0:T(8,128)(2,1)S(1)} %get-tuple-element.19), channel_id=1, source_target_pairs={{0,1},{1,0},{2,3},{3,2},{4,5},{5,4},{6,7},{7,6},{8,9},{9,8},{10,11... | collective-permute-start | bytes 417800 | tf_op jit(solution)/shard_map/ppermute | solution.py:331
  5.1 1.5 %collective-permute-start.2 = (bf16[144,256]{1,0:T(8,128)(2,1)S(1)}, bf16[144,256]{1,0:T(8,128)(2,1)S(1)}, u32[]{:S(2)}, u32[]{:S(2)}) collective-permute-start(bf16[144,256]{1,0:T(8,128)(2,1)S(1)} %get-tuple-element.20.near_ref), channel_id=1, source_target_pairs={{0,16},{1,17},{2,18},{3,19},{4,20},{5,21},{6,22},{7,23},{8,24},{9,... | collective-permute-start | bytes 221192 | tf_op jit(solution)/shard_map/ppermute | solution.py:331
  6.6 0.0 collective-permute-start.1
  6.7 3.6 %shard_map.78 = (bf16[30,256,256]{2,1,0:T(8,128)(2,1)S(1)}, bf16[15,256,256]{2,1,0:T(8,128)(2,1)S(1)}, bf16[30,512,128]{2,1,0:T(8,128)(2,1)S(1)}) custom-call(bf16[30,256,256]{2,1,0:T(8,128)(2,1)} %couple_ref.1, s32[30,512]{1,0:T(8,128)} %bitcast.2, s32[3]{0:T(128)S(1)} %get-tuple-element.14.place), custom_call_target="tpu_custom_call" | custom-call | bytes 7864320 | tf_op jit(solution)/shard_map/pallas_call | solution.py:351
  10.3 0.0 collective-permute-done.2.top_ref
  10.3 1.6 %collective-permute-done.1.cross_ref = bf16[144,256]{1,0:T(8,128)(2,1)S(1)} collective-permute-done((bf16[144,256]{1,0:T(8,128)(2,1)S(1)}, bf16[144,256]{1,0:T(8,128)(2,1)S(1)}, u32[]{:S(2)}, u32[]{:S(2)}) %collective-permute-start.1) | collective-permute-done | bytes 73760 | tf_op jit(solution)/shard_map/ppermute | solution.py:331
  11.9 0.0 collective-permute-done.far_ref.refs_2_
  11.9 0.1 collective-permute-start.3
  12.0 1.6 %collective-permute-done.3.refs_1_.refs_5_ = bf16[4,144,256]{2,1,0:T(8,128)(2,1)S(1)} collective-permute-done((bf16[4,144,256]{2,1,0:T(8,128)(2,1)S(1)}, bf16[4,144,256]{2,1,0:T(8,128)(2,1)S(1)}, u32[]{:S(2)}, u32[]{:S(2)}) %collective-permute-start.3) | collective-permute-done | bytes 294944 | tf_op jit(solution)/shard_map/ppermute | solution.py:331
  13.6 0.6 %shard_map.80.refs_0_.after_ref = bf16[64,640]{1,0:T(8,128)(2,1)S(1)} custom-call(s32[3]{0:T(128)S(1)} %get-tuple-element.14.place, bf16[2,32,512]{2,1,0:T(8,128)(2,1)S(1)} %get-tuple-element.15.both_ref, bf16[4,144,256]{2,1,0:T(8,128)(2,1)S(1)} %shard_map.79.refs_0_.refs_4_, bf16[4,144,256]{2,1,0:T(8,128)(2,1)S(1)} %collective-permute-done.3.refs_1_.refs_5_, ...), custom_call_target="tpu_custom_call" | custom-call | tf_op jit(solution)/shard_map/pallas_call | solution.py:386
  14.1 3.7 %collective-permute-start.6 = (bf16[64,640]{1,0:T(8,128)(2,1)S(1)}, bf16[64,640]{1,0:T(8,128)(2,1)S(1)}, u32[]{:S(2)}, u32[]{:S(2)}) collective-permute-start(bf16[64,640]{1,0:T(8,128)(2,1)S(1)} %shard_map.80.refs_0_.after_ref), channel_id=1, source_target_pairs={{0,6},{1,7},{2,4},{3,5},{4,2},{5,3},{6,0},{7,1},{8,14},{9,15},{10,... | collective-permute-start | bytes 245768 | tf_op jit(solution)/shard_map/ppermute | solution.py:331
  17.8 0.0 collective-permute-start.5
  17.8 0.8 %collective-permute-start.4 = (bf16[64,640]{1,0:T(8,128)(2,1)S(1)}, bf16[64,640]{1,0:T(8,128)(2,1)S(1)}, u32[]{:S(2)}, u32[]{:S(2)}) collective-permute-start(bf16[64,640]{1,0:T(8,128)(2,1)S(1)} %shard_map.80.refs_0_.after_ref), channel_id=1, source_target_pairs={{0,2},{1,3},{2,0},{3,1},{4,6},{5,7},{6,4},{7,5},{8,10},{9,11},{10,... | collective-permute-start | bytes 245768 | tf_op jit(solution)/shard_map/ppermute | solution.py:331
  18.6 2.8 %shard_map.82 = (f32[32,512]{1,0:T(8,128)S(1)}, bf16[32,512]{1,0:T(8,128)(2,1)S(1)}, bf16[32,512]{1,0:T(8,128)(2,1)S(1)}, bf16[32,512]{1,0:T(8,128)(2,1)S(1)}) custom-call(s32[3]{0:T(128)S(1)} %get-tuple-element.14.place, bf16[2,32,512]{2,1,0:T(8,128)(2,1)S(1)} %get-tuple-element.15.both_ref, bf16[272,256]{1,0:T(8,128)(2,1)S(1)} %collective-permute-done.far_ref.refs_2_, ...), custom_call_target="tpu_custom_call" | custom-call | flops 2550136832 | bytes 4980736 | tf_op jit(solution)/shard_map/pallas_call | solution.py:405
  21.4 3.7 %collective-permute-start.7 = (bf16[32,512]{1,0:T(8,128)(2,1)S(1)}, bf16[32,512]{1,0:T(8,128)(2,1)S(1)}, u32[]{:S(2)}, u32[]{:S(2)}) collective-permute-start(bf16[32,512]{1,0:T(8,128)(2,1)S(1)} %get-tuple-element.23), channel_id=1, source_target_pairs={{0,6},{1,7},{2,4},{3,5},{4,2},{5,3},{6,0},{7,1},{8,14},{9,15},{10,... | collective-permute-start | bytes 98312 | tf_op jit(solution)/shard_map/ppermute | solution.py:331
  25.1 0.0 collective-permute-start.8
  25.1 0.0 collective-permute-done.6.refs_3_
  25.1 0.8 %collective-permute-start.9 = (bf16[32,512]{1,0:T(8,128)(2,1)S(1)}, bf16[32,512]{1,0:T(8,128)(2,1)S(1)}, u32[]{:S(2)}, u32[]{:S(2)}) collective-permute-start(bf16[32,512]{1,0:T(8,128)(2,1)S(1)} %get-tuple-element.25), channel_id=1, source_target_pairs={{0,2},{1,3},{2,0},{3,1},{4,6},{5,7},{6,4},{7,5},{8,10},{9,11},{10,... | collective-permute-start | bytes 98312 | tf_op jit(solution)/shard_map/ppermute | solution.py:331
  25.9 0.0 collective-permute-done.5.refs_2_
  25.9 0.0 collective-permute-done.4.refs_1_
  25.9 4.0 %shard_map.81.after_ref = bf16[32,512]{1,0:T(8,128)(2,1)} custom-call(s32[3]{0:T(128)S(1)} %get-tuple-element.14.place, bf16[2,32,512]{2,1,0:T(8,128)(2,1)S(1)} %get-tuple-element.15.both_ref, s32[1,512]{1,0:T(1,128)S(1)} %get-tuple-element.16.class_ref, bf16[30,512,128]{2,1,0:T(8,128)(2,1)S(1)} %get-tuple-element.17.spread_ref, ...), custom_call_target="tpu_custom_call" | custom-call | flops 2550136832 | bytes 4980736 | tf_op jit(solution)/shard_map/pallas_call | solution.py:422
  29.9 0.0 collective-permute-done.7.refs_0_
  29.9 0.6 %shard_map.83 = bf16[32,512]{1,0:T(8,128)(2,1)} custom-call(bf16[2,32,512]{2,1,0:T(8,128)(2,1)S(1)} %get-tuple-element.15.both_ref, f32[32,512]{1,0:T(8,128)S(1)} %get-tuple-element.22.keep_ref, bf16[32,512]{1,0:T(8,128)(2,1)} %shard_map.81.after_ref, bf16[32,512]{1,0:T(8,128)(2,1)S(1)} %collective-permute-done.7.refs_0_, ...), custom_call_target="tpu_custom_call" | custom-call | tf_op jit(solution)/shard_map/pallas_call | solution.py:435
  (3 shorter events, 0.0 us)
Async XLA Ops:
  2.1 9.8 %collective-permute-start = (bf16[272,256]{1,0:T(8,128)(2,1)S(1)}, bf16[272,256]{1,0:T(8,128)(2,1)S(1)}, u32[]{:S(2)}, u32[]{:S(2)}) collective-permute-start(bf16[272,256]{1,0:T(8,128)(2,1)S(1)} %get-tuple-element.19), channel_id=1, source_target_pairs={{0,1},{1,0},{2,3},{3,2},{4,5},{5,4},{6,7},{7,6},{8,9},{9,8},{10,11... | collective-permute-start | bytes 417800 | tf_op jit(solution)/shard_map/ppermute | solution.py:331
  5.1 5.1 %collective-permute-start.2 = (bf16[144,256]{1,0:T(8,128)(2,1)S(1)}, bf16[144,256]{1,0:T(8,128)(2,1)S(1)}, u32[]{:S(2)}, u32[]{:S(2)}) collective-permute-start(bf16[144,256]{1,0:T(8,128)(2,1)S(1)} %get-tuple-element.20.near_ref), channel_id=1, source_target_pairs={{0,16},{1,17},{2,18},{3,19},{4,20},{5,21},{6,22},{7,23},{8,24},{9,... | collective-permute-start | bytes 221192 | tf_op jit(solution)/shard_map/ppermute | solution.py:331
  6.6 5.3 %collective-permute-start.1 = (bf16[144,256]{1,0:T(8,128)(2,1)S(1)}, bf16[144,256]{1,0:T(8,128)(2,1)S(1)}, u32[]{:S(2)}, u32[]{:S(2)}) collective-permute-start(bf16[144,256]{1,0:T(8,128)(2,1)S(1)} %get-tuple-element.20.near_ref), channel_id=1, source_target_pairs={{0,17},{1,16},{2,19},{3,18},{4,21},{5,20},{6,23},{7,22},{8,25},{9,... | collective-permute-start | bytes 221192 | tf_op jit(solution)/shard_map/ppermute | solution.py:331
  11.9 1.6 %collective-permute-start.3 = (bf16[4,144,256]{2,1,0:T(8,128)(2,1)S(1)}, bf16[4,144,256]{2,1,0:T(8,128)(2,1)S(1)}, u32[]{:S(2)}, u32[]{:S(2)}) collective-permute-start(bf16[4,144,256]{2,1,0:T(8,128)(2,1)S(1)} %shard_map.79.refs_0_.refs_4_), channel_id=1, source_target_pairs={{0,8},{1,9},{2,10},{3,11},{4,12},{5,13},{6,14},{7,15},{8,0},{9,1},... | collective-permute-start | bytes 884744 | tf_op jit(solution)/shard_map/ppermute | solution.py:331
  14.1 10.9 %collective-permute-start.6 = (bf16[64,640]{1,0:T(8,128)(2,1)S(1)}, bf16[64,640]{1,0:T(8,128)(2,1)S(1)}, u32[]{:S(2)}, u32[]{:S(2)}) collective-permute-start(bf16[64,640]{1,0:T(8,128)(2,1)S(1)} %shard_map.80.refs_0_.after_ref), channel_id=1, source_target_pairs={{0,6},{1,7},{2,4},{3,5},{4,2},{5,3},{6,0},{7,1},{8,14},{9,15},{10,... | collective-permute-start | bytes 245768 | tf_op jit(solution)/shard_map/ppermute | solution.py:331
  17.8 8.1 %collective-permute-start.5 = (bf16[64,640]{1,0:T(8,128)(2,1)S(1)}, bf16[64,640]{1,0:T(8,128)(2,1)S(1)}, u32[]{:S(2)}, u32[]{:S(2)}) collective-permute-start(bf16[64,640]{1,0:T(8,128)(2,1)S(1)} %shard_map.80.refs_0_.after_ref), channel_id=1, source_target_pairs={{0,4},{1,5},{2,6},{3,7},{4,0},{5,1},{6,2},{7,3},{8,12},{9,13},{10,... | collective-permute-start | bytes 245768 | tf_op jit(solution)/shard_map/ppermute | solution.py:331
  17.8 8.1 %collective-permute-start.4 = (bf16[64,640]{1,0:T(8,128)(2,1)S(1)}, bf16[64,640]{1,0:T(8,128)(2,1)S(1)}, u32[]{:S(2)}, u32[]{:S(2)}) collective-permute-start(bf16[64,640]{1,0:T(8,128)(2,1)S(1)} %shard_map.80.refs_0_.after_ref), channel_id=1, source_target_pairs={{0,2},{1,3},{2,0},{3,1},{4,6},{5,7},{6,4},{7,5},{8,10},{9,11},{10,... | collective-permute-start | bytes 245768 | tf_op jit(solution)/shard_map/ppermute | solution.py:331
  21.4 8.5 %collective-permute-start.7 = (bf16[32,512]{1,0:T(8,128)(2,1)S(1)}, bf16[32,512]{1,0:T(8,128)(2,1)S(1)}, u32[]{:S(2)}, u32[]{:S(2)}) collective-permute-start(bf16[32,512]{1,0:T(8,128)(2,1)S(1)} %get-tuple-element.23), channel_id=1, source_target_pairs={{0,6},{1,7},{2,4},{3,5},{4,2},{5,3},{6,0},{7,1},{8,14},{9,15},{10,... | collective-permute-start | bytes 98312 | tf_op jit(solution)/shard_map/ppermute | solution.py:331
  25.1 4.8 %collective-permute-start.8 = (bf16[32,512]{1,0:T(8,128)(2,1)S(1)}, bf16[32,512]{1,0:T(8,128)(2,1)S(1)}, u32[]{:S(2)}, u32[]{:S(2)}) collective-permute-start(bf16[32,512]{1,0:T(8,128)(2,1)S(1)} %get-tuple-element.24), channel_id=1, source_target_pairs={{0,4},{1,5},{2,6},{3,7},{4,0},{5,1},{6,2},{7,3},{8,12},{9,13},{10,... | collective-permute-start | bytes 98312 | tf_op jit(solution)/shard_map/ppermute | solution.py:331
  25.1 4.8 %collective-permute-start.9 = (bf16[32,512]{1,0:T(8,128)(2,1)S(1)}, bf16[32,512]{1,0:T(8,128)(2,1)S(1)}, u32[]{:S(2)}, u32[]{:S(2)}) collective-permute-start(bf16[32,512]{1,0:T(8,128)(2,1)S(1)} %get-tuple-element.25), channel_id=1, source_target_pairs={{0,2},{1,3},{2,0},{3,1},{4,6},{5,7},{6,4},{7,5},{8,10},{9,11},{10,... | collective-permute-start | bytes 98312 | tf_op jit(solution)/shard_map/ppermute | solution.py:331

commit v8 on v7

--- a/solution.py
+++ b/solution.py
@@ -40,18 +40,8 @@
     return 2 if rows % 32 == 0 else 1
 
 
-def far_spans(base, rows, width, depth, which):
-    starts = [base + (2 * part + which) * rows for part in range(width // depth)]
-    return [slice(start, start + rows) for start in starts]
-
-
-def far_cells(far_ref, base, rows, width, which):
-    spans = far_spans(base, rows, width, far_ref.shape[1], which)
-    return jnp.concatenate([far_ref[span, :] for span in spans], axis=1)
-
-
 def pack_kernel(
-    t_any, f_any, a_any, class_any, place, near_ref, far_ref, both_ref, class_ref, t_ref, sems
+    t_any, f_any, a_any, class_any, place, near_ref, both_ref, class_ref, t_ref, sems
 ):
     coef = lax.axis_index("coef")
     place[0] = lax.axis_index("tiles")
@@ -92,26 +82,22 @@
     for part in range(depth // EDGE):
         start = part * (rows // parts) if part < parts else 0
         near_ref[mats:base, part * EDGE : (part + 1) * EDGE] = edge[start : start + base - mats, :]
-    far_ref[:base, :] = near_ref[...]
-    for which, cells in enumerate((fields, adjoints)):
-        for part, span in enumerate(far_spans(base, rows, cells.shape[1], depth, which)):
-            far_ref[span, :] = cells[:, part * depth : (part + 1) * depth]
-
-
-def relay_kernel(far_ref, cross_ref, top_ref, near_ref, after_ref, out_ref):
+
+
+def relay_kernel(cross_ref, far_ref, top_ref, both_ref, beside_ref, near_ref, after_ref, out_ref):
     out_ref[0] = near_ref[...]
     out_ref[1] = top_ref[...]
-    out_ref[2] = far_ref[: near_ref.shape[0], :]
+    out_ref[2] = far_ref[...]
     out_ref[3] = cross_ref[...]
 
 
-def pick_halo(place, pieces, masks, mats, rows):
+def pick_halo(place, pieces, mats, rows):
     tile = place[0]
     parts = edge_parts(rows)
     lane = lax.broadcasted_iota(jnp.int32, (rows, EDGE), 1)
     above = jnp.zeros((rows, EDGE), F32)
     below = jnp.zeros((rows, EDGE), F32)
-    for (piece_ref, at), mask in zip(pieces, masks):
+    for piece_ref, at, mask in pieces:
         bands = [
             piece_ref[at, mats : mats + rows // parts, part * EDGE : (part + 1) * EDGE]
             for part in range(parts)
@@ -132,22 +118,42 @@
     return jnp.where(lane < EDGE // 2, above, below)
 
 
-def split_pieces(refs):
-    near = [(ref, at) for ref in refs for at in (0, 1)]
-    across = [(ref, at) for ref in refs for at in (2, 3)]
-    return near, across
-
-
-def fields_kernel(masks, count, place, both_ref, *refs):
-    (near, across), far_ref, out_ref = split_pieces(refs[:-2]), refs[-2], refs[-1]
+def find_pieces(spots, refs):
+    return [[(refs[which], at, mask) for which, at, mask in group] for group in spots]
+
+
+def fields_kernel(spots, count, place, both_ref, far_ref, *refs):
+    (near, across), (out_ref, halos) = find_pieces(spots, refs[:-2]), refs[-2:]
     unused, rows, width = both_ref.shape
     mats = count * rows
-    far_own = far_cells(far_ref, mats + rows // edge_parts(rows), rows, width, 0)
-    for start, source, pieces in ((place[1], both_ref[0], near), (1 - place[1], far_own, across)):
+    for start, source, pieces in ((place[1], both_ref[0], near), (1 - place[1], far_ref[0], across)):
         start = pl.multiple_of(start * rows, rows)
-        out_ref[pl.ds(start, rows), :width] = source
-        halo = join_halo(pick_halo(place, pieces, masks, mats, rows), 0)
-        out_ref[pl.ds(start, rows), width:] = halo.astype(BF16)
+        for part in range(width // EDGE):
+            lanes = slice(part * EDGE, (part + 1) * EDGE)
+            out_ref[pl.ds(part * 2 * rows + start, rows), :] = source[:, lanes]
+        halos[pl.ds(start, rows), :] = join_halo(pick_halo(place, pieces, mats, rows), 0)
+    lane = lax.broadcasted_iota(jnp.int32, (LEAD, EDGE), 1)
+    packed = jnp.zeros((LEAD, EDGE), F32)
+    for group in range(2 * rows // LEAD):
+        halo = halos[group * LEAD : (group + 1) * LEAD, :]
+        narrow = jnp.where(lane < LEAD, halo, pltpu.roll(halo, 2 * LEAD, 1))
+        first = 2 * LEAD * group
+        moved = pltpu.roll(narrow, first, 1) if group else narrow
+        packed = jnp.where((lane >= first) & (lane < first + 2 * LEAD), moved, packed)
+    out_ref[2 * rows * (width // EDGE) :, :] = packed.astype(BF16)
+
+
+def unpack_fields(piece_ref, padded, start, block):
+    width = padded.shape[1] - EDGE
+    for part in range(width // EDGE):
+        lanes = slice(part * EDGE, (part + 1) * EDGE)
+        padded[pl.ds(start, block), lanes] = piece_ref[part * block : (part + 1) * block, :]
+    packed = piece_ref[block * (width // EDGE) :, :].astype(F32)
+    lane = lax.broadcasted_iota(jnp.int32, (LEAD, EDGE), 1)
+    for group in range(block // LEAD):
+        narrow = pltpu.roll(packed, EDGE - 2 * LEAD * group, 1) if group else packed
+        halo = jnp.where(lane < EDGE // 2, narrow, pltpu.roll(narrow, EDGE - 2 * LEAD, 1))
+        padded[pl.ds(start + group * LEAD, LEAD), width:] = halo.astype(BF16)
 
 
 def prepare_kernel(rows, couple_ref, links_ref, place, mats_ref, own_ref, spread_ref, links, weights, sems):
@@ -236,31 +242,28 @@
 
 
 def adjoint_kernel(
-    masks, count, sends, place, both_ref, far_ref, class_ref, spread_ref, own_ref, after_ref, *refs
+    spots, count, sends, place, both_ref, far_ref, class_ref, spread_ref, own_ref, after_ref, *refs
 ):
-    half = len(masks)
-    near, across = split_pieces(refs[: -sends - 4])
+    near, across = find_pieces(spots, refs[: -sends - 4])
     keep_ref, *send_refs = refs[-sends - 4 : -4]
     total_ref, expanded, stacked, products = refs[-4:]
     unused, rows, width = both_ref.shape
     mats = count * rows
-    far_own = far_cells(far_ref, mats + rows // edge_parts(rows), rows, width, 1)
-    halos = [pick_halo(place, pieces, masks, mats, rows) for pieces in (near, across)]
+    halos = [pick_halo(place, pieces, mats, rows) for pieces in (near, across)]
     padded = [
         jnp.concatenate([own, join_halo(halo, A_SHIFT).astype(BF16)], axis=1)
-        for own, halo in ((both_ref[1], halos[0]), (far_own, halos[1]))
+        for own, halo in ((both_ref[1], halos[0]), (far_ref[1], halos[1]))
     ]
     class_halo = join_halo(tuple(cells[0:8, :] for cells in halos[0]), C_SHIFT)
     labels = jnp.concatenate([class_ref[...], class_halo[0:1, :].astype(jnp.int32)], axis=1)
     at = 0
-    for piece in range(half):
-        for which, pieces in ((0, near), (1, across)):
-            ref, spot = pieces[piece]
+    for own, pieces in zip(padded, (near, across)):
+        for ref, spot, mask in pieces:
             stacked[at : at + mats, :] = ref[spot, :mats, :]
             for local_class in range(count):
-                hit = labels == (place[0] ^ masks[piece]) * count + local_class
+                hit = labels == (place[0] ^ mask) * count + local_class
                 factor = jnp.where(hit, 1.0, 0.0).astype(BF16)
-                expanded[at : at + rows, :] = padded[which] * factor
+                expanded[at : at + rows, :] = own * factor
                 at += rows
     scattered = lax.dot_general(
         stacked[...], expanded[...], (((0,), (0,)), ((), ())), preferred_element_type=F32
@@ -272,7 +275,7 @@
     total_ref[...] = couple_own(upright, spread_ref, own_ref, products).T
 
     def block(rel):
-        start = ((place[2] ^ rel) * 2 + place[1]) * rows
+        start = (((place[2] + rel) & (sends - 1)) * 2 + place[1]) * rows
         moved = start - EDGE + jnp.where(place[1] == 1, -rows, rows)
         return pl.ds(pl.multiple_of(jnp.where(start < EDGE, start, moved), rows), rows)
 
@@ -282,28 +285,28 @@
 
 
 def forward_kernel(
-    masks, count, rels, place, both_ref, class_ref, spread_ref, mats_ref, *refs
+    spots, count, rels, place, both_ref, class_ref, spread_ref, mats_ref, *refs
 ):
     pieces, refs = refs[: len(rels)], refs[len(rels) :]
-    (near, across), (out_ref, padded, upright, stacked) = split_pieces(refs[:-4]), refs[-4:]
+    (near, across), (out_ref, padded, upright, stacked) = find_pieces(spots, refs[:-4]), refs[-4:]
     unused, rows, width = both_ref.shape
     mats = count * rows
     block = 2 * rows
     for rel, piece_ref in zip(rels, pieces):
-        start = pl.multiple_of((place[2] ^ rel) * block, block)
-        padded[pl.ds(start, block), :] = piece_ref[...]
+        start = pl.multiple_of(((place[2] - rel) & (len(rels) - 1)) * block, block)
+        unpack_fields(piece_ref, padded, start, block)
     stand_up(padded[...], upright)
     coupled = couple_slots(upright, spread_ref, mats_ref, range(SLOTS)).astype(BF16)
-    for piece, (ref, spot) in enumerate(near):
+    for piece, (ref, spot, mask) in enumerate(near):
         stacked[piece * mats : (piece + 1) * mats, :] = ref[spot, :mats, :]
     product = lax.dot_general(
         stacked[...], coupled, (((1,), (1,)), ((), ())), preferred_element_type=F32
     )
     applied = jnp.zeros((rows, width), F32)
     labels = class_ref[...]
-    for piece in range(len(masks)):
+    for piece, (ref, spot, mask) in enumerate(near):
         for local_class in range(count):
-            hit = labels == (place[0] ^ masks[piece]) * count + local_class
+            hit = labels == (place[0] ^ mask) * count + local_class
             at = piece * mats + local_class * rows
             applied = jnp.where(hit, product[at : at + rows, :], applied)
     out_ref[...] = (both_ref[0].astype(F32) - applied).astype(BF16)
@@ -330,21 +333,28 @@
         ]
         return lax.ppermute(cells, ("tiles", "coef"), pairs)
 
+    def shift(cells, rel):
+        pairs = [
+            (i * coefs + j, i * coefs + (j + 2 * rel) % coefs)
+            for i in range(tiles)
+            for j in range(coefs)
+        ]
+        return lax.ppermute(cells, ("tiles", "coef"), pairs)
+
     labels = classes.reshape(1, width)
     mats = count * rows
     near_rows = mats + rows // edge_parts(rows)
     total_rows = couple.shape[1]
-    place, near_own, far_own, both, labels = pl.pallas_call(
+    place, near_own, both, labels = pl.pallas_call(
         pack_kernel,
         out_shape=(
             jax.ShapeDtypeStruct((3,), jnp.int32),
             jax.ShapeDtypeStruct((near_rows, depth), BF16),
-            jax.ShapeDtypeStruct((near_rows + 2 * rows * (width // depth), depth), BF16),
             jax.ShapeDtypeStruct((2, rows, width), BF16),
             jax.ShapeDtypeStruct(labels.shape, jnp.int32),
         ),
         in_specs=[HBM] * 4,
-        out_specs=(SMEM,) + (VMEM,) * 4,
+        out_specs=(SMEM,) + (VMEM,) * 3,
         scratch_shapes=[pltpu.VMEM(tmatrices.shape, BF16), pltpu.SemaphoreType.DMA((4,))],
         compiler_params=PARAMS,
     )(*[in_hbm(cells) for cells in (tmatrices, fields, adjoints, labels)])
@@ -367,35 +377,53 @@
     )(in_hbm(couple), in_hbm(neighbours.T), place)
 
     top = tiles // 2
-    far = swap(far_own, 0, 1)
+    both_far = swap(both, 0, 1)
+    beside = swap(near_own, 1, 0)
     first = pl.pallas_call(
         relay_kernel,
         out_shape=jax.ShapeDtypeStruct((4, near_rows, depth), BF16),
-        in_specs=[VMEM] * 5,
+        in_specs=[VMEM] * 7,
         out_specs=VMEM,
         compiler_params=PARAMS,
-    )(far, swap(near_own, top, 1), swap(near_own, top, 0), near_own, mats_held)
+    )(
+        swap(near_own, top ^ 1, 1),
+        swap(near_own, 1, 1),
+        swap(near_own, top ^ 1, 0),
+        both_far,
+        beside,
+        near_own,
+        mats_held,
+    )
     held, lows = [first], [0]
     bit = top // 2
     while bit >= 1:
         held += [swap(block, bit, 0) for block in held]
         lows += [low ^ bit for low in lows]
         bit //= 2
-    masks = [low ^ high for low in lows for high in (0, top)]
+    spots = (
+        [(at, slot, low ^ (0, top ^ 1)[slot]) for at, low in enumerate(lows) for slot in (0, 1)],
+        [(at, slot, low ^ (1, top ^ 1)[slot - 2]) for at, low in enumerate(lows) for slot in (2, 3)],
+    )
+    if tiles == 4:
+        sources = [first, beside[None]]
+        edge_spots = ([(0, 1, 3), (1, 0, 1)], [(0, 2, 1), (0, 3, 3)])
+    else:
+        sources, edge_spots = held, spots
 
     padded_fields = pl.pallas_call(
-        functools.partial(fields_kernel, masks, count),
-        out_shape=jax.ShapeDtypeStruct((2 * rows, width + EDGE), BF16),
-        in_specs=[SMEM] + [VMEM] * (2 + len(held)),
+        functools.partial(fields_kernel, edge_spots, count),
+        out_shape=jax.ShapeDtypeStruct((2 * rows * (width // EDGE) + LEAD, EDGE), BF16),
+        in_specs=[SMEM] + [VMEM] * (2 + len(sources)),
         out_specs=VMEM,
-        compiler_params=PARAMS,
-    )(place, both, *held, far)
+        scratch_shapes=[pltpu.VMEM((2 * rows, EDGE), F32)],
+        compiler_params=PARAMS,
+    )(place, both, both_far, *sources)
 
     groups = coefs // 2
     gathered = {0: padded_fields}
     for rel in range(1, groups):
-        gathered[rel] = swap(padded_fields, 0, 2 * rel)
-    rels = sorted(gathered, reverse=False)
+        gathered[rel] = shift(padded_fields, rel)
+    rels = [0, 1, 2, 3] if groups == 4 else sorted(gathered)
 
 
     def work(slots):
@@ -403,31 +431,31 @@
         return pl.CostEstimate(flops=2 * size * width, bytes_accessed=2 * size, transcendentals=0)
 
     keep, *sent = pl.pallas_call(
-        functools.partial(adjoint_kernel, masks, count, groups),
+        functools.partial(adjoint_kernel, spots, count, groups),
         out_shape=(jax.ShapeDtypeStruct((rows, width), F32),)
         + (jax.ShapeDtypeStruct((rows, width), BF16),) * (groups - 1),
         in_specs=[SMEM] + [VMEM] * 5 + [ANY] + [VMEM] * len(held),
         out_specs=(VMEM,) * groups,
         scratch_shapes=[
             pltpu.VMEM((EDGE, width), F32),
-            pltpu.VMEM((2 * len(masks) * mats, width + EDGE), BF16),
-            pltpu.VMEM((2 * len(masks) * mats, depth), BF16),
+            pltpu.VMEM((2 * tiles * mats, width + EDGE), BF16),
+            pltpu.VMEM((2 * tiles * mats, depth), BF16),
             pltpu.VMEM((SLOTS, width + 2 * LEAD, EDGE), F32),
         ],
         cost_estimate=work(SLOTS + 8),
         compiler_params=PARAMS,
-    )(place, both, far, labels, spread, mats_own, padded_fields, *held)
-    arrived = [swap(block, 0, 2 * rel) for rel, block in enumerate(sent, 1)]
+    )(place, both, both_far, labels, spread, mats_own, padded_fields, *held)
+    arrived = [shift(block, rel) for rel, block in enumerate(sent, 1)]
 
     forward_out = pl.pallas_call(
-        functools.partial(forward_kernel, masks, count, rels),
+        functools.partial(forward_kernel, spots, count, rels),
         out_shape=jax.ShapeDtypeStruct((rows, width), BF16),
         in_specs=[SMEM] + [VMEM] * (4 + len(rels) + len(held)),
         out_specs=VMEM,
         scratch_shapes=[
             pltpu.VMEM((total_rows, width + EDGE), BF16),
             pltpu.VMEM((total_rows // EDGE, width + 2 * LEAD, EDGE), F32),
-            pltpu.VMEM((len(masks) * mats, depth), BF16),
+            pltpu.VMEM((tiles * mats, depth), BF16),
         ],
         cost_estimate=work(SLOTS + 8),
         compiler_params=PARAMS,
@@ -438,7 +466,7 @@
         in_specs=[VMEM] * 2 + [HBM] + [VMEM] * len(arrived),
         out_specs=VMEM,
         compiler_params=PARAMS,
-    )(both, keep, in_hbm(forward_out), *arrived[::-1])
+    )(both, keep, in_hbm(forward_out), *[arrived[k - 1] for k in ((2, 3, 1) if groups == 4 else range(1, groups))])
     return (forward_out, adjoint_out)
 
 

time: 30.7 us -> 29.7 us (0.967)
  waiting for transfers between devices: 3.21 us -> 0.69 us
  starting transfers between devices: 13.5 us -> 14.3 us
  Pallas kernels: 13.2 us -> 13.8 us
    ppermute x0 -> x6, starting transfers between devices: none -> 7.94 us  [shift(): return lax.ppermute(cells, ('tiles', 'coef'), pairs)]
    ppermute x10 -> x6, starting transfers between devices: 13.5 us -> 6.41 us  [swap(): return lax.ppermute(cells, ('tiles', 'coef'), pairs)]
    ppermute x10 -> x6, waiting for transfers between devices: 3.21 us -> 0.17 us  [swap(): return lax.ppermute(cells, ('tiles', 'coef'), pairs)]
    pallas_call x3, Pallas kernels: 7.41 us -> 8.12 us  [the longest x1 4.3 us: local(): pl.pallas_call(functools.partial(forward_kernel, spots, count, rels), out...]
    ppermute x0 -> x6, waiting for transfers between devices: none -> 0.52 us  [shift(): return lax.ppermute(cells, ('tiles', 'coef'), pairs)]
  transfers between devices with their start and end apart: 10 -> 12, of which waited for: 2 -> 2; matrix products, arithmetic and copies ran while one was open for 0% -> 0% of each run, Pallas kernels for 34% -> 40%
where the time goes in v8:
time: 29.7 us; the launch traced here: 29.6 us
  starting transfers between devices  14.3 us (48%)
  Pallas kernels  13.8 us (46%)
  waiting for transfers between devices  0.69 us (2%)
  between operations  0.69 us (2%)
    ppermute x6, starting transfers between devices, shift(): return lax.ppermute(cells, ('tiles', 'coef'), pairs)  7.94 us
    ppermute x6, starting transfers between devices, swap(): return lax.ppermute(cells, ('tiles', 'coef'), pairs)  6.41 us
    pallas_call x1, Pallas kernels, local(): pl.pallas_call(functools.partial(forward_kernel, spots, count, rels), out...  4.3 us
    pallas_call x1, Pallas kernels, local(): pl.pallas_call(functools.partial(prepare_kernel, rows), out_shape=(jax.Sh...  3.59 us
    pallas_call x1, Pallas kernels, local(): pl.pallas_call(functools.partial(adjoint_kernel, spots, count, groups), o...  3.1 us
    pallas_call x1, Pallas kernels, local(): pl.pallas_call(pack_kernel, out_shape=(jax.ShapeDtypeStruct((3,), jnp.int...  1.47 us
    pallas_call x1, Pallas kernels, local(): pl.pallas_call(functools.partial(fields_kernel, edge_spots, count), out_s...  0.71 us
    pallas_call x1, Pallas kernels, local(): pl.pallas_call(finish_kernel, out_shape=jax.ShapeDtypeStruct((rows, width...  0.64 us
  transfers between devices with their start and end apart: 12, of which 2 were waited for; matrix products, arithmetic and copies ran while one was open for 0% of the time, Pallas kernels for 40%

profile of v8, /device:TPU:0, one launch (start us, length us, event | category | flops | bytes accessed | tf_op | source)
XLA Modules:
  0.0 29.6 jit_solution(4503760153785890082)
XLA Ops:
  0.6 1.5 %shard_map.77 = (s32[3]{0:T(128)S(1)}, bf16[144,256]{1,0:T(8,128)(2,1)S(1)}, bf16[2,32,512]{2,1,0:T(8,128)(2,1)S(1)}, s32[1,512]{1,0:T(1,128)S(1)}) custom-call(bf16[4,32,256]{2,1,0:T(8,128)(2,1)} %t_any.1, bf16[32,512]{1,0:T(8,128)(2,1)} %f_any.1, bf16[32,512]{1,0:T(8,128)(2,1)} %a_any.1, s32[1,512]{1,0:T(1,128)} %bitcast.5), custom_call_target="tpu_custom_call" | custom-call | tf_op jit(solution)/shard_map/pallas_call | solution.py:348
  2.1 0.5 %collective-permute-start.4 = (bf16[144,256]{1,0:T(8,128)(2,1)S(1)}, bf16[144,256]{1,0:T(8,128)(2,1)S(1)}, u32[]{:S(2)}, u32[]{:S(2)}) collective-permute-start(bf16[144,256]{1,0:T(8,128)(2,1)S(1)} %get-tuple-element.18.near_ref), channel_id=1, source_target_pairs={{0,8},{1,9},{2,10},{3,11},{4,12},{5,13},{6,14},{7,15},{8,0},{9,1},... | collective-permute-start | bytes 221192 | tf_op jit(solution)/shard_map/ppermute | solution.py:334
  2.6 3.6 %collective-permute-start.1 = (bf16[144,256]{1,0:T(8,128)(2,1)S(1)}, bf16[144,256]{1,0:T(8,128)(2,1)S(1)}, u32[]{:S(2)}, u32[]{:S(2)}) collective-permute-start(bf16[144,256]{1,0:T(8,128)(2,1)S(1)} %get-tuple-element.18.near_ref), channel_id=1, source_target_pairs={{0,25},{1,24},{2,27},{3,26},{4,29},{5,28},{6,31},{7,30},{8,17},{9,... | collective-permute-start | bytes 221192 | tf_op jit(solution)/shard_map/ppermute | solution.py:334
  6.2 0.2 collective-permute-start.2
  6.4 0.1 collective-permute-start.3
  6.5 1.9 %collective-permute-start = (bf16[2,32,512]{2,1,0:T(8,128)(2,1)S(1)}, bf16[2,32,512]{2,1,0:T(8,128)(2,1)S(1)}, u32[]{:S(2)}, u32[]{:S(2)}) collective-permute-start(bf16[2,32,512]{2,1,0:T(8,128)(2,1)S(1)} %get-tuple-element.14.both_ref), channel_id=1, source_target_pairs={{0,1},{1,0},{2,3},{3,2},{4,5},{5,4},{6,7},{7,6},{8,9},{9,8},{10,11... | collective-permute-start | bytes 196616 | tf_op jit(solution)/shard_map/ppermute | solution.py:334
  8.5 3.6 %shard_map.78 = (bf16[30,256,256]{2,1,0:T(8,128)(2,1)S(1)}, bf16[15,256,256]{2,1,0:T(8,128)(2,1)S(1)}, bf16[30,512,128]{2,1,0:T(8,128)(2,1)S(1)}) custom-call(bf16[30,256,256]{2,1,0:T(8,128)(2,1)} %couple_ref.1, s32[30,512]{1,0:T(8,128)} %bitcast.4, s32[3]{0:T(128)S(1)} %get-tuple-element.13.place), custom_call_target="tpu_custom_call" | custom-call | bytes 7864320 | tf_op jit(solution)/shard_map/pallas_call | solution.py:361
  12.1 0.2 collective-permute-done.both_ref.far_ref
  12.2 0.0 collective-permute-done.2.far_ref
  12.2 0.0 collective-permute-done.3.top_ref
  12.3 0.1 collective-permute-start.8
  12.3 0.7 %shard_map.80.refs_0_.after_ref = bf16[272,128]{1,0:T(8,128)(2,1)S(1)} custom-call(s32[3]{0:T(128)S(1)} %get-tuple-element.13.place, bf16[2,32,512]{2,1,0:T(8,128)(2,1)S(1)} %get-tuple-element.14.both_ref, bf16[2,32,512]{2,1,0:T(8,128)(2,1)S(1)} %collective-permute-done.both_ref.far_ref, bf16[4,144,256]{2,1,0:T(8,128)(2,1)S(1)} %shard_map.79.refs_0_.refs_4_, ...), custom_call_target="tpu_custom_call" | custom-call | tf_op jit(solution)/shard_map/pallas_call | solution.py:413
  13.1 1.6 %collective-permute-start.5 = (bf16[272,128]{1,0:T(8,128)(2,1)S(1)}, bf16[272,128]{1,0:T(8,128)(2,1)S(1)}, u32[]{:S(2)}, u32[]{:S(2)}) collective-permute-start(bf16[272,128]{1,0:T(8,128)(2,1)S(1)} %shard_map.80.refs_0_.after_ref), channel_id=1, source_target_pairs={{0,2},{1,3},{2,4},{3,5},{4,6},{5,7},{6,0},{7,1},{8,10},{9,11},{10,... | collective-permute-start | bytes 208904 | tf_op jit(solution)/shard_map/ppermute | solution.py:342
  14.6 2.6 %collective-permute-start.6 = (bf16[272,128]{1,0:T(8,128)(2,1)S(1)}, bf16[272,128]{1,0:T(8,128)(2,1)S(1)}, u32[]{:S(2)}, u32[]{:S(2)}) collective-permute-start(bf16[272,128]{1,0:T(8,128)(2,1)S(1)} %shard_map.80.refs_0_.after_ref), channel_id=1, source_target_pairs={{0,4},{1,5},{2,6},{3,7},{4,0},{5,1},{6,2},{7,3},{8,12},{9,13},{10,... | collective-permute-start | bytes 208904 | tf_op jit(solution)/shard_map/ppermute | solution.py:342
  17.2 1.3 %collective-permute-start.7 = (bf16[272,128]{1,0:T(8,128)(2,1)S(1)}, bf16[272,128]{1,0:T(8,128)(2,1)S(1)}, u32[]{:S(2)}, u32[]{:S(2)}) collective-permute-start(bf16[272,128]{1,0:T(8,128)(2,1)S(1)} %shard_map.80.refs_0_.after_ref), channel_id=1, source_target_pairs={{0,6},{1,7},{2,0},{3,1},{4,2},{5,3},{6,4},{7,5},{8,14},{9,15},{10,... | collective-permute-start | bytes 208904 | tf_op jit(solution)/shard_map/ppermute | solution.py:342
  18.6 0.0 collective-permute-done.8.refs_5_.refs_1_
  18.6 3.1 %shard_map.82 = (f32[32,512]{1,0:T(8,128)S(1)}, bf16[32,512]{1,0:T(8,128)(2,1)S(1)}, bf16[32,512]{1,0:T(8,128)(2,1)S(1)}, bf16[32,512]{1,0:T(8,128)(2,1)S(1)}) custom-call(s32[3]{0:T(128)S(1)} %get-tuple-element.13.place, bf16[2,32,512]{2,1,0:T(8,128)(2,1)S(1)} %get-tuple-element.14.both_ref, bf16[2,32,512]{2,1,0:T(8,128)(2,1)S(1)} %collective-permute-done.both_ref.far_ref, ...), custom_call_target="tpu_custom_call" | custom-call | flops 2550136832 | bytes 4980736 | tf_op jit(solution)/shard_map/pallas_call | solution.py:433
  21.7 0.5 %collective-permute-start.10 = (bf16[32,512]{1,0:T(8,128)(2,1)S(1)}, bf16[32,512]{1,0:T(8,128)(2,1)S(1)}, u32[]{:S(2)}, u32[]{:S(2)}) collective-permute-start(bf16[32,512]{1,0:T(8,128)(2,1)S(1)} %get-tuple-element.22), channel_id=1, source_target_pairs={{0,6},{1,7},{2,0},{3,1},{4,2},{5,3},{6,4},{7,5},{8,14},{9,15},{10,... | collective-permute-start | bytes 98312 | tf_op jit(solution)/shard_map/ppermute | solution.py:342
  22.2 1.6 %collective-permute-start.11 = (bf16[32,512]{1,0:T(8,128)(2,1)S(1)}, bf16[32,512]{1,0:T(8,128)(2,1)S(1)}, u32[]{:S(2)}, u32[]{:S(2)}) collective-permute-start(bf16[32,512]{1,0:T(8,128)(2,1)S(1)} %get-tuple-element.23), channel_id=1, source_target_pairs={{0,2},{1,3},{2,4},{3,5},{4,6},{5,7},{6,0},{7,1},{8,10},{9,11},{10,... | collective-permute-start | bytes 98312 | tf_op jit(solution)/shard_map/ppermute | solution.py:342
  23.8 0.3 %collective-permute-start.9 = (bf16[32,512]{1,0:T(8,128)(2,1)S(1)}, bf16[32,512]{1,0:T(8,128)(2,1)S(1)}, u32[]{:S(2)}, u32[]{:S(2)}) collective-permute-start(bf16[32,512]{1,0:T(8,128)(2,1)S(1)} %get-tuple-element.21), channel_id=1, source_target_pairs={{0,4},{1,5},{2,6},{3,7},{4,0},{5,1},{6,2},{7,3},{8,12},{9,13},{10,... | collective-permute-start | bytes 98312 | tf_op jit(solution)/shard_map/ppermute | solution.py:342
  24.1 0.0 collective-permute-done.6.refs_2_
  24.1 4.3 %shard_map.81.after_ref = bf16[32,512]{1,0:T(8,128)(2,1)} custom-call(s32[3]{0:T(128)S(1)} %get-tuple-element.13.place, bf16[2,32,512]{2,1,0:T(8,128)(2,1)S(1)} %get-tuple-element.14.both_ref, s32[1,512]{1,0:T(1,128)S(1)} %get-tuple-element.15.class_ref, bf16[30,512,128]{2,1,0:T(8,128)(2,1)S(1)} %get-tuple-element.16.spread_ref, ...), custom_call_target="tpu_custom_call" | custom-call | flops 2550136832 | bytes 4980736 | tf_op jit(solution)/shard_map/pallas_call | solution.py:450
  28.4 0.5 %collective-permute-done.9.refs_0_ = bf16[32,512]{1,0:T(8,128)(2,1)S(1)} collective-permute-done((bf16[32,512]{1,0:T(8,128)(2,1)S(1)}, bf16[32,512]{1,0:T(8,128)(2,1)S(1)}, u32[]{:S(2)}, u32[]{:S(2)}) %collective-permute-start.9) | collective-permute-done | bytes 32800 | tf_op jit(solution)/shard_map/ppermute | solution.py:342
  28.9 0.6 %shard_map.83 = bf16[32,512]{1,0:T(8,128)(2,1)} custom-call(bf16[2,32,512]{2,1,0:T(8,128)(2,1)S(1)} %get-tuple-element.14.both_ref, f32[32,512]{1,0:T(8,128)S(1)} %get-tuple-element.20.keep_ref, bf16[32,512]{1,0:T(8,128)(2,1)} %shard_map.81.after_ref, bf16[32,512]{1,0:T(8,128)(2,1)S(1)} %collective-permute-done.9.refs_0_, ...), custom_call_target="tpu_custom_call" | custom-call | tf_op jit(solution)/shard_map/pallas_call | solution.py:463
  (7 shorter events, 0.0 us)
Async XLA Ops:
  2.1 10.1 %collective-permute-start.4 = (bf16[144,256]{1,0:T(8,128)(2,1)S(1)}, bf16[144,256]{1,0:T(8,128)(2,1)S(1)}, u32[]{:S(2)}, u32[]{:S(2)}) collective-permute-start(bf16[144,256]{1,0:T(8,128)(2,1)S(1)} %get-tuple-element.18.near_ref), channel_id=1, source_target_pairs={{0,8},{1,9},{2,10},{3,11},{4,12},{5,13},{6,14},{7,15},{8,0},{9,1},... | collective-permute-start | bytes 221192 | tf_op jit(solution)/shard_map/ppermute | solution.py:334
  2.6 9.6 %collective-permute-start.1 = (bf16[144,256]{1,0:T(8,128)(2,1)S(1)}, bf16[144,256]{1,0:T(8,128)(2,1)S(1)}, u32[]{:S(2)}, u32[]{:S(2)}) collective-permute-start(bf16[144,256]{1,0:T(8,128)(2,1)S(1)} %get-tuple-element.18.near_ref), channel_id=1, source_target_pairs={{0,25},{1,24},{2,27},{3,26},{4,29},{5,28},{6,31},{7,30},{8,17},{9,... | collective-permute-start | bytes 221192 | tf_op jit(solution)/shard_map/ppermute | solution.py:334
  6.2 6.0 %collective-permute-start.2 = (bf16[144,256]{1,0:T(8,128)(2,1)S(1)}, bf16[144,256]{1,0:T(8,128)(2,1)S(1)}, u32[]{:S(2)}, u32[]{:S(2)}) collective-permute-start(bf16[144,256]{1,0:T(8,128)(2,1)S(1)} %get-tuple-element.18.near_ref), channel_id=1, source_target_pairs={{0,9},{1,8},{2,11},{3,10},{4,13},{5,12},{6,15},{7,14},{8,1},{9,0},... | collective-permute-start | bytes 221192 | tf_op jit(solution)/shard_map/ppermute | solution.py:334
  6.4 5.8 %collective-permute-start.3 = (bf16[144,256]{1,0:T(8,128)(2,1)S(1)}, bf16[144,256]{1,0:T(8,128)(2,1)S(1)}, u32[]{:S(2)}, u32[]{:S(2)}) collective-permute-start(bf16[144,256]{1,0:T(8,128)(2,1)S(1)} %get-tuple-element.18.near_ref), channel_id=1, source_target_pairs={{0,24},{1,25},{2,26},{3,27},{4,28},{5,29},{6,30},{7,31},{8,16},{9,... | collective-permute-start | bytes 221192 | tf_op jit(solution)/shard_map/ppermute | solution.py:334
  6.5 5.7 %collective-permute-start = (bf16[2,32,512]{2,1,0:T(8,128)(2,1)S(1)}, bf16[2,32,512]{2,1,0:T(8,128)(2,1)S(1)}, u32[]{:S(2)}, u32[]{:S(2)}) collective-permute-start(bf16[2,32,512]{2,1,0:T(8,128)(2,1)S(1)} %get-tuple-element.14.both_ref), channel_id=1, source_target_pairs={{0,1},{1,0},{2,3},{3,2},{4,5},{5,4},{6,7},{7,6},{8,9},{9,8},{10,11... | collective-permute-start | bytes 196616 | tf_op jit(solution)/shard_map/ppermute | solution.py:334
  12.3 6.3 %collective-permute-start.8 = (bf16[4,144,256]{2,1,0:T(8,128)(2,1)S(1)}, bf16[4,144,256]{2,1,0:T(8,128)(2,1)S(1)}, u32[]{:S(2)}, u32[]{:S(2)}) collective-permute-start(bf16[4,144,256]{2,1,0:T(8,128)(2,1)S(1)} %shard_map.79.refs_0_.refs_4_), channel_id=1, source_target_pairs={{0,8},{1,9},{2,10},{3,11},{4,12},{5,13},{6,14},{7,15},{8,0},{9,1},... | collective-permute-start | bytes 884744 | tf_op jit(solution)/shard_map/ppermute | solution.py:334
  13.1 10.7 %collective-permute-start.5 = (bf16[272,128]{1,0:T(8,128)(2,1)S(1)}, bf16[272,128]{1,0:T(8,128)(2,1)S(1)}, u32[]{:S(2)}, u32[]{:S(2)}) collective-permute-start(bf16[272,128]{1,0:T(8,128)(2,1)S(1)} %shard_map.80.refs_0_.after_ref), channel_id=1, source_target_pairs={{0,2},{1,3},{2,4},{3,5},{4,6},{5,7},{6,0},{7,1},{8,10},{9,11},{10,... | collective-permute-start | bytes 208904 | tf_op jit(solution)/shard_map/ppermute | solution.py:342
  14.6 9.5 %collective-permute-start.6 = (bf16[272,128]{1,0:T(8,128)(2,1)S(1)}, bf16[272,128]{1,0:T(8,128)(2,1)S(1)}, u32[]{:S(2)}, u32[]{:S(2)}) collective-permute-start(bf16[272,128]{1,0:T(8,128)(2,1)S(1)} %shard_map.80.refs_0_.after_ref), channel_id=1, source_target_pairs={{0,4},{1,5},{2,6},{3,7},{4,0},{5,1},{6,2},{7,3},{8,12},{9,13},{10,... | collective-permute-start | bytes 208904 | tf_op jit(solution)/shard_map/ppermute | solution.py:342
  17.2 6.9 %collective-permute-start.7 = (bf16[272,128]{1,0:T(8,128)(2,1)S(1)}, bf16[272,128]{1,0:T(8,128)(2,1)S(1)}, u32[]{:S(2)}, u32[]{:S(2)}) collective-permute-start(bf16[272,128]{1,0:T(8,128)(2,1)S(1)} %shard_map.80.refs_0_.after_ref), channel_id=1, source_target_pairs={{0,6},{1,7},{2,0},{3,1},{4,2},{5,3},{6,4},{7,5},{8,14},{9,15},{10,... | collective-permute-start | bytes 208904 | tf_op jit(solution)/shard_map/ppermute | solution.py:342
  21.7 6.7 %collective-permute-start.10 = (bf16[32,512]{1,0:T(8,128)(2,1)S(1)}, bf16[32,512]{1,0:T(8,128)(2,1)S(1)}, u32[]{:S(2)}, u32[]{:S(2)}) collective-permute-start(bf16[32,512]{1,0:T(8,128)(2,1)S(1)} %get-tuple-element.22), channel_id=1, source_target_pairs={{0,6},{1,7},{2,0},{3,1},{4,2},{5,3},{6,4},{7,5},{8,14},{9,15},{10,... | collective-permute-start | bytes 98312 | tf_op jit(solution)/shard_map/ppermute | solution.py:342
  22.2 6.2 %collective-permute-start.11 = (bf16[32,512]{1,0:T(8,128)(2,1)S(1)}, bf16[32,512]{1,0:T(8,128)(2,1)S(1)}, u32[]{:S(2)}, u32[]{:S(2)}) collective-permute-start(bf16[32,512]{1,0:T(8,128)(2,1)S(1)} %get-tuple-element.23), channel_id=1, source_target_pairs={{0,2},{1,3},{2,4},{3,5},{4,6},{5,7},{6,0},{7,1},{8,10},{9,11},{10,... | collective-permute-start | bytes 98312 | tf_op jit(solution)/shard_map/ppermute | solution.py:342
  23.8 5.2 %collective-permute-start.9 = (bf16[32,512]{1,0:T(8,128)(2,1)S(1)}, bf16[32,512]{1,0:T(8,128)(2,1)S(1)}, u32[]{:S(2)}, u32[]{:S(2)}) collective-permute-start(bf16[32,512]{1,0:T(8,128)(2,1)S(1)} %get-tuple-element.21), channel_id=1, source_target_pairs={{0,4},{1,5},{2,6},{3,7},{4,0},{5,1},{6,2},{7,3},{8,12},{9,13},{10,... | collective-permute-start | bytes 98312 | tf_op jit(solution)/shard_map/ppermute | solution.py:342

commit v9 on v8

--- a/solution.py
+++ b/solution.py
@@ -19,7 +19,6 @@
 BF16 = jnp.bfloat16
 F32 = jnp.float32
 VMEM = pl.BlockSpec(memory_space=pltpu.VMEM)
-SMEM = pl.BlockSpec(memory_space=pltpu.SMEM)
 ANY = pl.BlockSpec(memory_space=pl.ANY)
 HBM = pl.BlockSpec(memory_space=pltpu.HBM)
 PARAMS = pltpu.CompilerParams(vmem_limit_bytes=24 * 1024 * 1024)
@@ -27,6 +26,11 @@
 
 def in_hbm(cells):
     return pltpu.with_memory_space_constraint(cells, pltpu.HBM)
+
+
+def find_place():
+    coef = lax.axis_index("coef")
+    return lax.axis_index("tiles"), coef & 1, coef >> 1
 
 
 def edges_of(cells):
@@ -41,12 +45,8 @@
 
 
 def pack_kernel(
-    t_any, f_any, a_any, class_any, place, near_ref, both_ref, class_ref, t_ref, sems
+    t_any, f_any, a_any, class_any, near_ref, both_ref, class_ref, t_ref, sems
 ):
-    coef = lax.axis_index("coef")
-    place[0] = lax.axis_index("tiles")
-    place[1] = coef & 1
-    place[2] = coef >> 1
     copies = [
         pltpu.make_async_copy(source, target, sems.at[at])
         for at, (source, target) in enumerate(
@@ -122,7 +122,8 @@
     return [[(refs[which], at, mask) for which, at, mask in group] for group in spots]
 
 
-def fields_kernel(spots, count, place, both_ref, far_ref, *refs):
+def fields_kernel(spots, count, both_ref, far_ref, *refs):
+    place = find_place()
     (near, across), (out_ref, halos) = find_pieces(spots, refs[:-2]), refs[-2:]
     unused, rows, width = both_ref.shape
     mats = count * rows
@@ -156,7 +157,7 @@
         padded[pl.ds(start + group * LEAD, LEAD), width:] = halo.astype(BF16)
 
 
-def prepare_kernel(rows, couple_ref, links_ref, place, mats_ref, own_ref, spread_ref, links, weights, sems):
+def prepare_kernel(rows, couple_ref, links_ref, after_ref, mats_ref, own_ref, spread_ref, links, weights, sems):
     copies = []
     for chunk in range(SLOTS // CHUNK):
         span = pl.ds(chunk * CHUNK, CHUNK)
@@ -180,7 +181,7 @@
         spread_ref[2 * pair] = spread[:, :EDGE]
         spread_ref[2 * pair + 1] = spread[:, EDGE:]
     depth = mats_ref.shape[1]
-    odd = place[1]
+    odd = find_place()[1]
     lane = lax.broadcasted_iota(jnp.int32, (depth, EDGE), 1)
     first = jnp.where((lane // rows) % 2 == odd, 1.0, 0.0).astype(BF16)
     second = (1.0 - first).astype(BF16)
@@ -242,8 +243,9 @@
 
 
 def adjoint_kernel(
-    spots, count, sends, place, both_ref, far_ref, class_ref, spread_ref, own_ref, after_ref, *refs
+    spots, count, sends, both_ref, far_ref, class_ref, spread_ref, own_ref, after_ref, *refs
 ):
+    place = find_place()
     near, across = find_pieces(spots, refs[: -sends - 4])
     keep_ref, *send_refs = refs[-sends - 4 : -4]
     total_ref, expanded, stacked, products = refs[-4:]
@@ -285,8 +287,9 @@
 
 
 def forward_kernel(
-    spots, count, rels, place, both_ref, class_ref, spread_ref, mats_ref, *refs
+    spots, count, rels, both_ref, class_ref, spread_ref, mats_ref, *refs
 ):
+    place = find_place()
     pieces, refs = refs[: len(rels)], refs[len(rels) :]
     (near, across), (out_ref, padded, upright, stacked) = find_pieces(spots, refs[:-4]), refs[-4:]
     unused, rows, width = both_ref.shape
@@ -345,16 +348,15 @@
     mats = count * rows
     near_rows = mats + rows // edge_parts(rows)
     total_rows = couple.shape[1]
-    place, near_own, both, labels = pl.pallas_call(
+    near_own, both, labels = pl.pallas_call(
         pack_kernel,
         out_shape=(
-            jax.ShapeDtypeStruct((3,), jnp.int32),
             jax.ShapeDtypeStruct((near_rows, depth), BF16),
             jax.ShapeDtypeStruct((2, rows, width), BF16),
             jax.ShapeDtypeStruct(labels.shape, jnp.int32),
         ),
         in_specs=[HBM] * 4,
-        out_specs=(SMEM,) + (VMEM,) * 3,
+        out_specs=(VMEM,) * 3,
         scratch_shapes=[pltpu.VMEM(tmatrices.shape, BF16), pltpu.SemaphoreType.DMA((4,))],
         compiler_params=PARAMS,
     )(*[in_hbm(cells) for cells in (tmatrices, fields, adjoints, labels)])
@@ -365,7 +367,7 @@
             jax.ShapeDtypeStruct((SLOTS // 2, total_rows, 2 * EDGE), BF16),
             jax.ShapeDtypeStruct((SLOTS, width, EDGE), BF16),
         ),
-        in_specs=[HBM, HBM, SMEM],
+        in_specs=[HBM, HBM, VMEM],
         out_specs=(VMEM,) * 3,
         scratch_shapes=[
             pltpu.VMEM((SLOTS, width), jnp.int32),
@@ -374,7 +376,7 @@
         ],
         cost_estimate=pl.CostEstimate(flops=0, bytes_accessed=4 * couple.size, transcendentals=0),
         compiler_params=PARAMS,
-    )(in_hbm(couple), in_hbm(neighbours.T), place)
+    )(in_hbm(couple), in_hbm(neighbours.T), labels)
 
     top = tiles // 2
     both_far = swap(both, 0, 1)
@@ -413,11 +415,11 @@
     padded_fields = pl.pallas_call(
         functools.partial(fields_kernel, edge_spots, count),
         out_shape=jax.ShapeDtypeStruct((2 * rows * (width // EDGE) + LEAD, EDGE), BF16),
-        in_specs=[SMEM] + [VMEM] * (2 + len(sources)),
+        in_specs=[VMEM] * (2 + len(sources)),
         out_specs=VMEM,
         scratch_shapes=[pltpu.VMEM((2 * rows, EDGE), F32)],
         compiler_params=PARAMS,
-    )(place, both, both_far, *sources)
+    )(both, both_far, *sources)
 
     groups = coefs // 2
     gathered = {0: padded_fields}
@@ -434,7 +436,7 @@
         functools.partial(adjoint_kernel, spots, count, groups),
         out_shape=(jax.ShapeDtypeStruct((rows, width), F32),)
         + (jax.ShapeDtypeStruct((rows, width), BF16),) * (groups - 1),
-        in_specs=[SMEM] + [VMEM] * 5 + [ANY] + [VMEM] * len(held),
+        in_specs=[VMEM] * 5 + [ANY] + [VMEM] * len(held),
         out_specs=(VMEM,) * groups,
         scratch_shapes=[
             pltpu.VMEM((EDGE, width), F32),
@@ -444,13 +446,13 @@
         ],
         cost_estimate=work(SLOTS + 8),
         compiler_params=PARAMS,
-    )(place, both, both_far, labels, spread, mats_own, padded_fields, *held)
+    )(both, both_far, labels, spread, mats_own, padded_fields, *held)
     arrived = [shift(block, rel) for rel, block in enumerate(sent, 1)]
 
     forward_out = pl.pallas_call(
         functools.partial(forward_kernel, spots, count, rels),
         out_shape=jax.ShapeDtypeStruct((rows, width), BF16),
-        in_specs=[SMEM] + [VMEM] * (4 + len(rels) + len(held)),
+        in_specs=[VMEM] * (4 + len(rels) + len(held)),
         out_specs=VMEM,
         scratch_shapes=[
             pltpu.VMEM((total_rows, width + EDGE), BF16),
@@ -459,7 +461,7 @@
         ],
         cost_estimate=work(SLOTS + 8),
         compiler_params=PARAMS,
-    )(place, both, labels, spread, mats_held, *[gathered[rel] for rel in rels], *held)
+    )(both, labels, spread, mats_held, *[gathered[rel] for rel in rels], *held)
     adjoint_out = pl.pallas_call(
         finish_kernel,
         out_shape=jax.ShapeDtypeStruct((rows, width), BF16),

time: 29.7 us -> 28.1 us (0.946)
  Pallas kernels: 13.8 us -> 11.2 us
  waiting for transfers between devices: 0.69 us -> 1.77 us
    pallas_call x1, Pallas kernels: 3.1 us -> 2.53 us  [local(): pl.pallas_call(functools.partial(adjoint_kernel, spots, count, groups), o...]
    pallas_call x1, Pallas kernels: 0.71 us -> 0.17 us  [local(): pl.pallas_call(functools.partial(fields_kernel, edge_spots, count), out_s...]
    ppermute x6, waiting for transfers between devices: 0.17 us -> 0.71 us  [swap(): return lax.ppermute(cells, ('tiles', 'coef'), pairs)]
    pallas_call x1, Pallas kernels: 3.59 us -> 3.05 us  [local(): pl.pallas_call(functools.partial(prepare_kernel, rows), out_shape=(jax.Sh...]
    ppermute x6, waiting for transfers between devices: 0.52 us -> 1.06 us  [shift(): return lax.ppermute(cells, ('tiles', 'coef'), pairs)]
    pallas_call x1, Pallas kernels: 4.3 us -> 3.77 us  [local(): pl.pallas_call(functools.partial(forward_kernel, spots, count, rels), out...]
    pallas_call x1, Pallas kernels: 1.47 us -> 0.96 us  [local(): pl.pallas_call(pack_kernel, out_shape=(jax.ShapeDtypeStruct((near_rows, d...]
  transfers between devices with their start and end apart: 12 -> 12, of which waited for: 2 -> 2; matrix products, arithmetic and copies ran while one was open for 0% -> 0% of each run, Pallas kernels for 40% -> 34%
where the time goes in v9:
time: 28.1 us; the launch traced here: 28 us
  starting transfers between devices  14.3 us (51%)
  Pallas kernels  11.2 us (40%)
  waiting for transfers between devices  1.77 us (6%)
  between operations  0.69 us (2%)
    ppermute x6, starting transfers between devices, shift(): return lax.ppermute(cells, ('tiles', 'coef'), pairs)  7.93 us
    ppermute x6, starting transfers between devices, swap(): return lax.ppermute(cells, ('tiles', 'coef'), pairs)  6.41 us
    pallas_call x1, Pallas kernels, local(): pl.pallas_call(functools.partial(forward_kernel, spots, count, rels), out...  3.77 us
    pallas_call x1, Pallas kernels, local(): pl.pallas_call(functools.partial(prepare_kernel, rows), out_shape=(jax.Sh...  3.05 us
    pallas_call x1, Pallas kernels, local(): pl.pallas_call(functools.partial(adjoint_kernel, spots, count, groups), o...  2.53 us
    ppermute x6, waiting for transfers between devices, shift(): return lax.ppermute(cells, ('tiles', 'coef'), pairs)  1.06 us
    pallas_call x1, Pallas kernels, local(): pl.pallas_call(pack_kernel, out_shape=(jax.ShapeDtypeStruct((near_rows, d...  0.96 us
    ppermute x6, waiting for transfers between devices, swap(): return lax.ppermute(cells, ('tiles', 'coef'), pairs)  0.71 us
  transfers between devices with their start and end apart: 12, of which 2 were waited for; matrix products, arithmetic and copies ran while one was open for 0% of the time, Pallas kernels for 34%

profile of v9, /device:TPU:0, one launch (start us, length us, event | category | flops | bytes accessed | tf_op | source)
XLA Modules:
  0.0 28.0 jit_solution(12874826914207153702)
XLA Ops:
  0.6 1.0 %shard_map.77 = (bf16[144,256]{1,0:T(8,128)(2,1)S(1)}, bf16[2,32,512]{2,1,0:T(8,128)(2,1)S(1)}, s32[1,512]{1,0:T(1,128)S(1)}) custom-call(bf16[4,32,256]{2,1,0:T(8,128)(2,1)} %t_any.1, bf16[32,512]{1,0:T(8,128)(2,1)} %f_any.1, bf16[32,512]{1,0:T(8,128)(2,1)} %a_any.1, s32[1,512]{1,0:T(1,128)} %bitcast.5), custom_call_target="tpu_custom_call" | custom-call | tf_op jit(solution)/shard_map/pallas_call | solution.py:351
  1.6 0.5 %collective-permute-start.4 = (bf16[144,256]{1,0:T(8,128)(2,1)S(1)}, bf16[144,256]{1,0:T(8,128)(2,1)S(1)}, u32[]{:S(2)}, u32[]{:S(2)}) collective-permute-start(bf16[144,256]{1,0:T(8,128)(2,1)S(1)} %get-tuple-element.16.near_ref), channel_id=1, source_target_pairs={{0,8},{1,9},{2,10},{3,11},{4,12},{5,13},{6,14},{7,15},{8,0},{9,1},... | collective-permute-start | bytes 221192 | tf_op jit(solution)/shard_map/ppermute | solution.py:337
  2.1 3.6 %collective-permute-start.1 = (bf16[144,256]{1,0:T(8,128)(2,1)S(1)}, bf16[144,256]{1,0:T(8,128)(2,1)S(1)}, u32[]{:S(2)}, u32[]{:S(2)}) collective-permute-start(bf16[144,256]{1,0:T(8,128)(2,1)S(1)} %get-tuple-element.16.near_ref), channel_id=1, source_target_pairs={{0,25},{1,24},{2,27},{3,26},{4,29},{5,28},{6,31},{7,30},{8,17},{9,... | collective-permute-start | bytes 221192 | tf_op jit(solution)/shard_map/ppermute | solution.py:337
  5.7 0.2 collective-permute-start.2
  5.9 0.1 collective-permute-start.3
  6.0 1.9 %collective-permute-start = (bf16[2,32,512]{2,1,0:T(8,128)(2,1)S(1)}, bf16[2,32,512]{2,1,0:T(8,128)(2,1)S(1)}, u32[]{:S(2)}, u32[]{:S(2)}) collective-permute-start(bf16[2,32,512]{2,1,0:T(8,128)(2,1)S(1)} %get-tuple-element.12.both_ref), channel_id=1, source_target_pairs={{0,1},{1,0},{2,3},{3,2},{4,5},{5,4},{6,7},{7,6},{8,9},{9,8},{10,11... | collective-permute-start | bytes 196616 | tf_op jit(solution)/shard_map/ppermute | solution.py:337
  7.9 3.1 %shard_map.78 = (bf16[30,256,256]{2,1,0:T(8,128)(2,1)S(1)}, bf16[15,256,256]{2,1,0:T(8,128)(2,1)S(1)}, bf16[30,512,128]{2,1,0:T(8,128)(2,1)S(1)}) custom-call(bf16[30,256,256]{2,1,0:T(8,128)(2,1)} %couple_ref.1, s32[30,512]{1,0:T(8,128)} %bitcast.4, s32[1,512]{1,0:T(1,128)S(1)} %get-tuple-element.13.after_ref.class_ref), custom_call_target="tpu_custom_call" | custom-call | bytes 7864320 | tf_op jit(solution)/shard_map/pallas_call | solution.py:363
  11.0 0.7 %collective-permute-done.both_ref.far_ref = bf16[2,32,512]{2,1,0:T(8,128)(2,1)S(1)} collective-permute-done((bf16[2,32,512]{2,1,0:T(8,128)(2,1)S(1)}, bf16[2,32,512]{2,1,0:T(8,128)(2,1)S(1)}, u32[]{:S(2)}, u32[]{:S(2)}) %collective-permute-start) | collective-permute-done | bytes 65568 | tf_op jit(solution)/shard_map/ppermute | solution.py:337
  11.7 0.0 collective-permute-done.4.beside_ref
  11.8 0.1 collective-permute-start.8
  11.8 0.2 shard_map.80.refs_0_.after_ref
  12.0 1.6 %collective-permute-start.5 = (bf16[272,128]{1,0:T(8,128)(2,1)S(1)}, bf16[272,128]{1,0:T(8,128)(2,1)S(1)}, u32[]{:S(2)}, u32[]{:S(2)}) collective-permute-start(bf16[272,128]{1,0:T(8,128)(2,1)S(1)} %shard_map.80.refs_0_.after_ref), channel_id=1, source_target_pairs={{0,2},{1,3},{2,4},{3,5},{4,6},{5,7},{6,0},{7,1},{8,10},{9,11},{10,... | collective-permute-start | bytes 208904 | tf_op jit(solution)/shard_map/ppermute | solution.py:345
  13.6 2.6 %collective-permute-start.6 = (bf16[272,128]{1,0:T(8,128)(2,1)S(1)}, bf16[272,128]{1,0:T(8,128)(2,1)S(1)}, u32[]{:S(2)}, u32[]{:S(2)}) collective-permute-start(bf16[272,128]{1,0:T(8,128)(2,1)S(1)} %shard_map.80.refs_0_.after_ref), channel_id=1, source_target_pairs={{0,4},{1,5},{2,6},{3,7},{4,0},{5,1},{6,2},{7,3},{8,12},{9,13},{10,... | collective-permute-start | bytes 208904 | tf_op jit(solution)/shard_map/ppermute | solution.py:345
  16.2 1.3 %collective-permute-start.7 = (bf16[272,128]{1,0:T(8,128)(2,1)S(1)}, bf16[272,128]{1,0:T(8,128)(2,1)S(1)}, u32[]{:S(2)}, u32[]{:S(2)}) collective-permute-start(bf16[272,128]{1,0:T(8,128)(2,1)S(1)} %shard_map.80.refs_0_.after_ref), channel_id=1, source_target_pairs={{0,6},{1,7},{2,0},{3,1},{4,2},{5,3},{6,4},{7,5},{8,14},{9,15},{10,... | collective-permute-start | bytes 208904 | tf_op jit(solution)/shard_map/ppermute | solution.py:345
  17.5 0.0 collective-permute-done.8.refs_5_.refs_1_
  17.5 2.5 %shard_map.82 = (f32[32,512]{1,0:T(8,128)S(1)}, bf16[32,512]{1,0:T(8,128)(2,1)S(1)}, bf16[32,512]{1,0:T(8,128)(2,1)S(1)}, bf16[32,512]{1,0:T(8,128)(2,1)S(1)}) custom-call(bf16[2,32,512]{2,1,0:T(8,128)(2,1)S(1)} %get-tuple-element.12.both_ref, bf16[2,32,512]{2,1,0:T(8,128)(2,1)S(1)} %collective-permute-done.both_ref.far_ref, ...), custom_call_target="tpu_custom_call" | custom-call | flops 2550136832 | bytes 4980736 | tf_op jit(solution)/shard_map/pallas_call | solution.py:435
  20.1 0.5 %collective-permute-start.10 = (bf16[32,512]{1,0:T(8,128)(2,1)S(1)}, bf16[32,512]{1,0:T(8,128)(2,1)S(1)}, u32[]{:S(2)}, u32[]{:S(2)}) collective-permute-start(bf16[32,512]{1,0:T(8,128)(2,1)S(1)} %get-tuple-element.20), channel_id=1, source_target_pairs={{0,6},{1,7},{2,0},{3,1},{4,2},{5,3},{6,4},{7,5},{8,14},{9,15},{10,... | collective-permute-start | bytes 98312 | tf_op jit(solution)/shard_map/ppermute | solution.py:345
  20.6 1.6 %collective-permute-start.11 = (bf16[32,512]{1,0:T(8,128)(2,1)S(1)}, bf16[32,512]{1,0:T(8,128)(2,1)S(1)}, u32[]{:S(2)}, u32[]{:S(2)}) collective-permute-start(bf16[32,512]{1,0:T(8,128)(2,1)S(1)} %get-tuple-element.21), channel_id=1, source_target_pairs={{0,2},{1,3},{2,4},{3,5},{4,6},{5,7},{6,0},{7,1},{8,10},{9,11},{10,... | collective-permute-start | bytes 98312 | tf_op jit(solution)/shard_map/ppermute | solution.py:345
  22.1 0.3 %collective-permute-start.9 = (bf16[32,512]{1,0:T(8,128)(2,1)S(1)}, bf16[32,512]{1,0:T(8,128)(2,1)S(1)}, u32[]{:S(2)}, u32[]{:S(2)}) collective-permute-start(bf16[32,512]{1,0:T(8,128)(2,1)S(1)} %get-tuple-element.19), channel_id=1, source_target_pairs={{0,4},{1,5},{2,6},{3,7},{4,0},{5,1},{6,2},{7,3},{8,12},{9,13},{10,... | collective-permute-start | bytes 98312 | tf_op jit(solution)/shard_map/ppermute | solution.py:345
  22.5 0.0 collective-permute-done.7.refs_3_
  22.5 3.8 %shard_map.81.after_ref = bf16[32,512]{1,0:T(8,128)(2,1)} custom-call(bf16[2,32,512]{2,1,0:T(8,128)(2,1)S(1)} %get-tuple-element.12.both_ref, s32[1,512]{1,0:T(1,128)S(1)} %get-tuple-element.13.after_ref.class_ref, bf16[30,512,128]{2,1,0:T(8,128)(2,1)S(1)} %get-tuple-element.14.spread_ref, bf16[30,256,256]{2,1,0:T(8,128)(2,1)S(1)} %get-tuple-element.15.after_ref.mats_ref, ...), custom_call_target="tpu_custom_call" | custom-call | flops 2550136832 | bytes 4980736 | tf_op jit(solution)/shard_map/pallas_call | solution.py:452
  26.3 0.0 collective-permute-done.11.refs_2_
  26.3 1.0 %collective-permute-done.9.refs_0_ = bf16[32,512]{1,0:T(8,128)(2,1)S(1)} collective-permute-done((bf16[32,512]{1,0:T(8,128)(2,1)S(1)}, bf16[32,512]{1,0:T(8,128)(2,1)S(1)}, u32[]{:S(2)}, u32[]{:S(2)}) %collective-permute-start.9) | collective-permute-done | bytes 32800 | tf_op jit(solution)/shard_map/ppermute | solution.py:345
  27.3 0.6 %shard_map.83 = bf16[32,512]{1,0:T(8,128)(2,1)} custom-call(bf16[2,32,512]{2,1,0:T(8,128)(2,1)S(1)} %get-tuple-element.12.both_ref, f32[32,512]{1,0:T(8,128)S(1)} %get-tuple-element.18.keep_ref, bf16[32,512]{1,0:T(8,128)(2,1)} %shard_map.81.after_ref, bf16[32,512]{1,0:T(8,128)(2,1)S(1)} %collective-permute-done.9.refs_0_, ...), custom_call_target="tpu_custom_call" | custom-call | tf_op jit(solution)/shard_map/pallas_call | solution.py:465
  (7 shorter events, 0.0 us)
Async XLA Ops:
  1.6 10.1 %collective-permute-start.4 = (bf16[144,256]{1,0:T(8,128)(2,1)S(1)}, bf16[144,256]{1,0:T(8,128)(2,1)S(1)}, u32[]{:S(2)}, u32[]{:S(2)}) collective-permute-start(bf16[144,256]{1,0:T(8,128)(2,1)S(1)} %get-tuple-element.16.near_ref), channel_id=1, source_target_pairs={{0,8},{1,9},{2,10},{3,11},{4,12},{5,13},{6,14},{7,15},{8,0},{9,1},... | collective-permute-start | bytes 221192 | tf_op jit(solution)/shard_map/ppermute | solution.py:337
  2.1 9.6 %collective-permute-start.1 = (bf16[144,256]{1,0:T(8,128)(2,1)S(1)}, bf16[144,256]{1,0:T(8,128)(2,1)S(1)}, u32[]{:S(2)}, u32[]{:S(2)}) collective-permute-start(bf16[144,256]{1,0:T(8,128)(2,1)S(1)} %get-tuple-element.16.near_ref), channel_id=1, source_target_pairs={{0,25},{1,24},{2,27},{3,26},{4,29},{5,28},{6,31},{7,30},{8,17},{9,... | collective-permute-start | bytes 221192 | tf_op jit(solution)/shard_map/ppermute | solution.py:337
  5.7 6.0 %collective-permute-start.2 = (bf16[144,256]{1,0:T(8,128)(2,1)S(1)}, bf16[144,256]{1,0:T(8,128)(2,1)S(1)}, u32[]{:S(2)}, u32[]{:S(2)}) collective-permute-start(bf16[144,256]{1,0:T(8,128)(2,1)S(1)} %get-tuple-element.16.near_ref), channel_id=1, source_target_pairs={{0,9},{1,8},{2,11},{3,10},{4,13},{5,12},{6,15},{7,14},{8,1},{9,0},... | collective-permute-start | bytes 221192 | tf_op jit(solution)/shard_map/ppermute | solution.py:337
  5.9 5.8 %collective-permute-start.3 = (bf16[144,256]{1,0:T(8,128)(2,1)S(1)}, bf16[144,256]{1,0:T(8,128)(2,1)S(1)}, u32[]{:S(2)}, u32[]{:S(2)}) collective-permute-start(bf16[144,256]{1,0:T(8,128)(2,1)S(1)} %get-tuple-element.16.near_ref), channel_id=1, source_target_pairs={{0,24},{1,25},{2,26},{3,27},{4,28},{5,29},{6,30},{7,31},{8,16},{9,... | collective-permute-start | bytes 221192 | tf_op jit(solution)/shard_map/ppermute | solution.py:337
  6.0 5.7 %collective-permute-start = (bf16[2,32,512]{2,1,0:T(8,128)(2,1)S(1)}, bf16[2,32,512]{2,1,0:T(8,128)(2,1)S(1)}, u32[]{:S(2)}, u32[]{:S(2)}) collective-permute-start(bf16[2,32,512]{2,1,0:T(8,128)(2,1)S(1)} %get-tuple-element.12.both_ref), channel_id=1, source_target_pairs={{0,1},{1,0},{2,3},{3,2},{4,5},{5,4},{6,7},{7,6},{8,9},{9,8},{10,11... | collective-permute-start | bytes 196616 | tf_op jit(solution)/shard_map/ppermute | solution.py:337
  11.8 5.8 %collective-permute-start.8 = (bf16[4,144,256]{2,1,0:T(8,128)(2,1)S(1)}, bf16[4,144,256]{2,1,0:T(8,128)(2,1)S(1)}, u32[]{:S(2)}, u32[]{:S(2)}) collective-permute-start(bf16[4,144,256]{2,1,0:T(8,128)(2,1)S(1)} %shard_map.79.refs_0_.refs_4_), channel_id=1, source_target_pairs={{0,8},{1,9},{2,10},{3,11},{4,12},{5,13},{6,14},{7,15},{8,0},{9,1},... | collective-permute-start | bytes 884744 | tf_op jit(solution)/shard_map/ppermute | solution.py:337
  12.0 10.1 %collective-permute-start.5 = (bf16[272,128]{1,0:T(8,128)(2,1)S(1)}, bf16[272,128]{1,0:T(8,128)(2,1)S(1)}, u32[]{:S(2)}, u32[]{:S(2)}) collective-permute-start(bf16[272,128]{1,0:T(8,128)(2,1)S(1)} %shard_map.80.refs_0_.after_ref), channel_id=1, source_target_pairs={{0,2},{1,3},{2,4},{3,5},{4,6},{5,7},{6,0},{7,1},{8,10},{9,11},{10,... | collective-permute-start | bytes 208904 | tf_op jit(solution)/shard_map/ppermute | solution.py:345
  13.6 8.9 %collective-permute-start.6 = (bf16[272,128]{1,0:T(8,128)(2,1)S(1)}, bf16[272,128]{1,0:T(8,128)(2,1)S(1)}, u32[]{:S(2)}, u32[]{:S(2)}) collective-permute-start(bf16[272,128]{1,0:T(8,128)(2,1)S(1)} %shard_map.80.refs_0_.after_ref), channel_id=1, source_target_pairs={{0,4},{1,5},{2,6},{3,7},{4,0},{5,1},{6,2},{7,3},{8,12},{9,13},{10,... | collective-permute-start | bytes 208904 | tf_op jit(solution)/shard_map/ppermute | solution.py:345
  16.2 6.3 %collective-permute-start.7 = (bf16[272,128]{1,0:T(8,128)(2,1)S(1)}, bf16[272,128]{1,0:T(8,128)(2,1)S(1)}, u32[]{:S(2)}, u32[]{:S(2)}) collective-permute-start(bf16[272,128]{1,0:T(8,128)(2,1)S(1)} %shard_map.80.refs_0_.after_ref), channel_id=1, source_target_pairs={{0,6},{1,7},{2,0},{3,1},{4,2},{5,3},{6,4},{7,5},{8,14},{9,15},{10,... | collective-permute-start | bytes 208904 | tf_op jit(solution)/shard_map/ppermute | solution.py:345
  20.1 6.2 %collective-permute-start.10 = (bf16[32,512]{1,0:T(8,128)(2,1)S(1)}, bf16[32,512]{1,0:T(8,128)(2,1)S(1)}, u32[]{:S(2)}, u32[]{:S(2)}) collective-permute-start(bf16[32,512]{1,0:T(8,128)(2,1)S(1)} %get-tuple-element.20), channel_id=1, source_target_pairs={{0,6},{1,7},{2,0},{3,1},{4,2},{5,3},{6,4},{7,5},{8,14},{9,15},{10,... | collective-permute-start | bytes 98312 | tf_op jit(solution)/shard_map/ppermute | solution.py:345
  20.6 5.7 %collective-permute-start.11 = (bf16[32,512]{1,0:T(8,128)(2,1)S(1)}, bf16[32,512]{1,0:T(8,128)(2,1)S(1)}, u32[]{:S(2)}, u32[]{:S(2)}) collective-permute-start(bf16[32,512]{1,0:T(8,128)(2,1)S(1)} %get-tuple-element.21), channel_id=1, source_target_pairs={{0,2},{1,3},{2,4},{3,5},{4,6},{5,7},{6,0},{7,1},{8,10},{9,11},{10,... | collective-permute-start | bytes 98312 | tf_op jit(solution)/shard_map/ppermute | solution.py:345
  22.1 5.2 %collective-permute-start.9 = (bf16[32,512]{1,0:T(8,128)(2,1)S(1)}, bf16[32,512]{1,0:T(8,128)(2,1)S(1)}, u32[]{:S(2)}, u32[]{:S(2)}) collective-permute-start(bf16[32,512]{1,0:T(8,128)(2,1)S(1)} %get-tuple-element.19), channel_id=1, source_target_pairs={{0,4},{1,5},{2,6},{3,7},{4,0},{5,1},{6,2},{7,3},{8,12},{9,13},{10,... | collective-permute-start | bytes 98312 | tf_op jit(solution)/shard_map/ppermute | solution.py:345

commit v10 on v9

--- a/solution.py
+++ b/solution.py
@@ -45,7 +45,7 @@
 
 
 def pack_kernel(
-    t_any, f_any, a_any, class_any, near_ref, both_ref, class_ref, t_ref, sems
+    t_any, f_any, a_any, class_any, near_ref, both_ref, sent_ref, class_ref, t_ref, sems
 ):
     copies = [
         pltpu.make_async_copy(source, target, sems.at[at])
@@ -82,6 +82,9 @@
     for part in range(depth // EDGE):
         start = part * (rows // parts) if part < parts else 0
         near_ref[mats:base, part * EDGE : (part + 1) * EDGE] = edge[start : start + base - mats, :]
+    sent_ref[:rows, :] = fields
+    sent_ref[rows : 2 * rows, :] = adjoints
+    sent_ref[2 * rows :, :] = jnp.zeros_like(sent_ref[2 * rows :, :])
 
 
 def relay_kernel(cross_ref, far_ref, top_ref, both_ref, beside_ref, near_ref, after_ref, out_ref):
@@ -127,7 +130,7 @@
     (near, across), (out_ref, halos) = find_pieces(spots, refs[:-2]), refs[-2:]
     unused, rows, width = both_ref.shape
     mats = count * rows
-    for start, source, pieces in ((place[1], both_ref[0], near), (1 - place[1], far_ref[0], across)):
+    for start, source, pieces in ((place[1], both_ref[0], near), (1 - place[1], far_ref[:rows, :], across)):
         start = pl.multiple_of(start * rows, rows)
         for part in range(width // EDGE):
             lanes = slice(part * EDGE, (part + 1) * EDGE)
@@ -254,7 +257,7 @@
     halos = [pick_halo(place, pieces, mats, rows) for pieces in (near, across)]
     padded = [
         jnp.concatenate([own, join_halo(halo, A_SHIFT).astype(BF16)], axis=1)
-        for own, halo in ((both_ref[1], halos[0]), (far_ref[1], halos[1]))
+        for own, halo in ((both_ref[1], halos[0]), (far_ref[rows : 2 * rows, :], halos[1]))
     ]
     class_halo = join_halo(tuple(cells[0:8, :] for cells in halos[0]), C_SHIFT)
     labels = jnp.concatenate([class_ref[...], class_halo[0:1, :].astype(jnp.int32)], axis=1)
@@ -277,7 +280,7 @@
     total_ref[...] = couple_own(upright, spread_ref, own_ref, products).T
 
     def block(rel):
-        start = (((place[2] + rel) & (sends - 1)) * 2 + place[1]) * rows
+        start = ((place[2] ^ rel) * 2 + place[1]) * rows
         moved = start - EDGE + jnp.where(place[1] == 1, -rows, rows)
         return pl.ds(pl.multiple_of(jnp.where(start < EDGE, start, moved), rows), rows)
 
@@ -296,7 +299,7 @@
     mats = count * rows
     block = 2 * rows
     for rel, piece_ref in zip(rels, pieces):
-        start = pl.multiple_of(((place[2] - rel) & (len(rels) - 1)) * block, block)
+        start = pl.multiple_of((place[2] ^ rel) * block, block)
         unpack_fields(piece_ref, padded, start, block)
     stand_up(padded[...], upright)
     coupled = couple_slots(upright, spread_ref, mats_ref, range(SLOTS)).astype(BF16)
@@ -315,12 +318,13 @@
     out_ref[...] = (both_ref[0].astype(F32) - applied).astype(BF16)
 
 
-def finish_kernel(both_ref, keep_ref, after_ref, *refs):
-    arrived, out_ref = refs[:-1], refs[-1]
+def finish_kernel(both_ref, keep_ref, forward_ref, *refs):
+    arrived, (out_ref, adjoint_ref) = refs[:-2], refs[-2:]
+    out_ref[...] = forward_ref[...]
     returned = keep_ref[...]
     for ref in arrived:
         returned = returned + ref[...].astype(F32)
-    out_ref[...] = (both_ref[1].astype(F32) - returned).astype(BF16)
+    adjoint_ref[...] = (both_ref[1].astype(F32) - returned).astype(BF16)
 
 
 def local(fields, adjoints, couple, tmatrices, neighbours, classes):
@@ -336,27 +340,20 @@
         ]
         return lax.ppermute(cells, ("tiles", "coef"), pairs)
 
-    def shift(cells, rel):
-        pairs = [
-            (i * coefs + j, i * coefs + (j + 2 * rel) % coefs)
-            for i in range(tiles)
-            for j in range(coefs)
-        ]
-        return lax.ppermute(cells, ("tiles", "coef"), pairs)
-
     labels = classes.reshape(1, width)
     mats = count * rows
     near_rows = mats + rows // edge_parts(rows)
     total_rows = couple.shape[1]
-    near_own, both, labels = pl.pallas_call(
+    near_own, both, sent_far, labels = pl.pallas_call(
         pack_kernel,
         out_shape=(
             jax.ShapeDtypeStruct((near_rows, depth), BF16),
             jax.ShapeDtypeStruct((2, rows, width), BF16),
+            jax.ShapeDtypeStruct((2 * rows + LEAD, width), BF16),
             jax.ShapeDtypeStruct(labels.shape, jnp.int32),
         ),
         in_specs=[HBM] * 4,
-        out_specs=(VMEM,) * 3,
+        out_specs=(VMEM,) * 4,
         scratch_shapes=[pltpu.VMEM(tmatrices.shape, BF16), pltpu.SemaphoreType.DMA((4,))],
         compiler_params=PARAMS,
     )(*[in_hbm(cells) for cells in (tmatrices, fields, adjoints, labels)])
@@ -379,7 +376,7 @@
     )(in_hbm(couple), in_hbm(neighbours.T), labels)
 
     top = tiles // 2
-    both_far = swap(both, 0, 1)
+    both_far = swap(sent_far, 0, 1)
     beside = swap(near_own, 1, 0)
     first = pl.pallas_call(
         relay_kernel,
@@ -424,8 +421,8 @@
     groups = coefs // 2
     gathered = {0: padded_fields}
     for rel in range(1, groups):
-        gathered[rel] = shift(padded_fields, rel)
-    rels = [0, 1, 2, 3] if groups == 4 else sorted(gathered)
+        gathered[rel] = swap(padded_fields, 0, 2 * rel)
+    rels = [0, 1, 3, 2] if groups == 4 else sorted(gathered)
 
 
     def work(slots):
@@ -447,9 +444,9 @@
         cost_estimate=work(SLOTS + 8),
         compiler_params=PARAMS,
     )(both, both_far, labels, spread, mats_own, padded_fields, *held)
-    arrived = [shift(block, rel) for rel, block in enumerate(sent, 1)]
-
-    forward_out = pl.pallas_call(
+    arrived = [swap(block, 0, 2 * rel) for rel, block in enumerate(sent, 1)]
+
+    forward = pl.pallas_call(
         functools.partial(forward_kernel, spots, count, rels),
         out_shape=jax.ShapeDtypeStruct((rows, width), BF16),
         in_specs=[VMEM] * (4 + len(rels) + len(held)),
@@ -462,14 +459,13 @@
         cost_estimate=work(SLOTS + 8),
         compiler_params=PARAMS,
     )(both, labels, spread, mats_held, *[gathered[rel] for rel in rels], *held)
-    adjoint_out = pl.pallas_call(
+    return pl.pallas_call(
         finish_kernel,
-        out_shape=jax.ShapeDtypeStruct((rows, width), BF16),
-        in_specs=[VMEM] * 2 + [HBM] + [VMEM] * len(arrived),
-        out_specs=VMEM,
-        compiler_params=PARAMS,
-    )(both, keep, in_hbm(forward_out), *[arrived[k - 1] for k in ((2, 3, 1) if groups == 4 else range(1, groups))])
-    return (forward_out, adjoint_out)
+        out_shape=(jax.ShapeDtypeStruct((rows, width), BF16),) * 2,
+        in_specs=[VMEM] * (3 + len(arrived)),
+        out_specs=(VMEM, VMEM),
+        compiler_params=PARAMS,
+    )(both, keep, forward, *[arrived[k - 1] for k in ((3, 2, 1) if groups == 4 else range(1, groups))])
 
 
 def solution(mesh):

time: 28.1 us -> 27.6 us (0.982)
  Pallas kernels: 11.2 us -> 10.5 us
  starting transfers between devices: 14.3 us -> 15 us
  waiting for transfers between devices: 1.77 us -> 1.16 us
    ppermute x6 -> x12, starting transfers between devices: 6.41 us -> 15 us  [swap(): return lax.ppermute(cells, ('tiles', 'coef'), pairs)]
    ppermute x6 -> x0, starting transfers between devices: 7.93 us -> none  [shift(): return lax.ppermute(cells, ('tiles', 'coef'), pairs)]
    ppermute x6 -> x0, waiting for transfers between devices: 1.06 us -> none  [shift(): return lax.ppermute(cells, ('tiles', 'coef'), pairs)]
    pallas_call x1, Pallas kernels: 3.77 us -> 3.15 us  [local(): pl.pallas_call(functools.partial(forward_kernel, spots, count, rels), out...]
    ppermute x6 -> x12, waiting for transfers between devices: 0.71 us -> 1.16 us  [swap(): return lax.ppermute(cells, ('tiles', 'coef'), pairs)]
  transfers between devices with their start and end apart: 12 -> 12, of which waited for: 2 -> 3; matrix products, arithmetic and copies ran while one was open for 0% -> 0% of each run, Pallas kernels for 34% -> 32%
where the time goes in v10:
time: 27.6 us; the launch traced here: 27.4 us
  starting transfers between devices  15 us (54%)
  Pallas kernels  10.5 us (38%)
  waiting for transfers between devices  1.16 us (4%)
  between operations  0.7 us (3%)
    ppermute x12, starting transfers between devices, swap(): return lax.ppermute(cells, ('tiles', 'coef'), pairs)  15 us
    pallas_call x1, Pallas kernels, local(): pl.pallas_call(functools.partial(forward_kernel, spots, count, rels), out...  3.15 us
    pallas_call x1, Pallas kernels, local(): pl.pallas_call(functools.partial(prepare_kernel, rows), out_shape=(jax.Sh...  3.05 us
    pallas_call x1, Pallas kernels, local(): pl.pallas_call(functools.partial(adjoint_kernel, spots, count, groups), o...  2.53 us
    ppermute x12, waiting for transfers between devices, swap(): return lax.ppermute(cells, ('tiles', 'coef'), pairs)  1.16 us
    pallas_call x1, Pallas kernels, local(): pl.pallas_call(pack_kernel, out_shape=(jax.ShapeDtypeStruct((near_rows, d...  0.96 us
    pallas_call x1, Pallas kernels, local(): pl.pallas_call(finish_kernel, out_shape=(jax.ShapeDtypeStruct((rows, widt...  0.64 us
  transfers between devices with their start and end apart: 12, of which 3 were waited for; matrix products, arithmetic and copies ran while one was open for 0% of the time, Pallas kernels for 32%

profile of v10, /device:TPU:0, one launch (start us, length us, event | category | flops | bytes accessed | tf_op | source)
XLA Modules:
  0.0 27.4 jit_solution(17030608742942684220)
XLA Ops:
  0.6 1.0 %shard_map.77 = (bf16[144,256]{1,0:T(8,128)(2,1)S(1)}, bf16[2,32,512]{2,1,0:T(8,128)(2,1)S(1)}, bf16[80,512]{1,0:T(8,128)(2,1)S(1)}, s32[1,512]{1,0:T(1,128)S(1)}) custom-call(bf16[4,32,256]{2,1,0:T(8,128)(2,1)} %t_any.1, bf16[32,512]{1,0:T(8,128)(2,1)} %f_any.1, bf16[32,512]{1,0:T(8,128)(2,1)} %a_any.1, s32[1,512]{1,0:T(1,128)} %bitcast.5), custom_call_target="tpu_custom_call" | custom-call | tf_op jit(solution)/shard_map/pallas_call | solution.py:347
  1.6 3.0 %collective-permute-start = (bf16[80,512]{1,0:T(8,128)(2,1)S(1)}, bf16[80,512]{1,0:T(8,128)(2,1)S(1)}, u32[]{:S(2)}, u32[]{:S(2)}) collective-permute-start(bf16[80,512]{1,0:T(8,128)(2,1)S(1)} %get-tuple-element.14), channel_id=1, source_target_pairs={{0,1},{1,0},{2,3},{3,2},{4,5},{5,4},{6,7},{7,6},{8,9},{9,8},{10,11... | collective-permute-start | bytes 245768 | tf_op jit(solution)/shard_map/ppermute | solution.py:341
  4.6 0.7 %collective-permute-start.1 = (bf16[144,256]{1,0:T(8,128)(2,1)S(1)}, bf16[144,256]{1,0:T(8,128)(2,1)S(1)}, u32[]{:S(2)}, u32[]{:S(2)}) collective-permute-start(bf16[144,256]{1,0:T(8,128)(2,1)S(1)} %get-tuple-element.18.near_ref), channel_id=1, source_target_pairs={{0,25},{1,24},{2,27},{3,26},{4,29},{5,28},{6,31},{7,30},{8,17},{9,... | collective-permute-start | bytes 221192 | tf_op jit(solution)/shard_map/ppermute | solution.py:341
  5.3 2.1 %collective-permute-start.2 = (bf16[144,256]{1,0:T(8,128)(2,1)S(1)}, bf16[144,256]{1,0:T(8,128)(2,1)S(1)}, u32[]{:S(2)}, u32[]{:S(2)}) collective-permute-start(bf16[144,256]{1,0:T(8,128)(2,1)S(1)} %get-tuple-element.18.near_ref), channel_id=1, source_target_pairs={{0,9},{1,8},{2,11},{3,10},{4,13},{5,12},{6,15},{7,14},{8,1},{9,0},... | collective-permute-start | bytes 221192 | tf_op jit(solution)/shard_map/ppermute | solution.py:341
  7.3 0.0 collective-permute-start.3
  7.3 0.6 %collective-permute-start.4 = (bf16[144,256]{1,0:T(8,128)(2,1)S(1)}, bf16[144,256]{1,0:T(8,128)(2,1)S(1)}, u32[]{:S(2)}, u32[]{:S(2)}) collective-permute-start(bf16[144,256]{1,0:T(8,128)(2,1)S(1)} %get-tuple-element.18.near_ref), channel_id=1, source_target_pairs={{0,8},{1,9},{2,10},{3,11},{4,12},{5,13},{6,14},{7,15},{8,0},{9,1},... | collective-permute-start | bytes 221192 | tf_op jit(solution)/shard_map/ppermute | solution.py:341
  7.9 3.0 %shard_map.78 = (bf16[30,256,256]{2,1,0:T(8,128)(2,1)S(1)}, bf16[15,256,256]{2,1,0:T(8,128)(2,1)S(1)}, bf16[30,512,128]{2,1,0:T(8,128)(2,1)S(1)}) custom-call(bf16[30,256,256]{2,1,0:T(8,128)(2,1)} %couple_ref.1, s32[30,512]{1,0:T(8,128)} %bitcast.4, s32[1,512]{1,0:T(1,128)S(1)} %get-tuple-element.15.after_ref.class_ref), custom_call_target="tpu_custom_call" | custom-call | bytes 7864320 | tf_op jit(solution)/shard_map/pallas_call | solution.py:360
  11.0 0.4 %collective-permute-done.2.far_ref = bf16[144,256]{1,0:T(8,128)(2,1)S(1)} collective-permute-done((bf16[144,256]{1,0:T(8,128)(2,1)S(1)}, bf16[144,256]{1,0:T(8,128)(2,1)S(1)}, u32[]{:S(2)}, u32[]{:S(2)}) %collective-permute-start.2) | collective-permute-done | bytes 73760 | tf_op jit(solution)/shard_map/ppermute | solution.py:341
  11.4 0.2 collective-permute-done.3.top_ref
  11.7 0.0 collective-permute-done.4.beside_ref
  11.7 0.0 collective-permute-done.both_ref.far_ref
  11.7 0.1 collective-permute-start.5
  11.8 0.2 shard_map.80.after_ref.refs_0_
  12.0 1.6 %collective-permute-start.6 = (bf16[272,128]{1,0:T(8,128)(2,1)S(1)}, bf16[272,128]{1,0:T(8,128)(2,1)S(1)}, u32[]{:S(2)}, u32[]{:S(2)}) collective-permute-start(bf16[272,128]{1,0:T(8,128)(2,1)S(1)} %shard_map.80.after_ref.refs_0_), channel_id=1, source_target_pairs={{0,2},{1,3},{2,0},{3,1},{4,6},{5,7},{6,4},{7,5},{8,10},{9,11},{10,... | collective-permute-start | bytes 208904 | tf_op jit(solution)/shard_map/ppermute | solution.py:341
  13.5 2.5 %collective-permute-start.7 = (bf16[272,128]{1,0:T(8,128)(2,1)S(1)}, bf16[272,128]{1,0:T(8,128)(2,1)S(1)}, u32[]{:S(2)}, u32[]{:S(2)}) collective-permute-start(bf16[272,128]{1,0:T(8,128)(2,1)S(1)} %shard_map.80.after_ref.refs_0_), channel_id=1, source_target_pairs={{0,6},{1,7},{2,4},{3,5},{4,2},{5,3},{6,0},{7,1},{8,14},{9,15},{10,... | collective-permute-start | bytes 208904 | tf_op jit(solution)/shard_map/ppermute | solution.py:341
  16.0 0.1 collective-permute-start.8
  16.1 2.5 %shard_map.81 = (f32[32,512]{1,0:T(8,128)S(1)}, bf16[32,512]{1,0:T(8,128)(2,1)S(1)}, bf16[32,512]{1,0:T(8,128)(2,1)S(1)}, bf16[32,512]{1,0:T(8,128)(2,1)S(1)}) custom-call(bf16[2,32,512]{2,1,0:T(8,128)(2,1)S(1)} %get-tuple-element.13.both_ref, bf16[80,512]{1,0:T(8,128)(2,1)S(1)} %collective-permute-done.both_ref.far_ref, ...), custom_call_target="tpu_custom_call" | custom-call | flops 2550136832 | bytes 4980736 | tf_op jit(solution)/shard_map/pallas_call | solution.py:432
  18.7 3.0 %collective-permute-start.9 = (bf16[32,512]{1,0:T(8,128)(2,1)S(1)}, bf16[32,512]{1,0:T(8,128)(2,1)S(1)}, u32[]{:S(2)}, u32[]{:S(2)}) collective-permute-start(bf16[32,512]{1,0:T(8,128)(2,1)S(1)} %get-tuple-element.21), channel_id=1, source_target_pairs={{0,6},{1,7},{2,4},{3,5},{4,2},{5,3},{6,0},{7,1},{8,14},{9,15},{10,... | collective-permute-start | bytes 98312 | tf_op jit(solution)/shard_map/ppermute | solution.py:341
  21.7 0.3 %collective-permute-start.10 = (bf16[32,512]{1,0:T(8,128)(2,1)S(1)}, bf16[32,512]{1,0:T(8,128)(2,1)S(1)}, u32[]{:S(2)}, u32[]{:S(2)}) collective-permute-start(bf16[32,512]{1,0:T(8,128)(2,1)S(1)} %get-tuple-element.22), channel_id=1, source_target_pairs={{0,4},{1,5},{2,6},{3,7},{4,0},{5,1},{6,2},{7,3},{8,12},{9,13},{10,... | collective-permute-start | bytes 98312 | tf_op jit(solution)/shard_map/ppermute | solution.py:341
  22.0 1.1 %collective-permute-start.11 = (bf16[32,512]{1,0:T(8,128)(2,1)S(1)}, bf16[32,512]{1,0:T(8,128)(2,1)S(1)}, u32[]{:S(2)}, u32[]{:S(2)}) collective-permute-start(bf16[32,512]{1,0:T(8,128)(2,1)S(1)} %get-tuple-element.23), channel_id=1, source_target_pairs={{0,2},{1,3},{2,0},{3,1},{4,6},{5,7},{6,4},{7,5},{8,10},{9,11},{10,... | collective-permute-start | bytes 98312 | tf_op jit(solution)/shard_map/ppermute | solution.py:341
  23.1 3.1 %shard_map.82.forward_ref = bf16[32,512]{1,0:T(8,128)(2,1)S(1)} custom-call(bf16[2,32,512]{2,1,0:T(8,128)(2,1)S(1)} %get-tuple-element.13.both_ref, s32[1,512]{1,0:T(1,128)S(1)} %get-tuple-element.15.after_ref.class_ref, bf16[30,512,128]{2,1,0:T(8,128)(2,1)S(1)} %get-tuple-element.16.spread_ref, ...), custom_call_target="tpu_custom_call" | custom-call | flops 2550136832 | bytes 4980736 | tf_op jit(solution)/shard_map/pallas_call | solution.py:449
  26.3 0.0 collective-permute-done.9.refs_0_
  26.3 0.5 %collective-permute-done.10.refs_1_ = bf16[32,512]{1,0:T(8,128)(2,1)S(1)} collective-permute-done((bf16[32,512]{1,0:T(8,128)(2,1)S(1)}, bf16[32,512]{1,0:T(8,128)(2,1)S(1)}, u32[]{:S(2)}, u32[]{:S(2)}) %collective-permute-start.10) | collective-permute-done | bytes 32800 | tf_op jit(solution)/shard_map/ppermute | solution.py:341
  26.8 0.6 %shard_map.83 = (bf16[32,512]{1,0:T(8,128)(2,1)}, bf16[32,512]{1,0:T(8,128)(2,1)}) custom-call(bf16[2,32,512]{2,1,0:T(8,128)(2,1)S(1)} %get-tuple-element.13.both_ref, f32[32,512]{1,0:T(8,128)S(1)} %get-tuple-element.20.keep_ref, bf16[32,512]{1,0:T(8,128)(2,1)S(1)} %shard_map.82.forward_ref, bf16[32,512]{1,0:T(8,128)(2,1)S(1)} %collective-permute-done.9.refs_0_, ...), custom_call_target="tpu_custom_call" | custom-call | tf_op jit(solution)/shard_map/pallas_call | solution.py:462
  (7 shorter events, 0.0 us)
Async XLA Ops:
  1.6 10.1 %collective-permute-start = (bf16[80,512]{1,0:T(8,128)(2,1)S(1)}, bf16[80,512]{1,0:T(8,128)(2,1)S(1)}, u32[]{:S(2)}, u32[]{:S(2)}) collective-permute-start(bf16[80,512]{1,0:T(8,128)(2,1)S(1)} %get-tuple-element.14), channel_id=1, source_target_pairs={{0,1},{1,0},{2,3},{3,2},{4,5},{5,4},{6,7},{7,6},{8,9},{9,8},{10,11... | collective-permute-start | bytes 245768 | tf_op jit(solution)/shard_map/ppermute | solution.py:341
  4.6 6.4 %collective-permute-start.1 = (bf16[144,256]{1,0:T(8,128)(2,1)S(1)}, bf16[144,256]{1,0:T(8,128)(2,1)S(1)}, u32[]{:S(2)}, u32[]{:S(2)}) collective-permute-start(bf16[144,256]{1,0:T(8,128)(2,1)S(1)} %get-tuple-element.18.near_ref), channel_id=1, source_target_pairs={{0,25},{1,24},{2,27},{3,26},{4,29},{5,28},{6,31},{7,30},{8,17},{9,... | collective-permute-start | bytes 221192 | tf_op jit(solution)/shard_map/ppermute | solution.py:341
  5.3 6.2 %collective-permute-start.2 = (bf16[144,256]{1,0:T(8,128)(2,1)S(1)}, bf16[144,256]{1,0:T(8,128)(2,1)S(1)}, u32[]{:S(2)}, u32[]{:S(2)}) collective-permute-start(bf16[144,256]{1,0:T(8,128)(2,1)S(1)} %get-tuple-element.18.near_ref), channel_id=1, source_target_pairs={{0,9},{1,8},{2,11},{3,10},{4,13},{5,12},{6,15},{7,14},{8,1},{9,0},... | collective-permute-start | bytes 221192 | tf_op jit(solution)/shard_map/ppermute | solution.py:341
  7.3 4.4 %collective-permute-start.3 = (bf16[144,256]{1,0:T(8,128)(2,1)S(1)}, bf16[144,256]{1,0:T(8,128)(2,1)S(1)}, u32[]{:S(2)}, u32[]{:S(2)}) collective-permute-start(bf16[144,256]{1,0:T(8,128)(2,1)S(1)} %get-tuple-element.18.near_ref), channel_id=1, source_target_pairs={{0,24},{1,25},{2,26},{3,27},{4,28},{5,29},{6,30},{7,31},{8,16},{9,... | collective-permute-start | bytes 221192 | tf_op jit(solution)/shard_map/ppermute | solution.py:341
  7.3 4.4 %collective-permute-start.4 = (bf16[144,256]{1,0:T(8,128)(2,1)S(1)}, bf16[144,256]{1,0:T(8,128)(2,1)S(1)}, u32[]{:S(2)}, u32[]{:S(2)}) collective-permute-start(bf16[144,256]{1,0:T(8,128)(2,1)S(1)} %get-tuple-element.18.near_ref), channel_id=1, source_target_pairs={{0,8},{1,9},{2,10},{3,11},{4,12},{5,13},{6,14},{7,15},{8,0},{9,1},... | collective-permute-start | bytes 221192 | tf_op jit(solution)/shard_map/ppermute | solution.py:341
  11.7 4.4 %collective-permute-start.5 = (bf16[4,144,256]{2,1,0:T(8,128)(2,1)S(1)}, bf16[4,144,256]{2,1,0:T(8,128)(2,1)S(1)}, u32[]{:S(2)}, u32[]{:S(2)}) collective-permute-start(bf16[4,144,256]{2,1,0:T(8,128)(2,1)S(1)} %shard_map.79.refs_0_.refs_4_), channel_id=1, source_target_pairs={{0,8},{1,9},{2,10},{3,11},{4,12},{5,13},{6,14},{7,15},{8,0},{9,1},... | collective-permute-start | bytes 884744 | tf_op jit(solution)/shard_map/ppermute | solution.py:341
  12.0 10.0 %collective-permute-start.6 = (bf16[272,128]{1,0:T(8,128)(2,1)S(1)}, bf16[272,128]{1,0:T(8,128)(2,1)S(1)}, u32[]{:S(2)}, u32[]{:S(2)}) collective-permute-start(bf16[272,128]{1,0:T(8,128)(2,1)S(1)} %shard_map.80.after_ref.refs_0_), channel_id=1, source_target_pairs={{0,2},{1,3},{2,0},{3,1},{4,6},{5,7},{6,4},{7,5},{8,10},{9,11},{10,... | collective-permute-start | bytes 208904 | tf_op jit(solution)/shard_map/ppermute | solution.py:341
  13.5 9.6 %collective-permute-start.7 = (bf16[272,128]{1,0:T(8,128)(2,1)S(1)}, bf16[272,128]{1,0:T(8,128)(2,1)S(1)}, u32[]{:S(2)}, u32[]{:S(2)}) collective-permute-start(bf16[272,128]{1,0:T(8,128)(2,1)S(1)} %shard_map.80.after_ref.refs_0_), channel_id=1, source_target_pairs={{0,6},{1,7},{2,4},{3,5},{4,2},{5,3},{6,0},{7,1},{8,14},{9,15},{10,... | collective-permute-start | bytes 208904 | tf_op jit(solution)/shard_map/ppermute | solution.py:341
  16.0 7.1 %collective-permute-start.8 = (bf16[272,128]{1,0:T(8,128)(2,1)S(1)}, bf16[272,128]{1,0:T(8,128)(2,1)S(1)}, u32[]{:S(2)}, u32[]{:S(2)}) collective-permute-start(bf16[272,128]{1,0:T(8,128)(2,1)S(1)} %shard_map.80.after_ref.refs_0_), channel_id=1, source_target_pairs={{0,4},{1,5},{2,6},{3,7},{4,0},{5,1},{6,2},{7,3},{8,12},{9,13},{10,... | collective-permute-start | bytes 208904 | tf_op jit(solution)/shard_map/ppermute | solution.py:341
  18.7 7.6 %collective-permute-start.9 = (bf16[32,512]{1,0:T(8,128)(2,1)S(1)}, bf16[32,512]{1,0:T(8,128)(2,1)S(1)}, u32[]{:S(2)}, u32[]{:S(2)}) collective-permute-start(bf16[32,512]{1,0:T(8,128)(2,1)S(1)} %get-tuple-element.21), channel_id=1, source_target_pairs={{0,6},{1,7},{2,4},{3,5},{4,2},{5,3},{6,0},{7,1},{8,14},{9,15},{10,... | collective-permute-start | bytes 98312 | tf_op jit(solution)/shard_map/ppermute | solution.py:341
  21.7 5.1 %collective-permute-start.10 = (bf16[32,512]{1,0:T(8,128)(2,1)S(1)}, bf16[32,512]{1,0:T(8,128)(2,1)S(1)}, u32[]{:S(2)}, u32[]{:S(2)}) collective-permute-start(bf16[32,512]{1,0:T(8,128)(2,1)S(1)} %get-tuple-element.22), channel_id=1, source_target_pairs={{0,4},{1,5},{2,6},{3,7},{4,0},{5,1},{6,2},{7,3},{8,12},{9,13},{10,... | collective-permute-start | bytes 98312 | tf_op jit(solution)/shard_map/ppermute | solution.py:341
  22.0 4.8 %collective-permute-start.11 = (bf16[32,512]{1,0:T(8,128)(2,1)S(1)}, bf16[32,512]{1,0:T(8,128)(2,1)S(1)}, u32[]{:S(2)}, u32[]{:S(2)}) collective-permute-start(bf16[32,512]{1,0:T(8,128)(2,1)S(1)} %get-tuple-element.23), channel_id=1, source_target_pairs={{0,2},{1,3},{2,0},{3,1},{4,6},{5,7},{6,4},{7,5},{8,10},{9,11},{10,... | collective-permute-start | bytes 98312 | tf_op jit(solution)/shard_map/ppermute | solution.py:341

commit v11 on v10

--- a/solution.py
+++ b/solution.py
@@ -87,7 +87,7 @@
     sent_ref[2 * rows :, :] = jnp.zeros_like(sent_ref[2 * rows :, :])
 
 
-def relay_kernel(cross_ref, far_ref, top_ref, both_ref, beside_ref, near_ref, after_ref, out_ref):
+def relay_kernel(cross_ref, top_ref, far_ref, both_ref, beside_ref, near_ref, after_ref, out_ref):
     out_ref[0] = near_ref[...]
     out_ref[1] = top_ref[...]
     out_ref[2] = far_ref[...]
@@ -386,8 +386,8 @@
         compiler_params=PARAMS,
     )(
         swap(near_own, top ^ 1, 1),
+        swap(near_own, top ^ 1, 0),
         swap(near_own, 1, 1),
-        swap(near_own, top ^ 1, 0),
         both_far,
         beside,
         near_own,

time: 27.6 us -> 27.4 us (level)
  transfers between devices with their start and end apart: 12 -> 12, of which waited for: 3 -> 2; matrix products, arithmetic and copies ran while one was open for 0% -> 0% of each run, Pallas kernels for 32% -> 33%
where the time goes in v11:
time: 27.4 us; the launch traced here: 27.2 us
  starting transfers between devices  15.1 us (55%)
  Pallas kernels  10.5 us (38%)
  waiting for transfers between devices  0.96 us (4%)
  between operations  0.69 us (3%)
    ppermute x12, starting transfers between devices, swap(): return lax.ppermute(cells, ('tiles', 'coef'), pairs)  15.1 us
    pallas_call x1, Pallas kernels, local(): pl.pallas_call(functools.partial(forward_kernel, spots, count, rels), out...  3.15 us
    pallas_call x1, Pallas kernels, local(): pl.pallas_call(functools.partial(prepare_kernel, rows), out_shape=(jax.Sh...  3.05 us
    pallas_call x1, Pallas kernels, local(): pl.pallas_call(functools.partial(adjoint_kernel, spots, count, groups), o...  2.54 us
    pallas_call x1, Pallas kernels, local(): pl.pallas_call(pack_kernel, out_shape=(jax.ShapeDtypeStruct((near_rows, d...  0.96 us
    ppermute x12, waiting for transfers between devices, swap(): return lax.ppermute(cells, ('tiles', 'coef'), pairs)  0.96 us
    pallas_call x1, Pallas kernels, local(): pl.pallas_call(finish_kernel, out_shape=(jax.ShapeDtypeStruct((rows, widt...  0.64 us
  transfers between devices with their start and end apart: 12, of which 2 were waited for; matrix products, arithmetic and copies ran while one was open for 0% of the time, Pallas kernels for 33%

profile of v11, /device:TPU:0, one launch (start us, length us, event | category | flops | bytes accessed | tf_op | source)
XLA Modules:
  0.0 27.2 jit_solution(6085846947785060031)
XLA Ops:
  0.6 1.0 %shard_map.77 = (bf16[144,256]{1,0:T(8,128)(2,1)S(1)}, bf16[2,32,512]{2,1,0:T(8,128)(2,1)S(1)}, bf16[80,512]{1,0:T(8,128)(2,1)S(1)}, s32[1,512]{1,0:T(1,128)S(1)}) custom-call(bf16[4,32,256]{2,1,0:T(8,128)(2,1)} %t_any.1, bf16[32,512]{1,0:T(8,128)(2,1)} %f_any.1, bf16[32,512]{1,0:T(8,128)(2,1)} %a_any.1, s32[1,512]{1,0:T(1,128)} %bitcast.5), custom_call_target="tpu_custom_call" | custom-call | tf_op jit(solution)/shard_map/pallas_call | solution.py:347
  1.6 3.0 %collective-permute-start = (bf16[80,512]{1,0:T(8,128)(2,1)S(1)}, bf16[80,512]{1,0:T(8,128)(2,1)S(1)}, u32[]{:S(2)}, u32[]{:S(2)}) collective-permute-start(bf16[80,512]{1,0:T(8,128)(2,1)S(1)} %get-tuple-element.14), channel_id=1, source_target_pairs={{0,1},{1,0},{2,3},{3,2},{4,5},{5,4},{6,7},{7,6},{8,9},{9,8},{10,11... | collective-permute-start | bytes 245768 | tf_op jit(solution)/shard_map/ppermute | solution.py:341
  4.6 0.7 %collective-permute-start.1 = (bf16[144,256]{1,0:T(8,128)(2,1)S(1)}, bf16[144,256]{1,0:T(8,128)(2,1)S(1)}, u32[]{:S(2)}, u32[]{:S(2)}) collective-permute-start(bf16[144,256]{1,0:T(8,128)(2,1)S(1)} %get-tuple-element.18.near_ref), channel_id=1, source_target_pairs={{0,25},{1,24},{2,27},{3,26},{4,29},{5,28},{6,31},{7,30},{8,17},{9,... | collective-permute-start | bytes 221192 | tf_op jit(solution)/shard_map/ppermute | solution.py:341
  5.3 0.6 %collective-permute-start.2 = (bf16[144,256]{1,0:T(8,128)(2,1)S(1)}, bf16[144,256]{1,0:T(8,128)(2,1)S(1)}, u32[]{:S(2)}, u32[]{:S(2)}) collective-permute-start(bf16[144,256]{1,0:T(8,128)(2,1)S(1)} %get-tuple-element.18.near_ref), channel_id=1, source_target_pairs={{0,24},{1,25},{2,26},{3,27},{4,28},{5,29},{6,30},{7,31},{8,16},{9,... | collective-permute-start | bytes 221192 | tf_op jit(solution)/shard_map/ppermute | solution.py:341
  5.9 1.4 %collective-permute-start.3 = (bf16[144,256]{1,0:T(8,128)(2,1)S(1)}, bf16[144,256]{1,0:T(8,128)(2,1)S(1)}, u32[]{:S(2)}, u32[]{:S(2)}) collective-permute-start(bf16[144,256]{1,0:T(8,128)(2,1)S(1)} %get-tuple-element.18.near_ref), channel_id=1, source_target_pairs={{0,9},{1,8},{2,11},{3,10},{4,13},{5,12},{6,15},{7,14},{8,1},{9,0},... | collective-permute-start | bytes 221192 | tf_op jit(solution)/shard_map/ppermute | solution.py:341
  7.3 0.6 %collective-permute-start.4 = (bf16[144,256]{1,0:T(8,128)(2,1)S(1)}, bf16[144,256]{1,0:T(8,128)(2,1)S(1)}, u32[]{:S(2)}, u32[]{:S(2)}) collective-permute-start(bf16[144,256]{1,0:T(8,128)(2,1)S(1)} %get-tuple-element.18.near_ref), channel_id=1, source_target_pairs={{0,8},{1,9},{2,10},{3,11},{4,12},{5,13},{6,14},{7,15},{8,0},{9,1},... | collective-permute-start | bytes 221192 | tf_op jit(solution)/shard_map/ppermute | solution.py:341
  7.9 3.0 %shard_map.78 = (bf16[30,256,256]{2,1,0:T(8,128)(2,1)S(1)}, bf16[15,256,256]{2,1,0:T(8,128)(2,1)S(1)}, bf16[30,512,128]{2,1,0:T(8,128)(2,1)S(1)}) custom-call(bf16[30,256,256]{2,1,0:T(8,128)(2,1)} %couple_ref.1, s32[30,512]{1,0:T(8,128)} %bitcast.4, s32[1,512]{1,0:T(1,128)S(1)} %get-tuple-element.15.after_ref.class_ref), custom_call_target="tpu_custom_call" | custom-call | bytes 7864320 | tf_op jit(solution)/shard_map/pallas_call | solution.py:360
  11.0 0.0 collective-permute-done.2.top_ref
  11.0 0.5 %collective-permute-done.3.far_ref = bf16[144,256]{1,0:T(8,128)(2,1)S(1)} collective-permute-done((bf16[144,256]{1,0:T(8,128)(2,1)S(1)}, bf16[144,256]{1,0:T(8,128)(2,1)S(1)}, u32[]{:S(2)}, u32[]{:S(2)}) %collective-permute-start.3) | collective-permute-done | bytes 73760 | tf_op jit(solution)/shard_map/ppermute | solution.py:341
  11.5 0.0 collective-permute-done.4.beside_ref
  11.5 0.0 collective-permute-done.both_ref.far_ref
  11.5 0.1 collective-permute-start.5
  11.6 0.2 shard_map.80.after_ref.refs_0_
  11.8 1.6 %collective-permute-start.6 = (bf16[272,128]{1,0:T(8,128)(2,1)S(1)}, bf16[272,128]{1,0:T(8,128)(2,1)S(1)}, u32[]{:S(2)}, u32[]{:S(2)}) collective-permute-start(bf16[272,128]{1,0:T(8,128)(2,1)S(1)} %shard_map.80.after_ref.refs_0_), channel_id=1, source_target_pairs={{0,2},{1,3},{2,0},{3,1},{4,6},{5,7},{6,4},{7,5},{8,10},{9,11},{10,... | collective-permute-start | bytes 208904 | tf_op jit(solution)/shard_map/ppermute | solution.py:341
  13.4 2.5 %collective-permute-start.7 = (bf16[272,128]{1,0:T(8,128)(2,1)S(1)}, bf16[272,128]{1,0:T(8,128)(2,1)S(1)}, u32[]{:S(2)}, u32[]{:S(2)}) collective-permute-start(bf16[272,128]{1,0:T(8,128)(2,1)S(1)} %shard_map.80.after_ref.refs_0_), channel_id=1, source_target_pairs={{0,6},{1,7},{2,4},{3,5},{4,2},{5,3},{6,0},{7,1},{8,14},{9,15},{10,... | collective-permute-start | bytes 208904 | tf_op jit(solution)/shard_map/ppermute | solution.py:341
  15.9 0.1 collective-permute-start.8
  16.0 0.0 collective-permute-done.5.refs_1_.refs_5_
  16.0 2.5 %shard_map.81 = (f32[32,512]{1,0:T(8,128)S(1)}, bf16[32,512]{1,0:T(8,128)(2,1)S(1)}, bf16[32,512]{1,0:T(8,128)(2,1)S(1)}, bf16[32,512]{1,0:T(8,128)(2,1)S(1)}) custom-call(bf16[2,32,512]{2,1,0:T(8,128)(2,1)S(1)} %get-tuple-element.13.both_ref, bf16[80,512]{1,0:T(8,128)(2,1)S(1)} %collective-permute-done.both_ref.far_ref, ...), custom_call_target="tpu_custom_call" | custom-call | flops 2550136832 | bytes 4980736 | tf_op jit(solution)/shard_map/pallas_call | solution.py:432
  18.5 3.0 %collective-permute-start.9 = (bf16[32,512]{1,0:T(8,128)(2,1)S(1)}, bf16[32,512]{1,0:T(8,128)(2,1)S(1)}, u32[]{:S(2)}, u32[]{:S(2)}) collective-permute-start(bf16[32,512]{1,0:T(8,128)(2,1)S(1)} %get-tuple-element.21), channel_id=1, source_target_pairs={{0,6},{1,7},{2,4},{3,5},{4,2},{5,3},{6,0},{7,1},{8,14},{9,15},{10,... | collective-permute-start | bytes 98312 | tf_op jit(solution)/shard_map/ppermute | solution.py:341
  21.5 0.3 %collective-permute-start.10 = (bf16[32,512]{1,0:T(8,128)(2,1)S(1)}, bf16[32,512]{1,0:T(8,128)(2,1)S(1)}, u32[]{:S(2)}, u32[]{:S(2)}) collective-permute-start(bf16[32,512]{1,0:T(8,128)(2,1)S(1)} %get-tuple-element.22), channel_id=1, source_target_pairs={{0,4},{1,5},{2,6},{3,7},{4,0},{5,1},{6,2},{7,3},{8,12},{9,13},{10,... | collective-permute-start | bytes 98312 | tf_op jit(solution)/shard_map/ppermute | solution.py:341
  21.8 1.1 %collective-permute-start.11 = (bf16[32,512]{1,0:T(8,128)(2,1)S(1)}, bf16[32,512]{1,0:T(8,128)(2,1)S(1)}, u32[]{:S(2)}, u32[]{:S(2)}) collective-permute-start(bf16[32,512]{1,0:T(8,128)(2,1)S(1)} %get-tuple-element.23), channel_id=1, source_target_pairs={{0,2},{1,3},{2,0},{3,1},{4,6},{5,7},{6,4},{7,5},{8,10},{9,11},{10,... | collective-permute-start | bytes 98312 | tf_op jit(solution)/shard_map/ppermute | solution.py:341
  23.0 3.1 %shard_map.82.forward_ref = bf16[32,512]{1,0:T(8,128)(2,1)S(1)} custom-call(bf16[2,32,512]{2,1,0:T(8,128)(2,1)S(1)} %get-tuple-element.13.both_ref, s32[1,512]{1,0:T(1,128)S(1)} %get-tuple-element.15.after_ref.class_ref, bf16[30,512,128]{2,1,0:T(8,128)(2,1)S(1)} %get-tuple-element.16.spread_ref, ...), custom_call_target="tpu_custom_call" | custom-call | flops 2550136832 | bytes 4980736 | tf_op jit(solution)/shard_map/pallas_call | solution.py:449
  26.1 0.4 %collective-permute-done.10.refs_1_ = bf16[32,512]{1,0:T(8,128)(2,1)S(1)} collective-permute-done((bf16[32,512]{1,0:T(8,128)(2,1)S(1)}, bf16[32,512]{1,0:T(8,128)(2,1)S(1)}, u32[]{:S(2)}, u32[]{:S(2)}) %collective-permute-start.10) | collective-permute-done | bytes 32800 | tf_op jit(solution)/shard_map/ppermute | solution.py:341
  26.6 0.6 %shard_map.83 = (bf16[32,512]{1,0:T(8,128)(2,1)}, bf16[32,512]{1,0:T(8,128)(2,1)}) custom-call(bf16[2,32,512]{2,1,0:T(8,128)(2,1)S(1)} %get-tuple-element.13.both_ref, f32[32,512]{1,0:T(8,128)S(1)} %get-tuple-element.20.keep_ref, bf16[32,512]{1,0:T(8,128)(2,1)S(1)} %shard_map.82.forward_ref, bf16[32,512]{1,0:T(8,128)(2,1)S(1)} %collective-permute-done.9.refs_0_, ...), custom_call_target="tpu_custom_call" | custom-call | tf_op jit(solution)/shard_map/pallas_call | solution.py:462
  (7 shorter events, 0.0 us)
Async XLA Ops:
  1.6 9.9 %collective-permute-start = (bf16[80,512]{1,0:T(8,128)(2,1)S(1)}, bf16[80,512]{1,0:T(8,128)(2,1)S(1)}, u32[]{:S(2)}, u32[]{:S(2)}) collective-permute-start(bf16[80,512]{1,0:T(8,128)(2,1)S(1)} %get-tuple-element.14), channel_id=1, source_target_pairs={{0,1},{1,0},{2,3},{3,2},{4,5},{5,4},{6,7},{7,6},{8,9},{9,8},{10,11... | collective-permute-start | bytes 245768 | tf_op jit(solution)/shard_map/ppermute | solution.py:341
  4.6 6.4 %collective-permute-start.1 = (bf16[144,256]{1,0:T(8,128)(2,1)S(1)}, bf16[144,256]{1,0:T(8,128)(2,1)S(1)}, u32[]{:S(2)}, u32[]{:S(2)}) collective-permute-start(bf16[144,256]{1,0:T(8,128)(2,1)S(1)} %get-tuple-element.18.near_ref), channel_id=1, source_target_pairs={{0,25},{1,24},{2,27},{3,26},{4,29},{5,28},{6,31},{7,30},{8,17},{9,... | collective-permute-start | bytes 221192 | tf_op jit(solution)/shard_map/ppermute | solution.py:341
  5.3 5.8 %collective-permute-start.2 = (bf16[144,256]{1,0:T(8,128)(2,1)S(1)}, bf16[144,256]{1,0:T(8,128)(2,1)S(1)}, u32[]{:S(2)}, u32[]{:S(2)}) collective-permute-start(bf16[144,256]{1,0:T(8,128)(2,1)S(1)} %get-tuple-element.18.near_ref), channel_id=1, source_target_pairs={{0,24},{1,25},{2,26},{3,27},{4,28},{5,29},{6,30},{7,31},{8,16},{9,... | collective-permute-start | bytes 221192 | tf_op jit(solution)/shard_map/ppermute | solution.py:341
  5.9 5.6 %collective-permute-start.3 = (bf16[144,256]{1,0:T(8,128)(2,1)S(1)}, bf16[144,256]{1,0:T(8,128)(2,1)S(1)}, u32[]{:S(2)}, u32[]{:S(2)}) collective-permute-start(bf16[144,256]{1,0:T(8,128)(2,1)S(1)} %get-tuple-element.18.near_ref), channel_id=1, source_target_pairs={{0,9},{1,8},{2,11},{3,10},{4,13},{5,12},{6,15},{7,14},{8,1},{9,0},... | collective-permute-start | bytes 221192 | tf_op jit(solution)/shard_map/ppermute | solution.py:341
  7.3 4.2 %collective-permute-start.4 = (bf16[144,256]{1,0:T(8,128)(2,1)S(1)}, bf16[144,256]{1,0:T(8,128)(2,1)S(1)}, u32[]{:S(2)}, u32[]{:S(2)}) collective-permute-start(bf16[144,256]{1,0:T(8,128)(2,1)S(1)} %get-tuple-element.18.near_ref), channel_id=1, source_target_pairs={{0,8},{1,9},{2,10},{3,11},{4,12},{5,13},{6,14},{7,15},{8,0},{9,1},... | collective-permute-start | bytes 221192 | tf_op jit(solution)/shard_map/ppermute | solution.py:341
  11.5 4.5 %collective-permute-start.5 = (bf16[4,144,256]{2,1,0:T(8,128)(2,1)S(1)}, bf16[4,144,256]{2,1,0:T(8,128)(2,1)S(1)}, u32[]{:S(2)}, u32[]{:S(2)}) collective-permute-start(bf16[4,144,256]{2,1,0:T(8,128)(2,1)S(1)} %shard_map.79.refs_0_.refs_4_), channel_id=1, source_target_pairs={{0,8},{1,9},{2,10},{3,11},{4,12},{5,13},{6,14},{7,15},{8,0},{9,1},... | collective-permute-start | bytes 884744 | tf_op jit(solution)/shard_map/ppermute | solution.py:341
  11.8 10.1 %collective-permute-start.6 = (bf16[272,128]{1,0:T(8,128)(2,1)S(1)}, bf16[272,128]{1,0:T(8,128)(2,1)S(1)}, u32[]{:S(2)}, u32[]{:S(2)}) collective-permute-start(bf16[272,128]{1,0:T(8,128)(2,1)S(1)} %shard_map.80.after_ref.refs_0_), channel_id=1, source_target_pairs={{0,2},{1,3},{2,0},{3,1},{4,6},{5,7},{6,4},{7,5},{8,10},{9,11},{10,... | collective-permute-start | bytes 208904 | tf_op jit(solution)/shard_map/ppermute | solution.py:341
  13.4 9.6 %collective-permute-start.7 = (bf16[272,128]{1,0:T(8,128)(2,1)S(1)}, bf16[272,128]{1,0:T(8,128)(2,1)S(1)}, u32[]{:S(2)}, u32[]{:S(2)}) collective-permute-start(bf16[272,128]{1,0:T(8,128)(2,1)S(1)} %shard_map.80.after_ref.refs_0_), channel_id=1, source_target_pairs={{0,6},{1,7},{2,4},{3,5},{4,2},{5,3},{6,0},{7,1},{8,14},{9,15},{10,... | collective-permute-start | bytes 208904 | tf_op jit(solution)/shard_map/ppermute | solution.py:341
  15.9 7.1 %collective-permute-start.8 = (bf16[272,128]{1,0:T(8,128)(2,1)S(1)}, bf16[272,128]{1,0:T(8,128)(2,1)S(1)}, u32[]{:S(2)}, u32[]{:S(2)}) collective-permute-start(bf16[272,128]{1,0:T(8,128)(2,1)S(1)} %shard_map.80.after_ref.refs_0_), channel_id=1, source_target_pairs={{0,4},{1,5},{2,6},{3,7},{4,0},{5,1},{6,2},{7,3},{8,12},{9,13},{10,... | collective-permute-start | bytes 208904 | tf_op jit(solution)/shard_map/ppermute | solution.py:341
  18.5 7.6 %collective-permute-start.9 = (bf16[32,512]{1,0:T(8,128)(2,1)S(1)}, bf16[32,512]{1,0:T(8,128)(2,1)S(1)}, u32[]{:S(2)}, u32[]{:S(2)}) collective-permute-start(bf16[32,512]{1,0:T(8,128)(2,1)S(1)} %get-tuple-element.21), channel_id=1, source_target_pairs={{0,6},{1,7},{2,4},{3,5},{4,2},{5,3},{6,0},{7,1},{8,14},{9,15},{10,... | collective-permute-start | bytes 98312 | tf_op jit(solution)/shard_map/ppermute | solution.py:341
  21.5 5.1 %collective-permute-start.10 = (bf16[32,512]{1,0:T(8,128)(2,1)S(1)}, bf16[32,512]{1,0:T(8,128)(2,1)S(1)}, u32[]{:S(2)}, u32[]{:S(2)}) collective-permute-start(bf16[32,512]{1,0:T(8,128)(2,1)S(1)} %get-tuple-element.22), channel_id=1, source_target_pairs={{0,4},{1,5},{2,6},{3,7},{4,0},{5,1},{6,2},{7,3},{8,12},{9,13},{10,... | collective-permute-start | bytes 98312 | tf_op jit(solution)/shard_map/ppermute | solution.py:341
  21.8 4.7 %collective-permute-start.11 = (bf16[32,512]{1,0:T(8,128)(2,1)S(1)}, bf16[32,512]{1,0:T(8,128)(2,1)S(1)}, u32[]{:S(2)}, u32[]{:S(2)}) collective-permute-start(bf16[32,512]{1,0:T(8,128)(2,1)S(1)} %get-tuple-element.23), channel_id=1, source_target_pairs={{0,2},{1,3},{2,0},{3,1},{4,6},{5,7},{6,4},{7,5},{8,10},{9,11},{10,... | collective-permute-start | bytes 98312 | tf_op jit(solution)/shard_map/ppermute | solution.py:341

commit v12 on v11

--- a/solution.py
+++ b/solution.py
@@ -169,20 +169,6 @@
     linked.start()
     for copy in copies:
         copy.start()
-    linked.wait()
-    weights[...] = jnp.zeros_like(weights)
-    weights[:SLOTS, :] = jnp.where(links[...] >= 0, 1.0, 0.0)
-    filled = weights[...].astype(BF16)
-    row = lax.broadcasted_iota(jnp.int32, (filled.shape[0], 2 * EDGE), 0)
-    lane = lax.broadcasted_iota(jnp.int32, (filled.shape[0], 2 * EDGE), 1)
-    for pair in range(SLOTS // 2):
-        chosen = row == 2 * pair + (lane >= EDGE).astype(jnp.int32)
-        unit = jnp.where(chosen, 1.0, 0.0).astype(BF16)
-        spread = lax.dot_general(
-            filled, unit, (((0,), (0,)), ((), ())), preferred_element_type=F32
-        ).astype(BF16)
-        spread_ref[2 * pair] = spread[:, :EDGE]
-        spread_ref[2 * pair + 1] = spread[:, EDGE:]
     depth = mats_ref.shape[1]
     odd = find_place()[1]
     lane = lax.broadcasted_iota(jnp.int32, (depth, EDGE), 1)
@@ -190,6 +176,21 @@
     second = (1.0 - first).astype(BF16)
     shift = jnp.where(odd == 1, EDGE - rows, rows)
     for chunk, copy in enumerate(copies):
+        if chunk == 1:
+            linked.wait()
+            weights[...] = jnp.zeros_like(weights)
+            weights[:SLOTS, :] = jnp.where(links[...] >= 0, 1.0, 0.0)
+            filled = weights[...].astype(BF16)
+            row = lax.broadcasted_iota(jnp.int32, (filled.shape[0], 2 * EDGE), 0)
+            lane = lax.broadcasted_iota(jnp.int32, (filled.shape[0], 2 * EDGE), 1)
+            for pair in range(SLOTS // 2):
+                chosen = row == 2 * pair + (lane >= EDGE).astype(jnp.int32)
+                unit = jnp.where(chosen, 1.0, 0.0).astype(BF16)
+                spread = lax.dot_general(
+                    filled, unit, (((0,), (0,)), ((), ())), preferred_element_type=F32
+                ).astype(BF16)
+                spread_ref[2 * pair] = spread[:, :EDGE]
+                spread_ref[2 * pair + 1] = spread[:, EDGE:]
         copy.wait()
         for mat in range(chunk * CHUNK, (chunk + 1) * CHUNK):
             moved = pltpu.roll(mats_ref[mat, :, EDGE : 2 * EDGE], shift, 1)

time: 27.4 us -> 27.4 us (level)
  Pallas kernels: 10.5 us -> 10.8 us
  waiting for transfers between devices: 0.96 us -> 0.66 us
    ppermute x12, waiting for transfers between devices: 0.96 us -> 0.66 us  [swap(): return lax.ppermute(cells, ('tiles', 'coef'), pairs)]
    pallas_call x1, Pallas kernels: 3.05 us -> 3.34 us  [local(): pl.pallas_call(functools.partial(prepare_kernel, rows), out_shape=(jax.Sh...]
  transfers between devices with their start and end apart: 12 -> 12, of which waited for: 2 -> 2; matrix products, arithmetic and copies ran while one was open for 0% -> 0% of each run, Pallas kernels for 33% -> 34%
where the time goes in v12:
time: 27.4 us; the launch traced here: 27.2 us
  starting transfers between devices  15.1 us (55%)
  Pallas kernels  10.8 us (39%)
  between operations  0.7 us (3%)
  waiting for transfers between devices  0.66 us (2%)
    ppermute x12, starting transfers between devices, swap(): return lax.ppermute(cells, ('tiles', 'coef'), pairs)  15.1 us
    pallas_call x1, Pallas kernels, local(): pl.pallas_call(functools.partial(prepare_kernel, rows), out_shape=(jax.Sh...  3.34 us
    pallas_call x1, Pallas kernels, local(): pl.pallas_call(functools.partial(forward_kernel, spots, count, rels), out...  3.15 us
    pallas_call x1, Pallas kernels, local(): pl.pallas_call(functools.partial(adjoint_kernel, spots, count, groups), o...  2.54 us
    pallas_call x1, Pallas kernels, local(): pl.pallas_call(pack_kernel, out_shape=(jax.ShapeDtypeStruct((near_rows, d...  0.96 us
    ppermute x12, waiting for transfers between devices, swap(): return lax.ppermute(cells, ('tiles', 'coef'), pairs)  0.66 us
    pallas_call x1, Pallas kernels, local(): pl.pallas_call(finish_kernel, out_shape=(jax.ShapeDtypeStruct((rows, widt...  0.64 us
  transfers between devices with their start and end apart: 12, of which 2 were waited for; matrix products, arithmetic and copies ran while one was open for 0% of the time, Pallas kernels for 34%

profile of v12, /device:TPU:0, one launch (start us, length us, event | category | flops | bytes accessed | tf_op | source)
XLA Modules:
  0.0 27.2 jit_solution(4619465351050389027)
XLA Ops:
  0.6 1.0 %shard_map.77 = (bf16[144,256]{1,0:T(8,128)(2,1)S(1)}, bf16[2,32,512]{2,1,0:T(8,128)(2,1)S(1)}, bf16[80,512]{1,0:T(8,128)(2,1)S(1)}, s32[1,512]{1,0:T(1,128)S(1)}) custom-call(bf16[4,32,256]{2,1,0:T(8,128)(2,1)} %t_any.1, bf16[32,512]{1,0:T(8,128)(2,1)} %f_any.1, bf16[32,512]{1,0:T(8,128)(2,1)} %a_any.1, s32[1,512]{1,0:T(1,128)} %bitcast.5), custom_call_target="tpu_custom_call" | custom-call | tf_op jit(solution)/shard_map/pallas_call | solution.py:348
  1.6 3.0 %collective-permute-start = (bf16[80,512]{1,0:T(8,128)(2,1)S(1)}, bf16[80,512]{1,0:T(8,128)(2,1)S(1)}, u32[]{:S(2)}, u32[]{:S(2)}) collective-permute-start(bf16[80,512]{1,0:T(8,128)(2,1)S(1)} %get-tuple-element.14), channel_id=1, source_target_pairs={{0,1},{1,0},{2,3},{3,2},{4,5},{5,4},{6,7},{7,6},{8,9},{9,8},{10,11... | collective-permute-start | bytes 245768 | tf_op jit(solution)/shard_map/ppermute | solution.py:342
  4.6 0.7 %collective-permute-start.1 = (bf16[144,256]{1,0:T(8,128)(2,1)S(1)}, bf16[144,256]{1,0:T(8,128)(2,1)S(1)}, u32[]{:S(2)}, u32[]{:S(2)}) collective-permute-start(bf16[144,256]{1,0:T(8,128)(2,1)S(1)} %get-tuple-element.18.near_ref), channel_id=1, source_target_pairs={{0,25},{1,24},{2,27},{3,26},{4,29},{5,28},{6,31},{7,30},{8,17},{9,... | collective-permute-start | bytes 221192 | tf_op jit(solution)/shard_map/ppermute | solution.py:342
  5.3 0.6 %collective-permute-start.2 = (bf16[144,256]{1,0:T(8,128)(2,1)S(1)}, bf16[144,256]{1,0:T(8,128)(2,1)S(1)}, u32[]{:S(2)}, u32[]{:S(2)}) collective-permute-start(bf16[144,256]{1,0:T(8,128)(2,1)S(1)} %get-tuple-element.18.near_ref), channel_id=1, source_target_pairs={{0,24},{1,25},{2,26},{3,27},{4,28},{5,29},{6,30},{7,31},{8,16},{9,... | collective-permute-start | bytes 221192 | tf_op jit(solution)/shard_map/ppermute | solution.py:342
  5.9 1.4 %collective-permute-start.3 = (bf16[144,256]{1,0:T(8,128)(2,1)S(1)}, bf16[144,256]{1,0:T(8,128)(2,1)S(1)}, u32[]{:S(2)}, u32[]{:S(2)}) collective-permute-start(bf16[144,256]{1,0:T(8,128)(2,1)S(1)} %get-tuple-element.18.near_ref), channel_id=1, source_target_pairs={{0,9},{1,8},{2,11},{3,10},{4,13},{5,12},{6,15},{7,14},{8,1},{9,0},... | collective-permute-start | bytes 221192 | tf_op jit(solution)/shard_map/ppermute | solution.py:342
  7.3 0.6 %collective-permute-start.4 = (bf16[144,256]{1,0:T(8,128)(2,1)S(1)}, bf16[144,256]{1,0:T(8,128)(2,1)S(1)}, u32[]{:S(2)}, u32[]{:S(2)}) collective-permute-start(bf16[144,256]{1,0:T(8,128)(2,1)S(1)} %get-tuple-element.18.near_ref), channel_id=1, source_target_pairs={{0,8},{1,9},{2,10},{3,11},{4,12},{5,13},{6,14},{7,15},{8,0},{9,1},... | collective-permute-start | bytes 221192 | tf_op jit(solution)/shard_map/ppermute | solution.py:342
  7.9 3.3 %shard_map.78 = (bf16[30,256,256]{2,1,0:T(8,128)(2,1)S(1)}, bf16[15,256,256]{2,1,0:T(8,128)(2,1)S(1)}, bf16[30,512,128]{2,1,0:T(8,128)(2,1)S(1)}) custom-call(bf16[30,256,256]{2,1,0:T(8,128)(2,1)} %couple_ref.1, s32[30,512]{1,0:T(8,128)} %bitcast.4, s32[1,512]{1,0:T(1,128)S(1)} %get-tuple-element.15.after_ref.class_ref), custom_call_target="tpu_custom_call" | custom-call | bytes 7864320 | tf_op jit(solution)/shard_map/pallas_call | solution.py:361
  11.3 0.0 collective-permute-done.1.cross_ref
  11.3 0.0 collective-permute-done.2.top_ref
  11.3 0.2 collective-permute-done.3.far_ref
  11.5 0.0 collective-permute-done.4.beside_ref
  11.5 0.0 collective-permute-done.both_ref.far_ref
  11.5 0.1 collective-permute-start.5
  11.6 0.2 shard_map.80.after_ref.refs_0_
  11.8 1.6 %collective-permute-start.6 = (bf16[272,128]{1,0:T(8,128)(2,1)S(1)}, bf16[272,128]{1,0:T(8,128)(2,1)S(1)}, u32[]{:S(2)}, u32[]{:S(2)}) collective-permute-start(bf16[272,128]{1,0:T(8,128)(2,1)S(1)} %shard_map.80.after_ref.refs_0_), channel_id=1, source_target_pairs={{0,2},{1,3},{2,0},{3,1},{4,6},{5,7},{6,4},{7,5},{8,10},{9,11},{10,... | collective-permute-start | bytes 208904 | tf_op jit(solution)/shard_map/ppermute | solution.py:342
  13.4 2.5 %collective-permute-start.7 = (bf16[272,128]{1,0:T(8,128)(2,1)S(1)}, bf16[272,128]{1,0:T(8,128)(2,1)S(1)}, u32[]{:S(2)}, u32[]{:S(2)}) collective-permute-start(bf16[272,128]{1,0:T(8,128)(2,1)S(1)} %shard_map.80.after_ref.refs_0_), channel_id=1, source_target_pairs={{0,6},{1,7},{2,4},{3,5},{4,2},{5,3},{6,0},{7,1},{8,14},{9,15},{10,... | collective-permute-start | bytes 208904 | tf_op jit(solution)/shard_map/ppermute | solution.py:342
  15.9 0.1 collective-permute-start.8
  16.0 2.5 %shard_map.81 = (f32[32,512]{1,0:T(8,128)S(1)}, bf16[32,512]{1,0:T(8,128)(2,1)S(1)}, bf16[32,512]{1,0:T(8,128)(2,1)S(1)}, bf16[32,512]{1,0:T(8,128)(2,1)S(1)}) custom-call(bf16[2,32,512]{2,1,0:T(8,128)(2,1)S(1)} %get-tuple-element.13.both_ref, bf16[80,512]{1,0:T(8,128)(2,1)S(1)} %collective-permute-done.both_ref.far_ref, ...), custom_call_target="tpu_custom_call" | custom-call | flops 2550136832 | bytes 4980736 | tf_op jit(solution)/shard_map/pallas_call | solution.py:433
  18.5 3.0 %collective-permute-start.9 = (bf16[32,512]{1,0:T(8,128)(2,1)S(1)}, bf16[32,512]{1,0:T(8,128)(2,1)S(1)}, u32[]{:S(2)}, u32[]{:S(2)}) collective-permute-start(bf16[32,512]{1,0:T(8,128)(2,1)S(1)} %get-tuple-element.21), channel_id=1, source_target_pairs={{0,6},{1,7},{2,4},{3,5},{4,2},{5,3},{6,0},{7,1},{8,14},{9,15},{10,... | collective-permute-start | bytes 98312 | tf_op jit(solution)/shard_map/ppermute | solution.py:342
  21.5 0.3 %collective-permute-start.10 = (bf16[32,512]{1,0:T(8,128)(2,1)S(1)}, bf16[32,512]{1,0:T(8,128)(2,1)S(1)}, u32[]{:S(2)}, u32[]{:S(2)}) collective-permute-start(bf16[32,512]{1,0:T(8,128)(2,1)S(1)} %get-tuple-element.22), channel_id=1, source_target_pairs={{0,4},{1,5},{2,6},{3,7},{4,0},{5,1},{6,2},{7,3},{8,12},{9,13},{10,... | collective-permute-start | bytes 98312 | tf_op jit(solution)/shard_map/ppermute | solution.py:342
  21.8 1.1 %collective-permute-start.11 = (bf16[32,512]{1,0:T(8,128)(2,1)S(1)}, bf16[32,512]{1,0:T(8,128)(2,1)S(1)}, u32[]{:S(2)}, u32[]{:S(2)}) collective-permute-start(bf16[32,512]{1,0:T(8,128)(2,1)S(1)} %get-tuple-element.23), channel_id=1, source_target_pairs={{0,2},{1,3},{2,0},{3,1},{4,6},{5,7},{6,4},{7,5},{8,10},{9,11},{10,... | collective-permute-start | bytes 98312 | tf_op jit(solution)/shard_map/ppermute | solution.py:342
  23.0 3.1 %shard_map.82.forward_ref = bf16[32,512]{1,0:T(8,128)(2,1)S(1)} custom-call(bf16[2,32,512]{2,1,0:T(8,128)(2,1)S(1)} %get-tuple-element.13.both_ref, s32[1,512]{1,0:T(1,128)S(1)} %get-tuple-element.15.after_ref.class_ref, bf16[30,512,128]{2,1,0:T(8,128)(2,1)S(1)} %get-tuple-element.16.spread_ref, ...), custom_call_target="tpu_custom_call" | custom-call | flops 2550136832 | bytes 4980736 | tf_op jit(solution)/shard_map/pallas_call | solution.py:450
  26.1 0.4 %collective-permute-done.10.refs_1_ = bf16[32,512]{1,0:T(8,128)(2,1)S(1)} collective-permute-done((bf16[32,512]{1,0:T(8,128)(2,1)S(1)}, bf16[32,512]{1,0:T(8,128)(2,1)S(1)}, u32[]{:S(2)}, u32[]{:S(2)}) %collective-permute-start.10) | collective-permute-done | bytes 32800 | tf_op jit(solution)/shard_map/ppermute | solution.py:342
  26.6 0.6 %shard_map.83 = (bf16[32,512]{1,0:T(8,128)(2,1)}, bf16[32,512]{1,0:T(8,128)(2,1)}) custom-call(bf16[2,32,512]{2,1,0:T(8,128)(2,1)S(1)} %get-tuple-element.13.both_ref, f32[32,512]{1,0:T(8,128)S(1)} %get-tuple-element.20.keep_ref, bf16[32,512]{1,0:T(8,128)(2,1)S(1)} %shard_map.82.forward_ref, bf16[32,512]{1,0:T(8,128)(2,1)S(1)} %collective-permute-done.9.refs_0_, ...), custom_call_target="tpu_custom_call" | custom-call | tf_op jit(solution)/shard_map/pallas_call | solution.py:463
  (7 shorter events, 0.0 us)
Async XLA Ops:
  1.6 9.9 %collective-permute-start = (bf16[80,512]{1,0:T(8,128)(2,1)S(1)}, bf16[80,512]{1,0:T(8,128)(2,1)S(1)}, u32[]{:S(2)}, u32[]{:S(2)}) collective-permute-start(bf16[80,512]{1,0:T(8,128)(2,1)S(1)} %get-tuple-element.14), channel_id=1, source_target_pairs={{0,1},{1,0},{2,3},{3,2},{4,5},{5,4},{6,7},{7,6},{8,9},{9,8},{10,11... | collective-permute-start | bytes 245768 | tf_op jit(solution)/shard_map/ppermute | solution.py:342
  4.6 6.7 %collective-permute-start.1 = (bf16[144,256]{1,0:T(8,128)(2,1)S(1)}, bf16[144,256]{1,0:T(8,128)(2,1)S(1)}, u32[]{:S(2)}, u32[]{:S(2)}) collective-permute-start(bf16[144,256]{1,0:T(8,128)(2,1)S(1)} %get-tuple-element.18.near_ref), channel_id=1, source_target_pairs={{0,25},{1,24},{2,27},{3,26},{4,29},{5,28},{6,31},{7,30},{8,17},{9,... | collective-permute-start | bytes 221192 | tf_op jit(solution)/shard_map/ppermute | solution.py:342
  5.3 6.0 %collective-permute-start.2 = (bf16[144,256]{1,0:T(8,128)(2,1)S(1)}, bf16[144,256]{1,0:T(8,128)(2,1)S(1)}, u32[]{:S(2)}, u32[]{:S(2)}) collective-permute-start(bf16[144,256]{1,0:T(8,128)(2,1)S(1)} %get-tuple-element.18.near_ref), channel_id=1, source_target_pairs={{0,24},{1,25},{2,26},{3,27},{4,28},{5,29},{6,30},{7,31},{8,16},{9,... | collective-permute-start | bytes 221192 | tf_op jit(solution)/shard_map/ppermute | solution.py:342
  5.9 5.6 %collective-permute-start.3 = (bf16[144,256]{1,0:T(8,128)(2,1)S(1)}, bf16[144,256]{1,0:T(8,128)(2,1)S(1)}, u32[]{:S(2)}, u32[]{:S(2)}) collective-permute-start(bf16[144,256]{1,0:T(8,128)(2,1)S(1)} %get-tuple-element.18.near_ref), channel_id=1, source_target_pairs={{0,9},{1,8},{2,11},{3,10},{4,13},{5,12},{6,15},{7,14},{8,1},{9,0},... | collective-permute-start | bytes 221192 | tf_op jit(solution)/shard_map/ppermute | solution.py:342
  7.3 4.2 %collective-permute-start.4 = (bf16[144,256]{1,0:T(8,128)(2,1)S(1)}, bf16[144,256]{1,0:T(8,128)(2,1)S(1)}, u32[]{:S(2)}, u32[]{:S(2)}) collective-permute-start(bf16[144,256]{1,0:T(8,128)(2,1)S(1)} %get-tuple-element.18.near_ref), channel_id=1, source_target_pairs={{0,8},{1,9},{2,10},{3,11},{4,12},{5,13},{6,14},{7,15},{8,0},{9,1},... | collective-permute-start | bytes 221192 | tf_op jit(solution)/shard_map/ppermute | solution.py:342
  11.5 4.5 %collective-permute-start.5 = (bf16[4,144,256]{2,1,0:T(8,128)(2,1)S(1)}, bf16[4,144,256]{2,1,0:T(8,128)(2,1)S(1)}, u32[]{:S(2)}, u32[]{:S(2)}) collective-permute-start(bf16[4,144,256]{2,1,0:T(8,128)(2,1)S(1)} %shard_map.79.refs_0_.refs_4_), channel_id=1, source_target_pairs={{0,8},{1,9},{2,10},{3,11},{4,12},{5,13},{6,14},{7,15},{8,0},{9,1},... | collective-permute-start | bytes 884744 | tf_op jit(solution)/shard_map/ppermute | solution.py:342
  11.8 10.1 %collective-permute-start.6 = (bf16[272,128]{1,0:T(8,128)(2,1)S(1)}, bf16[272,128]{1,0:T(8,128)(2,1)S(1)}, u32[]{:S(2)}, u32[]{:S(2)}) collective-permute-start(bf16[272,128]{1,0:T(8,128)(2,1)S(1)} %shard_map.80.after_ref.refs_0_), channel_id=1, source_target_pairs={{0,2},{1,3},{2,0},{3,1},{4,6},{5,7},{6,4},{7,5},{8,10},{9,11},{10,... | collective-permute-start | bytes 208904 | tf_op jit(solution)/shard_map/ppermute | solution.py:342
  13.4 9.6 %collective-permute-start.7 = (bf16[272,128]{1,0:T(8,128)(2,1)S(1)}, bf16[272,128]{1,0:T(8,128)(2,1)S(1)}, u32[]{:S(2)}, u32[]{:S(2)}) collective-permute-start(bf16[272,128]{1,0:T(8,128)(2,1)S(1)} %shard_map.80.after_ref.refs_0_), channel_id=1, source_target_pairs={{0,6},{1,7},{2,4},{3,5},{4,2},{5,3},{6,0},{7,1},{8,14},{9,15},{10,... | collective-permute-start | bytes 208904 | tf_op jit(solution)/shard_map/ppermute | solution.py:342
  15.9 7.1 %collective-permute-start.8 = (bf16[272,128]{1,0:T(8,128)(2,1)S(1)}, bf16[272,128]{1,0:T(8,128)(2,1)S(1)}, u32[]{:S(2)}, u32[]{:S(2)}) collective-permute-start(bf16[272,128]{1,0:T(8,128)(2,1)S(1)} %shard_map.80.after_ref.refs_0_), channel_id=1, source_target_pairs={{0,4},{1,5},{2,6},{3,7},{4,0},{5,1},{6,2},{7,3},{8,12},{9,13},{10,... | collective-permute-start | bytes 208904 | tf_op jit(solution)/shard_map/ppermute | solution.py:342
  18.5 7.6 %collective-permute-start.9 = (bf16[32,512]{1,0:T(8,128)(2,1)S(1)}, bf16[32,512]{1,0:T(8,128)(2,1)S(1)}, u32[]{:S(2)}, u32[]{:S(2)}) collective-permute-start(bf16[32,512]{1,0:T(8,128)(2,1)S(1)} %get-tuple-element.21), channel_id=1, source_target_pairs={{0,6},{1,7},{2,4},{3,5},{4,2},{5,3},{6,0},{7,1},{8,14},{9,15},{10,... | collective-permute-start | bytes 98312 | tf_op jit(solution)/shard_map/ppermute | solution.py:342
  21.5 5.1 %collective-permute-start.10 = (bf16[32,512]{1,0:T(8,128)(2,1)S(1)}, bf16[32,512]{1,0:T(8,128)(2,1)S(1)}, u32[]{:S(2)}, u32[]{:S(2)}) collective-permute-start(bf16[32,512]{1,0:T(8,128)(2,1)S(1)} %get-tuple-element.22), channel_id=1, source_target_pairs={{0,4},{1,5},{2,6},{3,7},{4,0},{5,1},{6,2},{7,3},{8,12},{9,13},{10,... | collective-permute-start | bytes 98312 | tf_op jit(solution)/shard_map/ppermute | solution.py:342
  21.8 4.7 %collective-permute-start.11 = (bf16[32,512]{1,0:T(8,128)(2,1)S(1)}, bf16[32,512]{1,0:T(8,128)(2,1)S(1)}, u32[]{:S(2)}, u32[]{:S(2)}) collective-permute-start(bf16[32,512]{1,0:T(8,128)(2,1)S(1)} %get-tuple-element.23), channel_id=1, source_target_pairs={{0,2},{1,3},{2,0},{3,1},{4,6},{5,7},{6,4},{7,5},{8,10},{9,11},{10,... | collective-permute-start | bytes 98312 | tf_op jit(solution)/shard_map/ppermute | solution.py:342

commit v13 on v11

--- a/solution.py
+++ b/solution.py
@@ -10,7 +10,7 @@
 SLOTS = 30
 HW = 15
 EDGE = 128
-CHUNK = 5
+CHUNK = 10
 LEAD = 16
 BAND = 128
 A_SHIFT = 32

time: 27.4 us -> 27.4 us (level)
  transfers between devices with their start and end apart: 12 -> 12, of which waited for: 2 -> 3; matrix products, arithmetic and copies ran while one was open for 0% -> 0% of each run, Pallas kernels for 33% -> 32%
where the time goes in v13:
time: 27.4 us; the launch traced here: 27.2 us
  starting transfers between devices  15.1 us (55%)
  Pallas kernels  10.3 us (38%)
  waiting for transfers between devices  1.2 us (4%)
  between operations  0.69 us (3%)
    ppermute x12, starting transfers between devices, swap(): return lax.ppermute(cells, ('tiles', 'coef'), pairs)  15.1 us
    pallas_call x1, Pallas kernels, local(): pl.pallas_call(functools.partial(forward_kernel, spots, count, rels), out...  3.15 us
    pallas_call x1, Pallas kernels, local(): pl.pallas_call(functools.partial(prepare_kernel, rows), out_shape=(jax.Sh...  2.81 us
    pallas_call x1, Pallas kernels, local(): pl.pallas_call(functools.partial(adjoint_kernel, spots, count, groups), o...  2.54 us
    ppermute x12, waiting for transfers between devices, swap(): return lax.ppermute(cells, ('tiles', 'coef'), pairs)  1.2 us
    pallas_call x1, Pallas kernels, local(): pl.pallas_call(pack_kernel, out_shape=(jax.ShapeDtypeStruct((near_rows, d...  0.96 us
    pallas_call x1, Pallas kernels, local(): pl.pallas_call(finish_kernel, out_shape=(jax.ShapeDtypeStruct((rows, widt...  0.64 us
  transfers between devices with their start and end apart: 12, of which 3 were waited for; matrix products, arithmetic and copies ran while one was open for 0% of the time, Pallas kernels for 32%

profile of v13, /device:TPU:0, one launch (start us, length us, event | category | flops | bytes accessed | tf_op | source)
XLA Modules:
  0.0 27.2 jit_solution(2271442516037241745)
XLA Ops:
  0.6 1.0 %shard_map.77 = (bf16[144,256]{1,0:T(8,128)(2,1)S(1)}, bf16[2,32,512]{2,1,0:T(8,128)(2,1)S(1)}, bf16[80,512]{1,0:T(8,128)(2,1)S(1)}, s32[1,512]{1,0:T(1,128)S(1)}) custom-call(bf16[4,32,256]{2,1,0:T(8,128)(2,1)} %t_any.1, bf16[32,512]{1,0:T(8,128)(2,1)} %f_any.1, bf16[32,512]{1,0:T(8,128)(2,1)} %a_any.1, s32[1,512]{1,0:T(1,128)} %bitcast.5), custom_call_target="tpu_custom_call" | custom-call | tf_op jit(solution)/shard_map/pallas_call | solution.py:347
  1.6 3.0 %collective-permute-start = (bf16[80,512]{1,0:T(8,128)(2,1)S(1)}, bf16[80,512]{1,0:T(8,128)(2,1)S(1)}, u32[]{:S(2)}, u32[]{:S(2)}) collective-permute-start(bf16[80,512]{1,0:T(8,128)(2,1)S(1)} %get-tuple-element.14), channel_id=1, source_target_pairs={{0,1},{1,0},{2,3},{3,2},{4,5},{5,4},{6,7},{7,6},{8,9},{9,8},{10,11... | collective-permute-start | bytes 245768 | tf_op jit(solution)/shard_map/ppermute | solution.py:341
  4.6 0.7 %collective-permute-start.1 = (bf16[144,256]{1,0:T(8,128)(2,1)S(1)}, bf16[144,256]{1,0:T(8,128)(2,1)S(1)}, u32[]{:S(2)}, u32[]{:S(2)}) collective-permute-start(bf16[144,256]{1,0:T(8,128)(2,1)S(1)} %get-tuple-element.18.near_ref), channel_id=1, source_target_pairs={{0,25},{1,24},{2,27},{3,26},{4,29},{5,28},{6,31},{7,30},{8,17},{9,... | collective-permute-start | bytes 221192 | tf_op jit(solution)/shard_map/ppermute | solution.py:341
  5.3 0.6 %collective-permute-start.2 = (bf16[144,256]{1,0:T(8,128)(2,1)S(1)}, bf16[144,256]{1,0:T(8,128)(2,1)S(1)}, u32[]{:S(2)}, u32[]{:S(2)}) collective-permute-start(bf16[144,256]{1,0:T(8,128)(2,1)S(1)} %get-tuple-element.18.near_ref), channel_id=1, source_target_pairs={{0,24},{1,25},{2,26},{3,27},{4,28},{5,29},{6,30},{7,31},{8,16},{9,... | collective-permute-start | bytes 221192 | tf_op jit(solution)/shard_map/ppermute | solution.py:341
  5.9 1.4 %collective-permute-start.3 = (bf16[144,256]{1,0:T(8,128)(2,1)S(1)}, bf16[144,256]{1,0:T(8,128)(2,1)S(1)}, u32[]{:S(2)}, u32[]{:S(2)}) collective-permute-start(bf16[144,256]{1,0:T(8,128)(2,1)S(1)} %get-tuple-element.18.near_ref), channel_id=1, source_target_pairs={{0,9},{1,8},{2,11},{3,10},{4,13},{5,12},{6,15},{7,14},{8,1},{9,0},... | collective-permute-start | bytes 221192 | tf_op jit(solution)/shard_map/ppermute | solution.py:341
  7.3 0.6 %collective-permute-start.4 = (bf16[144,256]{1,0:T(8,128)(2,1)S(1)}, bf16[144,256]{1,0:T(8,128)(2,1)S(1)}, u32[]{:S(2)}, u32[]{:S(2)}) collective-permute-start(bf16[144,256]{1,0:T(8,128)(2,1)S(1)} %get-tuple-element.18.near_ref), channel_id=1, source_target_pairs={{0,8},{1,9},{2,10},{3,11},{4,12},{5,13},{6,14},{7,15},{8,0},{9,1},... | collective-permute-start | bytes 221192 | tf_op jit(solution)/shard_map/ppermute | solution.py:341
  7.9 2.8 %shard_map.78 = (bf16[30,256,256]{2,1,0:T(8,128)(2,1)S(1)}, bf16[15,256,256]{2,1,0:T(8,128)(2,1)S(1)}, bf16[30,512,128]{2,1,0:T(8,128)(2,1)S(1)}) custom-call(bf16[30,256,256]{2,1,0:T(8,128)(2,1)} %couple_ref.1, s32[30,512]{1,0:T(8,128)} %bitcast.4, s32[1,512]{1,0:T(1,128)S(1)} %get-tuple-element.15.after_ref.class_ref), custom_call_target="tpu_custom_call" | custom-call | bytes 7864320 | tf_op jit(solution)/shard_map/pallas_call | solution.py:360
  10.8 0.3 %collective-permute-done.2.top_ref = bf16[144,256]{1,0:T(8,128)(2,1)S(1)} collective-permute-done((bf16[144,256]{1,0:T(8,128)(2,1)S(1)}, bf16[144,256]{1,0:T(8,128)(2,1)S(1)}, u32[]{:S(2)}, u32[]{:S(2)}) %collective-permute-start.2) | collective-permute-done | bytes 73760 | tf_op jit(solution)/shard_map/ppermute | solution.py:341
  11.0 0.5 %collective-permute-done.3.far_ref = bf16[144,256]{1,0:T(8,128)(2,1)S(1)} collective-permute-done((bf16[144,256]{1,0:T(8,128)(2,1)S(1)}, bf16[144,256]{1,0:T(8,128)(2,1)S(1)}, u32[]{:S(2)}, u32[]{:S(2)}) %collective-permute-start.3) | collective-permute-done | bytes 73760 | tf_op jit(solution)/shard_map/ppermute | solution.py:341
  11.5 0.0 collective-permute-done.4.beside_ref
  11.5 0.0 collective-permute-done.both_ref.far_ref
  11.5 0.1 collective-permute-start.5
  11.6 0.2 shard_map.80.after_ref.refs_0_
  11.8 1.6 %collective-permute-start.6 = (bf16[272,128]{1,0:T(8,128)(2,1)S(1)}, bf16[272,128]{1,0:T(8,128)(2,1)S(1)}, u32[]{:S(2)}, u32[]{:S(2)}) collective-permute-start(bf16[272,128]{1,0:T(8,128)(2,1)S(1)} %shard_map.80.after_ref.refs_0_), channel_id=1, source_target_pairs={{0,2},{1,3},{2,0},{3,1},{4,6},{5,7},{6,4},{7,5},{8,10},{9,11},{10,... | collective-permute-start | bytes 208904 | tf_op jit(solution)/shard_map/ppermute | solution.py:341
  13.4 2.5 %collective-permute-start.7 = (bf16[272,128]{1,0:T(8,128)(2,1)S(1)}, bf16[272,128]{1,0:T(8,128)(2,1)S(1)}, u32[]{:S(2)}, u32[]{:S(2)}) collective-permute-start(bf16[272,128]{1,0:T(8,128)(2,1)S(1)} %shard_map.80.after_ref.refs_0_), channel_id=1, source_target_pairs={{0,6},{1,7},{2,4},{3,5},{4,2},{5,3},{6,0},{7,1},{8,14},{9,15},{10,... | collective-permute-start | bytes 208904 | tf_op jit(solution)/shard_map/ppermute | solution.py:341
  15.9 0.1 collective-permute-start.8
  16.0 0.0 collective-permute-done.5.refs_1_.refs_5_
  16.0 2.5 %shard_map.81 = (f32[32,512]{1,0:T(8,128)S(1)}, bf16[32,512]{1,0:T(8,128)(2,1)S(1)}, bf16[32,512]{1,0:T(8,128)(2,1)S(1)}, bf16[32,512]{1,0:T(8,128)(2,1)S(1)}) custom-call(bf16[2,32,512]{2,1,0:T(8,128)(2,1)S(1)} %get-tuple-element.13.both_ref, bf16[80,512]{1,0:T(8,128)(2,1)S(1)} %collective-permute-done.both_ref.far_ref, ...), custom_call_target="tpu_custom_call" | custom-call | flops 2550136832 | bytes 4980736 | tf_op jit(solution)/shard_map/pallas_call | solution.py:432
  18.5 3.0 %collective-permute-start.9 = (bf16[32,512]{1,0:T(8,128)(2,1)S(1)}, bf16[32,512]{1,0:T(8,128)(2,1)S(1)}, u32[]{:S(2)}, u32[]{:S(2)}) collective-permute-start(bf16[32,512]{1,0:T(8,128)(2,1)S(1)} %get-tuple-element.21), channel_id=1, source_target_pairs={{0,6},{1,7},{2,4},{3,5},{4,2},{5,3},{6,0},{7,1},{8,14},{9,15},{10,... | collective-permute-start | bytes 98312 | tf_op jit(solution)/shard_map/ppermute | solution.py:341
  21.5 0.3 %collective-permute-start.10 = (bf16[32,512]{1,0:T(8,128)(2,1)S(1)}, bf16[32,512]{1,0:T(8,128)(2,1)S(1)}, u32[]{:S(2)}, u32[]{:S(2)}) collective-permute-start(bf16[32,512]{1,0:T(8,128)(2,1)S(1)} %get-tuple-element.22), channel_id=1, source_target_pairs={{0,4},{1,5},{2,6},{3,7},{4,0},{5,1},{6,2},{7,3},{8,12},{9,13},{10,... | collective-permute-start | bytes 98312 | tf_op jit(solution)/shard_map/ppermute | solution.py:341
  21.8 1.1 %collective-permute-start.11 = (bf16[32,512]{1,0:T(8,128)(2,1)S(1)}, bf16[32,512]{1,0:T(8,128)(2,1)S(1)}, u32[]{:S(2)}, u32[]{:S(2)}) collective-permute-start(bf16[32,512]{1,0:T(8,128)(2,1)S(1)} %get-tuple-element.23), channel_id=1, source_target_pairs={{0,2},{1,3},{2,0},{3,1},{4,6},{5,7},{6,4},{7,5},{8,10},{9,11},{10,... | collective-permute-start | bytes 98312 | tf_op jit(solution)/shard_map/ppermute | solution.py:341
  23.0 3.1 %shard_map.82.forward_ref = bf16[32,512]{1,0:T(8,128)(2,1)S(1)} custom-call(bf16[2,32,512]{2,1,0:T(8,128)(2,1)S(1)} %get-tuple-element.13.both_ref, s32[1,512]{1,0:T(1,128)S(1)} %get-tuple-element.15.after_ref.class_ref, bf16[30,512,128]{2,1,0:T(8,128)(2,1)S(1)} %get-tuple-element.16.spread_ref, ...), custom_call_target="tpu_custom_call" | custom-call | flops 2550136832 | bytes 4980736 | tf_op jit(solution)/shard_map/pallas_call | solution.py:449
  26.1 0.4 %collective-permute-done.10.refs_1_ = bf16[32,512]{1,0:T(8,128)(2,1)S(1)} collective-permute-done((bf16[32,512]{1,0:T(8,128)(2,1)S(1)}, bf16[32,512]{1,0:T(8,128)(2,1)S(1)}, u32[]{:S(2)}, u32[]{:S(2)}) %collective-permute-start.10) | collective-permute-done | bytes 32800 | tf_op jit(solution)/shard_map/ppermute | solution.py:341
  26.6 0.6 %shard_map.83 = (bf16[32,512]{1,0:T(8,128)(2,1)}, bf16[32,512]{1,0:T(8,128)(2,1)}) custom-call(bf16[2,32,512]{2,1,0:T(8,128)(2,1)S(1)} %get-tuple-element.13.both_ref, f32[32,512]{1,0:T(8,128)S(1)} %get-tuple-element.20.keep_ref, bf16[32,512]{1,0:T(8,128)(2,1)S(1)} %shard_map.82.forward_ref, bf16[32,512]{1,0:T(8,128)(2,1)S(1)} %collective-permute-done.9.refs_0_, ...), custom_call_target="tpu_custom_call" | custom-call | tf_op jit(solution)/shard_map/pallas_call | solution.py:462
  (7 shorter events, 0.0 us)
Async XLA Ops:
  1.6 9.9 %collective-permute-start = (bf16[80,512]{1,0:T(8,128)(2,1)S(1)}, bf16[80,512]{1,0:T(8,128)(2,1)S(1)}, u32[]{:S(2)}, u32[]{:S(2)}) collective-permute-start(bf16[80,512]{1,0:T(8,128)(2,1)S(1)} %get-tuple-element.14), channel_id=1, source_target_pairs={{0,1},{1,0},{2,3},{3,2},{4,5},{5,4},{6,7},{7,6},{8,9},{9,8},{10,11... | collective-permute-start | bytes 245768 | tf_op jit(solution)/shard_map/ppermute | solution.py:341
  4.6 6.1 %collective-permute-start.1 = (bf16[144,256]{1,0:T(8,128)(2,1)S(1)}, bf16[144,256]{1,0:T(8,128)(2,1)S(1)}, u32[]{:S(2)}, u32[]{:S(2)}) collective-permute-start(bf16[144,256]{1,0:T(8,128)(2,1)S(1)} %get-tuple-element.18.near_ref), channel_id=1, source_target_pairs={{0,25},{1,24},{2,27},{3,26},{4,29},{5,28},{6,31},{7,30},{8,17},{9,... | collective-permute-start | bytes 221192 | tf_op jit(solution)/shard_map/ppermute | solution.py:341
  5.3 5.8 %collective-permute-start.2 = (bf16[144,256]{1,0:T(8,128)(2,1)S(1)}, bf16[144,256]{1,0:T(8,128)(2,1)S(1)}, u32[]{:S(2)}, u32[]{:S(2)}) collective-permute-start(bf16[144,256]{1,0:T(8,128)(2,1)S(1)} %get-tuple-element.18.near_ref), channel_id=1, source_target_pairs={{0,24},{1,25},{2,26},{3,27},{4,28},{5,29},{6,30},{7,31},{8,16},{9,... | collective-permute-start | bytes 221192 | tf_op jit(solution)/shard_map/ppermute | solution.py:341
  5.9 5.6 %collective-permute-start.3 = (bf16[144,256]{1,0:T(8,128)(2,1)S(1)}, bf16[144,256]{1,0:T(8,128)(2,1)S(1)}, u32[]{:S(2)}, u32[]{:S(2)}) collective-permute-start(bf16[144,256]{1,0:T(8,128)(2,1)S(1)} %get-tuple-element.18.near_ref), channel_id=1, source_target_pairs={{0,9},{1,8},{2,11},{3,10},{4,13},{5,12},{6,15},{7,14},{8,1},{9,0},... | collective-permute-start | bytes 221192 | tf_op jit(solution)/shard_map/ppermute | solution.py:341
  7.3 4.2 %collective-permute-start.4 = (bf16[144,256]{1,0:T(8,128)(2,1)S(1)}, bf16[144,256]{1,0:T(8,128)(2,1)S(1)}, u32[]{:S(2)}, u32[]{:S(2)}) collective-permute-start(bf16[144,256]{1,0:T(8,128)(2,1)S(1)} %get-tuple-element.18.near_ref), channel_id=1, source_target_pairs={{0,8},{1,9},{2,10},{3,11},{4,12},{5,13},{6,14},{7,15},{8,0},{9,1},... | collective-permute-start | bytes 221192 | tf_op jit(solution)/shard_map/ppermute | solution.py:341
  11.5 4.5 %collective-permute-start.5 = (bf16[4,144,256]{2,1,0:T(8,128)(2,1)S(1)}, bf16[4,144,256]{2,1,0:T(8,128)(2,1)S(1)}, u32[]{:S(2)}, u32[]{:S(2)}) collective-permute-start(bf16[4,144,256]{2,1,0:T(8,128)(2,1)S(1)} %shard_map.79.refs_0_.refs_4_), channel_id=1, source_target_pairs={{0,8},{1,9},{2,10},{3,11},{4,12},{5,13},{6,14},{7,15},{8,0},{9,1},... | collective-permute-start | bytes 884744 | tf_op jit(solution)/shard_map/ppermute | solution.py:341
  11.8 10.1 %collective-permute-start.6 = (bf16[272,128]{1,0:T(8,128)(2,1)S(1)}, bf16[272,128]{1,0:T(8,128)(2,1)S(1)}, u32[]{:S(2)}, u32[]{:S(2)}) collective-permute-start(bf16[272,128]{1,0:T(8,128)(2,1)S(1)} %shard_map.80.after_ref.refs_0_), channel_id=1, source_target_pairs={{0,2},{1,3},{2,0},{3,1},{4,6},{5,7},{6,4},{7,5},{8,10},{9,11},{10,... | collective-permute-start | bytes 208904 | tf_op jit(solution)/shard_map/ppermute | solution.py:341
  13.4 9.6 %collective-permute-start.7 = (bf16[272,128]{1,0:T(8,128)(2,1)S(1)}, bf16[272,128]{1,0:T(8,128)(2,1)S(1)}, u32[]{:S(2)}, u32[]{:S(2)}) collective-permute-start(bf16[272,128]{1,0:T(8,128)(2,1)S(1)} %shard_map.80.after_ref.refs_0_), channel_id=1, source_target_pairs={{0,6},{1,7},{2,4},{3,5},{4,2},{5,3},{6,0},{7,1},{8,14},{9,15},{10,... | collective-permute-start | bytes 208904 | tf_op jit(solution)/shard_map/ppermute | solution.py:341
  15.9 7.1 %collective-permute-start.8 = (bf16[272,128]{1,0:T(8,128)(2,1)S(1)}, bf16[272,128]{1,0:T(8,128)(2,1)S(1)}, u32[]{:S(2)}, u32[]{:S(2)}) collective-permute-start(bf16[272,128]{1,0:T(8,128)(2,1)S(1)} %shard_map.80.after_ref.refs_0_), channel_id=1, source_target_pairs={{0,4},{1,5},{2,6},{3,7},{4,0},{5,1},{6,2},{7,3},{8,12},{9,13},{10,... | collective-permute-start | bytes 208904 | tf_op jit(solution)/shard_map/ppermute | solution.py:341
  18.5 7.6 %collective-permute-start.9 = (bf16[32,512]{1,0:T(8,128)(2,1)S(1)}, bf16[32,512]{1,0:T(8,128)(2,1)S(1)}, u32[]{:S(2)}, u32[]{:S(2)}) collective-permute-start(bf16[32,512]{1,0:T(8,128)(2,1)S(1)} %get-tuple-element.21), channel_id=1, source_target_pairs={{0,6},{1,7},{2,4},{3,5},{4,2},{5,3},{6,0},{7,1},{8,14},{9,15},{10,... | collective-permute-start | bytes 98312 | tf_op jit(solution)/shard_map/ppermute | solution.py:341
  21.5 5.1 %collective-permute-start.10 = (bf16[32,512]{1,0:T(8,128)(2,1)S(1)}, bf16[32,512]{1,0:T(8,128)(2,1)S(1)}, u32[]{:S(2)}, u32[]{:S(2)}) collective-permute-start(bf16[32,512]{1,0:T(8,128)(2,1)S(1)} %get-tuple-element.22), channel_id=1, source_target_pairs={{0,4},{1,5},{2,6},{3,7},{4,0},{5,1},{6,2},{7,3},{8,12},{9,13},{10,... | collective-permute-start | bytes 98312 | tf_op jit(solution)/shard_map/ppermute | solution.py:341
  21.8 4.7 %collective-permute-start.11 = (bf16[32,512]{1,0:T(8,128)(2,1)S(1)}, bf16[32,512]{1,0:T(8,128)(2,1)S(1)}, u32[]{:S(2)}, u32[]{:S(2)}) collective-permute-start(bf16[32,512]{1,0:T(8,128)(2,1)S(1)} %get-tuple-element.23), channel_id=1, source_target_pairs={{0,2},{1,3},{2,0},{3,1},{4,6},{5,7},{6,4},{7,5},{8,10},{9,11},{10,... | collective-permute-start | bytes 98312 | tf_op jit(solution)/shard_map/ppermute | solution.py:341
